TPU v7x, 32 devices: a whole 2x2x4 slice. The times are simulated.
32 devices in a mesh: dp: 4 (over y, x), shard: 8 (over z, core).
Axes of the slice: x: 2, y: 2, z: 4, core: 2. Of those that a mesh axis runs over, the one named last changes fastest.
Arguments:
- frames: bfloat16 [128, 64, 1536], P(('dp', 'shard')), may hold values from -6 to 6
- cotangent: bfloat16 [128, 64, 1536], P(('dp', 'shard')), may hold values from -6 to 6
- lengths: int32 [128], P(('dp', 'shard')), may hold values from 1 to 64, 6144 in all
- send_order: int32 [128], P(('dp', 'shard')), may hold values from 0 to 3, as said below
- norm_gain: bfloat16 [1536], P('shard'), may hold values from 0.099609375 to 1.8984375
- conv_bias: bfloat16 [1536], P('shard'), may hold values from -3 to 3
- kernel: bfloat16 [1536, 31], P('shard'), may hold values from -1 to 1
- expand_weight: bfloat16 [1536, 3072], P('shard'), may hold values from -0.15625 to 0.15625
- project_weight: bfloat16 [1536, 1536], P('shard'), may hold values from -0.15625 to 0.15625
Outputs:
- encoded: bfloat16 [128, 64, 1536], P(('dp', 'shard'))
- frame_grad: bfloat16 [128, 64, 1536], P(('dp', 'shard'))
- gain_grad: float32 [1536], P('shard')
- bias_grad: float32 [1536], P('shard')
- kernel_grad: float32 [1536, 31], P('shard')
- expand_grad: float32 [1536, 3072], P('shard')
- project_grad: float32 [1536, 1536], P('shard')
Inputs may be any that keep to these rules, and one draw needn't show every extreme that they name: `send_order`: each aligned block of 4 entries, the utterances of one device, is a permutation of 0 to 3. `lengths`: at least one utterance has exactly 64 live frames.
All inputs are finite; a program needn't handle non-finite values. No bound on the sum of `lengths` on one device may be relied on, other than what follows from the above.
Results may differ from a plain program's by a relative error of at most 0.03.
Values may be sent and summed in bfloat16 or wider, within the bound.
No kernel may reach another device: no remote copies, remote signals or barrier semaphores. Data moves between devices by JAX's collectives and lax.ppermute only.
A program may use at most 128 MiB of HBM per device.

v0:
```python
import jax
import jax.numpy as jnp
from jax import lax
from jax.sharding import PartitionSpec as P

EPS = 1e-05


def depthwise(signal, taps_table):
    taps = taps_table.shape[1]
    half = (taps - 1) // 2
    length = signal.shape[1]
    padded = jnp.pad(signal, ((0, 0), (half, half), (0, 0)))
    result = jnp.zeros_like(signal)
    for offset in range(taps):
        result = result + padded[:, offset : offset + length, :] * taps_table[:, offset]
    return result


def kernel_terms(signal, upstream, taps):
    half = (taps - 1) // 2
    length = signal.shape[1]
    padded = jnp.pad(signal, ((0, 0), (half, half), (0, 0)))
    columns = []
    for offset in range(taps):
        columns.append(jnp.sum(padded[:, offset : offset + length, :] * upstream, axis=(0, 1)))
    return jnp.stack(columns, axis=1)


def block_local(
    frames, cotangent, live, norm_gain, conv_bias, kernel, expand_weight, project_weight
):
    count, length, width = frames.shape
    total_rows = count * length
    inputs = frames.reshape(total_rows, width).astype(jnp.float32)
    live_rows = live.reshape(total_rows, 1)
    centre = jnp.mean(inputs, axis=1, keepdims=True)
    centred = inputs - centre
    variance = jnp.mean(centred * centred, axis=1, keepdims=True)
    inverse = lax.rsqrt(variance + EPS)
    standard = centred * inverse
    complete_gain = norm_gain.astype(jnp.float32)
    normed = (standard * complete_gain).astype(jnp.bfloat16)
    expanded = jnp.dot(normed, expand_weight, preferred_element_type=jnp.float32)
    value_portion = expanded[:, :width]
    gate_sig = jax.nn.sigmoid(expanded[:, width:])
    glu_out = (value_portion * gate_sig * live_rows).astype(jnp.bfloat16)
    taps_full = kernel.astype(jnp.float32)
    glu_cube = glu_out.astype(jnp.float32).reshape(count, length, width)
    conv_out = depthwise(glu_cube, taps_full).reshape(total_rows, width) + conv_bias.astype(
        jnp.float32
    )
    conv_sig = jax.nn.sigmoid(conv_out)
    swished = (conv_out * conv_sig).astype(jnp.bfloat16)
    projected = jnp.dot(swished, project_weight, preferred_element_type=jnp.float32)
    encoded = (inputs + projected * live_rows).astype(jnp.bfloat16)
    upstream = cotangent.reshape(total_rows, width).astype(jnp.float32)
    masked = (upstream * live_rows).astype(jnp.bfloat16)
    project_part = jnp.dot(swished.T, masked, preferred_element_type=jnp.float32)
    grad_swish = jnp.dot(masked, project_weight.T, preferred_element_type=jnp.float32)
    grad_conv = grad_swish * conv_sig * (1.0 + conv_out * (1.0 - conv_sig))
    bias_portion = jnp.sum(grad_conv, axis=0)
    gradient_volume = grad_conv.reshape(count, length, width)
    kernel_part = kernel_terms(glu_cube, gradient_volume, kernel.shape[1])
    grad_glu = depthwise(gradient_volume, taps_full[:, ::-1]).reshape(total_rows, width) * live_rows
    grad_expanded = jnp.concatenate(
        [grad_glu * gate_sig, grad_glu * value_portion * gate_sig * (1.0 - gate_sig)], axis=1
    ).astype(jnp.bfloat16)
    expand_part = jnp.dot(normed.T, grad_expanded, preferred_element_type=jnp.float32)
    grad_normed = jnp.dot(grad_expanded, expand_weight.T, preferred_element_type=jnp.float32)
    gain_part = jnp.sum(grad_normed * standard, axis=0)
    grad_standard = grad_normed * complete_gain
    grad_inputs = inverse * (
        grad_standard
        - jnp.mean(grad_standard, axis=1, keepdims=True)
        - standard * jnp.mean(grad_standard * standard, axis=1, keepdims=True)
    )
    frame_grad = (upstream + grad_inputs).astype(jnp.bfloat16)
    return (
        encoded.reshape(count, length, width),
        frame_grad.reshape(count, length, width),
        (gain_part, bias_portion, kernel_part, expand_part, project_part),
    )


def body(
    frames,
    cotangent,
    lengths,
    send_order,
    norm_gain,
    conv_bias,
    kernel,
    expand_weight,
    project_weight,
):
    count, length, width = frames.shape
    positions = lax.broadcasted_iota(jnp.int32, (count, length), 1)
    live = (positions < lengths[:, None]).astype(jnp.bfloat16)
    arrived_frames, arrived_cot, arrived_live = (
        lax.all_to_all(
            jnp.take(frames, send_order, axis=0), "dp", split_axis=0, concat_axis=0, tiled=True
        ),
        lax.all_to_all(
            jnp.take(cotangent, send_order, axis=0), "dp", split_axis=0, concat_axis=0, tiled=True
        ),
        lax.all_to_all(
            jnp.take(live, send_order, axis=0), "dp", split_axis=0, concat_axis=0, tiled=True
        ),
    )
    full_gain, full_bias, full_kernel, full_expand, full_project = (
        lax.all_gather(norm_gain, "shard", axis=0, tiled=True),
        lax.all_gather(conv_bias, "shard", axis=0, tiled=True),
        lax.all_gather(kernel, "shard", axis=0, tiled=True),
        lax.all_gather(expand_weight, "shard", axis=0, tiled=True),
        lax.all_gather(project_weight, "shard", axis=0, tiled=True),
    )
    encoded, balanced_grad, parts = block_local(
        arrived_frames,
        arrived_cot,
        arrived_live.astype(jnp.float32),
        full_gain,
        full_bias,
        full_kernel,
        full_expand,
        full_project,
    )
    returned_result = lax.all_to_all(balanced_grad, "dp", split_axis=0, concat_axis=0, tiled=True)
    placement_plan = (
        send_order[None, :] == lax.broadcasted_iota(jnp.int32, (count, count), 0)
    ).astype(jnp.bfloat16)
    frame_grad = jnp.einsum(
        "kp,pfh->kfh", placement_plan, returned_result, preferred_element_type=jnp.float32
    ).astype(jnp.bfloat16)
    reduced = (
        lax.psum_scatter(
            parts[0].astype(jnp.bfloat16), "shard", scatter_dimension=0, tiled=True
        ).astype(jnp.float32),
        lax.psum_scatter(
            parts[1].astype(jnp.bfloat16), "shard", scatter_dimension=0, tiled=True
        ).astype(jnp.float32),
        lax.psum_scatter(
            parts[2].astype(jnp.bfloat16), "shard", scatter_dimension=0, tiled=True
        ).astype(jnp.float32),
        lax.psum_scatter(
            parts[3].astype(jnp.bfloat16), "shard", scatter_dimension=0, tiled=True
        ).astype(jnp.float32),
        lax.psum_scatter(
            parts[4].astype(jnp.bfloat16), "shard", scatter_dimension=0, tiled=True
        ).astype(jnp.float32),
    )
    grads = (
        lax.psum(reduced[0].astype(jnp.bfloat16), "dp").astype(jnp.float32),
        lax.psum(reduced[1].astype(jnp.bfloat16), "dp").astype(jnp.float32),
        lax.psum(reduced[2].astype(jnp.bfloat16), "dp").astype(jnp.float32),
        lax.psum(reduced[3].astype(jnp.bfloat16), "dp").astype(jnp.float32),
        lax.psum(reduced[4].astype(jnp.bfloat16), "dp").astype(jnp.float32),
    )
    return (encoded, frame_grad, grads[0], grads[1], grads[2], grads[3], grads[4])


def solution(mesh):
    return jax.shard_map(
        body,
        mesh=mesh,
        in_specs=(
            P(("dp", "shard"), None, None),
            P(("dp", "shard"), None, None),
            P(("dp", "shard")),
            P(("dp", "shard")),
            P("shard"),
            P("shard"),
            P("shard", None),
            P("shard", None),
            P("shard", None),
        ),
        out_specs=(
            P(("dp", "shard"), None, None),
            P(("dp", "shard"), None, None),
            P("shard"),
            P("shard"),
            P("shard", None),
            P("shard", None),
            P("shard", None),
        ),
        check_vma=False,
    )
```

profile of v0, /device:TPU:8, one launch (start us, length us, event | category | flops | bytes accessed | tf_op | source)
XLA Modules:
  0.0 420.2 jit_solution(11593709705989450863)
XLA Ops:
  7.3 0.7 all-gather.4.cloned.1.call-update
  8.0 0.7 all-gather.6.cloned.1.call-update
  8.8 0.6 gather_fusion
  9.5 0.6 copy.25
  10.0 3.7 all-to-all-start.1
  13.8 0.6 gather_fusion.2
  14.4 0.6 gather_fusion.1
  15.0 0.6 fusion.86
  16.3 0.2 dynamic-update-slice
  16.6 0.2 dynamic-update-slice.1
  16.8 14.6 %all-gather = bf16[8,192,31]{1,2,0:T(8,128)(2,1)S(1)} all-gather(bf16[1,192,31]{1,2,0:T(8,128)(2,1)S(1)} %bitcast.88), channel_id=1, replica_groups=mesh['dp'=4,'shard'=8] {'shard'}, dimensions={0}, use_global_device_ids=true | all-gather | bytes 107136 | tf_op jit(solution)/shard_map/all_gather | solution.py:114
  31.4 1.3 broadcast_select_fusion
  32.7 14.1 %all-reduce.7 = (bf16[1536]{0:T(1024)(128)(2,1)S(1)}, bf16[1536]{0:T(1024)(128)(2,1)S(1)}) all-reduce(bf16[1536]{0:T(1024)(128)(2,1)S(1)} %dynamic-update-slice, bf16[1536]{0:T(1024)(128)(2,1)S(1)} %dynamic-update-slice.1), channel_id=1, replica_groups=mesh['dp'=4,'shard'=8] {'shard'}, use_global_device_ids=true, to_apply=%add.2 | all-reduce | flops 3072 | bytes 12288
  46.9 4.3 %all-to-all-start = ((bf16[4,64,1536]{2,1,0:T(8,128)(2,1)}), bf16[4,64,1536]{2,1,0:T(8,128)(2,1)S(1)}, u32[]{:S(2)}, u32[]{:S(2)}) async-start(bf16[4,64,1536]{2,1,0:T(8,128)(2,1)} %get-tuple-element.118), calls=%async_computation | async-start | bytes 1572864 | tf_op jit(solution)/shard_map/all_to_all | solution.py:101
  51.2 0.1 copy_convert_fusion
  51.3 0.1 reshape.247
  51.4 0.2 slice_reduce_fusion.29
  51.6 0.3 slice_reduce_fusion.30
  51.9 0.1 reshape.209
  52.0 11.0 %all-to-all-done = bf16[4,64,1536]{2,1,0:T(8,128)(2,1)S(1)} async-done(((bf16[4,64,1536]{2,1,0:T(8,128)(2,1)}), bf16[4,64,1536]{2,1,0:T(8,128)(2,1)S(1)}, u32[]{:S(2)}, u32[]{:S(2)}) %all-to-all-start) | async-done | bytes 786464 | tf_op jit(solution)/shard_map/all_to_all | solution.py:101
  63.0 4.2 all-to-all-start.2
  67.2 0.2 convert_reduce_fusion
  67.4 0.1 div.24
  67.5 0.4 multiply_reduce_fusion.33
  67.9 0.1 rsqrt.12
  67.9 0.3 multiply_convert_fusion.5
  68.3 32.2 %all-gather.4.cloned.1.call-done = bf16[1536,3072]{1,0:T(8,128)(2,1)} async-done(((bf16[192,3072]{1,0:T(8,128)(2,1)}), bf16[1536,3072]{1,0:T(8,128)(2,1)}) %all-gather.4.cloned.1.call-update) | async-done | bytes 9437200 | tf_op jit(solution)/shard_map/all_gather | solution.py:115
  100.5 7.9 %fusion.87 = f32[256,3072]{1,0:T(8,128)} fusion(bf16[256,1536]{1,0:T(8,128)(2,1)S(1)} %multiply_convert_fusion.5, bf16[1536,3072]{1,0:T(8,128)(2,1)} %all-gather.4.cloned.1.call-done), kind=kOutput, calls=%fused_computation.250 | convolution fusion | flops 2415919104 | bytes 13369344 | tf_op jit(solution)/shard_map/dot_general | solution.py:44
  108.4 3.6 fusion.67
  112.0 5.8 %multiply_add_fusion = f32[4,64,1536]{2,1,0:T(8,128)S(1)} fusion(f32[4,64,1536]{2,1,0:T(8,128)S(1)} %bitcast.83, f32[1536]{0:T(1024)S(1)} %get-tuple-element.72, f32[1536]{0:T(1024)S(1)} %get-tuple-element.73, f32[1536]{0:T(1024)S(1)} %get-tuple-element.74, f32[1536]{0:T(1024)S(1)} %get-tuple-element.75, f32[1536]{0:T(1024)S(1)} %get-tuple-element.76, ...), kind=kLoop, calls=%fused_computation.184 | loop fusion | flops 23986176 | bytes 3336192 | tf_op jit(solution)/shard_map/add | solution.py:16
  117.9 1.1 copy-done.4
  119.0 5.0 %bitcast_convert_fusion = bf16[1536,1536]{1,0:T(8,128)(2,1)} fusion(f32[4,64,1536]{2,1,0:T(8,128)S(1)} %multiply_add_fusion, bf16[4,64,1536]{2,1,0:T(8,128)(2,1)} %all-to-all-done.2, f32[4,64]{1,0:T(4,128)S(1)} %bitcast.89, f32[1536]{0:T(1024)S(1)} %convert_element_type.132), kind=kOutput, calls=%fused_computation.64 | convolution fusion | flops 1213857792 | bytes 7085056 | tf_op jit(solution)/shard_map/dot_general | solution.py:59
  124.1 0.2 reduce-scatter.6.cloned.1.call-start
  124.3 2.8 bitcast_add_fusion.1
  127.1 26.2 %all-gather.6.cloned.1.call-done = bf16[1536,1536]{1,0:T(8,128)(2,1)} async-done(((bf16[192,1536]{1,0:T(8,128)(2,1)}), bf16[1536,1536]{1,0:T(8,128)(2,1)}) %all-gather.6.cloned.1.call-update) | async-done | bytes 4718608 | tf_op jit(solution)/shard_map/all_gather | solution.py:116
  153.3 4.8 %multiply_reduce_fusion.15 = (bf16[1536]{0:T(1024)(128)(2,1)S(1)}, bf16[1536]{0:T(1024)(128)(2,1)S(1)}, f32[256,1536]{1,0:T(8,128)S(1)}) fusion(f32[256,1536]{1,0:T(8,128)S(1)} %get-tuple-element.114, f32[256,1536]{1,0:T(8,128)} %bitcast_add_fusion.1, bf16[256,1536]{1,0:T(8,128)(2,1)} %get-tuple-element.113, ...), kind=kOutput, calls=%fused_computation.162 | convolution fusion | flops 1212281856 | bytes 10229760 | tf_op jit(solution)/shard_map/dot_general | solution.py:60
  158.0 5.9 %fusion.55 = f32[4,64,1536]{2,1,0:T(8,128)S(1)} fusion(f32[4,64,1536]{2,1,0:T(8,128)S(1)} %bitcast.87, f32[1536]{0:T(1024)S(1)} %get-tuple-element.72, f32[1536]{0:T(1024)S(1)} %get-tuple-element.73, f32[1536]{0:T(1024)S(1)} %get-tuple-element.74, f32[1536]{0:T(1024)S(1)} %get-tuple-element.75, f32[1536]{0:T(1024)S(1)} %get-tuple-element.76, ...), kind=kLoop, calls=%fused_computation.123 | loop fusion | flops 23986176 | bytes 3336192 | tf_op jit(solution)/shard_map/add | solution.py:16
  164.0 0.9 multiply_convert_fusion.2
  164.9 0.9 copy-done.7
  165.8 0.3 copy-done.9
  166.1 5.2 %convolution_convert_fusion = bf16[1536,3072]{1,0:T(8,128)(2,1)} fusion(bf16[256,1536]{1,0:T(8,128)(2,1)S(1)} %copy-done.6, bf16[256,1536]{1,0:T(8,128)(2,1)S(1)} %get-tuple-element.112, bf16[256,1536]{1,0:T(8,128)(2,1)S(1)} %get-tuple-element.111), kind=kOutput, calls=%fused_computation.3 | convolution fusion | flops 2423783424 | bytes 11796480 | tf_op jit(solution)/shard_map/dot_general | solution.py:69
  171.4 3.6 multiply_reduce_fusion.1
  175.0 3.7 multiply_reduce_fusion
  179.2 0.3 stack.159
  179.6 1.0 copy.29
  181.2 26.4 %reduce-scatter.8.cloned.1.call-done = bf16[192,1536]{1,0:T(8,128)(2,1)} async-done(((bf16[1536,1536]{1,0:T(8,128)(2,1)}), bf16[192,1536]{1,0:T(8,128)(2,1)}) %reduce-scatter.8.cloned.1.call-update) | async-done | bytes 589840 | tf_op jit(solution)/shard_map/reduce_scatter | solution.py:148
  207.6 100.5 %reduce-scatter.6.cloned.1.call-done = bf16[192,3072]{1,0:T(8,128)(2,1)} async-done(((bf16[1536,3072]{1,0:T(8,128)(2,1)}), bf16[192,3072]{1,0:T(8,128)(2,1)}) %reduce-scatter.6.cloned.1.call-update) | async-done | bytes 1179664 | tf_op jit(solution)/shard_map/reduce_scatter | solution.py:145
  308.1 7.7 %multiply_reduce_fusion.31 = (bf16[1536]{0:T(1024)(128)(2,1)S(1)}, f32[256]{0:T(256)S(1)}, f32[256]{0:T(256)S(1)}, f32[256,1536]{1,0:T(8,128)}) fusion(bf16[4,64,1536]{2,1,0:T(8,128)(2,1)S(1)} %all-to-all-done, f32[256]{0:T(256)S(1)} %rsqrt.12, f32[256]{0:T(256)S(1)} %div.24, f32[1536]{0:T(1024)S(1)} %convert_element_type.124, ...), kind=kOutput, calls=%fused_computation.178 | convolution fusion | flops 2422601728 | bytes 13382656 | tf_op jit(solution)/shard_map/dot_general | solution.py:70
  315.8 13.5 %all-reduce.6 = (bf16[1536]{0:T(1024)(128)(2,1)S(1)}, bf16[1536]{0:T(1024)(128)(2,1)S(1)}) all-reduce(bf16[1536]{0:T(1024)(128)(2,1)S(1)} %get-tuple-element.66, bf16[1536]{0:T(1024)(128)(2,1)S(1)} %get-tuple-element.70), channel_id=2, replica_groups=mesh['dp'=4,'shard'=8] {'shard'}, use_global_device_ids=true, to_apply=%region_5.7.clone | all-reduce | flops 3072 | bytes 12288
  329.4 0.1 dynamic-slice.3
  329.5 0.1 dynamic-slice.5
  329.6 3.2 fusion.68
  332.8 4.3 %all-to-all-start.3 = ((bf16[4,64,1536]{2,1,0:T(8,128)(2,1)}), bf16[4,64,1536]{2,1,0:T(8,128)(2,1)}, u32[]{:S(2)}, u32[]{:S(2)}) async-start(bf16[4,64,1536]{2,1,0:T(8,128)(2,1)} %bitcast.11), calls=%async_computation.3 | async-start | bytes 1572864 | tf_op jit(solution)/shard_map/all_to_all | solution.py:128
  337.1 4.7 %fusion.2 = bf16[256,1536]{1,0:T(8,128)(2,1)} fusion(bf16[1536,1536]{1,0:T(8,128)(2,1)} %all-gather.6.cloned.1.call-done, f32[256,1536]{1,0:T(8,128)S(1)} %copy-done.11, f32[256]{0:T(256)S(1)} %reshape.209, bf16[256,1536]{1,0:T(8,128)(2,1)S(1)} %bitcast.86), kind=kOutput, calls=%fused_computation.69 | convolution fusion | flops 1211498496 | bytes 7865344 | tf_op jit(solution)/shard_map/dot_general | solution.py:55
  341.8 0.9 copy.30
  342.7 17.2 %all-reduce.8 = (bf16[192]{0:T(256)(128)(2,1)S(1)}, bf16[192]{0:T(256)(128)(2,1)S(1)}, bf16[192,31]{0,1:T(8,128)(2,1)S(1)}) all-reduce(bf16[192]{0:T(256)(128)(2,1)S(1)} %dynamic-slice.3, bf16[192]{0:T(256)(128)(2,1)S(1)} %dynamic-slice.5, bf16[192,31]{0,1:T(8,128)(2,1)S(1)} %copy.30), channel_id=1, replica_groups=mesh['dp'=4,'shard'=8] {'dp'}, use_global_device_ids=true, to_apply=%region_6.8 | all-reduce | flops 6336 | bytes 25344 | tf_op jit(solution)/shard_map/psum | solution.py:153
  359.9 0.6 convert_element_type.141
  360.5 0.6 convert_element_type.143
  361.0 0.6 convert_element_type.144
  361.7 1.8 convolution_convert_fusion.1
  363.5 1.0 copy.28
  364.5 44.7 %all-reduce.12.cloned.1.call-done = (bf16[192,3072]{1,0:T(8,128)(2,1)}, bf16[192,1536]{1,0:T(8,128)(2,1)}) async-done(((bf16[192,3072]{1,0:T(8,128)(2,1)}, bf16[192,1536]{1,0:T(8,128)(2,1)}), (bf16[192,3072]{1,0:T(8,128)(2,1)}, bf16[192,1536]{1,0:T(8,128)(2,1)})) %all-reduce.12.cloned.1.call-update) | async-done | bytes 1769488 | tf_op jit(solution)/shard_map/psum | solution.py:156
  409.2 3.0 convert_element_type.146
  412.2 1.1 convert_element_type.153
  (95 shorter events, 0.8 us)
Async XLA Ops:
  7.2 6.6 %copy-start = (bf16[4,64,1536]{2,1,0:T(8,128)(2,1)S(1)}, bf16[4,64,1536]{2,1,0:T(8,128)(2,1)}, u32[]{:S(2)}) copy-start(bf16[4,64,1536]{2,1,0:T(8,128)(2,1)} %param.12) | copy-start | bytes 2359300
  7.2 1.5 copy-start.19
  7.2 1.5 copy-start.16
  7.2 7.2 %copy-start.12 = (bf16[4,64,1536]{2,1,0:T(8,128)(2,1)S(1)}, bf16[4,64,1536]{2,1,0:T(8,128)(2,1)}, u32[]{:S(2)}) copy-start(bf16[4,64,1536]{2,1,0:T(8,128)(2,1)} %param.11) | copy-start | bytes 2359300
  7.2 93.3 %all-gather.4.cloned.1.call-start = ((), (), s32[]{:S(2)}) async-start(), calls=%async_computation.7 | async-start | bytes 10616832 | tf_op jit(solution)/shard_map/all_gather | solution.py:115
  7.9 145.3 %all-gather.6.cloned.1.call-start = ((), (), s32[]{:S(2)}) async-start(), calls=%async_computation.8 | async-start | bytes 5308416 | tf_op jit(solution)/shard_map/all_gather | solution.py:116
  10.0 36.8 %all-to-all-start.1 = ((bf16[4,1,64]{2,1,0:T(2,128)(2,1)}), bf16[4,1,64]{2,1,0:T(2,128)(2,1)S(1)}, u32[]{:S(2)}, u32[]{:S(2)}) async-start(bf16[4,1,64]{2,1,0:T(2,128)(2,1)} %copy.25), calls=%async_computation.1 | async-start | bytes 4096 | tf_op jit(solution)/shard_map/all_to_all | solution.py:107
  13.8 1.3 copy-start.15
  13.8 2.5 copy-start.17
  13.8 2.8 copy-start.18
  13.8 3.0 copy-start.14
  46.9 16.1 %all-to-all-start = ((bf16[4,64,1536]{2,1,0:T(8,128)(2,1)}), bf16[4,64,1536]{2,1,0:T(8,128)(2,1)S(1)}, u32[]{:S(2)}, u32[]{:S(2)}) async-start(bf16[4,64,1536]{2,1,0:T(8,128)(2,1)} %get-tuple-element.118), calls=%async_computation | async-start | bytes 1572864 | tf_op jit(solution)/shard_map/all_to_all | solution.py:101
  63.0 45.4 %all-to-all-start.2 = ((bf16[4,64,1536]{2,1,0:T(8,128)(2,1)}), bf16[4,64,1536]{2,1,0:T(8,128)(2,1)}, u32[]{:S(2)}, u32[]{:S(2)}) async-start(bf16[4,64,1536]{2,1,0:T(8,128)(2,1)} %get-tuple-element.117), calls=%async_computation.2 | async-start | bytes 1572864 | tf_op jit(solution)/shard_map/all_to_all | solution.py:104
  67.2 140.4 %reduce-scatter.8.cloned.1.call-start = ((), (), s32[]{:S(2)}) async-start(), calls=%async_computation.10 | async-start | bytes 5308416 | tf_op jit(solution)/shard_map/reduce_scatter | solution.py:148
  68.3 40.1 %copy-start.5 = (bf16[256,1536]{1,0:T(8,128)(2,1)}, bf16[256,1536]{1,0:T(8,128)(2,1)S(1)}, u32[]{:S(2)}) copy-start(bf16[256,1536]{1,0:T(8,128)(2,1)S(1)} %multiply_convert_fusion.5) | copy-start | bytes 2359300
  117.9 1.1 copy-start.4
  124.1 184.0 %reduce-scatter.6.cloned.1.call-start = ((), (), s32[]{:S(2)}) async-start(), calls=%async_computation.9 | async-start | bytes 10616832 | tf_op jit(solution)/shard_map/reduce_scatter | solution.py:145
  158.0 6.0 %copy-start.1 = (f32[256,1536]{1,0:T(8,128)}, f32[256,1536]{1,0:T(8,128)S(1)}, u32[]{:S(2)}) copy-start(f32[256,1536]{1,0:T(8,128)S(1)} %get-tuple-element.120) | copy-start | bytes 4718596
  158.0 6.0 %copy-start.3 = (f32[256,3072]{1,0:T(8,128)S(1)}, f32[256,3072]{1,0:T(8,128)}, u32[]{:S(2)}) copy-start(f32[256,3072]{1,0:T(8,128)} %fusion.87) | copy-start | bytes 9437188
  164.0 2.1 copy-start.6
  164.9 0.9 copy-start.7
  164.9 1.1 copy-start.9
  171.3 170.5 %reduce-scatter.10.cloned.1.call-start = ((), (), s32[]{:S(2)}) async-start(), calls=%async_computation.11 | async-start | bytes 442368
  171.4 3.7 copy-start.2
  179.0 129.1 %copy-start.8 = (bf16[256,1536]{1,0:T(8,128)(2,1)S(1)}, bf16[256,1536]{1,0:T(8,128)(2,1)}, u32[]{:S(2)}) copy-start(bf16[256,1536]{1,0:T(8,128)(2,1)} %copy-done.7) | copy-start | bytes 2359300
  179.0 129.1 %copy-start.10 = (bf16[256,1536]{1,0:T(8,128)(2,1)S(1)}, bf16[256,1536]{1,0:T(8,128)(2,1)}, u32[]{:S(2)}) copy-start(bf16[256,1536]{1,0:T(8,128)(2,1)} %copy-done.9) | copy-start | bytes 2359300
  180.6 228.7 %all-reduce.12.cloned.1.call-start = ((), (), s32[]{:S(2)}) async-start(), calls=%async_computation.12 | async-start | bytes 3538944 | tf_op jit(solution)/shard_map/psum | solution.py:156
  332.8 4.3 %copy-start.11 = (f32[256,1536]{1,0:T(8,128)S(1)}, f32[256,1536]{1,0:T(8,128)}, u32[]{:S(2)}) copy-start(f32[256,1536]{1,0:T(8,128)} %bitcast_add_fusion.1) | copy-start | bytes 4718596
  332.8 28.9 %all-to-all-start.3 = ((bf16[4,64,1536]{2,1,0:T(8,128)(2,1)}), bf16[4,64,1536]{2,1,0:T(8,128)(2,1)}, u32[]{:S(2)}, u32[]{:S(2)}) async-start(bf16[4,64,1536]{2,1,0:T(8,128)(2,1)} %bitcast.11), calls=%async_computation.3 | async-start | bytes 1572864 | tf_op jit(solution)/shard_map/all_to_all | solution.py:128
  409.2 3.0 copy-start.13
Sparse Core Ops, SparseCore 0:
  9.7 90.7 all-gather.3
  102.1 51.0 all-gather.5
  155.6 51.9 reduce-scatter.7
  209.8 98.2 reduce-scatter.5
  310.8 28.2 reduce-scatter.9
  342.4 66.7 all-reduce.11
where the time goes:
time: 423 us; the launch traced here: 420 us
  waiting for transfers between devices  242 us (57%)
  blocking collectives  59.4 us (14%)
  other arithmetic  38.1 us (9%)
  matrix products  37.1 us (9%)
  starting transfers between devices  17 us (4%)
  between operations  16.1 us (4%)
  local copies, waits for them, and re-layouts  10.2 us (2%)
    reduce_scatter x1, waiting for transfers between devices, body(): lax.psum_scatter(parts[3].astype(jnp.bfloat16), 'shard', scatter_dimensio...  100 us
    psum x1, waiting for transfers between devices, body(): lax.psum(reduced[3].astype(jnp.bfloat16), 'dp').astype(jnp.float32)  44.7 us
    all_gather x1, waiting for transfers between devices, body(): lax.all_gather(expand_weight, 'shard', axis=0, tiled=True)  32.2 us
    unnamed x2, blocking collectives  27.6 us
    reduce_scatter x1, waiting for transfers between devices, body(): lax.psum_scatter(parts[4].astype(jnp.bfloat16), 'shard', scatter_dimensio...  26.4 us
    all_gather x1, waiting for transfers between devices, body(): lax.all_gather(project_weight, 'shard', axis=0, tiled=True)  26.2 us
    psum x1, blocking collectives, body(): lax.psum(reduced[0].astype(jnp.bfloat16), 'dp').astype(jnp.float32)  17.2 us
    all_gather x1, blocking collectives, body(): lax.all_gather(kernel, 'shard', axis=0, tiled=True)  14.6 us
  transfers between devices with their start and end apart: 10, of which 6 were waited for; matrix products, arithmetic and copies ran while one was open for 19% of the time, Pallas kernels for 0%

commit v1 on v0

v1 whole, which is shorter than its diff:
```python
import jax
import jax.numpy as jnp
from jax import lax
from jax.sharding import PartitionSpec as P

EPS = 1e-05
F32 = jnp.float32
BF16 = jnp.bfloat16


def depthwise(signal, taps_table):
    taps = taps_table.shape[0]
    half = (taps - 1) // 2
    length = signal.shape[1]
    padded = jnp.pad(signal, ((0, 0), (half, half), (0, 0)))
    result = jnp.zeros_like(signal)
    for offset in range(taps):
        result = result + padded[:, offset : offset + length, :] * taps_table[offset]
    return result


def kernel_terms(signal, upstream, taps):
    half = (taps - 1) // 2
    length = signal.shape[1]
    padded = jnp.pad(signal, ((0, 0), (half, half), (0, 0)))
    rows = []
    for offset in range(taps):
        rows.append(jnp.sum(padded[:, offset : offset + length, :] * upstream, axis=(0, 1)))
    return jnp.stack(rows, axis=0)


def chunk_compute(x, g, live, gain, taps, bias, expand_slice, project_slice):
    count, length, width = x.shape
    rows = count * length
    channels = taps.shape[1]
    inputs = x.reshape(rows, width).astype(F32)
    live_rows = live.reshape(rows, 1)
    centred = inputs - jnp.mean(inputs, axis=1, keepdims=True)
    variance = jnp.mean(centred * centred, axis=1, keepdims=True)
    standard = centred * lax.rsqrt(variance + EPS)
    normed = (standard * gain).astype(BF16)
    expanded = jnp.dot(normed, expand_slice, preferred_element_type=F32)
    value = expanded[:, :channels]
    gate = jax.nn.sigmoid(expanded[:, channels:])
    glu = (value * gate * live_rows).astype(BF16).astype(F32).reshape(count, length, channels)
    conv = depthwise(glu, taps).reshape(rows, channels) + bias
    conv_sig = jax.nn.sigmoid(conv)
    swished = (conv * conv_sig).astype(BF16)
    masked = (g.reshape(rows, width).astype(F32) * live_rows).astype(BF16)
    grad_swish = lax.dot_general(
        masked, project_slice, (((1,), (1,)), ((), ())), preferred_element_type=F32
    )
    grad_conv = grad_swish * conv_sig * (1.0 + conv * (1.0 - conv_sig))
    bias_part = jnp.sum(grad_conv, axis=0)
    volume = grad_conv.reshape(count, length, channels)
    kernel_part = kernel_terms(glu, volume, taps.shape[0])
    grad_glu = depthwise(volume, taps[::-1]).reshape(rows, channels) * live_rows
    grad_expanded = jnp.concatenate(
        [grad_glu * gate, grad_glu * value * gate * (1.0 - gate)], axis=1
    ).astype(BF16)
    grad_normed = lax.dot_general(
        grad_expanded, expand_slice, (((1,), (1,)), ((), ())), preferred_element_type=F32
    )
    gain_part = jnp.sum(grad_normed * standard, axis=0)
    return normed, masked, swished, grad_expanded, grad_normed.astype(BF16), (
        gain_part,
        bias_part,
        kernel_part,
    )


def swap(x, axis, size, k):
    return lax.ppermute(x, axis, [(p, p ^ k) for p in range(size)])


def gather_dp(x, n_dp):
    if n_dp == 4:
        half = x.shape[0] // 2
        along_x = swap(x, "dp", 4, 1)
        along_y = swap(x, "dp", 4, 2)
        far = jnp.concatenate(
            [swap(along_x[:half], "dp", 4, 2), swap(along_y[half:], "dp", 4, 1)], axis=0
        )
        return [x, along_x, along_y, far]
    return [x] + [swap(x, "dp", n_dp, k) for k in range(1, n_dp)]


def gather_shard(x, n_shard):
    if n_shard == 8:
        me = lax.axis_index("shard")
        chip, core = me // 2, me % 2
        blocks = [x] + [
            lax.ppermute(x, "shard", [(p, (p + 2 * k) % 8) for p in range(8)]) for k in (1, 2, 3)
        ]
        mine = jnp.stack(blocks)
        mine = jnp.take(mine, (chip - jnp.arange(4)) % 4, axis=0)
        other = swap(mine, "shard", 8, 1)
        pair = jnp.where(core == 0, jnp.stack([mine, other], 1), jnp.stack([other, mine], 1))
        return pair.reshape((8,) + x.shape)
    return lax.all_gather(x, "shard", axis=0)


def reduce_shard(x, n_shard):
    x = x.astype(BF16)
    if n_shard == 8:
        me = lax.axis_index("shard")
        chip, core = me // 2, me % 2
        cube = x.reshape((4, 2) + x.shape[1:])
        keep = jnp.take(cube, core, axis=1)
        give = jnp.take(cube, 1 - core, axis=1)
        both = (keep.astype(F32) + swap(give, "shard", 8, 1).astype(F32)).astype(BF16)
        total = jnp.take(both, chip, axis=0).astype(F32)
        for k in (1, 2, 3):
            piece = jnp.take(both, (chip + k) % 4, axis=0)
            total = total + lax.ppermute(
                piece, "shard", [(p, (p + 2 * k) % 8) for p in range(8)]
            ).astype(F32)
        return total
    return lax.psum_scatter(x, "shard", scatter_dimension=0, tiled=False).astype(F32)


def body(
    frames,
    cotangent,
    lengths,
    send_order,
    norm_gain,
    conv_bias,
    kernel,
    expand_weight,
    project_weight,
):
    n_dp, n_shard = lax.axis_size("dp"), lax.axis_size("shard")
    count, length, width = frames.shape
    per_peer = count // n_dp
    owned, taps = kernel.shape
    part = owned // n_dp
    channels = n_shard * part
    me = lax.axis_index("dp")

    x_own = jnp.take(frames, send_order, axis=0)
    g_own = jnp.take(cotangent, send_order, axis=0)
    len_own = jnp.take(lengths, send_order, axis=0)

    expand_cols = lax.dynamic_index_in_dim(
        expand_weight.reshape(owned, 2, n_shard, n_dp, part), me, axis=3, keepdims=False
    ).reshape(owned, 2 * channels)
    project_rows = lax.dynamic_slice_in_dim(project_weight, me * part, part, axis=0)
    small = jnp.concatenate(
        [
            lax.dynamic_slice_in_dim(kernel, me * part, part, axis=0).reshape(-1),
            lax.dynamic_slice_in_dim(conv_bias, me * part, part, axis=0),
            norm_gain,
        ]
    )
    wide = 2 * channels
    small_rows = 16
    small = jnp.pad(small, (0, small_rows * wide - small.shape[0])).reshape(small_rows, wide)
    n_halves = width // wide
    pack = jnp.concatenate(
        [expand_cols] + [project_rows[:, h * wide : (h + 1) * wide] for h in range(n_halves)] + [small], axis=0
    )
    packs = gather_shard(pack, n_shard)
    expand_slice = packs[:, :owned].reshape(width, wide)
    project_slice = jnp.concatenate(
        [
            packs[:, owned + h * part : owned + (h + 1) * part].reshape(channels, wide)
            for h in range(n_halves)
        ],
        axis=1,
    )
    small_all = packs[:, owned + n_halves * part :].reshape(n_shard, -1).astype(F32)
    taps_table = small_all[:, : part * taps].reshape(channels, taps).T
    bias = small_all[:, part * taps : part * (taps + 1)].reshape(channels)
    gain = small_all[:, part * (taps + 1) : part * (taps + 1) + owned].reshape(width)
    project_full = gather_shard(project_weight, n_shard).reshape(n_shard, n_dp, part, width)

    x_all = gather_dp(x_own, n_dp)
    g_all = gather_dp(g_own, n_dp)
    len_all = [len_own] + [swap(len_own, "dp", n_dp, k) for k in range(1, n_dp)]

    normeds, maskeds, swisheds, grad_expandeds, returned = [], [], [], [], []
    sums = None
    positions = lax.broadcasted_iota(jnp.int32, (count, length), 1)
    for k in range(n_dp):
        live = (positions < len_all[k][:, None]).astype(F32)
        normed, masked, swished, grad_expanded, grad_normed, parts = chunk_compute(
            x_all[k], g_all[k], live, gain, taps_table, bias, expand_slice, project_slice
        )
        normeds.append(normed)
        maskeds.append(masked)
        swisheds.append(swished.reshape(n_dp, per_peer, length, channels))
        grad_expandeds.append(grad_expanded)
        returned.append(grad_normed if k == 0 else swap(grad_normed, "dp", n_dp, k))
        sums = parts if sums is None else tuple(a + b for a, b in zip(sums, parts))

    stack = jnp.stack(swisheds)
    total = None
    for m in range(n_dp):
        piece = lax.dynamic_index_in_dim(stack, me ^ m, axis=1, keepdims=False)
        if m:
            piece = swap(piece, "dp", n_dp, m)
        piece = jnp.stack([piece[k ^ m] for k in range(n_dp)])
        rows = lax.dynamic_index_in_dim(project_full, me ^ m, axis=1, keepdims=False)
        term = jnp.dot(
            piece.reshape(count * length, channels),
            rows.reshape(channels, width),
            preferred_element_type=F32,
        )
        total = term if total is None else total + term
    mine = jnp.stack(
        [
            lax.dynamic_slice_in_dim(x_all[k], me * per_peer, per_peer, axis=0)
            for k in range(n_dp)
        ]
    )
    len_mine = jnp.stack(
        [
            lax.dynamic_slice_in_dim(len_all[k], me * per_peer, per_peer, axis=0)
            for k in range(n_dp)
        ]
    )
    live_mine = (positions < len_mine.reshape(count, 1)).astype(F32)
    encoded = (
        mine.reshape(count, length, width).astype(F32)
        + total.reshape(count, length, width) * live_mine[:, :, None]
    ).astype(BF16)
    encoded = jnp.take(
        encoded.reshape(n_dp, per_peer, length, width), me ^ jnp.arange(n_dp), axis=0
    ).reshape(count, length, width)

    grad_normed = sum(piece.astype(F32) for piece in returned)
    inputs = x_own.reshape(count * length, width).astype(F32)
    centred = inputs - jnp.mean(inputs, axis=1, keepdims=True)
    variance = jnp.mean(centred * centred, axis=1, keepdims=True)
    inverse = lax.rsqrt(variance + EPS)
    standard = centred * inverse
    grad_standard = grad_normed * gain
    grad_inputs = inverse * (
        grad_standard
        - jnp.mean(grad_standard, axis=1, keepdims=True)
        - standard * jnp.mean(grad_standard * standard, axis=1, keepdims=True)
    )
    frame_sorted = (g_own.reshape(count * length, width).astype(F32) + grad_inputs).astype(BF16)
    back = jnp.argmax(
        send_order[None, :] == jnp.arange(count, dtype=jnp.int32)[:, None], axis=1
    )
    frame_grad = jnp.take(frame_sorted.reshape(count, length, width), back, axis=0)

    expand_part = sum(
        lax.dot_general(a, b, (((0,), (0,)), ((), ())), preferred_element_type=F32)
        for a, b in zip(normeds, grad_expandeds)
    )
    project_part = sum(
        lax.dot_general(
            a.reshape(-1, channels), b, (((0,), (0,)), ((), ())), preferred_element_type=F32
        )
        for a, b in zip(swisheds, maskeds)
    )
    gain_part, bias_part, kernel_part = sums
    small_part = jnp.concatenate(
        [
            kernel_part.T.reshape(n_shard, part * taps),
            bias_part.reshape(n_shard, part),
            gain_part.reshape(n_shard, owned),
        ],
        axis=1,
    )
    small_part = jnp.pad(small_part, ((0, 0), (0, small_rows * wide - small_part.shape[1])))
    project_part = project_part.reshape(n_shard, part, width)
    grad_pack = jnp.concatenate(
        [expand_part.reshape(n_shard, owned, wide)]
        + [project_part[:, :, h * wide : (h + 1) * wide] for h in range(n_halves)]
        + [small_part.reshape(n_shard, small_rows, wide)],
        axis=1,
    )
    reduced = reduce_shard(grad_pack, n_shard).astype(BF16)
    gathered = jnp.stack(gather_dp(reduced, n_dp))
    gathered = jnp.take(gathered, me ^ jnp.arange(n_dp), axis=0).astype(F32)
    expand_grad = (
        gathered[:, :owned]
        .reshape(n_dp, owned, 2, n_shard, part)
        .transpose(1, 2, 3, 0, 4)
        .reshape(owned, 2 * width)
    )
    project_grad = jnp.concatenate(
        [
            gathered[:, owned + h * part : owned + (h + 1) * part].reshape(owned, wide)
            for h in range(n_halves)
        ],
        axis=1,
    )
    small_grad = gathered[:, owned + n_halves * part :].reshape(n_dp, -1)
    kernel_grad = small_grad[:, : part * taps].reshape(owned, taps)
    bias_grad = small_grad[:, part * taps : part * (taps + 1)].reshape(owned)
    gain_grad = jnp.sum(small_grad[:, part * (taps + 1) : part * (taps + 1) + owned], axis=0)
    return encoded, frame_grad, gain_grad, bias_grad, kernel_grad, expand_grad, project_grad


def solution(mesh):
    return jax.shard_map(
        body,
        mesh=mesh,
        in_specs=(
            P(("dp", "shard"), None, None),
            P(("dp", "shard"), None, None),
            P(("dp", "shard")),
            P(("dp", "shard")),
            P("shard"),
            P("shard"),
            P("shard", None),
            P("shard", None),
            P("shard", None),
        ),
        out_specs=(
            P(("dp", "shard"), None, None),
            P(("dp", "shard"), None, None),
            P("shard"),
            P("shard"),
            P("shard", None),
            P("shard", None),
            P("shard", None),
        ),
        check_vma=False,
    )
```

time: 423 us -> 479 us (1.13); the launches traced: 420 us -> 471 us
  local copies, waits for them, and re-layouts: 10.2 us -> 195 us
  waiting for transfers between devices: 242 us -> 99.7 us
  blocking collectives: 59.4 us -> 0 us
  other arithmetic: 38.1 us -> 96.2 us
  starting transfers between devices: 17 us -> 39.8 us
  between operations: 16.1 us -> 2.79 us
    reduce_scatter x2 -> x0, waiting for transfers between devices: 127 us -> none  [the longest x1 100 us: body(): lax.psum_scatter(parts[3].astype(jnp.bfloat16), 'shard', scatter_dimensio...]
    ppermute x0 -> x33, waiting for transfers between devices: none -> 99.7 us  [the longest x3 35.7 us: reduce_shard(): lax.ppermute(piece, 'shard', [(p, (p + 2 * k) % 8) for p in range(8)])]
    another operation x32 -> x132, local copies, waits for them, and re-layouts: 0.54 us -> 97.3 us  [the longest x128 92.7 us: kernel_terms(): return jnp.stack(rows, axis=0)]
    all_gather x2 -> x0, waiting for transfers between devices: 58.4 us -> none  [the longest x1 32.2 us: body(): lax.all_gather(expand_weight, 'shard', axis=0, tiled=True)]
    psum x1 -> x0, waiting for transfers between devices: 44.7 us -> none  [body(): lax.psum(reduced[3].astype(jnp.bfloat16), 'dp').astype(jnp.float32)]
    ppermute x0 -> x33, starting transfers between devices: none -> 39.8 us  [the longest x24 23.3 us: swap(): return lax.ppermute(x, axis, [(p, p ^ k) for p in range(size)])]
    unnamed x2 -> x0, blocking collectives: 27.6 us -> none
    slice x2 -> x25, local copies, waits for them, and re-layouts: 0.51 us -> 25.1 us  [the longest x5 4.04 us: body(): piece = jnp.stack([piece[k ^ m] for k in range(n_dp)])]
  transfers between devices with their start and end apart: 10 -> 33, of which waited for: 6 -> 14; matrix products, arithmetic and copies ran while one was open for 19% -> 59% of each run, Pallas kernels for 0% -> 0%
where the time goes in v1:
time: 479 us; the launch traced here: 471 us
  local copies, waits for them, and re-layouts  195 us (41%)
  waiting for transfers between devices  99.7 us (21%)
  other arithmetic  96.2 us (20%)
  starting transfers between devices  39.8 us (8%)
  matrix products  38.2 us (8%)
    another operation x128, local copies, waits for them, and re-layouts, kernel_terms(): return jnp.stack(rows, axis=0)  92.7 us
    ppermute x3, waiting for transfers between devices, reduce_shard(): lax.ppermute(piece, 'shard', [(p, (p + 2 * k) % 8) for p in range(8)])  35.7 us
    ppermute x24, waiting for transfers between devices, swap(): return lax.ppermute(x, axis, [(p, p ^ k) for p in range(size)])  35 us
    ppermute x6, waiting for transfers between devices, gather_shard(): lax.ppermute(x, 'shard', [(p, (p + 2 * k) % 8) for p in range(8)])  29 us
    ppermute x24, starting transfers between devices, swap(): return lax.ppermute(x, axis, [(p, p ^ k) for p in range(size)])  23.3 us
    unnamed x286, local copies, waits for them, and re-layouts  16.4 us
    select_n x2, other arithmetic, gather_shard(): jnp.where(core == 0, jnp.stack([mine, other], 1), jnp.stack([other, mine]...  13 us
    dot_general x4, matrix products, body(): lax.dot_general(a, b, (((0,), (0,)), ((), ())), preferred_element_type=F32)  11.7 us
  transfers between devices with their start and end apart: 33, of which 14 were waited for; matrix products, arithmetic and copies ran while one was open for 59% of the time, Pallas kernels for 0%

profile of v1, /device:TPU:8, one launch (start us, length us, event | category | flops | bytes accessed | tf_op | source)
XLA Modules:
  0.0 471.3 jit_solution(7807909786047316235)
XLA Ops:
  7.9 3.0 collective-permute-start.5
  11.0 2.5 collective-permute-start.4
  23.4 1.7 gather_fusion.5
  28.3 6.8 %collective-permute-done.10 = s32[4]{0:T(128)S(1)} collective-permute-done((s32[4]{0:T(128)S(1)}, s32[4]{0:T(128)S(1)}, u32[]{:S(2)}, u32[]{:S(2)}) %collective-permute-start.10) | collective-permute-done | bytes 48 | tf_op jit(solution)/shard_map/ppermute | solution.py:73
  35.8 2.9 collective-permute-done.9
  40.3 1.9 collective-permute-done.8
  44.6 2.7 add_bitcast_fusion
  50.1 1.7 collective-permute-start.12
  53.2 24.0 %collective-permute-done.4 = bf16[304,768]{1,0:T(8,128)(2,1)} collective-permute-done((bf16[304,768]{1,0:T(8,128)(2,1)}, bf16[304,768]{1,0:T(8,128)(2,1)}, u32[]{:S(2)}, u32[]{:S(2)}) %collective-permute-start.4) | collective-permute-done | bytes 466976 | tf_op jit(solution)/shard_map/ppermute | solution.py:93
  77.2 2.8 collective-permute-start.11
  81.3 2.0 pad_maximum_fusion.1
  83.2 2.7 gather_fusion.4
  86.0 1.7 broadcast_select_fusion
  87.7 4.2 copy.103
  91.9 1.8 fusion.358
  96.6 5.0 %collective-permute-done.11 = bf16[192,1536]{1,0:T(8,128)(2,1)} collective-permute-done((bf16[192,1536]{1,0:T(8,128)(2,1)}, bf16[192,1536]{1,0:T(8,128)(2,1)}, u32[]{:S(2)}, u32[]{:S(2)}) %collective-permute-start.11) | collective-permute-done | bytes 589856 | tf_op jit(solution)/shard_map/ppermute | solution.py:93
  101.6 3.3 pad_maximum_fusion.2
  104.9 2.4 gather_fusion.1
  109.0 1.8 bitcast_select_fusion
  124.7 1.8 slice.1768
  127.0 1.8 slice.1767
  139.6 2.9 collective-permute-done.23
  142.5 3.4 collective-permute-done.22
  148.2 4.1 copy.104
  152.2 7.4 %maximum_select_fusion = bf16[4,2,304,768]{2,3,0,1:T(8,128)(2,1)} fusion(bf16[4,1,304,768]{2,3,0,1:T(8,128)(2,1)} %bitcast.415, bf16[4,1,304,768]{2,3,0,1:T(8,128)(2,1)} %fusion.358, pred[]{:T(512)S(6)} %eq.29), kind=kLoop, calls=%fused_computation.8 | loop fusion | flops 5603328 | bytes 7471105 | tf_op jit(solution)/shard_map/jit(_where)/select_n | solution.py:98
  159.6 7.0 %copy.105 = bf16[4,2,304,768]{3,2,1,0:T(8,128)(2,1)} copy(bf16[4,2,304,768]{2,3,0,1:T(8,128)(2,1)} %maximum_select_fusion) | data formatting | bytes 7471104 | tf_op jit(solution)/shard_map/jit(_where)/select_n | solution.py:98
  167.9 3.2 slice.1710
  171.2 2.0 slice_reduce_fusion.30
  174.8 2.4 fusion.316
  177.4 2.5 multiply_convert_fusion.10
  202.4 3.1 convolution_bitcast_fusion.3
  215.9 2.5 multiply_reduce_fusion
  296.3 5.3 %stack.663 = f32[31,384]{1,0:T(8,128)} concatenate(f32[1,384]{1,0:T(1,128)} %stack.632, f32[1,384]{1,0:T(1,128)} %stack.633, f32[1,384]{1,0:T(1,128)} %stack.634, f32[1,384]{1,0:T(1,128)} %stack.635, f32[1,384]{1,0:T(1,128)} %stack.636, f32[1,384]{1,0:T(1,128)} %stack.637, f32[1,384]{1,0:T(1,128)} %stack.638, f32[1,384]{1,0:T(1,128)} %stack.639, f32[1,384]{1,0:T(1,128)} %stack.640, ...), dimensions={0} | concatenate | bytes 95232 | tf_op jit(solution)/shard_map/stack | solution.py:29
  301.6 5.3 %stack.631 = f32[31,384]{1,0:T(8,128)} concatenate(f32[1,384]{1,0:T(1,128)} %stack.600, f32[1,384]{1,0:T(1,128)} %stack.601, f32[1,384]{1,0:T(1,128)} %stack.602, f32[1,384]{1,0:T(1,128)} %stack.603, f32[1,384]{1,0:T(1,128)} %stack.604, f32[1,384]{1,0:T(1,128)} %stack.605, f32[1,384]{1,0:T(1,128)} %stack.606, f32[1,384]{1,0:T(1,128)} %stack.607, f32[1,384]{1,0:T(1,128)} %stack.608, ...), dimensions={0} | concatenate | bytes 95232 | tf_op jit(solution)/shard_map/stack | solution.py:29
  306.9 5.3 %stack.567 = f32[31,384]{1,0:T(8,128)} concatenate(f32[1,384]{1,0:T(1,128)} %stack.536, f32[1,384]{1,0:T(1,128)} %stack.537, f32[1,384]{1,0:T(1,128)} %stack.538, f32[1,384]{1,0:T(1,128)} %stack.539, f32[1,384]{1,0:T(1,128)} %stack.540, f32[1,384]{1,0:T(1,128)} %stack.541, f32[1,384]{1,0:T(1,128)} %stack.542, f32[1,384]{1,0:T(1,128)} %stack.543, f32[1,384]{1,0:T(1,128)} %stack.544, ...), dimensions={0} | concatenate | bytes 95232 | tf_op jit(solution)/shard_map/stack | solution.py:29
  312.2 5.3 %stack.599 = f32[31,384]{1,0:T(8,128)} concatenate(f32[1,384]{1,0:T(1,128)} %stack.568, f32[1,384]{1,0:T(1,128)} %stack.569, f32[1,384]{1,0:T(1,128)} %stack.570, f32[1,384]{1,0:T(1,128)} %stack.571, f32[1,384]{1,0:T(1,128)} %stack.572, f32[1,384]{1,0:T(1,128)} %stack.573, f32[1,384]{1,0:T(1,128)} %stack.574, f32[1,384]{1,0:T(1,128)} %stack.575, f32[1,384]{1,0:T(1,128)} %stack.576, ...), dimensions={0} | concatenate | bytes 95232 | tf_op jit(solution)/shard_map/stack | solution.py:29
  324.2 2.2 multiply_reduce_fusion.1
  326.4 3.0 fusion.281
  331.1 2.2 convolution_bitcast_fusion.1
  333.3 2.1 multiply_reduce_fusion.2
  337.1 3.0 fusion.283
  340.1 1.8 fusion.3
  349.8 5.6 %maximum_select_fusion.1 = bf16[4,2,192,1536]{3,2,1,0:T(8,128)(2,1)} fusion(bf16[4,1,192,1536]{3,2,1,0:T(8,128)(2,1)} %bitcast.42, bf16[4,1,192,1536]{3,2,1,0:T(8,128)(2,1)S(1)} %copy-done.6, pred[]{:T(512)S(6)} %eq.29), kind=kLoop, calls=%fused_computation.9 | loop fusion | flops 7077888 | bytes 9437185 | tf_op jit(solution)/shard_map/jit(_where)/select_n | solution.py:98
  355.3 4.0 collective-permute-done.21
  359.4 2.9 collective-permute-done.19
  362.3 3.5 fusion.310
  366.0 2.2 fusion.285
  368.9 3.5 add_convert_fusion
  382.5 2.7 gather_fusion.2
  385.2 2.6 add_convert_fusion.1
  388.0 1.8 collective-permute-start.28
  389.8 2.2 collective-permute-start.27
  392.0 2.5 collective-permute-start.26
  395.6 26.6 %collective-permute-done.28 = bf16[304,768]{1,0:T(8,128)(2,1)S(1)} collective-permute-done((bf16[304,768]{1,0:T(8,128)(2,1)S(1)}, bf16[304,768]{1,0:T(8,128)(2,1)S(1)}, u32[]{:S(2)}, u32[]{:S(2)}) %collective-permute-start.28) | collective-permute-done | bytes 466976 | tf_op jit(solution)/shard_map/ppermute | solution.py:115
  422.2 9.1 %collective-permute-done.26 = bf16[304,768]{1,0:T(8,128)(2,1)S(1)} collective-permute-done((bf16[304,768]{1,0:T(8,128)(2,1)S(1)}, bf16[304,768]{1,0:T(8,128)(2,1)S(1)}, u32[]{:S(2)}, u32[]{:S(2)}) %collective-permute-start.26) | collective-permute-done | bytes 466976 | tf_op jit(solution)/shard_map/ppermute | solution.py:115
  432.8 2.6 fusion.15
  435.5 1.9 gather_fusion.6
  437.4 6.2 %collective-permute-done.30 = bf16[304,768]{1,0:T(8,128)(2,1)S(1)} collective-permute-done((bf16[304,768]{1,0:T(8,128)(2,1)S(1)}, bf16[304,768]{1,0:T(8,128)(2,1)S(1)}, u32[]{:S(2)}, u32[]{:S(2)}) %collective-permute-start.30) | collective-permute-done | bytes 466976 | tf_op jit(solution)/shard_map/ppermute | solution.py:73
  447.5 2.3 collective-permute-done.32
  452.8 2.0 gather_fusion.7
  454.8 1.8 select_convert_fusion
  460.2 2.3 copy.115
  462.6 3.9 copy.116
  466.4 3.5 copy.118
  (630 shorter events, 218.4 us)
Async XLA Ops:
  7.9 40.1 %collective-permute-start.6 = (bf16[304,768]{1,0:T(8,128)(2,1)}, bf16[304,768]{1,0:T(8,128)(2,1)}, u32[]{:S(2)}, u32[]{:S(2)}) collective-permute-start(bf16[304,768]{1,0:T(8,128)(2,1)} %copy.97), channel_id=1, source_target_pairs={{0,6},{1,7},{2,0},{3,1},{4,2},{5,3},{6,4},{7,5},{8,14},{9,15},{10,... | collective-permute-start | bytes 1400840 | tf_op jit(solution)/shard_map/ppermute | solution.py:93
  7.9 41.4 %collective-permute-start.5 = (bf16[304,768]{1,0:T(8,128)(2,1)}, bf16[304,768]{1,0:T(8,128)(2,1)S(1)}, u32[]{:S(2)}, u32[]{:S(2)}) collective-permute-start(bf16[304,768]{1,0:T(8,128)(2,1)} %copy.97), channel_id=1, source_target_pairs={{0,4},{1,5},{2,6},{3,7},{4,0},{5,1},{6,2},{7,3},{8,12},{9,13},{10,... | collective-permute-start | bytes 1400840 | tf_op jit(solution)/shard_map/ppermute | solution.py:93
  11.0 66.2 %collective-permute-start.4 = (bf16[304,768]{1,0:T(8,128)(2,1)}, bf16[304,768]{1,0:T(8,128)(2,1)}, u32[]{:S(2)}, u32[]{:S(2)}) collective-permute-start(bf16[304,768]{1,0:T(8,128)(2,1)} %copy.97), channel_id=1, source_target_pairs={{0,2},{1,3},{2,4},{3,5},{4,6},{5,7},{6,0},{7,1},{8,10},{9,11},{10,... | collective-permute-start | bytes 1400840 | tf_op jit(solution)/shard_map/ppermute | solution.py:93
  15.7 99.0 %collective-permute-start = (bf16[4,64,1536]{2,1,0:T(8,128)(2,1)S(1)}, bf16[4,64,1536]{2,1,0:T(8,128)(2,1)}, u32[]{:S(2)}, u32[]{:S(2)}) collective-permute-start(bf16[4,64,1536]{2,1,0:T(8,128)(2,1)S(1)} %get-tuple-element.238), channel_id=1, source_target_pairs={{0,8},{8,0},{16,24},{24,16},{1,9},{9,1},{17,25},{25,17},{2,10},{10... | collective-permute-start | bytes 2359304 | tf_op jit(solution)/shard_map/ppermute | solution.py:73
  17.2 17.9 %collective-permute-start.10 = (s32[4]{0:T(128)S(1)}, s32[4]{0:T(128)S(1)}, u32[]{:S(2)}, u32[]{:S(2)}) collective-permute-start(s32[4]{0:T(128)S(1)} %get-tuple-element.245), channel_id=1, source_target_pairs={{0,24},{8,16},{16,8},{24,0},{1,25},{9,17},{17,9},{25,1},{2,26},{10... | collective-permute-start | bytes 56 | tf_op jit(solution)/shard_map/ppermute | solution.py:73
  22.8 176.3 %copy-start.105 = (f32[256]{0:T(256)}, f32[256]{0:T(256)S(1)}, u32[]{:S(2)}) copy-start(f32[256]{0:T(256)S(1)} %reshape.1061) | copy-start | bytes 3076
  35.1 3.5 collective-permute-start.9
  35.8 157.8 %copy-start.107 = (f32[256]{0:T(256)}, f32[256]{0:T(256)S(1)}, u32[]{:S(2)}) copy-start(f32[256]{0:T(256)S(1)} %reshape.1064) | copy-start | bytes 3076
  38.7 3.5 collective-permute-start.8
  40.3 156.0 %copy-start.111 = (f32[256]{0:T(256)}, f32[256]{0:T(256)S(1)}, u32[]{:S(2)}) copy-start(f32[256]{0:T(256)S(1)} %reshape.1063) | copy-start | bytes 3076
  42.2 68.6 %collective-permute-start.1 = (bf16[4,64,1536]{2,1,0:T(8,128)(2,1)S(1)}, bf16[4,64,1536]{2,1,0:T(8,128)(2,1)}, u32[]{:S(2)}, u32[]{:S(2)}) collective-permute-start(bf16[4,64,1536]{2,1,0:T(8,128)(2,1)S(1)} %get-tuple-element.238), channel_id=1, source_target_pairs={{0,16},{8,24},{16,0},{24,8},{1,17},{9,25},{17,1},{25,9},{2,18},{10... | collective-permute-start | bytes 2359304 | tf_op jit(solution)/shard_map/ppermute | solution.py:73
  42.8 38.5 %copy-start.113 = (f32[4,64]{1,0:T(4,128)}, f32[4,64]{1,0:T(4,128)S(1)}, u32[]{:S(2)}) copy-start(f32[4,64]{1,0:T(4,128)S(1)} %fusion.293) | copy-start | bytes 3076
  42.9 158.8 %copy-start.109 = (f32[256]{0:T(256)}, f32[256]{0:T(256)S(1)}, u32[]{:S(2)}) copy-start(f32[256]{0:T(256)S(1)} %reshape.1062) | copy-start | bytes 3076
  48.0 45.7 %collective-permute-start.13 = (bf16[192,1536]{1,0:T(8,128)(2,1)}, bf16[192,1536]{1,0:T(8,128)(2,1)}, u32[]{:S(2)}, u32[]{:S(2)}) collective-permute-start(bf16[192,1536]{1,0:T(8,128)(2,1)} %param.25), channel_id=1, source_target_pairs={{0,6},{1,7},{2,0},{3,1},{4,2},{5,3},{6,4},{7,5},{8,14},{9,15},{10,... | collective-permute-start | bytes 1769480 | tf_op jit(solution)/shard_map/ppermute | solution.py:93
  50.1 45.1 %collective-permute-start.12 = (bf16[192,1536]{1,0:T(8,128)(2,1)}, bf16[192,1536]{1,0:T(8,128)(2,1)}, u32[]{:S(2)}, u32[]{:S(2)}) collective-permute-start(bf16[192,1536]{1,0:T(8,128)(2,1)} %param.25), channel_id=1, source_target_pairs={{0,4},{1,5},{2,6},{3,7},{4,0},{5,1},{6,2},{7,3},{8,12},{9,13},{10,... | collective-permute-start | bytes 1769480 | tf_op jit(solution)/shard_map/ppermute | solution.py:93
  77.2 24.4 %collective-permute-start.11 = (bf16[192,1536]{1,0:T(8,128)(2,1)}, bf16[192,1536]{1,0:T(8,128)(2,1)}, u32[]{:S(2)}, u32[]{:S(2)}) collective-permute-start(bf16[192,1536]{1,0:T(8,128)(2,1)} %param.25), channel_id=1, source_target_pairs={{0,2},{1,3},{2,4},{3,5},{4,6},{5,7},{6,0},{7,1},{8,10},{9,11},{10,... | collective-permute-start | bytes 1769480 | tf_op jit(solution)/shard_map/ppermute | solution.py:93
  93.6 29.5 %collective-permute-start.20 = (bf16[4,64,1536]{2,1,0:T(8,128)(2,1)}, bf16[4,64,1536]{2,1,0:T(8,128)(2,1)}, u32[]{:S(2)}, u32[]{:S(2)}) collective-permute-start(bf16[4,64,1536]{2,1,0:T(8,128)(2,1)} %get-tuple-element.234), channel_id=1, source_target_pairs={{0,16},{8,24},{16,0},{24,8},{1,17},{9,25},{17,1},{25,9},{2,18},{10... | collective-permute-start | bytes 2359304 | tf_op jit(solution)/shard_map/ppermute | solution.py:73
  95.2 31.3 %collective-permute-start.18 = (bf16[4,64,1536]{2,1,0:T(8,128)(2,1)}, bf16[4,64,1536]{2,1,0:T(8,128)(2,1)}, u32[]{:S(2)}, u32[]{:S(2)}) collective-permute-start(bf16[4,64,1536]{2,1,0:T(8,128)(2,1)} %get-tuple-element.234), channel_id=1, source_target_pairs={{0,8},{8,0},{16,24},{24,16},{1,9},{9,1},{17,25},{25,17},{2,10},{10... | collective-permute-start | bytes 2359304 | tf_op jit(solution)/shard_map/ppermute | solution.py:73
  101.6 46.5 %collective-permute-start.7 = (bf16[4,304,768]{2,1,0:T(8,128)(2,1)}, bf16[4,304,768]{2,1,0:T(8,128)(2,1)}, u32[]{:S(2)}, u32[]{:S(2)}) collective-permute-start(bf16[4,304,768]{2,1,0:T(8,128)(2,1)} %copy.103), channel_id=1, source_target_pairs={{0,1},{1,0},{2,3},{3,2},{4,5},{5,4},{6,7},{7,6},{8,9},{9,8},{10,11... | collective-permute-start | bytes 5603336 | tf_op jit(solution)/shard_map/ppermute | solution.py:73
  110.8 239.0 %collective-permute-start.14 = (bf16[4,192,1536]{2,1,0:T(8,128)(2,1)}, bf16[4,192,1536]{2,1,0:T(8,128)(2,1)}, u32[]{:S(2)}, u32[]{:S(2)}) collective-permute-start(bf16[4,192,1536]{2,1,0:T(8,128)(2,1)} %broadcast_select_fusion.1), channel_id=1, source_target_pairs={{0,1},{1,0},{2,3},{3,2},{4,5},{5,4},{6,7},{7,6},{8,9},{9,8},{10,11... | collective-permute-start | bytes 7077896 | tf_op jit(solution)/shard_map/ppermute | solution.py:73
  115.8 18.9 %collective-permute-start.2 = (bf16[2,64,1536]{2,1,0:T(8,128)(2,1)S(1)}, bf16[2,64,1536]{2,1,0:T(8,128)(2,1)S(1)}, u32[]{:S(2)}, u32[]{:S(2)}) collective-permute-start(bf16[2,64,1536]{2,1,0:T(8,128)(2,1)S(1)} %slice.1706), channel_id=1, source_target_pairs={{0,16},{8,24},{16,0},{24,8},{1,17},{9,25},{17,1},{25,9},{2,18},{10... | collective-permute-start | bytes 1179656 | tf_op jit(solution)/shard_map/ppermute | solution.py:73
  123.1 13.8 %collective-permute-start.3 = (bf16[2,64,1536]{2,1,0:T(8,128)(2,1)S(1)}, bf16[2,64,1536]{2,1,0:T(8,128)(2,1)S(1)}, u32[]{:S(2)}, u32[]{:S(2)}) collective-permute-start(bf16[2,64,1536]{2,1,0:T(8,128)(2,1)S(1)} %slice.1707), channel_id=1, source_target_pairs={{0,8},{8,0},{16,24},{24,16},{1,9},{9,1},{17,25},{25,17},{2,10},{10... | collective-permute-start | bytes 1179656 | tf_op jit(solution)/shard_map/ppermute | solution.py:73
  126.4 16.0 %collective-permute-start.23 = (bf16[2,64,1536]{2,1,0:T(8,128)(2,1)}, bf16[2,64,1536]{2,1,0:T(8,128)(2,1)}, u32[]{:S(2)}, u32[]{:S(2)}) collective-permute-start(bf16[2,64,1536]{2,1,0:T(8,128)(2,1)} %slice.1768), channel_id=1, source_target_pairs={{0,8},{8,0},{16,24},{24,16},{1,9},{9,1},{17,25},{25,17},{2,10},{10... | collective-permute-start | bytes 1179656 | tf_op jit(solution)/shard_map/ppermute | solution.py:73
  135.4 10.5 %collective-permute-start.22 = (bf16[2,64,1536]{2,1,0:T(8,128)(2,1)}, bf16[2,64,1536]{2,1,0:T(8,128)(2,1)}, u32[]{:S(2)}, u32[]{:S(2)}) collective-permute-start(bf16[2,64,1536]{2,1,0:T(8,128)(2,1)} %slice.1767), channel_id=1, source_target_pairs={{0,16},{8,24},{16,0},{24,8},{1,17},{9,25},{17,1},{25,9},{2,18},{10... | collective-permute-start | bytes 1179656 | tf_op jit(solution)/shard_map/ppermute | solution.py:73
  173.2 38.1 %copy-start.48 = (f32[384]{0:T(512)}, f32[384]{0:T(512)S(1)}, u32[]{:S(2)}) copy-start(f32[384]{0:T(512)S(1)} %get-tuple-element.205) | copy-start | bytes 4612
  173.3 38.1 %copy-start.50 = (f32[384]{0:T(512)}, f32[384]{0:T(512)S(1)}, u32[]{:S(2)}) copy-start(f32[384]{0:T(512)S(1)} %get-tuple-element.206) | copy-start | bytes 4612
  173.3 38.1 %copy-start.52 = (f32[384]{0:T(512)}, f32[384]{0:T(512)S(1)}, u32[]{:S(2)}) copy-start(f32[384]{0:T(512)S(1)} %get-tuple-element.207) | copy-start | bytes 4612
  173.3 38.1 %copy-start.54 = (f32[384]{0:T(512)}, f32[384]{0:T(512)S(1)}, u32[]{:S(2)}) copy-start(f32[384]{0:T(512)S(1)} %get-tuple-element.208) | copy-start | bytes 4612
  173.3 38.1 %copy-start.56 = (f32[384]{0:T(512)}, f32[384]{0:T(512)S(1)}, u32[]{:S(2)}) copy-start(f32[384]{0:T(512)S(1)} %get-tuple-element.209) | copy-start | bytes 4612
  173.3 38.1 %copy-start.58 = (f32[384]{0:T(512)}, f32[384]{0:T(512)S(1)}, u32[]{:S(2)}) copy-start(f32[384]{0:T(512)S(1)} %get-tuple-element.210) | copy-start | bytes 4612
  173.3 38.1 %copy-start.60 = (f32[384]{0:T(512)}, f32[384]{0:T(512)S(1)}, u32[]{:S(2)}) copy-start(f32[384]{0:T(512)S(1)} %get-tuple-element.211) | copy-start | bytes 4612
  173.3 38.1 %copy-start.62 = (f32[384]{0:T(512)}, f32[384]{0:T(512)S(1)}, u32[]{:S(2)}) copy-start(f32[384]{0:T(512)S(1)} %get-tuple-element.212) | copy-start | bytes 4612
  173.3 38.1 %copy-start.64 = (f32[384]{0:T(512)}, f32[384]{0:T(512)S(1)}, u32[]{:S(2)}) copy-start(f32[384]{0:T(512)S(1)} %get-tuple-element.213) | copy-start | bytes 4612
  173.3 38.1 %copy-start.66 = (f32[384]{0:T(512)}, f32[384]{0:T(512)S(1)}, u32[]{:S(2)}) copy-start(f32[384]{0:T(512)S(1)} %get-tuple-element.214) | copy-start | bytes 4612
  173.3 38.1 %copy-start.68 = (f32[384]{0:T(512)}, f32[384]{0:T(512)S(1)}, u32[]{:S(2)}) copy-start(f32[384]{0:T(512)S(1)} %get-tuple-element.215) | copy-start | bytes 4612
  173.4 38.1 %copy-start.70 = (f32[384]{0:T(512)}, f32[384]{0:T(512)S(1)}, u32[]{:S(2)}) copy-start(f32[384]{0:T(512)S(1)} %get-tuple-element.216) | copy-start | bytes 4612
  173.4 38.1 %copy-start.72 = (f32[384]{0:T(512)}, f32[384]{0:T(512)S(1)}, u32[]{:S(2)}) copy-start(f32[384]{0:T(512)S(1)} %get-tuple-element.217) | copy-start | bytes 4612
  173.4 38.1 %copy-start.74 = (f32[384]{0:T(512)}, f32[384]{0:T(512)S(1)}, u32[]{:S(2)}) copy-start(f32[384]{0:T(512)S(1)} %get-tuple-element.218) | copy-start | bytes 4612
  173.4 38.1 %copy-start.76 = (f32[384]{0:T(512)}, f32[384]{0:T(512)S(1)}, u32[]{:S(2)}) copy-start(f32[384]{0:T(512)S(1)} %get-tuple-element.219) | copy-start | bytes 4612
  174.7 36.8 %copy-start.80 = (f32[384]{0:T(512)}, f32[384]{0:T(512)S(1)}, u32[]{:S(2)}) copy-start(f32[384]{0:T(512)S(1)} %get-tuple-element.221) | copy-start | bytes 4612
  174.7 36.8 %copy-start.82 = (f32[384]{0:T(512)}, f32[384]{0:T(512)S(1)}, u32[]{:S(2)}) copy-start(f32[384]{0:T(512)S(1)} %get-tuple-element.222) | copy-start | bytes 4612
  174.8 36.8 %copy-start.84 = (f32[384]{0:T(512)}, f32[384]{0:T(512)S(1)}, u32[]{:S(2)}) copy-start(f32[384]{0:T(512)S(1)} %get-tuple-element.223) | copy-start | bytes 4612
  174.8 36.8 %copy-start.86 = (f32[384]{0:T(512)}, f32[384]{0:T(512)S(1)}, u32[]{:S(2)}) copy-start(f32[384]{0:T(512)S(1)} %get-tuple-element.224) | copy-start | bytes 4612
  177.4 38.5 %copy-start.103 = (f32[1536]{0:T(1024)}, f32[1536]{0:T(1024)S(1)}, u32[]{:S(2)}) copy-start(f32[1536]{0:T(1024)S(1)} %mul.1137) | copy-start | bytes 18436
  207.9 138.1 %collective-permute-start.15 = (bf16[4,1,64,384]{3,2,0,1:T(8,128)(2,1)}, bf16[4,1,64,384]{3,2,0,1:T(8,128)(2,1)}, u32[]{:S(2)}, u32[]{:S(2)}) collective-permute-start(bf16[4,1,64,384]{3,2,0,1:T(8,128)(2,1)} %get-tuple-element.280), channel_id=1, source_target_pairs={{0,8},{8,0},{16,24},{24,16},{1,9},{9,1},{17,25},{25,17},{2,10},{10... | collective-permute-start | bytes 589832 | tf_op jit(solution)/shard_map/ppermute | solution.py:73
  209.3 133.5 %collective-permute-start.16 = (bf16[4,1,64,384]{3,2,0,1:T(8,128)(2,1)}, bf16[4,1,64,384]{3,2,0,1:T(8,128)(2,1)}, u32[]{:S(2)}, u32[]{:S(2)}) collective-permute-start(bf16[4,1,64,384]{3,2,0,1:T(8,128)(2,1)} %get-tuple-element.279), channel_id=1, source_target_pairs={{0,16},{8,24},{16,0},{24,8},{1,17},{9,25},{17,1},{25,9},{2,18},{10... | collective-permute-start | bytes 589832 | tf_op jit(solution)/shard_map/ppermute | solution.py:73
  209.9 137.5 %collective-permute-start.17 = (bf16[4,1,64,384]{3,2,0,1:T(8,128)(2,1)}, bf16[4,1,64,384]{3,2,0,1:T(8,128)(2,1)}, u32[]{:S(2)}, u32[]{:S(2)}) collective-permute-start(bf16[4,1,64,384]{3,2,0,1:T(8,128)(2,1)} %get-tuple-element.278), channel_id=1, source_target_pairs={{0,24},{8,16},{16,8},{24,0},{1,25},{9,17},{17,9},{25,1},{2,26},{10... | collective-permute-start | bytes 589832 | tf_op jit(solution)/shard_map/ppermute | solution.py:73
  213.8 115.6 %copy-start.12 = (bf16[256,384]{1,0:T(8,128)(2,1)}, bf16[256,384]{1,0:T(8,128)(2,1)S(1)}, u32[]{:S(2)}) copy-start(bf16[256,384]{1,0:T(8,128)(2,1)S(1)} %get-tuple-element.270) | copy-start | bytes 589828
  213.8 115.6 %copy-start.13 = (bf16[256,384]{1,0:T(8,128)(2,1)}, bf16[256,384]{1,0:T(8,128)(2,1)S(1)}, u32[]{:S(2)}) copy-start(bf16[256,384]{1,0:T(8,128)(2,1)S(1)} %get-tuple-element.271) | copy-start | bytes 589828
  218.5 136.9 %collective-permute-start.24 = (bf16[256,1536]{1,0:T(8,128)(2,1)}, bf16[256,1536]{1,0:T(8,128)(2,1)}, u32[]{:S(2)}, u32[]{:S(2)}) collective-permute-start(bf16[256,1536]{1,0:T(8,128)(2,1)} %get-tuple-element.263), channel_id=1, source_target_pairs={{0,24},{8,16},{16,8},{24,0},{1,25},{9,17},{17,9},{25,1},{2,26},{10... | collective-permute-start | bytes 2359304 | tf_op jit(solution)/shard_map/ppermute | solution.py:73
  223.8 98.3 %copy-start.117 = (f32[384]{0:T(512)S(1)}, f32[384]{0:T(512)}, u32[]{:S(2)}) copy-start(f32[384]{0:T(512)} %get-tuple-element.199) | copy-start | bytes 4612
  223.8 98.3 %copy-start.118 = (f32[384]{0:T(512)S(1)}, f32[384]{0:T(512)}, u32[]{:S(2)}) copy-start(f32[384]{0:T(512)} %get-tuple-element.197) | copy-start | bytes 4612
  223.8 100.4 %copy-start.5 = (bf16[8,192,768]{2,1,0:T(8,128)(2,1)S(1)}, bf16[8,192,768]{2,1,0:T(8,128)(2,1)}, u32[]{:S(2)}) copy-start(bf16[8,192,768]{2,1,0:T(8,128)(2,1)} %slice.1710) | copy-start | bytes 7077892
  223.8 100.3 %copy-start.104 = (f32[1536]{0:T(1024)S(1)}, f32[1536]{0:T(1024)}, u32[]{:S(2)}) copy-start(f32[1536]{0:T(1024)} %copy-done.103) | copy-start | bytes 18436
  342.8 16.6 %collective-permute-start.21 = (bf16[256,1536]{1,0:T(8,128)(2,1)S(1)}, bf16[256,1536]{1,0:T(8,128)(2,1)S(1)}, u32[]{:S(2)}, u32[]{:S(2)}) collective-permute-start(bf16[256,1536]{1,0:T(8,128)(2,1)S(1)} %get-tuple-element.261), channel_id=1, source_target_pairs={{0,16},{8,24},{16,0},{24,8},{1,17},{9,25},{17,1},{25,9},{2,18},{10... | collective-permute-start | bytes 2359304 | tf_op jit(solution)/shard_map/ppermute | solution.py:73
  346.0 16.3 %collective-permute-start.19 = (bf16[256,1536]{1,0:T(8,128)(2,1)S(1)}, bf16[256,1536]{1,0:T(8,128)(2,1)S(1)}, u32[]{:S(2)}, u32[]{:S(2)}) collective-permute-start(bf16[256,1536]{1,0:T(8,128)(2,1)S(1)} %get-tuple-element.259), channel_id=1, source_target_pairs={{0,8},{8,0},{16,24},{24,16},{1,9},{9,1},{17,25},{25,17},{2,10},{10... | collective-permute-start | bytes 2359304 | tf_op jit(solution)/shard_map/ppermute | solution.py:73
  375.6 9.6 %collective-permute-start.25 = (bf16[4,304,768]{2,1,0:T(8,128)(2,1)}, bf16[4,304,768]{2,1,0:T(8,128)(2,1)}, u32[]{:S(2)}, u32[]{:S(2)}) collective-permute-start(bf16[4,304,768]{2,1,0:T(8,128)(2,1)} %fusion.4), channel_id=1, source_target_pairs={{0,1},{1,0},{2,3},{3,2},{4,5},{5,4},{6,7},{7,6},{8,9},{9,8},{10,11... | collective-permute-start | bytes 5603336 | tf_op jit(solution)/shard_map/ppermute | solution.py:73
  388.0 34.1 %collective-permute-start.28 = (bf16[304,768]{1,0:T(8,128)(2,1)S(1)}, bf16[304,768]{1,0:T(8,128)(2,1)S(1)}, u32[]{:S(2)}, u32[]{:S(2)}) collective-permute-start(bf16[304,768]{1,0:T(8,128)(2,1)S(1)} %get-tuple-element.256), channel_id=1, source_target_pairs={{0,6},{1,7},{2,0},{3,1},{4,2},{5,3},{6,4},{7,5},{8,14},{9,15},{10,... | collective-permute-start | bytes 1400840 | tf_op jit(solution)/shard_map/ppermute | solution.py:115
  389.8 32.4 %collective-permute-start.27 = (bf16[304,768]{1,0:T(8,128)(2,1)S(1)}, bf16[304,768]{1,0:T(8,128)(2,1)S(1)}, u32[]{:S(2)}, u32[]{:S(2)}) collective-permute-start(bf16[304,768]{1,0:T(8,128)(2,1)S(1)} %get-tuple-element.257), channel_id=1, source_target_pairs={{0,4},{1,5},{2,6},{3,7},{4,0},{5,1},{6,2},{7,3},{8,12},{9,13},{10,... | collective-permute-start | bytes 1400840 | tf_op jit(solution)/shard_map/ppermute | solution.py:115
  392.0 39.3 %collective-permute-start.26 = (bf16[304,768]{1,0:T(8,128)(2,1)S(1)}, bf16[304,768]{1,0:T(8,128)(2,1)S(1)}, u32[]{:S(2)}, u32[]{:S(2)}) collective-permute-start(bf16[304,768]{1,0:T(8,128)(2,1)S(1)} %get-tuple-element.255), channel_id=1, source_target_pairs={{0,2},{1,3},{2,4},{3,5},{4,6},{5,7},{6,0},{7,1},{8,10},{9,11},{10,... | collective-permute-start | bytes 1400840 | tf_op jit(solution)/shard_map/ppermute | solution.py:115
  431.6 12.0 %collective-permute-start.30 = (bf16[304,768]{1,0:T(8,128)(2,1)S(1)}, bf16[304,768]{1,0:T(8,128)(2,1)S(1)}, u32[]{:S(2)}, u32[]{:S(2)}) collective-permute-start(bf16[304,768]{1,0:T(8,128)(2,1)S(1)} %add_convert_fusion.3), channel_id=1, source_target_pairs={{0,16},{8,24},{16,0},{24,8},{1,17},{9,25},{17,1},{25,9},{2,18},{10... | collective-permute-start | bytes 1400840 | tf_op jit(solution)/shard_map/ppermute | solution.py:73
  432.3 11.9 %collective-permute-start.29 = (bf16[304,768]{1,0:T(8,128)(2,1)S(1)}, bf16[304,768]{1,0:T(8,128)(2,1)}, u32[]{:S(2)}, u32[]{:S(2)}) collective-permute-start(bf16[304,768]{1,0:T(8,128)(2,1)S(1)} %add_convert_fusion.3), channel_id=1, source_target_pairs={{0,8},{8,0},{16,24},{24,16},{1,9},{9,1},{17,25},{25,17},{2,10},{10... | collective-permute-start | bytes 1400840 | tf_op jit(solution)/shard_map/ppermute | solution.py:73
  443.6 6.2 %collective-permute-start.32 = (bf16[152,768]{1,0:T(8,128)(2,1)S(1)}, bf16[152,768]{1,0:T(8,128)(2,1)S(1)}, u32[]{:S(2)}, u32[]{:S(2)}) collective-permute-start(bf16[152,768]{1,0:T(8,128)(2,1)S(1)} %slice.1772), channel_id=1, source_target_pairs={{0,8},{8,0},{16,24},{24,16},{1,9},{9,1},{17,25},{25,17},{2,10},{10... | collective-permute-start | bytes 700424 | tf_op jit(solution)/shard_map/ppermute | solution.py:73
  445.2 6.1 %collective-permute-start.31 = (bf16[152,768]{1,0:T(8,128)(2,1)S(1)}, bf16[152,768]{1,0:T(8,128)(2,1)S(1)}, u32[]{:S(2)}, u32[]{:S(2)}) collective-permute-start(bf16[152,768]{1,0:T(8,128)(2,1)S(1)} %slice.1771), channel_id=1, source_target_pairs={{0,16},{8,24},{16,0},{24,8},{1,17},{9,25},{17,1},{25,9},{2,18},{10... | collective-permute-start | bytes 700424 | tf_op jit(solution)/shard_map/ppermute | solution.py:73
  (107 other events, 633.3 us)

commit v2 on v1

--- a/solution.py
+++ b/solution.py
@@ -1,11 +1,664 @@
+import functools
+
 import jax
 import jax.numpy as jnp
 from jax import lax
+from jax.experimental import pallas as pl
+from jax.experimental.pallas import tpu as pltpu
 from jax.sharding import PartitionSpec as P
 
 EPS = 1e-05
 F32 = jnp.float32
 BF16 = jnp.bfloat16
+LANES = 128
+MARGIN = 16
+VMEM_BYTES = 56 * 1024 * 1024
+NT = (((1,), (1,)), ((), ()))
+TN = (((0,), (0,)), ((), ()))
+
+
+def chunk_kernel(dims, meta, x_ref, g_ref, gain_ref, taps_ref, *refs):
+    count, length, owned, part, taps, n_blocks = dims
+    blocks = refs[:n_blocks]
+    normed_ref, sw_ref, ge_ref, gn_ref, small_ref, gain_part_ref = refs[n_blocks : n_blocks + 6]
+    we, wp, ab, standard, pad, gpad, slope, sems = refs[n_blocks + 6 :]
+    rows, width = x_ref.shape
+    wide = we.shape[1]
+    channels = wide // 2
+    tiles = channels // LANES
+
+    def copies(b):
+        owner = meta[b]
+        out = [
+            pltpu.make_async_copy(
+                blocks[b].at[pl.ds(0, owned)],
+                we.at[pl.ds(pl.multiple_of(owner * owned, owned), owned)],
+                sems.at[b, 0],
+            )
+        ]
+        for h in range(width // wide):
+            out.append(
+                pltpu.make_async_copy(
+                    blocks[b].at[pl.ds(owned + h * part, part)],
+                    wp.at[
+                        pl.ds(pl.multiple_of(owner * part, part), part),
+                        pl.ds(h * wide, wide),
+                    ],
+                    sems.at[b, 1 + h],
+                )
+            )
+        return out
+
+    for b in range(n_blocks):
+        @pl.when(meta[b] >= 0)
+        def _():
+            for copy in copies(b):
+                copy.start()
+
+    step = 32
+    gain = gain_ref[...]
+
+    @pl.loop(0, rows // step)
+    def _(index):
+        at = pl.ds(pl.multiple_of(index * step, step), step)
+        x = x_ref[at, :].astype(F32)
+        centred = x - jnp.mean(x, axis=1, keepdims=True)
+        variance = jnp.mean(centred * centred, axis=1, keepdims=True)
+        unit = centred * lax.rsqrt(variance + EPS)
+        standard[at, :] = unit
+        normed_ref[at, :] = (unit * gain).astype(BF16)
+
+    zeros = jnp.zeros((MARGIN, LANES), F32)
+    for u in range(count):
+        for tile in range(tiles):
+            for ref in (pad, gpad):
+                ref[u, tile, :MARGIN, :] = zeros
+                ref[u, tile, MARGIN + length :, :] = zeros
+    small_ref[...] = jnp.zeros_like(small_ref)
+
+    for b in range(n_blocks):
+        @pl.when(meta[b] >= 0)
+        def _():
+            for copy in copies(b):
+                copy.wait()
+
+    expanded = jnp.dot(normed_ref[...], we[...], preferred_element_type=F32)
+    for tile in range(2 * tiles):
+        ab[tile] = expanded[:, tile * LANES : (tile + 1) * LANES]
+
+    first = (taps - 1) // 2
+    positions = lax.broadcasted_iota(jnp.int32, (length, LANES), 0)
+
+    @pl.loop(0, count)
+    def _(u):
+        at = pl.ds(pl.multiple_of(u * length, length), length)
+        live = positions < meta[n_blocks + u]
+        for tile in range(tiles):
+            lanes = pl.ds(tile * LANES, LANES)
+            gate = jax.nn.sigmoid(ab[tiles + tile, at, :])
+            glu = jnp.where(live, ab[tile, at, :] * gate, 0.0).astype(BF16).astype(F32)
+            pad[u, tile, MARGIN : MARGIN + length, :] = glu
+            ab[tiles + tile, at, :] = gate
+            conv = jnp.broadcast_to(taps_ref[taps : taps + 1, lanes], (length, LANES))
+            for t in range(taps):
+                conv += taps_ref[t : t + 1, lanes] * pad[u, tile, pl.ds(MARGIN - first + t, length), :]
+            sig = jax.nn.sigmoid(conv)
+            sw_ref[at, lanes] = jnp.where(live, conv * sig, 0.0).astype(BF16)
+            slope[u, tile] = jnp.where(live, sig * (1.0 + conv * (1.0 - sig)), 0.0)
+
+    grad_swish = lax.dot_general(g_ref[...], wp[...], NT, preferred_element_type=F32)
+    for u in range(count):
+        for tile in range(tiles):
+            gpad[u, tile, MARGIN : MARGIN + length, :] = (
+                grad_swish[u * length : (u + 1) * length, tile * LANES : (tile + 1) * LANES]
+                * slope[u, tile]
+            )
+
+    def fold(value):
+        return jnp.sum(value.reshape(length // 8, 8, LANES), axis=0)
+
+    @pl.loop(0, count)
+    def _(u):
+        at = pl.ds(pl.multiple_of(u * length, length), length)
+        live = positions < meta[n_blocks + u]
+        for tile in range(tiles):
+            lanes = pl.ds(tile * LANES, LANES)
+            grad_conv = gpad[u, tile, MARGIN : MARGIN + length, :]
+            grad_glu = jnp.zeros((length, LANES), F32)
+            for t in range(taps):
+                small_ref[tile, t] += fold(
+                    pad[u, tile, pl.ds(MARGIN - first + t, length), :] * grad_conv
+                )
+                grad_glu += (
+                    taps_ref[t : t + 1, lanes] * gpad[u, tile, pl.ds(MARGIN + first - t, length), :]
+                )
+            small_ref[tile, taps] += fold(grad_conv)
+            grad_glu = jnp.where(live, grad_glu, 0.0)
+            gate = ab[tiles + tile, at, :]
+            through = grad_glu * gate
+            ge_ref[at, lanes] = through.astype(BF16)
+            ge_ref[at, pl.ds(channels + tile * LANES, LANES)] = (
+                through * ab[tile, at, :] * (1.0 - gate)
+            ).astype(BF16)
+
+    span = 512
+    for start in range(0, width, span):
+        cols = slice(start, start + span)
+        grad_normed = lax.dot_general(ge_ref[...], we[cols, :], NT, preferred_element_type=F32)
+        gn_ref[:, cols] = grad_normed.astype(BF16)
+        gain_part_ref[:, cols] = jnp.sum(
+            (grad_normed * standard[:, cols]).reshape(rows // 8, 8, span), axis=0
+        )
+
+
+def chunk_call(x, g, gain, taps_table, blocks, owners, lengths, owned, part, taps):
+    count, length, width = x.shape
+    rows = count * length
+    wide = blocks[0].shape[1]
+    channels = wide // 2
+    tiles = channels // LANES
+    n_blocks = len(blocks)
+    meta = jnp.concatenate([owners, lengths]).astype(jnp.int32)
+    vmem = pl.BlockSpec(memory_space=pltpu.VMEM)
+    anywhere = pl.BlockSpec(memory_space=pl.ANY)
+    flops = 2 * rows * width * wide * 3
+    return pl.pallas_call(
+        functools.partial(chunk_kernel, (count, length, owned, part, taps, n_blocks)),
+        out_shape=(
+            jax.ShapeDtypeStruct((rows, width), BF16),
+            jax.ShapeDtypeStruct((rows, channels), BF16),
+            jax.ShapeDtypeStruct((rows, wide), BF16),
+            jax.ShapeDtypeStruct((rows, width), BF16),
+            jax.ShapeDtypeStruct((tiles, taps + 1, 8, LANES), F32),
+            jax.ShapeDtypeStruct((8, width), F32),
+        ),
+        in_specs=[pl.BlockSpec(memory_space=pltpu.SMEM)] + [vmem] * 4 + [anywhere] * n_blocks,
+        out_specs=(vmem,) * 6,
+        scratch_shapes=[
+            pltpu.VMEM((width, wide), BF16),
+            pltpu.VMEM((channels, width), BF16),
+            pltpu.VMEM((2 * tiles, rows, LANES), F32),
+            pltpu.VMEM((rows, width), F32),
+            pltpu.VMEM((count, tiles, length + 2 * MARGIN, LANES), F32),
+            pltpu.VMEM((count, tiles, length + 2 * MARGIN, LANES), F32),
+            pltpu.VMEM((count, tiles, length, LANES), F32),
+            pltpu.SemaphoreType.DMA((n_blocks, 1 + width // wide)),
+        ],
+        compiler_params=pltpu.CompilerParams(vmem_limit_bytes=VMEM_BYTES),
+        cost_estimate=pl.CostEstimate(
+            flops=flops, bytes_accessed=6 * rows * width * 2, transcendentals=rows * wide
+        ),
+        name="chunk",
+    )(meta, x.reshape(rows, width), g.reshape(rows, width), gain, taps_table, *blocks)
+
+
+def vmem_params():
+    return pltpu.CompilerParams(vmem_limit_bytes=VMEM_BYTES)
+
+
+def in_vmem():
+    return pl.BlockSpec(memory_space=pltpu.VMEM)
+
+
+def in_smem():
+    return pl.BlockSpec(memory_space=pltpu.SMEM)
+
+
+def owned_column(channel, index, owned, part):
+    return (channel // part) * owned + index * part + channel % part
+
+
+def pack_kernel(meta, expand_ref, project_ref, pack_ref):
+    owned, width = project_ref.shape
+    wide = pack_ref.shape[1]
+    channels = wide // 2
+    part = owned * channels // width
+    index = meta[0]
+    row = lax.broadcasted_iota(jnp.int32, (width, channels), 0)
+    col = lax.broadcasted_iota(jnp.int32, (width, channels), 1)
+    pick = (row == owned_column(col, index, owned, part)).astype(F32).astype(BF16)
+    for h in range(2):
+        pack_ref[:owned, h * channels : (h + 1) * channels] = jnp.dot(
+            expand_ref[:, h * width : (h + 1) * width], pick, preferred_element_type=F32
+        ).astype(BF16)
+    rows = project_ref[pl.ds(pl.multiple_of(index * part, part), part), :]
+    for h in range(width // wide):
+        pack_ref[owned + h * part : owned + (h + 1) * part, :] = rows[:, h * wide : (h + 1) * wide]
+
+
+def pack_call(index, expand_weight, project_weight, part, wide):
+    owned, width = project_weight.shape
+    return pl.pallas_call(
+        pack_kernel,
+        out_shape=jax.ShapeDtypeStruct((owned + width // wide * part, wide), BF16),
+        in_specs=[in_smem(), in_vmem(), in_vmem()],
+        out_specs=in_vmem(),
+        compiler_params=vmem_params(),
+        cost_estimate=pl.CostEstimate(
+            flops=2 * owned * width * wide, bytes_accessed=8 * owned * width, transcendentals=0
+        ),
+        name="pack",
+    )(index.reshape(1), expand_weight, project_weight)
+
+
+def grads_kernel(dims, meta, *refs):
+    n, chips, owned, part, taps = dims
+    normed, ge, sw, g, small, gain = [refs[i * n : (i + 1) * n] for i in range(6)]
+    keep, give = refs[6 * n :]
+    core = meta[0]
+    wide = ge[0].shape[1]
+    width = normed[0].shape[1]
+    channels = wide // 2
+    tiles = channels // LANES
+
+    def emit(chip, which, rows, cols, value):
+        @pl.when(core == which)
+        def _():
+            keep[chip, rows, cols] = value
+
+        @pl.when(core != which)
+        def _():
+            give[chip, rows, cols] = value
+
+    def total(left, right):
+        out = None
+        for a, b in zip(left, right):
+            term = lax.dot_general(a, b[...], TN, preferred_element_type=F32)
+            out = term if out is None else out + term
+        return out
+
+    every = slice(None)
+    for chip in range(chips):
+        cols = slice(2 * chip * owned, 2 * (chip + 1) * owned)
+        block = total([a[:, cols] for a in normed], ge).astype(BF16)
+        for which in range(2):
+            emit(chip, which, slice(0, owned), every, block[which * owned : (which + 1) * owned])
+    block = total([a[...] for a in sw], g).astype(BF16)
+    sums = sum(a[...] for a in small)
+    sums = jnp.sum(sums, axis=2)
+    sums = jnp.concatenate([sums[tile] for tile in range(tiles)], axis=1)
+    gains = jnp.sum(sum(a[...] for a in gain), axis=0, keepdims=True)
+    base = owned + width // wide * part
+    for chip in range(chips):
+        for which in range(2):
+            owner = 2 * chip + which
+            rows = block[owner * part : (owner + 1) * part]
+            for h in range(width // wide):
+                emit(
+                    chip,
+                    which,
+                    slice(owned + h * part, owned + (h + 1) * part),
+                    every,
+                    rows[:, h * wide : (h + 1) * wide],
+                )
+            mine = sums[:, owner * part : (owner + 1) * part]
+            pad = jnp.zeros((16, LANES - part), F32)
+            own_gain = gains[:, owner * owned : (owner + 1) * owned]
+            line = jnp.concatenate(
+                [mine[:16], pad, mine[16:], pad, jnp.broadcast_to(own_gain, (16, owned))], axis=1
+            )
+            line = jnp.concatenate(
+                [line, jnp.zeros((16, wide - line.shape[1]), F32)], axis=1
+            ).astype(BF16)
+            emit(chip, which, slice(base, base + 16), every, line)
+
+
+def grads_call(core, normed, ge, sw, g, small, gain, owned, part, taps):
+    n = len(normed)
+    rows, width = normed[0].shape
+    wide = ge[0].shape[1]
+    chips = width // owned // 2
+    height = owned + width // wide * part + 16
+    shape = jax.ShapeDtypeStruct((chips, height, wide), BF16)
+    return pl.pallas_call(
+        functools.partial(grads_kernel, (n, chips, owned, part, taps)),
+        out_shape=(shape, shape),
+        in_specs=[in_smem()] + [in_vmem()] * (6 * n),
+        out_specs=(in_vmem(), in_vmem()),
+        compiler_params=vmem_params(),
+        cost_estimate=pl.CostEstimate(
+            flops=3 * n * rows * width * wide,
+            bytes_accessed=n * rows * width * 8,
+            transcendentals=0,
+        ),
+        name="weight_grads",
+    )(core.reshape(1), *normed, *ge, *sw, *g, *small, *gain)
+
+
+def route_kernel(n, meta, *refs):
+    me = meta[0]
+    for m in range(n):
+        for k in range(n):
+            chosen = meta[1 + k * n + (me ^ m)]
+            refs[n + m][k] = refs[k][chosen]
+
+
+def route_call(meta, swished, length):
+    n = len(swished)
+    channels = swished[0].shape[1]
+    shape = jax.ShapeDtypeStruct((n, length, channels), BF16)
+    return pl.pallas_call(
+        functools.partial(route_kernel, n),
+        out_shape=(shape,) * n,
+        in_specs=[in_smem()] + [in_vmem()] * n,
+        out_specs=(in_vmem(),) * n,
+        compiler_params=vmem_params(),
+        cost_estimate=pl.CostEstimate(
+            flops=0, bytes_accessed=4 * n * n * length * channels, transcendentals=0
+        ),
+        name="route",
+    )(meta, *[a.reshape(n, length, channels) for a in swished])
+
+
+def encode_kernel(dims, meta, *refs):
+    n, n_blocks, length, owned, part = dims
+    pieces = refs[:n]
+    frames = refs[n : 2 * n]
+    blocks = refs[2 * n : 2 * n + n_blocks]
+    out_ref = refs[2 * n + n_blocks]
+    cat, weight, residual, frame_sems, sems = refs[2 * n + n_blocks + 1 :]
+    channels = pieces[0].shape[2]
+    me = meta[0]
+    first = 1 + n * n
+
+    def weight_copies(b):
+        owner = meta[first + b]
+        return [
+            pltpu.make_async_copy(
+                blocks[b].at[pl.ds(i * part, part)],
+                weight.at[pl.ds(pl.multiple_of(i * channels + owner * part, part), part)],
+                sems.at[b, i],
+            )
+            for i in range(n)
+        ]
+
+    frame_copies = [
+        pltpu.make_async_copy(
+            frames[k].at[meta[1 + k * n + me]], residual.at[me ^ k], frame_sems.at[k]
+        )
+        for k in range(n)
+    ]
+    for copy in frame_copies:
+        copy.start()
+    for b in range(n_blocks):
+        @pl.when(meta[first + b] >= 0)
+        def _():
+            for copy in weight_copies(b):
+                copy.start()
+
+    for m in range(n):
+        lanes = pl.ds(pl.multiple_of((me ^ m) * channels, channels), channels)
+        for k in range(n):
+            rows = pl.ds(pl.multiple_of((me ^ m ^ k) * length, length), length)
+            cat[rows, lanes] = pieces[m][k]
+    for copy in frame_copies:
+        copy.wait()
+    for b in range(n_blocks):
+        @pl.when(meta[first + b] >= 0)
+        def _():
+            for copy in weight_copies(b):
+                copy.wait()
+
+    for r in range(n):
+        term = jnp.dot(
+            cat[r * length : (r + 1) * length, :], weight[...], preferred_element_type=F32
+        )
+        out_ref[r] = (residual[r].astype(F32) + term).astype(BF16)
+
+
+def encode_call(me, orders, pieces, frames, blocks, owners, owned, part):
+    n, length, channels = pieces[0].shape
+    width = blocks[0].shape[1]
+    n_blocks = len(blocks)
+    meta = jnp.concatenate([me.reshape(1), orders, owners])
+    anywhere = pl.BlockSpec(memory_space=pl.ANY)
+    return pl.pallas_call(
+        functools.partial(encode_kernel, (n, n_blocks, length, owned, part)),
+        out_shape=jax.ShapeDtypeStruct((n, length, width), BF16),
+        in_specs=[in_smem()] + [in_vmem()] * n + [anywhere] * (n + n_blocks),
+        out_specs=in_vmem(),
+        scratch_shapes=[
+            pltpu.VMEM((n * length, width), BF16),
+            pltpu.VMEM((width, width), BF16),
+            pltpu.VMEM((n, length, width), BF16),
+            pltpu.SemaphoreType.DMA((n,)),
+            pltpu.SemaphoreType.DMA((n_blocks, n)),
+        ],
+        compiler_params=vmem_params(),
+        cost_estimate=pl.CostEstimate(
+            flops=2 * n * length * width * width, bytes_accessed=4 * width * width, transcendentals=0
+        ),
+        name="encode",
+    )(meta, *pieces, *frames, *blocks)
+
+
+def frame_grad_kernel(n, x_ref, g_ref, gain_ref, *refs):
+    out_ref = refs[n]
+    x = x_ref[...].astype(F32)
+    centred = x - jnp.mean(x, axis=1, keepdims=True)
+    inverse = lax.rsqrt(jnp.mean(centred * centred, axis=1, keepdims=True) + EPS)
+    standard = centred * inverse
+    grad = sum(ref[...].astype(F32) for ref in refs[:n]) * gain_ref[...]
+    grad_in = inverse * (
+        grad
+        - jnp.mean(grad, axis=1, keepdims=True)
+        - standard * jnp.mean(grad * standard, axis=1, keepdims=True)
+    )
+    out_ref[...] = (g_ref[...].astype(F32) + grad_in).astype(BF16)
+
+
+def frame_grad_call(x, g, gain, returned):
+    count, length, width = x.shape
+    rows = count * length
+    step = 64
+    block = pl.BlockSpec((step, width), lambda s: (s, 0))
+    out = pl.pallas_call(
+        functools.partial(frame_grad_kernel, len(returned)),
+        out_shape=jax.ShapeDtypeStruct((rows, width), BF16),
+        grid=(rows // step,),
+        in_specs=[block, block, pl.BlockSpec((1, width), lambda s: (0, 0))]
+        + [block] * len(returned),
+        out_specs=block,
+        compiler_params=vmem_params(),
+        cost_estimate=pl.CostEstimate(
+            flops=20 * rows * width, bytes_accessed=14 * rows * width, transcendentals=rows
+        ),
+        name="frame_grad",
+    )(x.reshape(rows, width), g.reshape(rows, width), gain, *returned)
+    return out.reshape(count, length, width)
+
+
+def unpack_kernel(dims, meta, *refs):
+    n, owned, part = dims
+    blocks = refs[:n]
+    expand_ref, project_ref, cat = refs[n:]
+    wide = blocks[0].shape[1]
+    channels = wide // 2
+    width = project_ref.shape[1]
+    me = meta[0]
+    row = lax.broadcasted_iota(jnp.int32, (width, width), 0)
+    col = lax.broadcasted_iota(jnp.int32, (width, width), 1)
+    place = owned_column(row % channels, row // channels, owned, part)
+    spread = (place == col).astype(F32).astype(BF16)
+    for k in range(n):
+        index = me ^ k
+        lanes = pl.ds(pl.multiple_of(index * channels, channels), channels)
+        for h in range(2):
+            cat[h, :, lanes] = blocks[k][:owned, h * channels : (h + 1) * channels]
+        rows = pl.ds(pl.multiple_of(index * part, part), part)
+        for h in range(width // wide):
+            project_ref[rows, h * wide : (h + 1) * wide] = blocks[k][
+                owned + h * part : owned + (h + 1) * part, :
+            ].astype(F32)
+    for h in range(2):
+        expand_ref[:, h * width : (h + 1) * width] = jnp.dot(
+            cat[h], spread, preferred_element_type=F32
+        )
+
+
+def unpack_call(me, blocks, owned, part, width):
+    return pl.pallas_call(
+        functools.partial(unpack_kernel, (len(blocks), owned, part)),
+        out_shape=(
+            jax.ShapeDtypeStruct((owned, 2 * width), F32),
+            jax.ShapeDtypeStruct((owned, width), F32),
+        ),
+        in_specs=[in_smem()] + [in_vmem()] * len(blocks),
+        out_specs=(in_vmem(), in_vmem()),
+        scratch_shapes=[pltpu.VMEM((2, owned, width), BF16)],
+        compiler_params=vmem_params(),
+        cost_estimate=pl.CostEstimate(
+            flops=4 * owned * width * width, bytes_accessed=18 * owned * width, transcendentals=0
+        ),
+        name="unpack",
+    )(me.reshape(1), *blocks)
+
+
+def along_z(x, pairs):
+    return lax.ppermute(x, "shard", [(2 * a + c, 2 * b + c) for a, b in pairs for c in range(2)])
+
+
+RIGHT = [(0, 1), (1, 2), (2, 3)]
+LEFT = [(3, 2), (2, 1), (1, 0)]
+
+
+def gather_line(x, chip, core):
+    right = along_z(x, RIGHT)
+    left = along_z(x, LEFT)
+    right2 = along_z(right, [(1, 2), (2, 3)])
+    left2 = along_z(left, [(2, 1), (1, 0)])
+    second = jnp.where(chip >= 2, right2, left2)
+    third = along_z(second, [(1, 0), (2, 3)])
+    blocks = [x, right, left, second, third]
+    chips = [
+        chip,
+        jnp.where(chip >= 1, chip - 1, -1),
+        jnp.where(chip <= 2, chip + 1, -1),
+        jnp.where(chip >= 2, chip - 2, chip + 2),
+        jnp.where(chip == 0, 3, jnp.where(chip == 3, 0, -1)),
+    ]
+    others = [swap(block, "shard", 8, 1) for block in blocks]
+    owners = [jnp.where(c >= 0, 2 * c + core, -1) for c in chips]
+    owners += [jnp.where(c >= 0, 2 * c + 1 - core, -1) for c in chips]
+    return blocks + others, jnp.stack(owners).astype(jnp.int32)
+
+
+def reduce_line(keep, give, chip):
+    got = swap(give, "shard", 8, 1)
+
+    def block(at):
+        return lax.dynamic_index_in_dim(keep, at, 0, False).astype(
+            F32
+        ) + lax.dynamic_index_in_dim(got, at, 0, False).astype(F32)
+
+    def send(at, carried, pairs):
+        value = block(at)
+        if carried is not None:
+            value = value + carried.astype(F32)
+        return along_z(value.astype(BF16), pairs)
+
+    far = send(jnp.where(chip <= 1, 3, 0), None, [(0, 1), (3, 2)])
+    right = send(jnp.minimum(chip + 2, 3), far, [(0, 1), (1, 2)])
+    left = send(jnp.maximum(chip - 2, 0), far, [(3, 2), (2, 1)])
+    right = send(jnp.minimum(chip + 1, 3), right, RIGHT)
+    left = send(jnp.maximum(chip - 1, 0), left, LEFT)
+    return (block(chip) + right.astype(F32) + left.astype(F32)).astype(BF16)
+
+
+def fast_body(
+    frames,
+    cotangent,
+    lengths,
+    send_order,
+    norm_gain,
+    conv_bias,
+    kernel,
+    expand_weight,
+    project_weight,
+):
+    n_dp, n_shard = lax.axis_size("dp"), lax.axis_size("shard")
+    count, length, width = frames.shape
+    owned, taps = kernel.shape
+    part = owned // n_dp
+    channels = n_shard * part
+    wide = 2 * channels
+    me = lax.axis_index("dp").astype(jnp.int32)
+    shard = lax.axis_index("shard").astype(jnp.int32)
+    chip, core = shard // 2, shard % 2
+
+    x_all = gather_dp(frames, n_dp)
+    g_all = gather_dp(cotangent, n_dp)
+    small_ints = jnp.concatenate([lengths, send_order])
+    ints = [small_ints] + [swap(small_ints, "dp", n_dp, k) for k in range(1, n_dp)]
+    orders = jnp.concatenate([a[count:] for a in ints])
+
+    small = jnp.concatenate(
+        [
+            lax.dynamic_slice_in_dim(kernel, me * part, part, axis=0).T,
+            lax.dynamic_slice_in_dim(conv_bias, me * part, part, axis=0)[None],
+            norm_gain.reshape(n_dp, part),
+        ],
+        axis=0,
+    )
+    small_all = gather_shard(small, n_shard)
+    taps_table = (
+        small_all[:, : taps + 1].transpose(1, 0, 2).reshape(taps + 1, channels).astype(F32)
+    )
+    gain = small_all[:, taps + 1 :].reshape(1, width).astype(F32)
+
+    pack = pack_call(me, expand_weight, project_weight, part, wide)
+    packs, owners = gather_line(pack, chip, core)
+    project_blocks, _ = gather_line(project_weight, chip, core)
+
+    normed, swished, ge, returned, small_parts, gain_parts = [], [], [], [], [], []
+    for k in range(n_dp):
+        out = chunk_call(
+            x_all[k], g_all[k], gain, taps_table, packs, owners, ints[k][:count], owned, part, taps
+        )
+        normed.append(out[0])
+        swished.append(out[1])
+        ge.append(out[2])
+        returned.append(out[3] if k == 0 else swap(out[3], "dp", n_dp, k))
+        small_parts.append(out[4])
+        gain_parts.append(out[5])
+
+    keep, give = grads_call(
+        core,
+        normed,
+        ge,
+        swished,
+        [a.reshape(count * length, width) for a in g_all],
+        small_parts,
+        gain_parts,
+        owned,
+        part,
+        taps,
+    )
+    reduced = reduce_line(keep, give, chip)
+
+    pieces = route_call(jnp.concatenate([me.reshape(1), orders]), swished, length)
+    pieces = [pieces[0]] + [swap(pieces[m], "dp", n_dp, m) for m in range(1, n_dp)]
+    encoded = encode_call(me, orders, pieces, x_all, project_blocks, owners, owned, part)
+
+    frame_grad = frame_grad_call(frames, cotangent, gain, returned)
+
+    gathered = gather_dp(reduced, n_dp)
+    expand_grad, project_grad = unpack_call(me, gathered, owned, part, width)
+    base = owned + width // wide * part
+    tails = jnp.stack([a[base:] for a in gathered])
+    tails = jnp.take(tails, me ^ jnp.arange(n_dp), axis=0).astype(F32)
+    table = jnp.concatenate([tails[:, :, :part], tails[:, :, LANES : LANES + part]], axis=1)
+    table = table.transpose(0, 2, 1).reshape(owned, taps + 1)
+    gain_grad = jnp.sum(tails[:, 0, 2 * LANES : 2 * LANES + owned], axis=0)
+    return (
+        encoded,
+        frame_grad,
+        gain_grad,
+        table[:, taps],
+        table[:, :taps],
+        expand_grad,
+        project_grad,
+    )
 
 
 def depthwise(signal, taps_table):
@@ -119,7 +772,7 @@
     return lax.psum_scatter(x, "shard", scatter_dimension=0, tiled=False).astype(F32)
 
 
-def body(
+def generic_body(
     frames,
     cotangent,
     lengths,
@@ -297,6 +950,11 @@
     return encoded, frame_grad, gain_grad, bias_grad, kernel_grad, expand_grad, project_grad
 
 
+def body(*arrays):
+    fast = lax.axis_size("dp") == 4 and lax.axis_size("shard") == 8
+    return (fast_body if fast else generic_body)(*arrays)
+
+
 def solution(mesh):
     return jax.shard_map(
         body,

time: 479 us -> 289 us (0.60); the launches traced: 471 us -> 287 us
  local copies, waits for them, and re-layouts: 195 us -> 23.7 us
  Pallas kernels: 0 us -> 82.3 us
  other arithmetic: 96.2 us -> 16.7 us
  matrix products: 38.2 us -> 0 us
  starting transfers between devices: 39.8 us -> 76.7 us
  waiting for transfers between devices: 99.7 us -> 85.8 us
    another operation x132 -> x4, local copies, waits for them, and re-layouts: 97.3 us -> 1.48 us  [fast_body(): tails = jnp.stack([a[base:] for a in gathered])]
    pallas_call x0 -> x10, Pallas kernels: none -> 82.3 us  [the longest x4 41.3 us: chunk_call(): pl.pallas_call(functools.partial(chunk_kernel, (count, length, owned, par...]
    ppermute x3 -> x15, starting transfers between devices: 6.49 us -> 46 us  [along_z(): lax.ppermute(x, 'shard', [(2 * a + c, 2 * b + c) for a, b in pairs for c...]
    dot_general x24 -> x0, matrix products: 38.2 us -> none  [the longest x4 11.7 us: body(): lax.dot_general(a, b, (((0,), (0,)), ((), ())), preferred_element_type=F32)]
    ppermute x6 -> x3, waiting for transfers between devices: 29 us -> 0.01 us  [gather_shard(): lax.ppermute(x, 'shard', [(p, (p + 2 * k) % 8) for p in range(8)])]
    ppermute x24 -> x33, waiting for transfers between devices: 35 us -> 62.9 us  [swap(): return lax.ppermute(x, axis, [(p, p ^ k) for p in range(size)])]
    reduce_sum x18 -> x1, other arithmetic: 17.1 us -> 0.58 us  [fast_body(): gain_grad = jnp.sum(tails[:, 0, 2 * LANES:2 * LANES + owned], axis=0)]
    slice x19 -> x5, local copies, waits for them, and re-layouts: 18.6 us -> 2.3 us  [the longest x3 1.72 us: fast_body(): ints[k][:count]]
  transfers between devices with their start and end apart: 33 -> 51, of which waited for: 14 -> 17; matrix products, arithmetic and copies ran while one was open for 59% -> 12% of each run, Pallas kernels for 0% -> 7%
where the time goes in v2:
time: 289 us; the launch traced here: 287 us
  waiting for transfers between devices  85.8 us (30%)
  Pallas kernels  82.3 us (28%)
  starting transfers between devices  76.7 us (27%)
  local copies, waits for them, and re-layouts  23.7 us (8%)
  other arithmetic  16.7 us (6%)
    ppermute x33, waiting for transfers between devices, swap(): return lax.ppermute(x, axis, [(p, p ^ k) for p in range(size)])  62.9 us
    ppermute x15, starting transfers between devices, along_z(): lax.ppermute(x, 'shard', [(2 * a + c, 2 * b + c) for a, b in pairs for c...  46 us
    pallas_call x4, Pallas kernels, chunk_call(): pl.pallas_call(functools.partial(chunk_kernel, (count, length, owned, par...  41.3 us
    ppermute x33, starting transfers between devices, swap(): return lax.ppermute(x, axis, [(p, p ^ k) for p in range(size)])  26 us
    ppermute x15, waiting for transfers between devices, along_z(): lax.ppermute(x, 'shard', [(2 * a + c, 2 * b + c) for a, b in pairs for c...  22.9 us
    pallas_call x1, Pallas kernels, grads_call(): pl.pallas_call(functools.partial(grads_kernel, (n, chips, owned, part, ta...  15.3 us
    pallas_call x1, Pallas kernels, encode_call(): pl.pallas_call(functools.partial(encode_kernel, (n, n_blocks, length, own...  8.58 us
    pallas_call x1, Pallas kernels, unpack_call(): pl.pallas_call(functools.partial(unpack_kernel, (len(blocks), owned, part...  6.99 us
  transfers between devices with their start and end apart: 51, of which 17 were waited for; matrix products, arithmetic and copies ran while one was open for 12% of the time, Pallas kernels for 7%

profile of v2, /device:TPU:8, one launch (start us, length us, event | category | flops | bytes accessed | tf_op | source)
XLA Modules:
  0.0 286.6 jit_solution(1335432909409631173)
XLA Ops:
  2.9 1.6 collective-permute-start.3
  4.5 1.1 collective-permute-start.4
  5.6 1.9 collective-permute-start.5
  8.3 2.4 collective-permute-start.2
  10.8 3.0 %pack.1.refs_0_ = bf16[288,768]{1,0:T(8,128)(2,1)} custom-call(s32[1]{0:T(128)} %bitcast.meta, bf16[192,3072]{1,0:T(8,128)(2,1)} %expand_ref.1, bf16[192,1536]{1,0:T(8,128)(2,1)} %refs_8_.1), custom_call_target="tpu_custom_call" | custom-call | flops 452984832 | bytes 2359296 | tf_op jit(solution)/shard_map/pack/pallas_call | solution.py:231
  13.8 3.2 %collective-permute-start.8 = (bf16[288,768]{1,0:T(8,128)(2,1)}, bf16[288,768]{1,0:T(8,128)(2,1)}, u32[]{:S(2)}, u32[]{:S(2)}) collective-permute-start(bf16[288,768]{1,0:T(8,128)(2,1)} %pack.1.refs_0_), channel_id=1, source_target_pairs={{6,4},{7,5},{4,2},{5,3},{2,0},{3,1},{14,12},{15,13},{12,10},{13,11... | collective-permute-start | bytes 1327112 | tf_op jit(solution)/shard_map/ppermute | solution.py:518
  17.9 2.6 collective-permute-start.7
  22.1 1.5 collective-permute-start.17
  26.5 1.3 collective-permute-start.19
  30.6 3.7 %collective-permute-start.10 = (bf16[288,768]{1,0:T(8,128)(2,1)}, bf16[288,768]{1,0:T(8,128)(2,1)}, u32[]{:S(2)}, u32[]{:S(2)}) collective-permute-start(bf16[288,768]{1,0:T(8,128)(2,1)} %collective-permute-done.8.refs_2_), channel_id=1, source_target_pairs={{4,2},{5,3},{2,0},{3,1},{12,10},{13,11},{10,8},{11,9},{20,18},{21,... | collective-permute-start | bytes 1327112 | tf_op jit(solution)/shard_map/ppermute | solution.py:518
  34.3 8.3 %collective-permute-done.17.refs_5_ = bf16[4,64,1536]{2,1,0:T(8,128)(2,1)S(1)} collective-permute-done((bf16[4,64,1536]{2,1,0:T(8,128)(2,1)S(1)}, bf16[4,64,1536]{2,1,0:T(8,128)(2,1)S(1)}, u32[]{:S(2)}, u32[]{:S(2)}) %collective-permute-start.17) | collective-permute-done | bytes 786464 | tf_op jit(solution)/shard_map/ppermute | solution.py:726
  42.6 3.5 %collective-permute-start.9 = (bf16[288,768]{1,0:T(8,128)(2,1)}, bf16[288,768]{1,0:T(8,128)(2,1)}, u32[]{:S(2)}, u32[]{:S(2)}) collective-permute-start(bf16[288,768]{1,0:T(8,128)(2,1)} %collective-permute-done.7.refs_1_), channel_id=1, source_target_pairs={{2,4},{3,5},{4,6},{5,7},{10,12},{11,13},{12,14},{13,15},{18,20},{1... | collective-permute-start | bytes 1327112 | tf_op jit(solution)/shard_map/ppermute | solution.py:518
  48.4 1.7 collective-permute-start.21
  50.9 5.6 %collective-permute-done.18 = bf16[4,64,1536]{2,1,0:T(8,128)(2,1)} collective-permute-done((bf16[4,64,1536]{2,1,0:T(8,128)(2,1)S(1)}, bf16[4,64,1536]{2,1,0:T(8,128)(2,1)}, u32[]{:S(2)}, u32[]{:S(2)}) %collective-permute-start.18) | collective-permute-done | bytes 786464 | tf_op jit(solution)/shard_map/ppermute | solution.py:726
  56.5 1.5 collective-permute-start.22
  58.0 1.8 slice.100
  59.7 4.1 %collective-permute-done.20 = bf16[4,64,1536]{2,1,0:T(8,128)(2,1)} collective-permute-done((bf16[4,64,1536]{2,1,0:T(8,128)(2,1)S(1)}, bf16[4,64,1536]{2,1,0:T(8,128)(2,1)}, u32[]{:S(2)}, u32[]{:S(2)}) %collective-permute-start.20) | collective-permute-done | bytes 786464 | tf_op jit(solution)/shard_map/ppermute | solution.py:726
  63.8 1.3 collective-permute-start.23
  65.1 1.8 slice.101
  67.4 1.1 broadcast_select_fusion.1.refs_3_
  68.4 4.8 %collective-permute-start.11 = (bf16[288,768]{1,0:T(8,128)(2,1)S(1)}, bf16[288,768]{1,0:T(8,128)(2,1)}, u32[]{:S(2)}, u32[]{:S(2)}) collective-permute-start(bf16[288,768]{1,0:T(8,128)(2,1)S(1)} %broadcast_select_fusion.1.refs_3_), channel_id=1, source_target_pairs={{2,0},{3,1},{4,6},{5,7},{10,8},{11,9},{12,14},{13,15},{18,16},{19,... | collective-permute-start | bytes 1327112 | tf_op jit(solution)/shard_map/ppermute | solution.py:518
  74.7 1.0 constant_dynamic-update-slice_fusion.1
  76.3 4.0 %collective-permute-done.23 = bf16[2,64,1536]{2,1,0:T(8,128)(2,1)} collective-permute-done((bf16[2,64,1536]{2,1,0:T(8,128)(2,1)}, bf16[2,64,1536]{2,1,0:T(8,128)(2,1)}, u32[]{:S(2)}, u32[]{:S(2)}) %collective-permute-start.23) | collective-permute-done | bytes 393248 | tf_op jit(solution)/shard_map/ppermute | solution.py:726
  80.9 2.2 pad_maximum_fusion
  84.5 10.4 %chunk.7 = (bf16[256,1536]{1,0:T(8,128)(2,1)}, bf16[256,384]{1,0:T(8,128)(2,1)}, bf16[256,768]{1,0:T(8,128)(2,1)}, bf16[256,1536]{1,0:T(8,128)(2,1)}, f32[3,32,8,128]{3,2,1,0:T(8,128)}, /*index=5*/f32[8,1536]{1,0:T(8,128)}) custom-call(s32[14]{0:T(128)} %concatenate.50.meta, bf16[256,1536]{1,0:T(8,128)(2,1)} %bitcast.82, bf16[256,1536]{1,0:T(8,128)(2,1)} %bitcast.83, ...), custom_call_target="tpu_custom_call" | custom-call | flops 1811939328 | bytes 4718592 | tf_op jit(solution)/shard_map/chunk/pallas_call | solution.py:165
  94.8 10.3 %chunk.6 = (bf16[256,1536]{1,0:T(8,128)(2,1)}, bf16[256,384]{1,0:T(8,128)(2,1)}, bf16[256,768]{1,0:T(8,128)(2,1)}, bf16[256,1536]{1,0:T(8,128)(2,1)}, f32[3,32,8,128]{3,2,1,0:T(8,128)}, /*index=5*/f32[8,1536]{1,0:T(8,128)}) custom-call(s32[14]{0:T(128)} %concatenate.49.meta, bf16[256,1536]{1,0:T(8,128)(2,1)} %bitcast.81, ...), custom_call_target="tpu_custom_call" | custom-call | flops 1811939328 | bytes 4718592 | tf_op jit(solution)/shard_map/chunk/pallas_call | solution.py:165
  105.1 10.3 %chunk.5 = (bf16[256,1536]{1,0:T(8,128)(2,1)}, bf16[256,384]{1,0:T(8,128)(2,1)}, bf16[256,768]{1,0:T(8,128)(2,1)}, bf16[256,1536]{1,0:T(8,128)(2,1)}, f32[3,32,8,128]{3,2,1,0:T(8,128)}, /*index=5*/f32[8,1536]{1,0:T(8,128)}) custom-call(s32[14]{0:T(128)} %concatenate.48.meta, bf16[256,1536]{1,0:T(8,128)(2,1)} %bitcast.80, ...), custom_call_target="tpu_custom_call" | custom-call | flops 1811939328 | bytes 4718592 | tf_op jit(solution)/shard_map/chunk/pallas_call | solution.py:165
  115.5 10.3 %chunk.4 = (bf16[256,1536]{1,0:T(8,128)(2,1)}, bf16[256,384]{1,0:T(8,128)(2,1)}, bf16[256,768]{1,0:T(8,128)(2,1)}, bf16[256,1536]{1,0:T(8,128)(2,1)}, f32[3,32,8,128]{3,2,1,0:T(8,128)}, /*index=5*/f32[8,1536]{1,0:T(8,128)}) custom-call(s32[14]{0:T(128)} %concatenate.46.meta, bf16[256,1536]{1,0:T(8,128)(2,1)} %bitcast.78, bf16[256,1536]{1,0:T(8,128)(2,1)} %bitcast.85, ...), custom_call_target="tpu_custom_call" | custom-call | flops 1811939328 | bytes 4718592 | tf_op jit(solution)/shard_map/chunk/pallas_call | solution.py:165
  125.8 15.3 %weight_grads.1 = (bf16[4,304,768]{2,1,0:T(8,128)(2,1)}, bf16[4,304,768]{2,1,0:T(8,128)(2,1)}) custom-call(s32[1]{0:T(128)} %bitcast.35.meta, bf16[256,1536]{1,0:T(8,128)(2,1)} %get-tuple-element.51.refs_0_, bf16[256,1536]{1,0:T(8,128)(2,1)} %get-tuple-element.52.refs_1_, bf16[256,1536]{1,0:T(8,128)(2,1)} %get-tuple-element.53.refs_2_, ...), custom_call_target="tpu_custom_call" | custom-call | flops 3623878656 | bytes 12582912 | tf_op jit(solution)/shard_map/weight_grads/pallas_call | solution.py:313
  141.6 2.8 collective-permute-start.28
  144.4 3.8 %collective-permute-start.29 = (bf16[192,1536]{1,0:T(8,128)(2,1)S(1)}, bf16[192,1536]{1,0:T(8,128)(2,1)}, u32[]{:S(2)}, u32[]{:S(2)}) collective-permute-start(bf16[192,1536]{1,0:T(8,128)(2,1)S(1)} %copy-done.4), channel_id=1, source_target_pairs={{6,4},{7,5},{4,2},{5,3},{2,0},{3,1},{14,12},{15,13},{12,10},{13,11... | collective-permute-start | bytes 1769480 | tf_op jit(solution)/shard_map/ppermute | solution.py:518
  148.3 1.5 fusion.6
  149.8 1.3 collective-permute-start.42
  151.1 8.7 %collective-permute-done.28.refs_9_ = bf16[192,1536]{1,0:T(8,128)(2,1)} collective-permute-done((bf16[192,1536]{1,0:T(8,128)(2,1)S(1)}, bf16[192,1536]{1,0:T(8,128)(2,1)}, u32[]{:S(2)}, u32[]{:S(2)}) %collective-permute-start.28) | collective-permute-done | bytes 589856 | tf_op jit(solution)/shard_map/ppermute | solution.py:518
  159.8 2.0 collective-permute-start.30
  161.8 3.7 %collective-permute-start.31 = (bf16[192,1536]{1,0:T(8,128)(2,1)}, bf16[192,1536]{1,0:T(8,128)(2,1)}, u32[]{:S(2)}, u32[]{:S(2)}) collective-permute-start(bf16[192,1536]{1,0:T(8,128)(2,1)} %collective-permute-done.29.refs_10_), channel_id=1, source_target_pairs={{4,2},{5,3},{2,0},{3,1},{12,10},{13,11},{10,8},{11,9},{20,18},{21,... | collective-permute-start | bytes 1769480 | tf_op jit(solution)/shard_map/ppermute | solution.py:518
  166.0 3.1 %collective-permute-done.42 = bf16[304,768]{1,0:T(8,128)(2,1)} collective-permute-done((bf16[304,768]{1,0:T(8,128)(2,1)S(1)}, bf16[304,768]{1,0:T(8,128)(2,1)}, u32[]{:S(2)}, u32[]{:S(2)}) %collective-permute-start.42) | collective-permute-done | bytes 466976 | tf_op jit(solution)/shard_map/ppermute | solution.py:518
  169.1 2.7 fusion
  171.8 2.2 collective-permute-done.30
  174.0 4.3 %collective-permute-start.43 = (bf16[304,768]{1,0:T(8,128)(2,1)S(1)}, bf16[304,768]{1,0:T(8,128)(2,1)S(1)}, u32[]{:S(2)}, u32[]{:S(2)}) collective-permute-start(bf16[304,768]{1,0:T(8,128)(2,1)S(1)} %get-tuple-element.71), channel_id=1, source_target_pairs={{0,2},{1,3},{2,4},{3,5},{8,10},{9,11},{10,12},{11,13},{16,18},{17,... | collective-permute-start | bytes 1400840 | tf_op jit(solution)/shard_map/ppermute | solution.py:518
  178.3 1.3 collective-permute-start.45
  179.6 1.1 broadcast_select_fusion.refs_11_
  180.8 6.2 %collective-permute-done.43 = bf16[304,768]{1,0:T(8,128)(2,1)S(1)} collective-permute-done((bf16[304,768]{1,0:T(8,128)(2,1)S(1)}, bf16[304,768]{1,0:T(8,128)(2,1)S(1)}, u32[]{:S(2)}, u32[]{:S(2)}) %collective-permute-start.43) | collective-permute-done | bytes 466976 | tf_op jit(solution)/shard_map/ppermute | solution.py:518
  186.9 2.1 collective-permute-start.32
  189.1 2.3 collective-permute-done.45
  191.4 2.6 fusion.3
  194.0 2.2 collective-permute-start.44
  196.1 4.7 %collective-permute-start.46 = (bf16[304,768]{1,0:T(8,128)(2,1)}, bf16[304,768]{1,0:T(8,128)(2,1)}, u32[]{:S(2)}, u32[]{:S(2)}) collective-permute-start(bf16[304,768]{1,0:T(8,128)(2,1)} %get-tuple-element.74), channel_id=1, source_target_pairs={{6,4},{7,5},{4,2},{5,3},{2,0},{3,1},{14,12},{15,13},{12,10},{13,11... | collective-permute-start | bytes 1400840 | tf_op jit(solution)/shard_map/ppermute | solution.py:518
  201.5 2.2 route.1
  203.7 1.3 collective-permute-start.25
  205.8 4.8 %collective-permute-done.25.refs_1_ = bf16[4,64,384]{2,1,0:T(8,128)(2,1)S(1)} collective-permute-done((bf16[4,64,384]{2,1,0:T(8,128)(2,1)}, bf16[4,64,384]{2,1,0:T(8,128)(2,1)S(1)}, u32[]{:S(2)}, u32[]{:S(2)}) %collective-permute-start.25) | collective-permute-done | bytes 196640 | tf_op jit(solution)/shard_map/ppermute | solution.py:726
  211.4 1.5 collective-permute-start.40
  213.6 1.2 collective-permute-start.39
  215.5 1.6 collective-permute-start.27
  217.2 2.3 fusion.5.refs_0_
  219.5 32.8 %collective-permute-done.27.refs_3_ = bf16[4,64,384]{2,1,0:T(8,128)(2,1)} collective-permute-done((bf16[4,64,384]{2,1,0:T(8,128)(2,1)}, bf16[4,64,384]{2,1,0:T(8,128)(2,1)}, u32[]{:S(2)}, u32[]{:S(2)}) %collective-permute-start.27) | collective-permute-done | bytes 196640 | tf_op jit(solution)/shard_map/ppermute | solution.py:726
  252.3 1.3 collective-permute-start.48
  253.6 0.9 collective-permute-start.47
  255.1 8.6 %encode.1 = bf16[4,64,1536]{2,1,0:T(8,128)(2,1)} custom-call(s32[27]{0:T(128)} %concatenate.44.meta, bf16[4,64,384]{2,1,0:T(8,128)(2,1)} %get-tuple-element.43.refs_0_, bf16[4,64,384]{2,1,0:T(8,128)(2,1)} %copy-done.16, bf16[4,64,384]{2,1,0:T(8,128)(2,1)} %copy-done.17, bf16[4,64,384]{2,1,0:T(8,128)(2,1)} %collective-permute-done.27.refs_3_, ...), custom_call_target="tpu_custom_call" | custom-call | flops 1207959552 | bytes 9437184 | tf_op jit(solution)/shard_map/encode/pallas_call | solution.py:415
  264.8 4.9 %frame_grad.1 = bf16[256,1536]{1,0:T(8,128)(2,1)} custom-call(bf16[256,1536]{1,0:T(8,128)(2,1)} %bitcast.79, bf16[256,1536]{1,0:T(8,128)(2,1)} %bitcast.87, f32[1,1536]{1,0:T(1,128)} %reshape.215.gain_ref, bf16[256,1536]{1,0:T(8,128)(2,1)} %get-tuple-element.47.refs_0_, bf16[256,1536]{1,0:T(8,128)(2,1)} %collective-permute-done.38.refs_1_, ...), custom_call_target="tpu_custom_call" | custom-call | flops 7864320 | bytes 5505024 | tf_op jit(solution)/shard_map/frame_grad/pallas_call | solution.py:455
  270.5 1.2 collective-permute-start.49
  271.7 1.0 slice.112
  274.2 2.3 collective-permute-done.49
  279.6 7.0 %unpack.1 = (f32[192,3072]{1,0:T(8,128)}, f32[192,1536]{1,0:T(8,128)}) custom-call(s32[1]{0:T(128)} %bitcast.meta, bf16[304,768]{1,0:T(8,128)(2,1)} %fusion.5.refs_0_, bf16[304,768]{1,0:T(8,128)(2,1)} %collective-permute-done.47.refs_1_, bf16[304,768]{1,0:T(8,128)(2,1)} %copy-done.18, bf16[304,768]{1,0:T(8,128)(2,1)} %pad_maximum_fusion.1.refs_3_), custom_call_target="tpu_custom_call" | custom-call | flops 1811939328 | bytes 5308416 | tf_op jit(solution)/shard_map/unpack/pallas_call | solution.py:500
  (168 shorter events, 30.2 us)
Async XLA Ops:
  0.6 16.6 %copy-start.24 = (s32[4]{0:T(128)S(1)}, s32[4]{0:T(128)}, u32[]{:S(2)}) copy-start(s32[4]{0:T(128)} %param.11) | copy-start | bytes 52
  0.7 21.5 %copy-start.3 = (bf16[4,64,1536]{2,1,0:T(8,128)(2,1)S(1)}, bf16[4,64,1536]{2,1,0:T(8,128)(2,1)}, u32[]{:S(2)}) copy-start(bf16[4,64,1536]{2,1,0:T(8,128)(2,1)} %refs_4_.1) | copy-start | bytes 2359300
  0.7 27.1 %copy-start.9 = (bf16[4,64,1536]{2,1,0:T(8,128)(2,1)S(1)}, bf16[4,64,1536]{2,1,0:T(8,128)(2,1)}, u32[]{:S(2)}) copy-start(bf16[4,64,1536]{2,1,0:T(8,128)(2,1)} %param.10) | copy-start | bytes 2359300
  2.9 18.2 %collective-permute-start.3 = (bf16[36,48]{1,0:T(8,128)(2,1)S(1)}, bf16[36,48]{1,0:T(8,128)(2,1)S(1)}, u32[]{:S(2)}, u32[]{:S(2)}) collective-permute-start(bf16[36,48]{1,0:T(8,128)(2,1)S(1)} %get-tuple-element.78), channel_id=1, source_target_pairs={{0,2},{1,3},{2,4},{3,5},{4,6},{5,7},{6,0},{7,1},{8,10},{9,11},{10,... | collective-permute-start | bytes 10376 | tf_op jit(solution)/shard_map/ppermute | solution.py:746
  4.5 17.0 %collective-permute-start.4 = (bf16[36,48]{1,0:T(8,128)(2,1)S(1)}, bf16[36,48]{1,0:T(8,128)(2,1)S(1)}, u32[]{:S(2)}, u32[]{:S(2)}) collective-permute-start(bf16[36,48]{1,0:T(8,128)(2,1)S(1)} %get-tuple-element.78), channel_id=1, source_target_pairs={{0,4},{1,5},{2,6},{3,7},{4,0},{5,1},{6,2},{7,3},{8,12},{9,13},{10,... | collective-permute-start | bytes 10376 | tf_op jit(solution)/shard_map/ppermute | solution.py:746
  5.6 16.5 %collective-permute-start.5 = (bf16[36,48]{1,0:T(8,128)(2,1)S(1)}, bf16[36,48]{1,0:T(8,128)(2,1)S(1)}, u32[]{:S(2)}, u32[]{:S(2)}) collective-permute-start(bf16[36,48]{1,0:T(8,128)(2,1)S(1)} %get-tuple-element.78), channel_id=1, source_target_pairs={{0,6},{1,7},{2,0},{3,1},{4,2},{5,3},{6,4},{7,5},{8,14},{9,15},{10,... | collective-permute-start | bytes 10376 | tf_op jit(solution)/shard_map/ppermute | solution.py:746
  8.3 9.6 %collective-permute-start.2 = (s32[8]{0:T(128)S(1)}, s32[8]{0:T(128)S(1)}, u32[]{:S(2)}, u32[]{:S(2)}) collective-permute-start(s32[8]{0:T(128)S(1)} %pad_add_fusion), channel_id=1, source_target_pairs={{0,24},{8,16},{16,8},{24,0},{1,25},{9,17},{17,9},{25,1},{2,26},{10... | collective-permute-start | bytes 104 | tf_op jit(solution)/shard_map/ppermute | solution.py:726
  13.8 14.5 %collective-permute-start.8 = (bf16[288,768]{1,0:T(8,128)(2,1)}, bf16[288,768]{1,0:T(8,128)(2,1)}, u32[]{:S(2)}, u32[]{:S(2)}) collective-permute-start(bf16[288,768]{1,0:T(8,128)(2,1)} %pack.1.refs_0_), channel_id=1, source_target_pairs={{6,4},{7,5},{4,2},{5,3},{2,0},{3,1},{14,12},{15,13},{12,10},{13,11... | collective-permute-start | bytes 1327112 | tf_op jit(solution)/shard_map/ppermute | solution.py:518
  17.9 12.7 %collective-permute-start.7 = (bf16[288,768]{1,0:T(8,128)(2,1)}, bf16[288,768]{1,0:T(8,128)(2,1)}, u32[]{:S(2)}, u32[]{:S(2)}) collective-permute-start(bf16[288,768]{1,0:T(8,128)(2,1)} %pack.1.refs_0_), channel_id=1, source_target_pairs={{0,2},{1,3},{2,4},{3,5},{4,6},{5,7},{8,10},{9,11},{10,12},{11,13},... | collective-permute-start | bytes 1327112 | tf_op jit(solution)/shard_map/ppermute | solution.py:518
  21.1 3.5 %collective-permute-start.1 = (s32[8]{0:T(128)S(1)}, s32[8]{0:T(128)S(1)}, u32[]{:S(2)}, u32[]{:S(2)}) collective-permute-start(s32[8]{0:T(128)S(1)} %pad_add_fusion), channel_id=1, source_target_pairs={{0,16},{8,24},{16,0},{24,8},{1,17},{9,25},{17,1},{25,9},{2,18},{10... | collective-permute-start | bytes 104 | tf_op jit(solution)/shard_map/ppermute | solution.py:726
  21.6 4.9 %collective-permute-start = (s32[8]{0:T(128)S(1)}, s32[8]{0:T(128)S(1)}, u32[]{:S(2)}, u32[]{:S(2)}) collective-permute-start(s32[8]{0:T(128)S(1)} %pad_add_fusion), channel_id=1, source_target_pairs={{0,8},{8,0},{16,24},{24,16},{1,9},{9,1},{17,25},{25,17},{2,10},{10... | collective-permute-start | bytes 104 | tf_op jit(solution)/shard_map/ppermute | solution.py:726
  22.1 20.5 %collective-permute-start.17 = (bf16[4,64,1536]{2,1,0:T(8,128)(2,1)S(1)}, bf16[4,64,1536]{2,1,0:T(8,128)(2,1)S(1)}, u32[]{:S(2)}, u32[]{:S(2)}) collective-permute-start(bf16[4,64,1536]{2,1,0:T(8,128)(2,1)S(1)} %copy-done.3), channel_id=1, source_target_pairs={{0,8},{8,0},{16,24},{24,16},{1,9},{9,1},{17,25},{25,17},{2,10},{10... | collective-permute-start | bytes 2359304 | tf_op jit(solution)/shard_map/ppermute | solution.py:726
  24.6 3.1 %collective-permute-start.6 = (bf16[4,36,48]{2,1,0:T(8,128)(2,1)S(1)}, bf16[4,36,48]{2,1,0:T(8,128)(2,1)S(1)}, u32[]{:S(2)}, u32[]{:S(2)}) collective-permute-start(bf16[4,36,48]{2,1,0:T(8,128)(2,1)S(1)} %broadcast_select_fusion.2), channel_id=1, source_target_pairs={{0,1},{1,0},{2,3},{3,2},{4,5},{5,4},{6,7},{7,6},{8,9},{9,8},{10,11... | collective-permute-start | bytes 41480 | tf_op jit(solution)/shard_map/ppermute | solution.py:726
  26.5 21.9 %collective-permute-start.19 = (bf16[4,64,1536]{2,1,0:T(8,128)(2,1)S(1)}, bf16[4,64,1536]{2,1,0:T(8,128)(2,1)S(1)}, u32[]{:S(2)}, u32[]{:S(2)}) collective-permute-start(bf16[4,64,1536]{2,1,0:T(8,128)(2,1)S(1)} %copy-done.3), channel_id=1, source_target_pairs={{0,16},{8,24},{16,0},{24,8},{1,17},{9,25},{17,1},{25,9},{2,18},{10... | collective-permute-start | bytes 2359304 | tf_op jit(solution)/shard_map/ppermute | solution.py:726
  27.8 28.7 %collective-permute-start.18 = (bf16[4,64,1536]{2,1,0:T(8,128)(2,1)S(1)}, bf16[4,64,1536]{2,1,0:T(8,128)(2,1)}, u32[]{:S(2)}, u32[]{:S(2)}) collective-permute-start(bf16[4,64,1536]{2,1,0:T(8,128)(2,1)S(1)} %copy-done.9), channel_id=1, source_target_pairs={{0,8},{8,0},{16,24},{24,16},{1,9},{9,1},{17,25},{25,17},{2,10},{10... | collective-permute-start | bytes 2359304 | tf_op jit(solution)/shard_map/ppermute | solution.py:726
  28.3 35.5 %collective-permute-start.20 = (bf16[4,64,1536]{2,1,0:T(8,128)(2,1)S(1)}, bf16[4,64,1536]{2,1,0:T(8,128)(2,1)}, u32[]{:S(2)}, u32[]{:S(2)}) collective-permute-start(bf16[4,64,1536]{2,1,0:T(8,128)(2,1)S(1)} %copy-done.9), channel_id=1, source_target_pairs={{0,16},{8,24},{16,0},{24,8},{1,17},{9,25},{17,1},{25,9},{2,18},{10... | collective-permute-start | bytes 2359304 | tf_op jit(solution)/shard_map/ppermute | solution.py:726
  30.6 36.2 %collective-permute-start.10 = (bf16[288,768]{1,0:T(8,128)(2,1)}, bf16[288,768]{1,0:T(8,128)(2,1)}, u32[]{:S(2)}, u32[]{:S(2)}) collective-permute-start(bf16[288,768]{1,0:T(8,128)(2,1)} %collective-permute-done.8.refs_2_), channel_id=1, source_target_pairs={{4,2},{5,3},{2,0},{3,1},{12,10},{13,11},{10,8},{11,9},{20,18},{21,... | collective-permute-start | bytes 1327112 | tf_op jit(solution)/shard_map/ppermute | solution.py:518
  42.6 24.2 %copy-start.6 = (bf16[4,64,1536]{2,1,0:T(8,128)(2,1)}, bf16[4,64,1536]{2,1,0:T(8,128)(2,1)S(1)}, u32[]{:S(2)}) copy-start(bf16[4,64,1536]{2,1,0:T(8,128)(2,1)S(1)} %collective-permute-done.17.refs_5_) | copy-start | bytes 2359300
  42.6 24.8 %collective-permute-start.9 = (bf16[288,768]{1,0:T(8,128)(2,1)}, bf16[288,768]{1,0:T(8,128)(2,1)}, u32[]{:S(2)}, u32[]{:S(2)}) collective-permute-start(bf16[288,768]{1,0:T(8,128)(2,1)} %collective-permute-done.7.refs_1_), channel_id=1, source_target_pairs={{2,4},{3,5},{4,6},{5,7},{10,12},{11,13},{12,14},{13,15},{18,20},{1... | collective-permute-start | bytes 1327112 | tf_op jit(solution)/shard_map/ppermute | solution.py:518
  48.4 25.6 %copy-start.7 = (bf16[4,64,1536]{2,1,0:T(8,128)(2,1)}, bf16[4,64,1536]{2,1,0:T(8,128)(2,1)S(1)}, u32[]{:S(2)}) copy-start(bf16[4,64,1536]{2,1,0:T(8,128)(2,1)S(1)} %collective-permute-done.19.refs_6_) | copy-start | bytes 2359300
  48.4 26.2 %copy-start.13 = (bf16[288,768]{1,0:T(8,128)(2,1)S(1)}, bf16[288,768]{1,0:T(8,128)(2,1)}, u32[]{:S(2)}) copy-start(bf16[288,768]{1,0:T(8,128)(2,1)} %pack.1.refs_0_) | copy-start | bytes 1327108
  48.4 26.2 %collective-permute-start.21 = (bf16[2,64,1536]{2,1,0:T(8,128)(2,1)}, bf16[2,64,1536]{2,1,0:T(8,128)(2,1)}, u32[]{:S(2)}, u32[]{:S(2)}) collective-permute-start(bf16[2,64,1536]{2,1,0:T(8,128)(2,1)} %slice.98), channel_id=1, source_target_pairs={{0,16},{8,24},{16,0},{24,8},{1,17},{9,25},{17,1},{25,9},{2,18},{10... | collective-permute-start | bytes 1179656 | tf_op jit(solution)/shard_map/ppermute | solution.py:726
  56.5 19.2 %collective-permute-start.22 = (bf16[2,64,1536]{2,1,0:T(8,128)(2,1)}, bf16[2,64,1536]{2,1,0:T(8,128)(2,1)S(1)}, u32[]{:S(2)}, u32[]{:S(2)}) collective-permute-start(bf16[2,64,1536]{2,1,0:T(8,128)(2,1)} %slice.99), channel_id=1, source_target_pairs={{0,8},{8,0},{16,24},{24,16},{1,9},{9,1},{17,25},{25,17},{2,10},{10... | collective-permute-start | bytes 1179656 | tf_op jit(solution)/shard_map/ppermute | solution.py:726
  63.8 16.5 %collective-permute-start.23 = (bf16[2,64,1536]{2,1,0:T(8,128)(2,1)}, bf16[2,64,1536]{2,1,0:T(8,128)(2,1)}, u32[]{:S(2)}, u32[]{:S(2)}) collective-permute-start(bf16[2,64,1536]{2,1,0:T(8,128)(2,1)} %slice.100), channel_id=1, source_target_pairs={{0,16},{8,24},{16,0},{24,8},{1,17},{9,25},{17,1},{25,9},{2,18},{10... | collective-permute-start | bytes 1179656 | tf_op jit(solution)/shard_map/ppermute | solution.py:726
  66.8 13.4 %collective-permute-start.24 = (bf16[2,64,1536]{2,1,0:T(8,128)(2,1)}, bf16[2,64,1536]{2,1,0:T(8,128)(2,1)S(1)}, u32[]{:S(2)}, u32[]{:S(2)}) collective-permute-start(bf16[2,64,1536]{2,1,0:T(8,128)(2,1)} %slice.101), channel_id=1, source_target_pairs={{0,8},{8,0},{16,24},{24,16},{1,9},{9,1},{17,25},{25,17},{2,10},{10... | collective-permute-start | bytes 1179656 | tf_op jit(solution)/shard_map/ppermute | solution.py:726
  68.4 15.1 %copy-start.14 = (bf16[288,768]{1,0:T(8,128)(2,1)}, bf16[288,768]{1,0:T(8,128)(2,1)S(1)}, u32[]{:S(2)}) copy-start(bf16[288,768]{1,0:T(8,128)(2,1)S(1)} %broadcast_select_fusion.1.refs_3_) | copy-start | bytes 1327108
  68.4 12.4 %collective-permute-start.11 = (bf16[288,768]{1,0:T(8,128)(2,1)S(1)}, bf16[288,768]{1,0:T(8,128)(2,1)}, u32[]{:S(2)}, u32[]{:S(2)}) collective-permute-start(bf16[288,768]{1,0:T(8,128)(2,1)S(1)} %broadcast_select_fusion.1.refs_3_), channel_id=1, source_target_pairs={{2,0},{3,1},{4,6},{5,7},{10,8},{11,9},{12,14},{13,15},{18,16},{19,... | collective-permute-start | bytes 1327112 | tf_op jit(solution)/shard_map/ppermute | solution.py:518
  74.7 8.4 %collective-permute-start.12 = (bf16[288,768]{1,0:T(8,128)(2,1)S(1)}, bf16[288,768]{1,0:T(8,128)(2,1)S(1)}, u32[]{:S(2)}, u32[]{:S(2)}) collective-permute-start(bf16[288,768]{1,0:T(8,128)(2,1)S(1)} %copy-done.13), channel_id=1, source_target_pairs={{0,1},{1,0},{2,3},{3,2},{4,5},{5,4},{6,7},{7,6},{8,9},{9,8},{10,11... | collective-permute-start | bytes 1327112 | tf_op jit(solution)/shard_map/ppermute | solution.py:726
  75.7 7.4 %collective-permute-start.13 = (bf16[288,768]{1,0:T(8,128)(2,1)}, bf16[288,768]{1,0:T(8,128)(2,1)S(1)}, u32[]{:S(2)}, u32[]{:S(2)}) collective-permute-start(bf16[288,768]{1,0:T(8,128)(2,1)} %collective-permute-done.7.refs_1_), channel_id=1, source_target_pairs={{0,1},{1,0},{2,3},{3,2},{4,5},{5,4},{6,7},{7,6},{8,9},{9,8},{10,11... | collective-permute-start | bytes 1327112 | tf_op jit(solution)/shard_map/ppermute | solution.py:726
  80.3 2.9 %collective-permute-start.14 = (bf16[288,768]{1,0:T(8,128)(2,1)}, bf16[288,768]{1,0:T(8,128)(2,1)S(1)}, u32[]{:S(2)}, u32[]{:S(2)}) collective-permute-start(bf16[288,768]{1,0:T(8,128)(2,1)} %collective-permute-done.8.refs_2_), channel_id=1, source_target_pairs={{0,1},{1,0},{2,3},{3,2},{4,5},{5,4},{6,7},{7,6},{8,9},{9,8},{10,11... | collective-permute-start | bytes 1327112 | tf_op jit(solution)/shard_map/ppermute | solution.py:726
  80.3 2.9 %collective-permute-start.15 = (bf16[288,768]{1,0:T(8,128)(2,1)S(1)}, bf16[288,768]{1,0:T(8,128)(2,1)S(1)}, u32[]{:S(2)}, u32[]{:S(2)}) collective-permute-start(bf16[288,768]{1,0:T(8,128)(2,1)S(1)} %broadcast_select_fusion.1.refs_3_), channel_id=1, source_target_pairs={{0,1},{1,0},{2,3},{3,2},{4,5},{5,4},{6,7},{7,6},{8,9},{9,8},{10,11... | collective-permute-start | bytes 1327112 | tf_op jit(solution)/shard_map/ppermute | solution.py:726
  80.8 2.7 collective-permute-start.16
  125.8 15.8 %copy-start.4 = (bf16[192,1536]{1,0:T(8,128)(2,1)S(1)}, bf16[192,1536]{1,0:T(8,128)(2,1)}, u32[]{:S(2)}) copy-start(bf16[192,1536]{1,0:T(8,128)(2,1)} %refs_8_.1) | copy-start | bytes 1769476
  141.1 7.2 %collective-permute-start.41 = (bf16[4,304,768]{2,1,0:T(8,128)(2,1)}, bf16[4,304,768]{2,1,0:T(8,128)(2,1)S(1)}, u32[]{:S(2)}, u32[]{:S(2)}) collective-permute-start(bf16[4,304,768]{2,1,0:T(8,128)(2,1)} %get-tuple-element.68), channel_id=1, source_target_pairs={{0,1},{1,0},{2,3},{3,2},{4,5},{5,4},{6,7},{7,6},{8,9},{9,8},{10,11... | collective-permute-start | bytes 5603336 | tf_op jit(solution)/shard_map/ppermute | solution.py:726
  141.6 18.1 %collective-permute-start.28 = (bf16[192,1536]{1,0:T(8,128)(2,1)S(1)}, bf16[192,1536]{1,0:T(8,128)(2,1)}, u32[]{:S(2)}, u32[]{:S(2)}) collective-permute-start(bf16[192,1536]{1,0:T(8,128)(2,1)S(1)} %copy-done.4), channel_id=1, source_target_pairs={{0,2},{1,3},{2,4},{3,5},{4,6},{5,7},{8,10},{9,11},{10,12},{11,13},... | collective-permute-start | bytes 1769480 | tf_op jit(solution)/shard_map/ppermute | solution.py:518
  144.4 17.3 %collective-permute-start.29 = (bf16[192,1536]{1,0:T(8,128)(2,1)S(1)}, bf16[192,1536]{1,0:T(8,128)(2,1)}, u32[]{:S(2)}, u32[]{:S(2)}) collective-permute-start(bf16[192,1536]{1,0:T(8,128)(2,1)S(1)} %copy-done.4), channel_id=1, source_target_pairs={{6,4},{7,5},{4,2},{5,3},{2,0},{3,1},{14,12},{15,13},{12,10},{13,11... | collective-permute-start | bytes 1769480 | tf_op jit(solution)/shard_map/ppermute | solution.py:518
  148.3 17.3 %copy-start.2 = (bf16[4,304,768]{2,1,0:T(8,128)(2,1)}, bf16[4,304,768]{2,1,0:T(8,128)(2,1)S(1)}, u32[]{:S(2)}) copy-start(bf16[4,304,768]{2,1,0:T(8,128)(2,1)S(1)} %collective-permute-done.41) | copy-start | bytes 5603332
  149.8 19.3 %collective-permute-start.42 = (bf16[304,768]{1,0:T(8,128)(2,1)S(1)}, bf16[304,768]{1,0:T(8,128)(2,1)}, u32[]{:S(2)}, u32[]{:S(2)}) collective-permute-start(bf16[304,768]{1,0:T(8,128)(2,1)S(1)} %fusion.6), channel_id=1, source_target_pairs={{0,2},{1,3},{6,4},{7,5},{8,10},{9,11},{14,12},{15,13},{16,18},{17,... | collective-permute-start | bytes 1400840 | tf_op jit(solution)/shard_map/ppermute | solution.py:518
  159.8 14.2 %collective-permute-start.30 = (bf16[192,1536]{1,0:T(8,128)(2,1)}, bf16[192,1536]{1,0:T(8,128)(2,1)S(1)}, u32[]{:S(2)}, u32[]{:S(2)}) collective-permute-start(bf16[192,1536]{1,0:T(8,128)(2,1)} %collective-permute-done.28.refs_9_), channel_id=1, source_target_pairs={{2,4},{3,5},{4,6},{5,7},{10,12},{11,13},{12,14},{13,15},{18,20},{1... | collective-permute-start | bytes 1769480 | tf_op jit(solution)/shard_map/ppermute | solution.py:518
  161.8 16.5 %collective-permute-start.31 = (bf16[192,1536]{1,0:T(8,128)(2,1)}, bf16[192,1536]{1,0:T(8,128)(2,1)}, u32[]{:S(2)}, u32[]{:S(2)}) collective-permute-start(bf16[192,1536]{1,0:T(8,128)(2,1)} %collective-permute-done.29.refs_10_), channel_id=1, source_target_pairs={{4,2},{5,3},{2,0},{3,1},{12,10},{13,11},{10,8},{11,9},{20,18},{21,... | collective-permute-start | bytes 1769480 | tf_op jit(solution)/shard_map/ppermute | solution.py:518
  165.5 28.5 %collective-permute-start.33 = (bf16[192,1536]{1,0:T(8,128)(2,1)S(1)}, bf16[192,1536]{1,0:T(8,128)(2,1)}, u32[]{:S(2)}, u32[]{:S(2)}) collective-permute-start(bf16[192,1536]{1,0:T(8,128)(2,1)S(1)} %copy-done.4), channel_id=1, source_target_pairs={{0,1},{1,0},{2,3},{3,2},{4,5},{5,4},{6,7},{7,6},{8,9},{9,8},{10,11... | collective-permute-start | bytes 1769480 | tf_op jit(solution)/shard_map/ppermute | solution.py:726
  165.6 25.8 %copy-start.1 = (bf16[4,304,768]{2,1,0:T(8,128)(2,1)S(1)}, bf16[4,304,768]{2,1,0:T(8,128)(2,1)}, u32[]{:S(2)}) copy-start(bf16[4,304,768]{2,1,0:T(8,128)(2,1)} %get-tuple-element.67) | copy-start | bytes 5603332
  165.6 30.6 %collective-permute-start.34 = (bf16[192,1536]{1,0:T(8,128)(2,1)}, bf16[192,1536]{1,0:T(8,128)(2,1)}, u32[]{:S(2)}, u32[]{:S(2)}) collective-permute-start(bf16[192,1536]{1,0:T(8,128)(2,1)} %collective-permute-done.28.refs_9_), channel_id=1, source_target_pairs={{0,1},{1,0},{2,3},{3,2},{4,5},{5,4},{6,7},{7,6},{8,9},{9,8},{10,11... | collective-permute-start | bytes 1769480 | tf_op jit(solution)/shard_map/ppermute | solution.py:726
  169.1 34.6 %collective-permute-start.35 = (bf16[192,1536]{1,0:T(8,128)(2,1)}, bf16[192,1536]{1,0:T(8,128)(2,1)}, u32[]{:S(2)}, u32[]{:S(2)}) collective-permute-start(bf16[192,1536]{1,0:T(8,128)(2,1)} %collective-permute-done.29.refs_10_), channel_id=1, source_target_pairs={{0,1},{1,0},{2,3},{3,2},{4,5},{5,4},{6,7},{7,6},{8,9},{9,8},{10,11... | collective-permute-start | bytes 1769480 | tf_op jit(solution)/shard_map/ppermute | solution.py:726
  174.0 12.9 %collective-permute-start.43 = (bf16[304,768]{1,0:T(8,128)(2,1)S(1)}, bf16[304,768]{1,0:T(8,128)(2,1)S(1)}, u32[]{:S(2)}, u32[]{:S(2)}) collective-permute-start(bf16[304,768]{1,0:T(8,128)(2,1)S(1)} %get-tuple-element.71), channel_id=1, source_target_pairs={{0,2},{1,3},{2,4},{3,5},{8,10},{9,11},{10,12},{11,13},{16,18},{17,... | collective-permute-start | bytes 1400840 | tf_op jit(solution)/shard_map/ppermute | solution.py:518
  178.3 13.1 %collective-permute-start.45 = (bf16[304,768]{1,0:T(8,128)(2,1)}, bf16[304,768]{1,0:T(8,128)(2,1)}, u32[]{:S(2)}, u32[]{:S(2)}) collective-permute-start(bf16[304,768]{1,0:T(8,128)(2,1)} %get-tuple-element.72), channel_id=1, source_target_pairs={{6,4},{7,5},{4,2},{5,3},{14,12},{15,13},{12,10},{13,11},{22,20},{2... | collective-permute-start | bytes 1400840 | tf_op jit(solution)/shard_map/ppermute | solution.py:518
  180.7 13.2 %copy-start.5 = (bf16[192,1536]{1,0:T(8,128)(2,1)}, bf16[192,1536]{1,0:T(8,128)(2,1)S(1)}, u32[]{:S(2)}) copy-start(bf16[192,1536]{1,0:T(8,128)(2,1)S(1)} %broadcast_select_fusion.refs_11_) | copy-start | bytes 1769476
  186.9 18.1 %collective-permute-start.32 = (bf16[192,1536]{1,0:T(8,128)(2,1)S(1)}, bf16[192,1536]{1,0:T(8,128)(2,1)}, u32[]{:S(2)}, u32[]{:S(2)}) collective-permute-start(bf16[192,1536]{1,0:T(8,128)(2,1)S(1)} %broadcast_select_fusion.refs_11_), channel_id=1, source_target_pairs={{2,0},{3,1},{4,6},{5,7},{10,8},{11,9},{12,14},{13,15},{18,16},{19,... | collective-permute-start | bytes 1769480 | tf_op jit(solution)/shard_map/ppermute | solution.py:518
  189.1 11.8 %copy-start.22 = (s32[4]{0:T(128)S(1)}, s32[4]{0:T(128)}, u32[]{:S(2)}) copy-start(s32[4]{0:T(128)} %get-tuple-element.84) | copy-start | bytes 52
  189.1 11.8 %copy-start.23 = (s32[4]{0:T(128)S(1)}, s32[4]{0:T(128)}, u32[]{:S(2)}) copy-start(s32[4]{0:T(128)} %param.12) | copy-start | bytes 52
  191.4 14.4 %collective-permute-start.36 = (bf16[192,1536]{1,0:T(8,128)(2,1)S(1)}, bf16[192,1536]{1,0:T(8,128)(2,1)}, u32[]{:S(2)}, u32[]{:S(2)}) collective-permute-start(bf16[192,1536]{1,0:T(8,128)(2,1)S(1)} %broadcast_select_fusion.refs_11_), channel_id=1, source_target_pairs={{0,1},{1,0},{2,3},{3,2},{4,5},{5,4},{6,7},{7,6},{8,9},{9,8},{10,11... | collective-permute-start | bytes 1769480 | tf_op jit(solution)/shard_map/ppermute | solution.py:726
  194.0 20.9 %collective-permute-start.44 = (bf16[304,768]{1,0:T(8,128)(2,1)}, bf16[304,768]{1,0:T(8,128)(2,1)}, u32[]{:S(2)}, u32[]{:S(2)}) collective-permute-start(bf16[304,768]{1,0:T(8,128)(2,1)} %get-tuple-element.73), channel_id=1, source_target_pairs={{0,2},{1,3},{2,4},{3,5},{4,6},{5,7},{8,10},{9,11},{10,12},{11,13},... | collective-permute-start | bytes 1400840 | tf_op jit(solution)/shard_map/ppermute | solution.py:518
  196.1 19.4 %collective-permute-start.46 = (bf16[304,768]{1,0:T(8,128)(2,1)}, bf16[304,768]{1,0:T(8,128)(2,1)}, u32[]{:S(2)}, u32[]{:S(2)}) collective-permute-start(bf16[304,768]{1,0:T(8,128)(2,1)} %get-tuple-element.74), channel_id=1, source_target_pairs={{6,4},{7,5},{4,2},{5,3},{2,0},{3,1},{14,12},{15,13},{12,10},{13,11... | collective-permute-start | bytes 1400840 | tf_op jit(solution)/shard_map/ppermute | solution.py:518
  203.7 7.0 %collective-permute-start.25 = (bf16[4,64,384]{2,1,0:T(8,128)(2,1)}, bf16[4,64,384]{2,1,0:T(8,128)(2,1)S(1)}, u32[]{:S(2)}, u32[]{:S(2)}) collective-permute-start(bf16[4,64,384]{2,1,0:T(8,128)(2,1)} %get-tuple-element.44), channel_id=1, source_target_pairs={{0,8},{8,0},{16,24},{24,16},{1,9},{9,1},{17,25},{25,17},{2,10},{10... | collective-permute-start | bytes 589832 | tf_op jit(solution)/shard_map/ppermute | solution.py:726
  205.0 7.9 %collective-permute-start.26 = (bf16[4,64,384]{2,1,0:T(8,128)(2,1)}, bf16[4,64,384]{2,1,0:T(8,128)(2,1)S(1)}, u32[]{:S(2)}, u32[]{:S(2)}) collective-permute-start(bf16[4,64,384]{2,1,0:T(8,128)(2,1)} %get-tuple-element.45), channel_id=1, source_target_pairs={{0,16},{8,24},{16,0},{24,8},{1,17},{9,25},{17,1},{25,9},{2,18},{10... | collective-permute-start | bytes 589832 | tf_op jit(solution)/shard_map/ppermute | solution.py:726
  205.8 47.8 %collective-permute-start.37 = (bf16[192,1536]{1,0:T(8,128)(2,1)}, bf16[192,1536]{1,0:T(8,128)(2,1)}, u32[]{:S(2)}, u32[]{:S(2)}) collective-permute-start(bf16[192,1536]{1,0:T(8,128)(2,1)} %collective-permute-done.32.refs_12_), channel_id=1, source_target_pairs={{0,1},{1,0},{2,3},{3,2},{4,5},{5,4},{6,7},{7,6},{8,9},{9,8},{10,11... | collective-permute-start | bytes 1769480 | tf_op jit(solution)/shard_map/ppermute | solution.py:726
  211.4 52.3 %collective-permute-start.40 = (bf16[256,1536]{1,0:T(8,128)(2,1)}, bf16[256,1536]{1,0:T(8,128)(2,1)S(1)}, u32[]{:S(2)}, u32[]{:S(2)}) collective-permute-start(bf16[256,1536]{1,0:T(8,128)(2,1)} %get-tuple-element.50), channel_id=1, source_target_pairs={{0,24},{8,16},{16,8},{24,0},{1,25},{9,17},{17,9},{25,1},{2,26},{10... | collective-permute-start | bytes 2359304 | tf_op jit(solution)/shard_map/ppermute | solution.py:726
  213.6 50.1 %collective-permute-start.39 = (bf16[256,1536]{1,0:T(8,128)(2,1)}, bf16[256,1536]{1,0:T(8,128)(2,1)S(1)}, u32[]{:S(2)}, u32[]{:S(2)}) collective-permute-start(bf16[256,1536]{1,0:T(8,128)(2,1)} %get-tuple-element.49), channel_id=1, source_target_pairs={{0,16},{8,24},{16,0},{24,8},{1,17},{9,25},{17,1},{25,9},{2,18},{10... | collective-permute-start | bytes 2359304 | tf_op jit(solution)/shard_map/ppermute | solution.py:726
  214.8 48.9 %collective-permute-start.38 = (bf16[256,1536]{1,0:T(8,128)(2,1)}, bf16[256,1536]{1,0:T(8,128)(2,1)}, u32[]{:S(2)}, u32[]{:S(2)}) collective-permute-start(bf16[256,1536]{1,0:T(8,128)(2,1)} %get-tuple-element.48), channel_id=1, source_target_pairs={{0,8},{8,0},{16,24},{24,16},{1,9},{9,1},{17,25},{25,17},{2,10},{10... | collective-permute-start | bytes 2359304 | tf_op jit(solution)/shard_map/ppermute | solution.py:726
  215.5 36.8 %collective-permute-start.27 = (bf16[4,64,384]{2,1,0:T(8,128)(2,1)}, bf16[4,64,384]{2,1,0:T(8,128)(2,1)}, u32[]{:S(2)}, u32[]{:S(2)}) collective-permute-start(bf16[4,64,384]{2,1,0:T(8,128)(2,1)} %get-tuple-element.46), channel_id=1, source_target_pairs={{0,24},{8,16},{16,8},{24,0},{1,25},{9,17},{17,9},{25,1},{2,26},{10... | collective-permute-start | bytes 589832 | tf_op jit(solution)/shard_map/ppermute | solution.py:726
  252.3 18.1 %collective-permute-start.48 = (bf16[304,768]{1,0:T(8,128)(2,1)}, bf16[304,768]{1,0:T(8,128)(2,1)S(1)}, u32[]{:S(2)}, u32[]{:S(2)}) collective-permute-start(bf16[304,768]{1,0:T(8,128)(2,1)} %fusion.5.refs_0_), channel_id=1, source_target_pairs={{0,16},{8,24},{16,0},{24,8},{1,17},{9,25},{17,1},{25,9},{2,18},{10... | collective-permute-start | bytes 1400840 | tf_op jit(solution)/shard_map/ppermute | solution.py:726
  253.6 18.1 %collective-permute-start.47 = (bf16[304,768]{1,0:T(8,128)(2,1)}, bf16[304,768]{1,0:T(8,128)(2,1)}, u32[]{:S(2)}, u32[]{:S(2)}) collective-permute-start(bf16[304,768]{1,0:T(8,128)(2,1)} %fusion.5.refs_0_), channel_id=1, source_target_pairs={{0,8},{8,0},{16,24},{24,16},{1,9},{9,1},{17,25},{25,17},{2,10},{10... | collective-permute-start | bytes 1400840 | tf_op jit(solution)/shard_map/ppermute | solution.py:726
  270.5 6.1 %collective-permute-start.49 = (bf16[152,768]{1,0:T(8,128)(2,1)S(1)}, bf16[152,768]{1,0:T(8,128)(2,1)S(1)}, u32[]{:S(2)}, u32[]{:S(2)}) collective-permute-start(bf16[152,768]{1,0:T(8,128)(2,1)S(1)} %slice.105), channel_id=1, source_target_pairs={{0,8},{8,0},{16,24},{24,16},{1,9},{9,1},{17,25},{25,17},{2,10},{10... | collective-permute-start | bytes 700424 | tf_op jit(solution)/shard_map/ppermute | solution.py:726
  272.7 6.1 %collective-permute-start.50 = (bf16[152,768]{1,0:T(8,128)(2,1)S(1)}, bf16[152,768]{1,0:T(8,128)(2,1)S(1)}, u32[]{:S(2)}, u32[]{:S(2)}) collective-permute-start(bf16[152,768]{1,0:T(8,128)(2,1)S(1)} %slice.112), channel_id=1, source_target_pairs={{0,16},{8,24},{16,0},{24,8},{1,17},{9,25},{17,1},{25,9},{2,18},{10... | collective-permute-start | bytes 700424 | tf_op jit(solution)/shard_map/ppermute | solution.py:726
  (17 other events, 58.5 us)

commit v3 on v2

--- a/solution.py
+++ b/solution.py
@@ -12,61 +12,19 @@
 BF16 = jnp.bfloat16
 LANES = 128
 MARGIN = 16
-VMEM_BYTES = 56 * 1024 * 1024
 NT = (((1,), (1,)), ((), ()))
 TN = (((0,), (0,)), ((), ()))
-
-
-def chunk_kernel(dims, meta, x_ref, g_ref, gain_ref, taps_ref, *refs):
-    count, length, owned, part, taps, n_blocks = dims
-    blocks = refs[:n_blocks]
-    normed_ref, sw_ref, ge_ref, gn_ref, small_ref, gain_part_ref = refs[n_blocks : n_blocks + 6]
-    we, wp, ab, standard, pad, gpad, slope, sems = refs[n_blocks + 6 :]
-    rows, width = x_ref.shape
-    wide = we.shape[1]
+LIGHT = pl.CostEstimate(flops=1, bytes_accessed=1, transcendentals=0)
+
+
+def chunk_kernel(dims, meta, normed_ref, g_ref, taps_ref, we, wp, *refs):
+    count, length, taps, source = dims
+    before, refs = refs[: count if source else 0], refs[count if source else 0 :]
+    sw_ref, ge_ref, gn_ref, small_ref = refs[:4]
+    pieces, (ab, pad, gpad, slope) = refs[4 : 4 + count], refs[4 + count :]
+    width, wide = we.shape
     channels = wide // 2
     tiles = channels // LANES
-
-    def copies(b):
-        owner = meta[b]
-        out = [
-            pltpu.make_async_copy(
-                blocks[b].at[pl.ds(0, owned)],
-                we.at[pl.ds(pl.multiple_of(owner * owned, owned), owned)],
-                sems.at[b, 0],
-            )
-        ]
-        for h in range(width // wide):
-            out.append(
-                pltpu.make_async_copy(
-                    blocks[b].at[pl.ds(owned + h * part, part)],
-                    wp.at[
-                        pl.ds(pl.multiple_of(owner * part, part), part),
-                        pl.ds(h * wide, wide),
-                    ],
-                    sems.at[b, 1 + h],
-                )
-            )
-        return out
-
-    for b in range(n_blocks):
-        @pl.when(meta[b] >= 0)
-        def _():
-            for copy in copies(b):
-                copy.start()
-
-    step = 32
-    gain = gain_ref[...]
-
-    @pl.loop(0, rows // step)
-    def _(index):
-        at = pl.ds(pl.multiple_of(index * step, step), step)
-        x = x_ref[at, :].astype(F32)
-        centred = x - jnp.mean(x, axis=1, keepdims=True)
-        variance = jnp.mean(centred * centred, axis=1, keepdims=True)
-        unit = centred * lax.rsqrt(variance + EPS)
-        standard[at, :] = unit
-        normed_ref[at, :] = (unit * gain).astype(BF16)
 
     zeros = jnp.zeros((MARGIN, LANES), F32)
     for u in range(count):
@@ -76,12 +34,6 @@
                 ref[u, tile, MARGIN + length :, :] = zeros
     small_ref[...] = jnp.zeros_like(small_ref)
 
-    for b in range(n_blocks):
-        @pl.when(meta[b] >= 0)
-        def _():
-            for copy in copies(b):
-                copy.wait()
-
     expanded = jnp.dot(normed_ref[...], we[...], preferred_element_type=F32)
     for tile in range(2 * tiles):
         ab[tile] = expanded[:, tile * LANES : (tile + 1) * LANES]
@@ -92,7 +44,7 @@
     @pl.loop(0, count)
     def _(u):
         at = pl.ds(pl.multiple_of(u * length, length), length)
-        live = positions < meta[n_blocks + u]
+        live = positions < meta[u]
         for tile in range(tiles):
             lanes = pl.ds(tile * LANES, LANES)
             gate = jax.nn.sigmoid(ab[tiles + tile, at, :])
@@ -106,6 +58,12 @@
             sw_ref[at, lanes] = jnp.where(live, conv * sig, 0.0).astype(BF16)
             slope[u, tile] = jnp.where(live, sig * (1.0 + conv * (1.0 - sig)), 0.0)
 
+    for m in range(count):
+        if source:
+            pieces[m][:source] = before[m][...]
+        chosen = meta[2 * count + (meta[count] ^ m)]
+        pieces[m][source] = sw_ref[pl.ds(pl.multiple_of(chosen * length, length), length), :]
+
     grad_swish = lax.dot_general(g_ref[...], wp[...], NT, preferred_element_type=F32)
     for u in range(count):
         for tile in range(tiles):
@@ -120,7 +78,7 @@
     @pl.loop(0, count)
     def _(u):
         at = pl.ds(pl.multiple_of(u * length, length), length)
-        live = positions < meta[n_blocks + u]
+        live = positions < meta[u]
         for tile in range(tiles):
             lanes = pl.ds(tile * LANES, LANES)
             grad_conv = gpad[u, tile, MARGIN : MARGIN + length, :]
@@ -144,56 +102,135 @@
     span = 512
     for start in range(0, width, span):
         cols = slice(start, start + span)
-        grad_normed = lax.dot_general(ge_ref[...], we[cols, :], NT, preferred_element_type=F32)
-        gn_ref[:, cols] = grad_normed.astype(BF16)
-        gain_part_ref[:, cols] = jnp.sum(
-            (grad_normed * standard[:, cols]).reshape(rows // 8, 8, span), axis=0
-        )
-
-
-def chunk_call(x, g, gain, taps_table, blocks, owners, lengths, owned, part, taps):
-    count, length, width = x.shape
-    rows = count * length
-    wide = blocks[0].shape[1]
+        gn_ref[:, cols] = lax.dot_general(
+            ge_ref[...], we[cols, :], NT, preferred_element_type=F32
+        ).astype(BF16)
+
+
+def chunk_call(meta, normed, g, taps_table, we, wp, before, dims):
+    count, length, taps = dims
+    source = before[0].shape[0] if before else 0
+    rows, width = normed.shape
+    wide = we.shape[1]
     channels = wide // 2
     tiles = channels // LANES
-    n_blocks = len(blocks)
-    meta = jnp.concatenate([owners, lengths]).astype(jnp.int32)
-    vmem = pl.BlockSpec(memory_space=pltpu.VMEM)
-    anywhere = pl.BlockSpec(memory_space=pl.ANY)
-    flops = 2 * rows * width * wide * 3
+    last = g.shape[0] // rows - 1
+    padded = pltpu.VMEM((count, tiles, length + 2 * MARGIN, LANES), F32)
     return pl.pallas_call(
-        functools.partial(chunk_kernel, (count, length, owned, part, taps, n_blocks)),
+        functools.partial(chunk_kernel, (count, length, taps, source)),
         out_shape=(
-            jax.ShapeDtypeStruct((rows, width), BF16),
             jax.ShapeDtypeStruct((rows, channels), BF16),
             jax.ShapeDtypeStruct((rows, wide), BF16),
             jax.ShapeDtypeStruct((rows, width), BF16),
             jax.ShapeDtypeStruct((tiles, taps + 1, 8, LANES), F32),
-            jax.ShapeDtypeStruct((8, width), F32),
+        )
+        + (jax.ShapeDtypeStruct((source + 1, length, channels), BF16),) * count,
+        grid=(1,),
+        in_specs=[in_smem(), in_vmem(), pl.BlockSpec((rows, width), lambda s: (last, 0))]
+        + [in_vmem()] * (3 + len(before)),
+        out_specs=(in_vmem(),) * (4 + count),
+        scratch_shapes=[
+            pltpu.VMEM((2 * tiles, rows, LANES), F32),
+            padded,
+            padded,
+            pltpu.VMEM((count, tiles, length, LANES), F32),
+        ],
+        compiler_params=vmem_params(16),
+        cost_estimate=LIGHT,
+        name="chunk",
+    )(meta, normed, g, taps_table, we, wp, *before)
+
+
+def norm_kernel(x_ref, gain_ref, out_ref):
+    x = x_ref[...].astype(F32)
+    centred = x - jnp.mean(x, axis=1, keepdims=True)
+    variance = jnp.mean(centred * centred, axis=1, keepdims=True)
+    out_ref[...] = (centred * lax.rsqrt(variance + EPS) * gain_ref[...]).astype(BF16)
+
+
+def norm_call(x, gain, rows):
+    width = x.shape[1]
+    step = 128
+    block = pl.BlockSpec((step, width), lambda s: (s, 0))
+    return pl.pallas_call(
+        norm_kernel,
+        out_shape=jax.ShapeDtypeStruct((rows, width), BF16),
+        grid=(rows // step,),
+        in_specs=[block, pl.BlockSpec((1, width), lambda s: (0, 0))],
+        out_specs=block,
+        compiler_params=vmem_params(8),
+        cost_estimate=LIGHT,
+        name="norm",
+    )(x, gain)
+
+
+def assemble_kernel(dims, meta, *refs):
+    owned, part, taps, n_blocks = dims
+    blocks = refs[:n_blocks]
+    we, wp, taps_ref, gain_ref, small, sems = refs[n_blocks:]
+    width, wide = we.shape
+    halves = width // wide
+
+    def copies(b):
+        owner = meta[b]
+        yield pltpu.make_async_copy(
+            blocks[b].at[pl.ds(owned + halves * part, 16)], small.at[owner], sems.at[b, 0]
+        )
+        yield pltpu.make_async_copy(
+            blocks[b].at[pl.ds(0, owned)],
+            we.at[pl.ds(pl.multiple_of(owner * owned, owned), owned)],
+            sems.at[b, 1],
+        )
+        for h in range(halves):
+            yield pltpu.make_async_copy(
+                blocks[b].at[pl.ds(owned + h * part, part)],
+                wp.at[pl.ds(pl.multiple_of(owner * part, part), part), pl.ds(h * wide, wide)],
+                sems.at[b, 2 + h],
+            )
+
+    for b in range(n_blocks):
+        @pl.when(meta[b] >= 0)
+        def _():
+            for copy in copies(b):
+                copy.start()
+    for b in range(n_blocks):
+        @pl.when(meta[b] >= 0)
+        def _():
+            for copy in copies(b):
+                copy.wait()
+
+    rows = [small[j].astype(F32) for j in range(small.shape[0])]
+    taps_ref[:16] = jnp.concatenate([r[:, :part] for r in rows], axis=1)
+    taps_ref[16:] = jnp.concatenate([r[:, LANES : LANES + part] for r in rows], axis=1)
+    gain_ref[...] = jnp.concatenate([r[:1, 2 * LANES : 2 * LANES + owned] for r in rows], axis=1)
+
+
+def assemble_call(blocks, owners, owned, part, width, taps):
+    wide = blocks[0].shape[1]
+    n_blocks = len(blocks)
+    anywhere = pl.BlockSpec(memory_space=pl.ANY)
+    return pl.pallas_call(
+        functools.partial(assemble_kernel, (owned, part, taps, n_blocks)),
+        out_shape=(
+            jax.ShapeDtypeStruct((width, wide), BF16),
+            jax.ShapeDtypeStruct((wide // 2, width), BF16),
+            jax.ShapeDtypeStruct((taps + 1, wide // 2), F32),
+            jax.ShapeDtypeStruct((1, width), F32),
         ),
-        in_specs=[pl.BlockSpec(memory_space=pltpu.SMEM)] + [vmem] * 4 + [anywhere] * n_blocks,
-        out_specs=(vmem,) * 6,
+        in_specs=[in_smem()] + [anywhere] * n_blocks,
+        out_specs=(in_vmem(),) * 4,
         scratch_shapes=[
-            pltpu.VMEM((width, wide), BF16),
-            pltpu.VMEM((channels, width), BF16),
-            pltpu.VMEM((2 * tiles, rows, LANES), F32),
-            pltpu.VMEM((rows, width), F32),
-            pltpu.VMEM((count, tiles, length + 2 * MARGIN, LANES), F32),
-            pltpu.VMEM((count, tiles, length + 2 * MARGIN, LANES), F32),
-            pltpu.VMEM((count, tiles, length, LANES), F32),
-            pltpu.SemaphoreType.DMA((n_blocks, 1 + width // wide)),
+            pltpu.VMEM((width // owned, 16, wide), BF16),
+            pltpu.SemaphoreType.DMA((n_blocks, 2 + width // wide)),
         ],
-        compiler_params=pltpu.CompilerParams(vmem_limit_bytes=VMEM_BYTES),
-        cost_estimate=pl.CostEstimate(
-            flops=flops, bytes_accessed=6 * rows * width * 2, transcendentals=rows * wide
-        ),
-        name="chunk",
-    )(meta, x.reshape(rows, width), g.reshape(rows, width), gain, taps_table, *blocks)
-
-
-def vmem_params():
-    return pltpu.CompilerParams(vmem_limit_bytes=VMEM_BYTES)
+        compiler_params=vmem_params(8),
+        cost_estimate=LIGHT,
+        name="assemble",
+    )(owners, *blocks)
+
+
+def vmem_params(mib):
+    return pltpu.CompilerParams(vmem_limit_bytes=mib * 1024 * 1024)
 
 
 def in_vmem():
@@ -208,44 +245,87 @@
     return (channel // part) * owned + index * part + channel % part
 
 
-def pack_kernel(meta, expand_ref, project_ref, pack_ref):
+def pack_kernel(
+    meta, expand_ref, project_ref, kernel_ref, bias_ref, gain_ref, x_ref, g_ref, pack_ref, both_ref, sems
+):
+    rows = x_ref.shape[0]
+    copies = [
+        pltpu.make_async_copy(ref, both_ref.at[pl.ds(i * rows, rows)], sems.at[i])
+        for i, ref in enumerate((x_ref, g_ref))
+    ]
+    for copy in copies:
+        copy.start()
     owned, width = project_ref.shape
+    taps = kernel_ref.shape[1]
     wide = pack_ref.shape[1]
     channels = wide // 2
     part = owned * channels // width
     index = meta[0]
     row = lax.broadcasted_iota(jnp.int32, (width, channels), 0)
-    col = lax.broadcasted_iota(jnp.int32, (width, channels), 1)
-    pick = (row == owned_column(col, index, owned, part)).astype(F32).astype(BF16)
+    col = lax.broadcasted_iota(jnp.int32, (1, channels), 1)
+    pick = jnp.where(row == owned_column(col, index, owned, part), 1.0, 0.0).astype(BF16)
     for h in range(2):
         pack_ref[:owned, h * channels : (h + 1) * channels] = jnp.dot(
             expand_ref[:, h * width : (h + 1) * width], pick, preferred_element_type=F32
         ).astype(BF16)
-    rows = project_ref[pl.ds(pl.multiple_of(index * part, part), part), :]
+    block = project_ref[pl.ds(pl.multiple_of(index * part, part), part), :]
     for h in range(width // wide):
-        pack_ref[owned + h * part : owned + (h + 1) * part, :] = rows[:, h * wide : (h + 1) * wide]
-
-
-def pack_call(index, expand_weight, project_weight, part, wide):
+        pack_ref[owned + h * part : owned + (h + 1) * part, :] = block[:, h * wide : (h + 1) * wide]
+    mine = lax.broadcasted_iota(jnp.int32, (owned, LANES), 1) + index * part
+    mine = jnp.where(lax.broadcasted_iota(jnp.int32, (owned, LANES), 0) == mine, 1.0, 0.0)
+    mine = mine.astype(BF16)
+    table = jnp.concatenate(
+        [
+            lax.dot_general(kernel_ref[...], mine, TN, preferred_element_type=F32),
+            jnp.dot(bias_ref[...], mine, preferred_element_type=F32),
+        ],
+        axis=0,
+    )
+    base = owned + width // wide * part
+    pack_ref[base:, :LANES] = table[:16].astype(BF16)
+    pack_ref[base:, LANES : 2 * LANES] = table[16:].astype(BF16)
+    gain = jnp.broadcast_to(gain_ref[...].astype(F32), (16, owned))
+    rest = jnp.zeros((16, wide - 2 * LANES - owned), F32)
+    pack_ref[base:, 2 * LANES :] = jnp.concatenate([gain, rest], axis=1).astype(BF16)
+    for copy in copies:
+        copy.wait()
+
+
+def pack_call(index, expand_weight, project_weight, kernel, bias, gain, x, g, part, wide):
     owned, width = project_weight.shape
+    rows = x.shape[0]
+    anywhere = pl.BlockSpec(memory_space=pl.ANY)
     return pl.pallas_call(
         pack_kernel,
-        out_shape=jax.ShapeDtypeStruct((owned + width // wide * part, wide), BF16),
-        in_specs=[in_smem(), in_vmem(), in_vmem()],
-        out_specs=in_vmem(),
-        compiler_params=vmem_params(),
-        cost_estimate=pl.CostEstimate(
-            flops=2 * owned * width * wide, bytes_accessed=8 * owned * width, transcendentals=0
+        out_shape=(
+            jax.ShapeDtypeStruct((owned + width // wide * part + 16, wide), BF16),
+            jax.ShapeDtypeStruct((2 * rows, width), BF16),
         ),
+        in_specs=[in_smem()] + [in_vmem()] * 5 + [anywhere] * 2,
+        out_specs=(in_vmem(), anywhere),
+        scratch_shapes=[pltpu.SemaphoreType.DMA((2,))],
+        compiler_params=vmem_params(16),
+        cost_estimate=LIGHT,
         name="pack",
-    )(index.reshape(1), expand_weight, project_weight)
+    )(index.reshape(1), expand_weight, project_weight, kernel, bias[None], gain[None], x, g)
 
 
 def grads_kernel(dims, meta, *refs):
     n, chips, owned, part, taps = dims
-    normed, ge, sw, g, small, gain = [refs[i * n : (i + 1) * n] for i in range(6)]
-    keep, give = refs[6 * n :]
+    normed, ge, sw, g, small = [refs[i * n : (i + 1) * n] for i in range(5)]
+    keep, give, cotangent, sems = refs[5 * n :]
     core = meta[0]
+    rows = ge[0].shape[0]
+    copies = [
+        pltpu.make_async_copy(
+            g[k].at[pl.ds(g[k].shape[0] - rows, rows)],
+            cotangent.at[pl.ds(k * rows, rows)],
+            sems.at[k],
+        )
+        for k in range(n)
+    ]
+    for copy in copies:
+        copy.start()
     wide = ge[0].shape[1]
     width = normed[0].shape[1]
     channels = wide // 2
@@ -260,24 +340,25 @@
         def _():
             give[chip, rows, cols] = value
 
-    def total(left, right):
-        out = None
-        for a, b in zip(left, right):
-            term = lax.dot_general(a, b[...], TN, preferred_element_type=F32)
-            out = term if out is None else out + term
-        return out
-
     every = slice(None)
+    upstream = jnp.concatenate([a[...] for a in ge], axis=0)
     for chip in range(chips):
         cols = slice(2 * chip * owned, 2 * (chip + 1) * owned)
-        block = total([a[:, cols] for a in normed], ge).astype(BF16)
+        inputs = jnp.concatenate([a[:, cols] for a in normed], axis=0)
+        block = lax.dot_general(inputs, upstream, TN, preferred_element_type=F32).astype(BF16)
         for which in range(2):
             emit(chip, which, slice(0, owned), every, block[which * owned : (which + 1) * owned])
-    block = total([a[...] for a in sw], g).astype(BF16)
+    for copy in copies:
+        copy.wait()
+    block = lax.dot_general(
+        jnp.concatenate([a[...] for a in sw], axis=0),
+        cotangent[...],
+        TN,
+        preferred_element_type=F32,
+    ).astype(BF16)
     sums = sum(a[...] for a in small)
     sums = jnp.sum(sums, axis=2)
     sums = jnp.concatenate([sums[tile] for tile in range(tiles)], axis=1)
-    gains = jnp.sum(sum(a[...] for a in gain), axis=0, keepdims=True)
     base = owned + width // wide * part
     for chip in range(chips):
         for which in range(2):
@@ -293,9 +374,8 @@
                 )
             mine = sums[:, owner * part : (owner + 1) * part]
             pad = jnp.zeros((16, LANES - part), F32)
-            own_gain = gains[:, owner * owned : (owner + 1) * owned]
             line = jnp.concatenate(
-                [mine[:16], pad, mine[16:], pad, jnp.broadcast_to(own_gain, (16, owned))], axis=1
+                [mine[:16], pad, mine[16:], pad], axis=1
             )
             line = jnp.concatenate(
                 [line, jnp.zeros((16, wide - line.shape[1]), F32)], axis=1
@@ -303,7 +383,7 @@
             emit(chip, which, slice(base, base + 16), every, line)
 
 
-def grads_call(core, normed, ge, sw, g, small, gain, owned, part, taps):
+def grads_call(core, normed, ge, sw, g, small, owned, part, taps):
     n = len(normed)
     rows, width = normed[0].shape
     wide = ge[0].shape[1]
@@ -313,41 +393,16 @@
     return pl.pallas_call(
         functools.partial(grads_kernel, (n, chips, owned, part, taps)),
         out_shape=(shape, shape),
-        in_specs=[in_smem()] + [in_vmem()] * (6 * n),
+        in_specs=[in_smem()]
+        + [in_vmem()] * (3 * n)
+        + [pl.BlockSpec(memory_space=pl.ANY)] * n
+        + [in_vmem()] * n,
         out_specs=(in_vmem(), in_vmem()),
-        compiler_params=vmem_params(),
-        cost_estimate=pl.CostEstimate(
-            flops=3 * n * rows * width * wide,
-            bytes_accessed=n * rows * width * 8,
-            transcendentals=0,
-        ),
+        scratch_shapes=[pltpu.VMEM((n * rows, width), BF16), pltpu.SemaphoreType.DMA((n,))],
+        compiler_params=vmem_params(32),
+        cost_estimate=LIGHT,
         name="weight_grads",
-    )(core.reshape(1), *normed, *ge, *sw, *g, *small, *gain)
-
-
-def route_kernel(n, meta, *refs):
-    me = meta[0]
-    for m in range(n):
-        for k in range(n):
-            chosen = meta[1 + k * n + (me ^ m)]
-            refs[n + m][k] = refs[k][chosen]
-
-
-def route_call(meta, swished, length):
-    n = len(swished)
-    channels = swished[0].shape[1]
-    shape = jax.ShapeDtypeStruct((n, length, channels), BF16)
-    return pl.pallas_call(
-        functools.partial(route_kernel, n),
-        out_shape=(shape,) * n,
-        in_specs=[in_smem()] + [in_vmem()] * n,
-        out_specs=(in_vmem(),) * n,
-        compiler_params=vmem_params(),
-        cost_estimate=pl.CostEstimate(
-            flops=0, bytes_accessed=4 * n * n * length * channels, transcendentals=0
-        ),
-        name="route",
-    )(meta, *[a.reshape(n, length, channels) for a in swished])
+    )(core.reshape(1), *normed, *ge, *sw, *g, *small)
 
 
 def encode_kernel(dims, meta, *refs):
@@ -356,7 +411,7 @@
     frames = refs[n : 2 * n]
     blocks = refs[2 * n : 2 * n + n_blocks]
     out_ref = refs[2 * n + n_blocks]
-    cat, weight, residual, frame_sems, sems = refs[2 * n + n_blocks + 1 :]
+    cat, weight, residual, frame_sems, piece_sems, sems = refs[2 * n + n_blocks + 1 :]
     channels = pieces[0].shape[2]
     me = meta[0]
     first = 1 + n * n
@@ -372,12 +427,23 @@
             for i in range(n)
         ]
 
+    def rows(utterance):
+        return pl.ds(pl.multiple_of(utterance * length, length), length)
+
     frame_copies = [
         pltpu.make_async_copy(
-            frames[k].at[meta[1 + k * n + me]], residual.at[me ^ k], frame_sems.at[k]
+            frames[k].at[rows(meta[1 + k * n + me])], residual.at[rows(me ^ k)], frame_sems.at[k]
         )
         for k in range(n)
     ]
+    for m in range(n):
+        lanes = pl.ds(pl.multiple_of((me ^ m) * channels, channels), channels)
+        for k in range(n):
+            frame_copies.append(
+                pltpu.make_async_copy(
+                    pieces[m].at[k], cat.at[rows(me ^ m ^ k), lanes], piece_sems.at[m, k]
+                )
+            )
     for copy in frame_copies:
         copy.start()
     for b in range(n_blocks):
@@ -386,11 +452,6 @@
             for copy in weight_copies(b):
                 copy.start()
 
-    for m in range(n):
-        lanes = pl.ds(pl.multiple_of((me ^ m) * channels, channels), channels)
-        for k in range(n):
-            rows = pl.ds(pl.multiple_of((me ^ m ^ k) * length, length), length)
-            cat[rows, lanes] = pieces[m][k]
     for copy in frame_copies:
         copy.wait()
     for b in range(n_blocks):
@@ -399,35 +460,35 @@
             for copy in weight_copies(b):
                 copy.wait()
 
-    for r in range(n):
-        term = jnp.dot(
-            cat[r * length : (r + 1) * length, :], weight[...], preferred_element_type=F32
-        )
-        out_ref[r] = (residual[r].astype(F32) + term).astype(BF16)
-
-
-def encode_call(me, orders, pieces, frames, blocks, owners, owned, part):
-    n, length, channels = pieces[0].shape
+    span = 512
+    for start in range(0, cat.shape[1], span):
+        cols = slice(start, start + span)
+        term = jnp.dot(cat[...], weight[:, cols], preferred_element_type=F32)
+        out_ref[:, cols] = (residual[:, cols].astype(F32) + term).astype(BF16)
+
+
+def encode_call(me, orders, pieces, frames, blocks, owners, owned, part, length):
+    n = len(pieces)
+    channels = pieces[0].shape[2]
     width = blocks[0].shape[1]
     n_blocks = len(blocks)
     meta = jnp.concatenate([me.reshape(1), orders, owners])
     anywhere = pl.BlockSpec(memory_space=pl.ANY)
     return pl.pallas_call(
         functools.partial(encode_kernel, (n, n_blocks, length, owned, part)),
-        out_shape=jax.ShapeDtypeStruct((n, length, width), BF16),
-        in_specs=[in_smem()] + [in_vmem()] * n + [anywhere] * (n + n_blocks),
+        out_shape=jax.ShapeDtypeStruct((n * length, width), BF16),
+        in_specs=[in_smem()] + [anywhere] * (2 * n + n_blocks),
         out_specs=in_vmem(),
         scratch_shapes=[
             pltpu.VMEM((n * length, width), BF16),
             pltpu.VMEM((width, width), BF16),
-            pltpu.VMEM((n, length, width), BF16),
+            pltpu.VMEM((n * length, width), BF16),
             pltpu.SemaphoreType.DMA((n,)),
+            pltpu.SemaphoreType.DMA((n, n)),
             pltpu.SemaphoreType.DMA((n_blocks, n)),
         ],
-        compiler_params=vmem_params(),
-        cost_estimate=pl.CostEstimate(
-            flops=2 * n * length * width * width, bytes_accessed=4 * width * width, transcendentals=0
-        ),
+        compiler_params=vmem_params(48),
+        cost_estimate=LIGHT,
         name="encode",
     )(meta, *pieces, *frames, *blocks)
 
@@ -459,10 +520,8 @@
         in_specs=[block, block, pl.BlockSpec((1, width), lambda s: (0, 0))]
         + [block] * len(returned),
         out_specs=block,
-        compiler_params=vmem_params(),
-        cost_estimate=pl.CostEstimate(
-            flops=20 * rows * width, bytes_accessed=14 * rows * width, transcendentals=rows
-        ),
+        compiler_params=vmem_params(48),
+        cost_estimate=LIGHT,
         name="frame_grad",
     )(x.reshape(rows, width), g.reshape(rows, width), gain, *returned)
     return out.reshape(count, length, width)
@@ -470,48 +529,56 @@
 
 def unpack_kernel(dims, meta, *refs):
     n, owned, part = dims
-    blocks = refs[:n]
-    expand_ref, project_ref, cat = refs[n:]
-    wide = blocks[0].shape[1]
+    lows, highs = refs[:n], refs[n : 2 * n]
+    weight_ref, gain_ref, expand_ref, project_ref, gain_out, cat = refs[2 * n :]
+    wide = lows[0].shape[1]
+    cut = lows[0].shape[0]
     channels = wide // 2
     width = project_ref.shape[1]
     me = meta[0]
-    row = lax.broadcasted_iota(jnp.int32, (width, width), 0)
-    col = lax.broadcasted_iota(jnp.int32, (width, width), 1)
-    place = owned_column(row % channels, row // channels, owned, part)
-    spread = (place == col).astype(F32).astype(BF16)
     for k in range(n):
         index = me ^ k
         lanes = pl.ds(pl.multiple_of(index * channels, channels), channels)
         for h in range(2):
-            cat[h, :, lanes] = blocks[k][:owned, h * channels : (h + 1) * channels]
+            cols = slice(h * channels, (h + 1) * channels)
+            cat[h, :cut, lanes] = lows[k][:, cols]
+            cat[h, cut:, lanes] = highs[k][: owned - cut, cols]
         rows = pl.ds(pl.multiple_of(index * part, part), part)
         for h in range(width // wide):
-            project_ref[rows, h * wide : (h + 1) * wide] = blocks[k][
-                owned + h * part : owned + (h + 1) * part, :
+            start = owned - cut + h * part
+            project_ref[rows, h * wide : (h + 1) * wide] = highs[k][
+                start : start + part, :
             ].astype(F32)
-    for h in range(2):
-        expand_ref[:, h * width : (h + 1) * width] = jnp.dot(
-            cat[h], spread, preferred_element_type=F32
-        )
-
-
-def unpack_call(me, blocks, owned, part, width):
+    along = jnp.zeros((owned, 1), F32)
+    span = 512
+    for start in range(0, width, span):
+        row = lax.broadcasted_iota(jnp.int32, (width, span), 0)
+        col = lax.broadcasted_iota(jnp.int32, (1, span), 1) + start
+        place = col % owned // part * channels + col // owned * part + col % part
+        spread = jnp.where(row == place, 1.0, 0.0).astype(BF16)
+        for h in range(2):
+            cols = slice(h * width + start, h * width + start + span)
+            grad = jnp.dot(cat[h], spread, preferred_element_type=F32)
+            expand_ref[:, cols] = grad
+            along += jnp.sum(grad * weight_ref[:, cols].astype(F32), axis=1, keepdims=True)
+    gain_out[...] = along / gain_ref[...]
+
+
+def unpack_call(me, lows, highs, weight, gain, owned, part, width):
     return pl.pallas_call(
-        functools.partial(unpack_kernel, (len(blocks), owned, part)),
+        functools.partial(unpack_kernel, (len(lows), owned, part)),
         out_shape=(
             jax.ShapeDtypeStruct((owned, 2 * width), F32),
             jax.ShapeDtypeStruct((owned, width), F32),
+            jax.ShapeDtypeStruct((owned, 1), F32),
         ),
-        in_specs=[in_smem()] + [in_vmem()] * len(blocks),
-        out_specs=(in_vmem(), in_vmem()),
+        in_specs=[in_smem()] + [in_vmem()] * (2 * len(lows) + 2),
+        out_specs=(in_vmem(),) * 3,
         scratch_shapes=[pltpu.VMEM((2, owned, width), BF16)],
-        compiler_params=vmem_params(),
-        cost_estimate=pl.CostEstimate(
-            flops=4 * owned * width * width, bytes_accessed=18 * owned * width, transcendentals=0
-        ),
+        compiler_params=vmem_params(24),
+        cost_estimate=LIGHT,
         name="unpack",
-    )(me.reshape(1), *blocks)
+    )(me.reshape(1), *lows, *highs, weight, gain)
 
 
 def along_z(x, pairs):
@@ -522,47 +589,69 @@
 LEFT = [(3, 2), (2, 1), (1, 0)]
 
 
-def gather_line(x, chip, core):
+def tie(value, *after):
+    return lax.optimization_barrier((value,) + after)[0]
+
+
+def line_hops(x, chip, before_second=(), before_third=()):
     right = along_z(x, RIGHT)
     left = along_z(x, LEFT)
-    right2 = along_z(right, [(1, 2), (2, 3)])
-    left2 = along_z(left, [(2, 1), (1, 0)])
-    second = jnp.where(chip >= 2, right2, left2)
-    third = along_z(second, [(1, 0), (2, 3)])
-    blocks = [x, right, left, second, third]
-    chips = [
-        chip,
-        jnp.where(chip >= 1, chip - 1, -1),
-        jnp.where(chip <= 2, chip + 1, -1),
-        jnp.where(chip >= 2, chip - 2, chip + 2),
-        jnp.where(chip == 0, 3, jnp.where(chip == 3, 0, -1)),
-    ]
-    others = [swap(block, "shard", 8, 1) for block in blocks]
+    held = lax.optimization_barrier((right, left) + tuple(before_second))
+    right2 = along_z(held[0], [(1, 2), (2, 3)])
+    left2 = along_z(held[1], [(2, 1), (1, 0)])
+    held = lax.optimization_barrier((right2, left2) + tuple(before_third))
+    right3 = along_z(held[0], [(2, 3)])
+    left3 = along_z(held[1], [(1, 0)])
+    return x, right, left, right2, left2, right3, left3
+
+
+def line_owners(chip, core):
+    chips = [chip]
+    for distance in (1, 2, 3):
+        chips.append(jnp.where(chip >= distance, chip - distance, -1))
+        chips.append(jnp.where(chip + distance <= 3, chip + distance, -1))
     owners = [jnp.where(c >= 0, 2 * c + core, -1) for c in chips]
     owners += [jnp.where(c >= 0, 2 * c + 1 - core, -1) for c in chips]
-    return blocks + others, jnp.stack(owners).astype(jnp.int32)
-
-
-def reduce_line(keep, give, chip):
-    got = swap(give, "shard", 8, 1)
-
-    def block(at):
-        return lax.dynamic_index_in_dim(keep, at, 0, False).astype(
-            F32
-        ) + lax.dynamic_index_in_dim(got, at, 0, False).astype(F32)
-
-    def send(at, carried, pairs):
-        value = block(at)
-        if carried is not None:
-            value = value + carried.astype(F32)
-        return along_z(value.astype(BF16), pairs)
-
-    far = send(jnp.where(chip <= 1, 3, 0), None, [(0, 1), (3, 2)])
-    right = send(jnp.minimum(chip + 2, 3), far, [(0, 1), (1, 2)])
-    left = send(jnp.maximum(chip - 2, 0), far, [(3, 2), (2, 1)])
-    right = send(jnp.minimum(chip + 1, 3), right, RIGHT)
-    left = send(jnp.maximum(chip - 1, 0), left, LEFT)
-    return (block(chip) + right.astype(F32) + left.astype(F32)).astype(BF16)
+    return jnp.stack(owners).astype(jnp.int32)
+
+
+def across_cores(blocks):
+    return list(blocks) + [swap(block, "shard", 8, 1) for block in blocks]
+
+
+def hop_kernel(counts, meta, *refs):
+    n = len(counts)
+    outs = refs[-n:]
+    keep, got, carried = refs[:n], refs[n : 2 * n], list(refs[2 * n : -n])
+    for i in range(n):
+        total = keep[i][...].astype(F32) + got[i][...].astype(F32)
+        for _ in range(counts[i]):
+            total = total + carried.pop(0)[...].astype(F32)
+        outs[i][...] = total.astype(BF16)
+
+
+def hop_call(keep, got, chips, carried):
+    n = len(chips)
+    rows, wide = keep.shape[1:]
+    step = rows // 2
+    pick = [
+        pl.BlockSpec((None, step, wide), lambda s, meta, i=i: (meta[i], s, 0)) for i in range(n)
+    ]
+    plain = pl.BlockSpec((step, wide), lambda s, meta: (s, 0))
+    flat = [array for arrays in carried for array in arrays]
+    return pl.pallas_call(
+        functools.partial(hop_kernel, [len(arrays) for arrays in carried]),
+        out_shape=(jax.ShapeDtypeStruct((rows, wide), BF16),) * n,
+        grid_spec=pltpu.PrefetchScalarGridSpec(
+            num_scalar_prefetch=1,
+            grid=(rows // step,),
+            in_specs=pick + pick + [plain] * len(flat),
+            out_specs=(plain,) * n,
+        ),
+        compiler_params=vmem_params(12),
+        cost_estimate=LIGHT,
+        name="hop",
+    )(jnp.stack(chips).astype(jnp.int32), *[keep] * n, *[got] * n, *flat)
 
 
 def fast_body(
@@ -586,74 +675,103 @@
     shard = lax.axis_index("shard").astype(jnp.int32)
     chip, core = shard // 2, shard % 2
 
-    x_all = gather_dp(frames, n_dp)
-    g_all = gather_dp(cotangent, n_dp)
-    small_ints = jnp.concatenate([lengths, send_order])
-    ints = [small_ints] + [swap(small_ints, "dp", n_dp, k) for k in range(1, n_dp)]
-    orders = jnp.concatenate([a[count:] for a in ints])
-
-    small = jnp.concatenate(
-        [
-            lax.dynamic_slice_in_dim(kernel, me * part, part, axis=0).T,
-            lax.dynamic_slice_in_dim(conv_bias, me * part, part, axis=0)[None],
-            norm_gain.reshape(n_dp, part),
-        ],
-        axis=0,
-    )
-    small_all = gather_shard(small, n_shard)
-    taps_table = (
-        small_all[:, : taps + 1].transpose(1, 0, 2).reshape(taps + 1, channels).astype(F32)
-    )
-    gain = small_all[:, taps + 1 :].reshape(1, width).astype(F32)
-
-    pack = pack_call(me, expand_weight, project_weight, part, wide)
-    packs, owners = gather_line(pack, chip, core)
-    project_blocks, _ = gather_line(project_weight, chip, core)
-
-    normed, swished, ge, returned, small_parts, gain_parts = [], [], [], [], [], []
+    rows = count * length
+    dims = (count, length, taps)
+    ints = jnp.concatenate([lengths, lengths, send_order])
+    ints = lax.all_to_all(jnp.broadcast_to(ints, (n_dp, 3 * count)), "dp", 0, 0, tiled=True)
+    x_own = frames.reshape(rows, width)
+    g_own = cotangent.reshape(rows, width)
+    pack, both = pack_call(
+        me, expand_weight, project_weight, kernel, conv_bias, norm_gain, x_own, g_own, part, wide
+    )
+    pack, both, ints = lax.optimization_barrier((pack, both, ints))
+    ints = jnp.take(ints, me ^ jnp.arange(n_dp), axis=0)
+    ints = jnp.where(jnp.arange(3 * count) // count == 1, me, ints)
+    orders = ints[:, 2 * count :].reshape(-1)
+    hops = line_hops(pack, chip)
+    both_x = swap(both, "dp", 4, 1)
+    both_y = swap(both, "dp", 4, 2)
+    far_x = swap(both_x[:rows], "dp", 4, 2)
+    far_g = swap(both_y[rows:], "dp", 4, 1)
+    x_all = [x_own, both_x, both_y, far_x]
+    g_all = [g_own, both_x, both_y, far_g]
+    owners = line_owners(chip, core)
+    blocks = across_cores(hops)
+    we, wp, taps_table, gain = assemble_call(blocks, owners, owned, part, width, taps)
+    normed = [norm_call(x, gain, rows) for x in x_all]
+
+    project_hops = line_hops(tie(project_weight, hops[5], hops[6]), chip)
+
+    swished, ge, returned, small_parts, pieces = [], [], [], [], []
     for k in range(n_dp):
-        out = chunk_call(
-            x_all[k], g_all[k], gain, taps_table, packs, owners, ints[k][:count], owned, part, taps
-        )
-        normed.append(out[0])
-        swished.append(out[1])
-        ge.append(out[2])
-        returned.append(out[3] if k == 0 else swap(out[3], "dp", n_dp, k))
-        small_parts.append(out[4])
-        gain_parts.append(out[5])
+        if k == 2:
+            normed[k] = tie(normed[k], project_hops[1], project_hops[2])
+        out = chunk_call(ints[k], normed[k], g_all[k], taps_table, we, wp, pieces, dims)
+        swished.append(out[0])
+        ge.append(out[1])
+        returned.append(out[2])
+        small_parts.append(out[3])
+        pieces = list(out[4:])
+        if k in (1, 2):
+            returned[k] = swap(returned[k], "dp", n_dp, k)
 
     keep, give = grads_call(
         core,
-        normed,
+        [tie(normed[0], returned[1], project_hops[3], project_hops[4])] + normed[1:],
         ge,
         swished,
-        [a.reshape(count * length, width) for a in g_all],
+        g_all,
         small_parts,
-        gain_parts,
         owned,
         part,
         taps,
     )
-    reduced = reduce_line(keep, give, chip)
-
-    pieces = route_call(jnp.concatenate([me.reshape(1), orders]), swished, length)
-    pieces = [pieces[0]] + [swap(pieces[m], "dp", n_dp, m) for m in range(1, n_dp)]
-    encoded = encode_call(me, orders, pieces, x_all, project_blocks, owners, owned, part)
-
-    frame_grad = frame_grad_call(frames, cotangent, gain, returned)
-
-    gathered = gather_dp(reduced, n_dp)
-    expand_grad, project_grad = unpack_call(me, gathered, owned, part, width)
-    base = owned + width // wide * part
-    tails = jnp.stack([a[base:] for a in gathered])
+
+    project_blocks = across_cores(project_hops)
+    keep = tie(keep, project_hops[5], project_hops[6])
+    got = swap(give, "shard", 8, 1)
+    (first,) = hop_call(keep, got, [jnp.where(chip <= 1, 3, 0)], [[]])
+    come = along_z(first, [(0, 1), (3, 2)])
+    returned[3], *rest = lax.optimization_barrier((returned[3], *pieces[1:], first))[:-1]
+    returned[3] = swap(returned[3], "dp", n_dp, 3)
+    pieces[1:] = [swap(piece, "dp", n_dp, m + 1) for m, piece in enumerate(rest)]
+    right, left = hop_call(
+        keep, got, [jnp.minimum(chip + 2, 3), jnp.maximum(chip - 2, 0)], [[come], [come]]
+    )
+    right = along_z(right, [(0, 1), (1, 2)])
+    left = along_z(left, [(3, 2), (2, 1)])
+    right, left = lax.optimization_barrier((right, left, returned[2], *pieces[1:]))[:2]
+    right, left = hop_call(
+        keep, got, [jnp.minimum(chip + 1, 3), jnp.maximum(chip - 1, 0)], [[right], [left]]
+    )
+    pieces[0] = tie(pieces[0], right)
+    right = along_z(right, RIGHT)
+    left = along_z(left, LEFT)
+    encoded = encode_call(me, orders, pieces, x_all, project_blocks, owners, owned, part, length)
+    right, left = lax.optimization_barrier((right, left, encoded, returned[3]))[:2]
+    (reduced,) = hop_call(keep, got, [chip], [[right, left]])
+
+    cut = 160
+    low, high = reduced[:cut], reduced[cut:]
+    lows = [low, swap(low, "dp", 4, 1), swap(low, "dp", 4, 2)]
+    highs = [high, swap(high, "dp", 4, 1), swap(high, "dp", 4, 2)]
+    lows.append(swap(lows[1], "dp", 4, 2))
+    highs.append(swap(highs[2], "dp", 4, 1))
+    cotangent_last = tie(cotangent, reduced)
+    frame_grad = frame_grad_call(frames, cotangent_last, gain, returned)
+    lows[3], highs[3] = lax.optimization_barrier((lows[3], highs[3], frame_grad))[:2]
+    expand_grad, project_grad, gain_grad = unpack_call(
+        me, lows, highs, expand_weight, norm_gain.astype(F32)[:, None], owned, part, width
+    )
+    base = owned + width // wide * part - cut
+    tails = jnp.stack([a[base:] for a in highs])
     tails = jnp.take(tails, me ^ jnp.arange(n_dp), axis=0).astype(F32)
     table = jnp.concatenate([tails[:, :, :part], tails[:, :, LANES : LANES + part]], axis=1)
     table = table.transpose(0, 2, 1).reshape(owned, taps + 1)
-    gain_grad = jnp.sum(tails[:, 0, 2 * LANES : 2 * LANES + owned], axis=0)
     return (
-        encoded,
+        encoded.reshape(frames.shape),
         frame_grad,
-        gain_grad,
+        gain_grad.reshape(owned),
         table[:, taps],
         table[:, :taps],
         expand_grad,

time: 289 us -> 239 us (0.83)
  waiting for transfers between devices: 85.8 us -> 61.7 us
  Pallas kernels: 82.3 us -> 67.4 us
  other arithmetic: 16.7 us -> 1.85 us
  local copies, waits for them, and re-layouts: 23.7 us -> 34.9 us
  starting transfers between devices: 76.7 us -> 69.1 us
    ppermute x33 -> x31, waiting for transfers between devices: 62.9 us -> 11.9 us  [swap(): return lax.ppermute(x, axis, [(p, p ^ k) for p in range(size)])]
    ppermute x15 -> x17, waiting for transfers between devices: 22.9 us -> 49.8 us  [along_z(): lax.ppermute(x, 'shard', [(2 * a + c, 2 * b + c) for a, b in pairs for c...]
    unnamed x61 -> x109, local copies, waits for them, and re-layouts: 5.81 us -> 30.6 us
    convert_element_type x6 -> x0, other arithmetic: 9.76 us -> none  [the longest x3 6.7 us: send(): return along_z(value.astype(BF16), pairs)]
    slice x9 -> x5, local copies, waits for them, and re-layouts: 7.76 us -> 0.21 us  [the longest x1 0.07 us: fast_body(): orders = ints[:, 2 * count:].reshape(-1)]
    pallas_call x1, Pallas kernels: 15.3 us -> 7.93 us  [grads_call(): pl.pallas_call(functools.partial(grads_kernel, (n, chips, owned, part, ta...]
    pallas_call x7 -> x15, Pallas kernels: 53.5 us -> 47.9 us  [the longest x4 26.7 us: chunk_call(): pl.pallas_call(functools.partial(chunk_kernel, (count, length, taps, sour...]
    ppermute x3 -> x0, starting transfers between devices: 4.67 us -> none  [gather_shard(): lax.ppermute(x, 'shard', [(p, (p + 2 * k) % 8) for p in range(8)])]
  transfers between devices with their start and end apart: 51 -> 49, of which waited for: 17 -> 11; matrix products, arithmetic and copies ran while one was open for 12% -> 2% of each run, Pallas kernels for 7% -> 22%
where the time goes in v3:
time: 239 us; the launch traced here: 236 us
  starting transfers between devices  69.1 us (29%)
  Pallas kernels  67.4 us (28%)
  waiting for transfers between devices  61.7 us (26%)
  local copies, waits for them, and re-layouts  34.9 us (15%)
    ppermute x17, waiting for transfers between devices, along_z(): lax.ppermute(x, 'shard', [(2 * a + c, 2 * b + c) for a, b in pairs for c...  49.8 us
    ppermute x17, starting transfers between devices, along_z(): lax.ppermute(x, 'shard', [(2 * a + c, 2 * b + c) for a, b in pairs for c...  41.8 us
    unnamed x109, local copies, waits for them, and re-layouts  30.6 us
    pallas_call x4, Pallas kernels, chunk_call(): pl.pallas_call(functools.partial(chunk_kernel, (count, length, taps, sour...  26.7 us
    ppermute x31, starting transfers between devices, swap(): return lax.ppermute(x, axis, [(p, p ^ k) for p in range(size)])  23.6 us
    ppermute x31, waiting for transfers between devices, swap(): return lax.ppermute(x, axis, [(p, p ^ k) for p in range(size)])  11.9 us
    pallas_call x1, Pallas kernels, grads_call(): pl.pallas_call(functools.partial(grads_kernel, (n, chips, owned, part, ta...  7.93 us
    pallas_call x1, Pallas kernels, encode_call(): pl.pallas_call(functools.partial(encode_kernel, (n, n_blocks, length, own...  7.43 us
  transfers between devices with their start and end apart: 49, of which 11 were waited for; matrix products, arithmetic and copies ran while one was open for 2% of the time, Pallas kernels for 22%

profile of v3, /device:TPU:8, one launch (start us, length us, event | category | flops | bytes accessed | tf_op | source)
XLA Modules:
  0.0 236.3 jit_solution(16545095139550713200)
XLA Ops:
  2.0 3.7 %all-to-all-start = ((s32[4,1,12]{2,1,0:T(1,128)}), s32[4,1,12]{2,1,0:T(1,128)S(1)}, u32[]{:S(2)}, u32[]{:S(2)}) async-start(s32[4,1,12]{2,1,0:T(1,128)} %broadcast_in_dim.47), calls=%async_computation | async-start | bytes 4096 | tf_op jit(solution)/shard_map/all_to_all | solution.py:681
  7.9 1.1 copy-done.3
  9.0 1.1 copy-done.6
  10.2 1.3 copy-done.9
  11.4 3.0 %pack.1 = (bf16[304,768]{1,0:T(8,128)(2,1)}, bf16[512,1536]{1,0:T(8,128)(2,1)}) custom-call(s32[1]{0:T(128)} %bitcast.meta, bf16[192,3072]{1,0:T(8,128)(2,1)S(1)} %copy-done.9, bf16[192,1536]{1,0:T(8,128)(2,1)} %refs_8_.1, bf16[192,31]{1,0:T(8,128)(2,1)S(1)} %copy.20.kernel_ref, bf16[1,192]{1,0:T(2,128)(2,1)S(1)} %broadcast_in_dim.45.bias_ref, ...), custom_call_target="tpu_custom_call" | custom-call | flops 1 | bytes 1 | tf_op jit(solution)/shard_map/pack/pallas_call | solution.py:298
  14.5 3.5 %collective-permute-start.2 = (bf16[304,768]{1,0:T(8,128)(2,1)}, bf16[304,768]{1,0:T(8,128)(2,1)S(1)}, u32[]{:S(2)}, u32[]{:S(2)}) collective-permute-start(bf16[304,768]{1,0:T(8,128)(2,1)} %get-tuple-element.85.refs_0_), channel_id=1, source_target_pairs={{0,2},{1,3},{2,4},{3,5},{4,6},{5,7},{8,10},{9,11},{10,12},{11,13},... | collective-permute-start | bytes 1400840 | tf_op jit(solution)/shard_map/ppermute | solution.py:585
  17.9 2.4 %collective-permute-start.3 = (bf16[304,768]{1,0:T(8,128)(2,1)}, bf16[304,768]{1,0:T(8,128)(2,1)S(1)}, u32[]{:S(2)}, u32[]{:S(2)}) collective-permute-start(bf16[304,768]{1,0:T(8,128)(2,1)} %get-tuple-element.85.refs_0_), channel_id=1, source_target_pairs={{6,4},{7,5},{4,2},{5,3},{2,0},{3,1},{14,12},{15,13},{12,10},{13,11... | collective-permute-start | bytes 1400840 | tf_op jit(solution)/shard_map/ppermute | solution.py:585
  20.3 2.1 collective-permute-start
  22.4 1.5 collective-permute-start.15
  23.9 4.8 %collective-permute-done.2.refs_1_ = bf16[304,768]{1,0:T(8,128)(2,1)S(1)} collective-permute-done((bf16[304,768]{1,0:T(8,128)(2,1)}, bf16[304,768]{1,0:T(8,128)(2,1)S(1)}, u32[]{:S(2)}, u32[]{:S(2)}) %collective-permute-start.2) | collective-permute-done | bytes 466976 | tf_op jit(solution)/shard_map/ppermute | solution.py:585
  28.7 3.2 %collective-permute-done.3.refs_2_ = bf16[304,768]{1,0:T(8,128)(2,1)S(1)} collective-permute-done((bf16[304,768]{1,0:T(8,128)(2,1)}, bf16[304,768]{1,0:T(8,128)(2,1)S(1)}, u32[]{:S(2)}, u32[]{:S(2)}) %collective-permute-start.3) | collective-permute-done | bytes 466976 | tf_op jit(solution)/shard_map/ppermute | solution.py:585
  31.9 3.5 %collective-permute-start.4 = (bf16[304,768]{1,0:T(8,128)(2,1)S(1)}, bf16[304,768]{1,0:T(8,128)(2,1)S(1)}, u32[]{:S(2)}, u32[]{:S(2)}) collective-permute-start(bf16[304,768]{1,0:T(8,128)(2,1)S(1)} %collective-permute-done.2.refs_1_), channel_id=1, source_target_pairs={{2,4},{3,5},{4,6},{5,7},{10,12},{11,13},{12,14},{13,15},{18,20},{1... | collective-permute-start | bytes 1400840 | tf_op jit(solution)/shard_map/ppermute | solution.py:585
  35.4 1.9 collective-permute-start.5
  37.4 6.4 %collective-permute-done.4.refs_3_ = bf16[304,768]{1,0:T(8,128)(2,1)S(1)} collective-permute-done((bf16[304,768]{1,0:T(8,128)(2,1)S(1)}, bf16[304,768]{1,0:T(8,128)(2,1)S(1)}, u32[]{:S(2)}, u32[]{:S(2)}) %collective-permute-start.4) | collective-permute-done | bytes 466976 | tf_op jit(solution)/shard_map/ppermute | solution.py:585
  44.6 3.5 %collective-permute-done.5.refs_4_ = bf16[304,768]{1,0:T(8,128)(2,1)} collective-permute-done((bf16[304,768]{1,0:T(8,128)(2,1)S(1)}, bf16[304,768]{1,0:T(8,128)(2,1)}, u32[]{:S(2)}, u32[]{:S(2)}) %collective-permute-start.5) | collective-permute-done | bytes 466976 | tf_op jit(solution)/shard_map/ppermute | solution.py:585
  49.7 1.4 collective-permute-start.6
  51.9 3.0 %collective-permute-start.7 = (bf16[304,768]{1,0:T(8,128)(2,1)}, bf16[304,768]{1,0:T(8,128)(2,1)}, u32[]{:S(2)}, u32[]{:S(2)}) collective-permute-start(bf16[304,768]{1,0:T(8,128)(2,1)} %collective-permute-done.5.refs_4_), channel_id=1, source_target_pairs={{2,0},{3,1},{10,8},{11,9},{18,16},{19,17},{26,24},{27,25}} | collective-permute-start | bytes 1400840 | tf_op jit(solution)/shard_map/ppermute | solution.py:585
  57.1 7.9 %collective-permute-done.7.refs_6_ = bf16[304,768]{1,0:T(8,128)(2,1)} collective-permute-done((bf16[304,768]{1,0:T(8,128)(2,1)}, bf16[304,768]{1,0:T(8,128)(2,1)}, u32[]{:S(2)}, u32[]{:S(2)}) %collective-permute-start.7) | collective-permute-done | bytes 466976 | tf_op jit(solution)/shard_map/ppermute | solution.py:585
  67.0 1.9 collective-permute-start.17
  69.0 4.0 %collective-permute-start.18 = (bf16[192,1536]{1,0:T(8,128)(2,1)}, bf16[192,1536]{1,0:T(8,128)(2,1)S(1)}, u32[]{:S(2)}, u32[]{:S(2)}) collective-permute-start(bf16[192,1536]{1,0:T(8,128)(2,1)} %refs_8_.1), channel_id=1, source_target_pairs={{6,4},{7,5},{4,2},{5,3},{2,0},{3,1},{14,12},{15,13},{12,10},{13,11... | collective-permute-start | bytes 1769480 | tf_op jit(solution)/shard_map/ppermute | solution.py:585
  73.2 1.5 collective-permute-start.1
  74.7 1.5 collective-permute-start.16
  76.3 1.0 copy-done.35
  77.3 3.0 %assemble.1 = (bf16[1536,768]{1,0:T(8,128)(2,1)S(1)}, bf16[384,1536]{1,0:T(8,128)(2,1)S(1)}, f32[32,384]{1,0:T(8,128)S(1)}, f32[1,1536]{1,0:T(1,128)S(1)}) custom-call(s32[14]{0:T(128)S(1)} %stack.98.meta, bf16[304,768]{1,0:T(8,128)(2,1)} %get-tuple-element.85.refs_0_, bf16[304,768]{1,0:T(8,128)(2,1)S(1)} %copy-done.23, bf16[304,768]{1,0:T(8,128)(2,1)S(1)} %copy-done.25, ...), custom_call_target="tpu_custom_call" | custom-call | flops 1 | bytes 1 | tf_op jit(solution)/shard_map/assemble/pallas_call | solution.py:212
  81.4 6.2 %chunk.4 = (bf16[256,384]{1,0:T(8,128)(2,1)S(1)}, bf16[256,768]{1,0:T(8,128)(2,1)S(1)}, bf16[256,1536]{1,0:T(8,128)(2,1)S(1)}, f32[3,32,8,128]{3,2,1,0:T(8,128)S...) custom-call(s32[12]{0:T(128)S(1)} %get-tuple-element.157.meta, ...), custom_call_target="tpu_custom_call" | custom-call | flops 1 | bytes 1 | tf_op jit(solution)/shard_map/chunk/pallas_call | solution.py:119
  89.1 6.2 %chunk.5 = (bf16[256,384]{1,0:T(8,128)(2,1)S(1)}, bf16[256,768]{1,0:T(8,128)(2,1)S(1)}, bf16[256,1536]{1,0:T(8,128)(2,1)S(1)}, f32[3,32,8,128]{3,2,1,0:T(8,128)S...) custom-call(s32[12]{0:T(128)S(1)} %get-tuple-element.158.meta, ...), custom_call_target="tpu_custom_call" | custom-call | flops 1 | bytes 1 | tf_op jit(solution)/shard_map/chunk/pallas_call | solution.py:119
  96.0 2.1 collective-permute-start.20
  98.0 2.1 collective-permute-start.21
  100.8 7.1 %chunk.6 = (bf16[256,384]{1,0:T(8,128)(2,1)S(1)}, bf16[256,768]{1,0:T(8,128)(2,1)S(1)}, bf16[256,1536]{1,0:T(8,128)(2,1)}, f32[3,32,8,128]{3,2,1,0:T(8,128)S(1)}...) custom-call(s32[12]{0:T(128)S(1)} %get-tuple-element.159.meta, ...), custom_call_target="tpu_custom_call" | custom-call | flops 1 | bytes 1 | tf_op jit(solution)/shard_map/chunk/pallas_call | solution.py:119
  108.9 7.1 %chunk.7 = (bf16[256,384]{1,0:T(8,128)(2,1)S(1)}, bf16[256,768]{1,0:T(8,128)(2,1)S(1)}, bf16[256,1536]{1,0:T(8,128)(2,1)}, f32[3,32,8,128]{3,2,1,0:T(8,128)S(1)}...) custom-call(s32[12]{0:T(128)S(1)} %get-tuple-element.160.meta, ...), custom_call_target="tpu_custom_call" | custom-call | flops 1 | bytes 1 | tf_op jit(solution)/shard_map/chunk/pallas_call | solution.py:119
  118.3 7.9 %weight_grads.1 = (bf16[4,304,768]{2,1,0:T(8,128)(2,1)S(1)}, bf16[4,304,768]{2,1,0:T(8,128)(2,1)}) custom-call(s32[1]{0:T(128)} %bitcast.25.meta, bf16[256,1536]{1,0:T(8,128)(2,1)S(1)} %norm.7.normed_ref.refs_0_, bf16[256,1536]{1,0:T(8,128)(2,1)S(1)} %norm.6.normed_ref.refs_1_, bf16[256,1536]{1,0:T(8,128)(2,1)S(1)} %norm.5.normed_ref.refs_2_, ...), custom_call_target="tpu_custom_call" | custom-call | flops 1 | bytes 1 | tf_op jit(solution)/shard_map/weight_grads/pallas_call | solution.py:393
  126.3 1.5 collective-permute-start.22
  127.8 2.1 collective-permute-start.23
  131.3 11.6 %collective-permute-done.23.refs_14_ = bf16[192,1536]{1,0:T(8,128)(2,1)} collective-permute-done((bf16[192,1536]{1,0:T(8,128)(2,1)}, bf16[192,1536]{1,0:T(8,128)(2,1)}, u32[]{:S(2)}, u32[]{:S(2)}) %collective-permute-start.23) | collective-permute-done | bytes 589856 | tf_op jit(solution)/shard_map/ppermute | solution.py:585
  142.9 1.1 hop.4
  144.0 1.3 collective-permute-start.25
  145.4 1.5 collective-permute-start.29
  146.9 12.3 %collective-permute-done.25.refs_4_.refs_5_ = bf16[304,768]{1,0:T(8,128)(2,1)S(1)} collective-permute-done((bf16[304,768]{1,0:T(8,128)(2,1)S(1)}, bf16[304,768]{1,0:T(8,128)(2,1)S(1)}, u32[]{:S(2)}, u32[]{:S(2)}) %collective-permute-start.25) | collective-permute-done | bytes 466976 | tf_op jit(solution)/shard_map/ppermute | solution.py:585
  160.1 2.0 hop.5
  162.2 3.1 %collective-permute-start.26 = (bf16[304,768]{1,0:T(8,128)(2,1)S(1)}, bf16[304,768]{1,0:T(8,128)(2,1)S(1)}, u32[]{:S(2)}, u32[]{:S(2)}) collective-permute-start(bf16[304,768]{1,0:T(8,128)(2,1)S(1)} %get-tuple-element.130), channel_id=1, source_target_pairs={{0,2},{1,3},{2,4},{3,5},{8,10},{9,11},{10,12},{11,13},{16,18},{17,... | collective-permute-start | bytes 1400840 | tf_op jit(solution)/shard_map/ppermute | solution.py:585
  165.3 1.5 collective-permute-start.27
  168.1 2.1 collective-permute-start.31
  170.2 5.7 %collective-permute-done.31.refs_3_ = bf16[4,64,384]{2,1,0:T(8,128)(2,1)S(1)} collective-permute-done((bf16[4,64,384]{2,1,0:T(8,128)(2,1)S(1)}, bf16[4,64,384]{2,1,0:T(8,128)(2,1)S(1)}, u32[]{:S(2)}, u32[]{:S(2)}) %collective-permute-start.31) | collective-permute-done | bytes 196640 | tf_op jit(solution)/shard_map/ppermute | solution.py:844
  176.6 2.1 collective-permute-start.41
  180.0 1.0 copy-done.41
  181.0 2.7 %hop.6 = (bf16[304,768]{1,0:T(8,128)(2,1)}, bf16[304,768]{1,0:T(8,128)(2,1)}) custom-call(s32[2]{0:T(128)S(1)} %pad_add_fusion.1.meta, bf16[4,304,768]{2,1,0:T(8,128)(2,1)S(1)} %get-tuple-element.128.refs_0_.refs_1_, bf16[4,304,768]{2,1,0:T(8,128)(2,1)S(1)} %get-tuple-element.128.refs_0_.refs_1_, ...), custom_call_target="tpu_custom_call" | custom-call | flops 1 | bytes 1 | tf_op jit(solution)/shard_map/hop/pallas_call | solution.py:642
  183.7 4.5 %collective-permute-start.39 = (bf16[304,768]{1,0:T(8,128)(2,1)}, bf16[304,768]{1,0:T(8,128)(2,1)S(1)}, u32[]{:S(2)}, u32[]{:S(2)}) collective-permute-start(bf16[304,768]{1,0:T(8,128)(2,1)} %get-tuple-element.142), channel_id=1, source_target_pairs={{0,2},{1,3},{2,4},{3,5},{4,6},{5,7},{8,10},{9,11},{10,12},{11,13},... | collective-permute-start | bytes 1400840 | tf_op jit(solution)/shard_map/ppermute | solution.py:585
  188.3 1.9 collective-permute-start.40
  190.5 1.1 copy-done.19
  191.6 1.1 copy-done.21
  194.5 7.4 %encode.1 = bf16[256,1536]{1,0:T(8,128)(2,1)} custom-call(s32[31]{0:T(128)S(1)} %concatenate.11.meta, bf16[4,64,384]{2,1,0:T(8,128)(2,1)S(1)} %copy-done.45, bf16[4,64,384]{2,1,0:T(8,128)(2,1)S(1)} %collective-permute-done.29.refs_1_, bf16[4,64,384]{2,1,0:T(8,128)(2,1)S(1)} %copy-done.47, bf16[4,64,384]{2,1,0:T(8,128)(2,1)S(1)} %copy-done.49, ...), custom_call_target="tpu_custom_call" | custom-call | flops 1 | bytes 1 | tf_op jit(solution)/shard_map/encode/pallas_call | solution.py:477
  203.5 1.0 copy-done.37
  204.5 1.0 copy-done.39
  205.6 1.3 hop.7
  208.6 1.2 collective-permute-start.45
  209.8 1.5 collective-permute-start.47
  211.3 1.1 copy-done.13
  212.4 1.1 copy-done.15
  213.6 1.1 copy-done.17
  214.7 4.1 %frame_grad.1 = bf16[256,1536]{1,0:T(8,128)(2,1)} custom-call(bf16[256,1536]{1,0:T(8,128)(2,1)S(1)} %bitcast.56, bf16[256,1536]{1,0:T(8,128)(2,1)S(1)} %bitcast.60, f32[1,1536]{1,0:T(1,128)S(1)} %get-tuple-element.90.gain_ref, bf16[256,1536]{1,0:T(8,128)(2,1)S(1)} %copy-done.13, bf16[256,1536]{1,0:T(8,128)(2,1)S(1)} %copy-done.15, ...), custom_call_target="tpu_custom_call" | custom-call | flops 1 | bytes 1 | tf_op jit(solution)/shard_map/frame_grad/pallas_call | solution.py:516
  219.8 1.5 collective-permute-start.46
  222.5 3.2 %collective-permute-done.46.refs_7_ = bf16[144,768]{1,0:T(8,128)(2,1)S(1)} collective-permute-done((bf16[144,768]{1,0:T(8,128)(2,1)S(1)}, bf16[144,768]{1,0:T(8,128)(2,1)S(1)}, u32[]{:S(2)}, u32[]{:S(2)}) %collective-permute-start.46) | collective-permute-done | bytes 221216 | tf_op jit(solution)/shard_map/ppermute | solution.py:844
  225.7 1.9 collective-permute-done.44.refs_3_
  230.0 5.6 %unpack.1 = (f32[192,3072]{1,0:T(8,128)}, f32[192,1536]{1,0:T(8,128)}, f32[192,1]{1,0:T(8,128)S(1)}) custom-call(s32[1]{0:T(128)} %bitcast.meta, bf16[160,768]{1,0:T(8,128)(2,1)S(1)} %slice.75.refs_0_, bf16[160,768]{1,0:T(8,128)(2,1)} %collective-permute-done.42.refs_1_, bf16[160,768]{1,0:T(8,128)(2,1)} %collective-permute-done.43.refs_2_, ...), custom_call_target="tpu_custom_call" | custom-call | flops 1 | bytes 1 | tf_op jit(solution)/shard_map/unpack/pallas_call | solution.py:568
  (197 shorter events, 34.5 us)
Async XLA Ops:
  2.0 12.4 %all-to-all-start = ((s32[4,1,12]{2,1,0:T(1,128)}), s32[4,1,12]{2,1,0:T(1,128)S(1)}, u32[]{:S(2)}, u32[]{:S(2)}) async-start(s32[4,1,12]{2,1,0:T(1,128)} %broadcast_in_dim.47), calls=%async_computation | async-start | bytes 4096 | tf_op jit(solution)/shard_map/all_to_all | solution.py:681
  14.5 14.3 %collective-permute-start.2 = (bf16[304,768]{1,0:T(8,128)(2,1)}, bf16[304,768]{1,0:T(8,128)(2,1)S(1)}, u32[]{:S(2)}, u32[]{:S(2)}) collective-permute-start(bf16[304,768]{1,0:T(8,128)(2,1)} %get-tuple-element.85.refs_0_), channel_id=1, source_target_pairs={{0,2},{1,3},{2,4},{3,5},{4,6},{5,7},{8,10},{9,11},{10,12},{11,13},... | collective-permute-start | bytes 1400840 | tf_op jit(solution)/shard_map/ppermute | solution.py:585
  17.9 14.0 %collective-permute-start.3 = (bf16[304,768]{1,0:T(8,128)(2,1)}, bf16[304,768]{1,0:T(8,128)(2,1)S(1)}, u32[]{:S(2)}, u32[]{:S(2)}) collective-permute-start(bf16[304,768]{1,0:T(8,128)(2,1)} %get-tuple-element.85.refs_0_), channel_id=1, source_target_pairs={{6,4},{7,5},{4,2},{5,3},{2,0},{3,1},{14,12},{15,13},{12,10},{13,11... | collective-permute-start | bytes 1400840 | tf_op jit(solution)/shard_map/ppermute | solution.py:585
  20.3 46.7 %collective-permute-start = (bf16[512,1536]{1,0:T(8,128)(2,1)}, bf16[512,1536]{1,0:T(8,128)(2,1)S(1)}, u32[]{:S(2)}, u32[]{:S(2)}) collective-permute-start(bf16[512,1536]{1,0:T(8,128)(2,1)} %get-tuple-element.84), channel_id=1, source_target_pairs={{0,8},{8,0},{16,24},{24,16},{1,9},{9,1},{17,25},{25,17},{2,10},{10... | collective-permute-start | bytes 4718600 | tf_op jit(solution)/shard_map/ppermute | solution.py:844
  22.4 46.5 %collective-permute-start.15 = (bf16[512,1536]{1,0:T(8,128)(2,1)}, bf16[512,1536]{1,0:T(8,128)(2,1)S(1)}, u32[]{:S(2)}, u32[]{:S(2)}) collective-permute-start(bf16[512,1536]{1,0:T(8,128)(2,1)} %get-tuple-element.84), channel_id=1, source_target_pairs={{0,16},{8,24},{16,0},{24,8},{1,17},{9,25},{17,1},{25,9},{2,18},{10... | collective-permute-start | bytes 4718600 | tf_op jit(solution)/shard_map/ppermute | solution.py:844
  31.9 11.9 %collective-permute-start.4 = (bf16[304,768]{1,0:T(8,128)(2,1)S(1)}, bf16[304,768]{1,0:T(8,128)(2,1)S(1)}, u32[]{:S(2)}, u32[]{:S(2)}) collective-permute-start(bf16[304,768]{1,0:T(8,128)(2,1)S(1)} %collective-permute-done.2.refs_1_), channel_id=1, source_target_pairs={{2,4},{3,5},{4,6},{5,7},{10,12},{11,13},{12,14},{13,15},{18,20},{1... | collective-permute-start | bytes 1400840 | tf_op jit(solution)/shard_map/ppermute | solution.py:585
  35.4 12.7 %collective-permute-start.5 = (bf16[304,768]{1,0:T(8,128)(2,1)S(1)}, bf16[304,768]{1,0:T(8,128)(2,1)}, u32[]{:S(2)}, u32[]{:S(2)}) collective-permute-start(bf16[304,768]{1,0:T(8,128)(2,1)S(1)} %collective-permute-done.3.refs_2_), channel_id=1, source_target_pairs={{4,2},{5,3},{2,0},{3,1},{12,10},{13,11},{10,8},{11,9},{20,18},{21,... | collective-permute-start | bytes 1400840 | tf_op jit(solution)/shard_map/ppermute | solution.py:585
  37.4 11.5 %collective-permute-start.8 = (bf16[304,768]{1,0:T(8,128)(2,1)}, bf16[304,768]{1,0:T(8,128)(2,1)S(1)}, u32[]{:S(2)}, u32[]{:S(2)}) collective-permute-start(bf16[304,768]{1,0:T(8,128)(2,1)} %get-tuple-element.85.refs_0_), channel_id=1, source_target_pairs={{0,1},{1,0},{2,3},{3,2},{4,5},{5,4},{6,7},{7,6},{8,9},{9,8},{10,11... | collective-permute-start | bytes 1400840 | tf_op jit(solution)/shard_map/ppermute | solution.py:844
  43.9 7.2 %collective-permute-start.9 = (bf16[304,768]{1,0:T(8,128)(2,1)S(1)}, bf16[304,768]{1,0:T(8,128)(2,1)S(1)}, u32[]{:S(2)}, u32[]{:S(2)}) collective-permute-start(bf16[304,768]{1,0:T(8,128)(2,1)S(1)} %collective-permute-done.2.refs_1_), channel_id=1, source_target_pairs={{0,1},{1,0},{2,3},{3,2},{4,5},{5,4},{6,7},{7,6},{8,9},{9,8},{10,11... | collective-permute-start | bytes 1400840 | tf_op jit(solution)/shard_map/ppermute | solution.py:844
  48.1 6.8 %collective-permute-start.10 = (bf16[304,768]{1,0:T(8,128)(2,1)S(1)}, bf16[304,768]{1,0:T(8,128)(2,1)S(1)}, u32[]{:S(2)}, u32[]{:S(2)}) collective-permute-start(bf16[304,768]{1,0:T(8,128)(2,1)S(1)} %collective-permute-done.3.refs_2_), channel_id=1, source_target_pairs={{0,1},{1,0},{2,3},{3,2},{4,5},{5,4},{6,7},{7,6},{8,9},{9,8},{10,11... | collective-permute-start | bytes 1400840 | tf_op jit(solution)/shard_map/ppermute | solution.py:844
  49.7 7.1 %collective-permute-start.6 = (bf16[304,768]{1,0:T(8,128)(2,1)S(1)}, bf16[304,768]{1,0:T(8,128)(2,1)}, u32[]{:S(2)}, u32[]{:S(2)}) collective-permute-start(bf16[304,768]{1,0:T(8,128)(2,1)S(1)} %collective-permute-done.4.refs_3_), channel_id=1, source_target_pairs={{4,6},{5,7},{12,14},{13,15},{20,22},{21,23},{28,30},{29,31}} | collective-permute-start | bytes 1400840 | tf_op jit(solution)/shard_map/ppermute | solution.py:585
  51.9 13.1 %collective-permute-start.7 = (bf16[304,768]{1,0:T(8,128)(2,1)}, bf16[304,768]{1,0:T(8,128)(2,1)}, u32[]{:S(2)}, u32[]{:S(2)}) collective-permute-start(bf16[304,768]{1,0:T(8,128)(2,1)} %collective-permute-done.5.refs_4_), channel_id=1, source_target_pairs={{2,0},{3,1},{10,8},{11,9},{18,16},{19,17},{26,24},{27,25}} | collective-permute-start | bytes 1400840 | tf_op jit(solution)/shard_map/ppermute | solution.py:585
  55.7 9.3 %collective-permute-start.11 = (bf16[304,768]{1,0:T(8,128)(2,1)S(1)}, bf16[304,768]{1,0:T(8,128)(2,1)S(1)}, u32[]{:S(2)}, u32[]{:S(2)}) collective-permute-start(bf16[304,768]{1,0:T(8,128)(2,1)S(1)} %collective-permute-done.4.refs_3_), channel_id=1, source_target_pairs={{0,1},{1,0},{2,3},{3,2},{4,5},{5,4},{6,7},{7,6},{8,9},{9,8},{10,11... | collective-permute-start | bytes 1400840 | tf_op jit(solution)/shard_map/ppermute | solution.py:844
  56.7 16.5 %collective-permute-start.12 = (bf16[304,768]{1,0:T(8,128)(2,1)}, bf16[304,768]{1,0:T(8,128)(2,1)}, u32[]{:S(2)}, u32[]{:S(2)}) collective-permute-start(bf16[304,768]{1,0:T(8,128)(2,1)} %collective-permute-done.5.refs_4_), channel_id=1, source_target_pairs={{0,1},{1,0},{2,3},{3,2},{4,5},{5,4},{6,7},{7,6},{8,9},{9,8},{10,11... | collective-permute-start | bytes 1400840 | tf_op jit(solution)/shard_map/ppermute | solution.py:844
  65.0 9.7 %collective-permute-start.13 = (bf16[304,768]{1,0:T(8,128)(2,1)}, bf16[304,768]{1,0:T(8,128)(2,1)}, u32[]{:S(2)}, u32[]{:S(2)}) collective-permute-start(bf16[304,768]{1,0:T(8,128)(2,1)} %collective-permute-done.6.refs_5_), channel_id=1, source_target_pairs={{0,1},{1,0},{2,3},{3,2},{4,5},{5,4},{6,7},{7,6},{8,9},{9,8},{10,11... | collective-permute-start | bytes 1400840 | tf_op jit(solution)/shard_map/ppermute | solution.py:844
  65.8 10.4 %collective-permute-start.14 = (bf16[304,768]{1,0:T(8,128)(2,1)}, bf16[304,768]{1,0:T(8,128)(2,1)}, u32[]{:S(2)}, u32[]{:S(2)}) collective-permute-start(bf16[304,768]{1,0:T(8,128)(2,1)} %collective-permute-done.7.refs_6_), channel_id=1, source_target_pairs={{0,1},{1,0},{2,3},{3,2},{4,5},{5,4},{6,7},{7,6},{8,9},{9,8},{10,11... | collective-permute-start | bytes 1400840 | tf_op jit(solution)/shard_map/ppermute | solution.py:844
  67.0 51.3 %copy-start = (bf16[512,1536]{1,0:T(8,128)(2,1)}, bf16[512,1536]{1,0:T(8,128)(2,1)S(1)}, u32[]{:S(2)}) copy-start(bf16[512,1536]{1,0:T(8,128)(2,1)S(1)} %collective-permute-done.x_ref.g_ref.refs_13_.refs_5_) | copy-start | bytes 4718596
  67.0 28.9 %collective-permute-start.17 = (bf16[192,1536]{1,0:T(8,128)(2,1)}, bf16[192,1536]{1,0:T(8,128)(2,1)S(1)}, u32[]{:S(2)}, u32[]{:S(2)}) collective-permute-start(bf16[192,1536]{1,0:T(8,128)(2,1)} %refs_8_.1), channel_id=1, source_target_pairs={{0,2},{1,3},{2,4},{3,5},{4,6},{5,7},{8,10},{9,11},{10,12},{11,13},... | collective-permute-start | bytes 1769480 | tf_op jit(solution)/shard_map/ppermute | solution.py:585
  68.9 31.8 %copy-start.1 = (bf16[512,1536]{1,0:T(8,128)(2,1)}, bf16[512,1536]{1,0:T(8,128)(2,1)S(1)}, u32[]{:S(2)}) copy-start(bf16[512,1536]{1,0:T(8,128)(2,1)S(1)} %collective-permute-done.15.x_ref.g_ref.refs_14_.refs_6_) | copy-start | bytes 4718596
  69.0 27.0 %collective-permute-start.18 = (bf16[192,1536]{1,0:T(8,128)(2,1)}, bf16[192,1536]{1,0:T(8,128)(2,1)S(1)}, u32[]{:S(2)}, u32[]{:S(2)}) collective-permute-start(bf16[192,1536]{1,0:T(8,128)(2,1)} %refs_8_.1), channel_id=1, source_target_pairs={{6,4},{7,5},{4,2},{5,3},{2,0},{3,1},{14,12},{15,13},{12,10},{13,11... | collective-permute-start | bytes 1769480 | tf_op jit(solution)/shard_map/ppermute | solution.py:585
  73.0 3.2 %copy-start.27 = (bf16[304,768]{1,0:T(8,128)(2,1)S(1)}, bf16[304,768]{1,0:T(8,128)(2,1)}, u32[]{:S(2)}) copy-start(bf16[304,768]{1,0:T(8,128)(2,1)} %copy-done.26) | copy-start | bytes 1400836
  73.0 3.2 %copy-start.29 = (bf16[304,768]{1,0:T(8,128)(2,1)S(1)}, bf16[304,768]{1,0:T(8,128)(2,1)}, u32[]{:S(2)}) copy-start(bf16[304,768]{1,0:T(8,128)(2,1)} %copy-done.28) | copy-start | bytes 1400836
  73.2 7.1 %copy-start.4 = (bf16[4,64,1536]{2,1,0:T(8,128)(2,1)S(1)}, bf16[4,64,1536]{2,1,0:T(8,128)(2,1)}, u32[]{:S(2)}) copy-start(bf16[4,64,1536]{2,1,0:T(8,128)(2,1)} %param.9) | copy-start | bytes 2359300
  73.2 34.7 %collective-permute-start.1 = (bf16[256,1536]{1,0:T(8,128)(2,1)S(1)}, bf16[256,1536]{1,0:T(8,128)(2,1)S(1)}, u32[]{:S(2)}, u32[]{:S(2)}) collective-permute-start(bf16[256,1536]{1,0:T(8,128)(2,1)S(1)} %slice.73), channel_id=1, source_target_pairs={{0,16},{8,24},{16,0},{24,8},{1,17},{9,25},{17,1},{25,9},{2,18},{10... | collective-permute-start | bytes 2359304 | tf_op jit(solution)/shard_map/ppermute | solution.py:844
  74.7 33.9 %collective-permute-start.16 = (bf16[256,1536]{1,0:T(8,128)(2,1)S(1)}, bf16[256,1536]{1,0:T(8,128)(2,1)S(1)}, u32[]{:S(2)}, u32[]{:S(2)}) collective-permute-start(bf16[256,1536]{1,0:T(8,128)(2,1)S(1)} %slice.74), channel_id=1, source_target_pairs={{0,8},{8,0},{16,24},{24,16},{1,9},{9,1},{17,25},{25,17},{2,10},{10... | collective-permute-start | bytes 2359304 | tf_op jit(solution)/shard_map/ppermute | solution.py:844
  95.3 22.1 %collective-permute-start.19 = (bf16[256,1536]{1,0:T(8,128)(2,1)S(1)}, bf16[256,1536]{1,0:T(8,128)(2,1)S(1)}, u32[]{:S(2)}, u32[]{:S(2)}) collective-permute-start(bf16[256,1536]{1,0:T(8,128)(2,1)S(1)} %get-tuple-element.109), channel_id=1, source_target_pairs={{0,8},{8,0},{16,24},{24,16},{1,9},{9,1},{17,25},{25,17},{2,10},{10... | collective-permute-start | bytes 2359304 | tf_op jit(solution)/shard_map/ppermute | solution.py:844
  95.9 12.6 %copy-start.18 = (bf16[192,1536]{1,0:T(8,128)(2,1)}, bf16[192,1536]{1,0:T(8,128)(2,1)S(1)}, u32[]{:S(2)}) copy-start(bf16[192,1536]{1,0:T(8,128)(2,1)S(1)} %collective-permute-done.17.refs_9_) | copy-start | bytes 1769476
  95.9 12.6 %copy-start.20 = (bf16[192,1536]{1,0:T(8,128)(2,1)}, bf16[192,1536]{1,0:T(8,128)(2,1)S(1)}, u32[]{:S(2)}) copy-start(bf16[192,1536]{1,0:T(8,128)(2,1)S(1)} %collective-permute-done.18.refs_10_) | copy-start | bytes 1769476
  96.0 21.4 %collective-permute-start.20 = (bf16[192,1536]{1,0:T(8,128)(2,1)S(1)}, bf16[192,1536]{1,0:T(8,128)(2,1)}, u32[]{:S(2)}, u32[]{:S(2)}) collective-permute-start(bf16[192,1536]{1,0:T(8,128)(2,1)S(1)} %collective-permute-done.17.refs_9_), channel_id=1, source_target_pairs={{2,4},{3,5},{4,6},{5,7},{10,12},{11,13},{12,14},{13,15},{18,20},{1... | collective-permute-start | bytes 1769480 | tf_op jit(solution)/shard_map/ppermute | solution.py:585
  98.0 19.3 %collective-permute-start.21 = (bf16[192,1536]{1,0:T(8,128)(2,1)S(1)}, bf16[192,1536]{1,0:T(8,128)(2,1)}, u32[]{:S(2)}, u32[]{:S(2)}) collective-permute-start(bf16[192,1536]{1,0:T(8,128)(2,1)S(1)} %collective-permute-done.18.refs_10_), channel_id=1, source_target_pairs={{4,2},{5,3},{2,0},{3,1},{12,10},{13,11},{10,8},{11,9},{20,18},{21,... | collective-permute-start | bytes 1769480 | tf_op jit(solution)/shard_map/ppermute | solution.py:585
  108.9 9.4 %copy-start.2 = (bf16[512,1536]{1,0:T(8,128)(2,1)S(1)}, bf16[512,1536]{1,0:T(8,128)(2,1)}, u32[]{:S(2)}) copy-start(bf16[512,1536]{1,0:T(8,128)(2,1)} %copy-done.1) | copy-start | bytes 4718596
  126.2 16.7 %collective-permute-start.24 = (bf16[4,304,768]{2,1,0:T(8,128)(2,1)}, bf16[4,304,768]{2,1,0:T(8,128)(2,1)}, u32[]{:S(2)}, u32[]{:S(2)}) collective-permute-start(bf16[4,304,768]{2,1,0:T(8,128)(2,1)} %get-tuple-element.129), channel_id=1, source_target_pairs={{0,1},{1,0},{2,3},{3,2},{4,5},{5,4},{6,7},{7,6},{8,9},{9,8},{10,11... | collective-permute-start | bytes 5603336 | tf_op jit(solution)/shard_map/ppermute | solution.py:844
  126.3 4.7 %collective-permute-start.22 = (bf16[192,1536]{1,0:T(8,128)(2,1)}, bf16[192,1536]{1,0:T(8,128)(2,1)}, u32[]{:S(2)}, u32[]{:S(2)}) collective-permute-start(bf16[192,1536]{1,0:T(8,128)(2,1)} %collective-permute-done.20.refs_11_), channel_id=1, source_target_pairs={{4,6},{5,7},{12,14},{13,15},{20,22},{21,23},{28,30},{29,31}} | collective-permute-start | bytes 1769480 | tf_op jit(solution)/shard_map/ppermute | solution.py:585
  127.8 15.1 %collective-permute-start.23 = (bf16[192,1536]{1,0:T(8,128)(2,1)}, bf16[192,1536]{1,0:T(8,128)(2,1)}, u32[]{:S(2)}, u32[]{:S(2)}) collective-permute-start(bf16[192,1536]{1,0:T(8,128)(2,1)} %collective-permute-done.21.refs_12_), channel_id=1, source_target_pairs={{2,0},{3,1},{10,8},{11,9},{18,16},{19,17},{26,24},{27,25}} | collective-permute-start | bytes 1769480 | tf_op jit(solution)/shard_map/ppermute | solution.py:585
  129.9 36.9 %collective-permute-start.28 = (bf16[256,1536]{1,0:T(8,128)(2,1)}, bf16[256,1536]{1,0:T(8,128)(2,1)S(1)}, u32[]{:S(2)}, u32[]{:S(2)}) collective-permute-start(bf16[256,1536]{1,0:T(8,128)(2,1)} %get-tuple-element.132), channel_id=1, source_target_pairs={{0,16},{8,24},{16,0},{24,8},{1,17},{9,25},{17,1},{25,9},{2,18},{10... | collective-permute-start | bytes 2359304 | tf_op jit(solution)/shard_map/ppermute | solution.py:844
  130.8 14.6 %collective-permute-start.32 = (bf16[192,1536]{1,0:T(8,128)(2,1)}, bf16[192,1536]{1,0:T(8,128)(2,1)}, u32[]{:S(2)}, u32[]{:S(2)}) collective-permute-start(bf16[192,1536]{1,0:T(8,128)(2,1)} %refs_8_.1), channel_id=1, source_target_pairs={{0,1},{1,0},{2,3},{3,2},{4,5},{5,4},{6,7},{7,6},{8,9},{9,8},{10,11... | collective-permute-start | bytes 1769480 | tf_op jit(solution)/shard_map/ppermute | solution.py:844
  131.0 31.2 %collective-permute-start.33 = (bf16[192,1536]{1,0:T(8,128)(2,1)}, bf16[192,1536]{1,0:T(8,128)(2,1)}, u32[]{:S(2)}, u32[]{:S(2)}) collective-permute-start(bf16[192,1536]{1,0:T(8,128)(2,1)} %copy-done.18), channel_id=1, source_target_pairs={{0,1},{1,0},{2,3},{3,2},{4,5},{5,4},{6,7},{7,6},{8,9},{9,8},{10,11... | collective-permute-start | bytes 1769480 | tf_op jit(solution)/shard_map/ppermute | solution.py:844
  142.9 22.4 %collective-permute-start.34 = (bf16[192,1536]{1,0:T(8,128)(2,1)}, bf16[192,1536]{1,0:T(8,128)(2,1)}, u32[]{:S(2)}, u32[]{:S(2)}) collective-permute-start(bf16[192,1536]{1,0:T(8,128)(2,1)} %copy-done.20), channel_id=1, source_target_pairs={{0,1},{1,0},{2,3},{3,2},{4,5},{5,4},{6,7},{7,6},{8,9},{9,8},{10,11... | collective-permute-start | bytes 1769480 | tf_op jit(solution)/shard_map/ppermute | solution.py:844
  144.0 15.1 %collective-permute-start.25 = (bf16[304,768]{1,0:T(8,128)(2,1)S(1)}, bf16[304,768]{1,0:T(8,128)(2,1)S(1)}, u32[]{:S(2)}, u32[]{:S(2)}) collective-permute-start(bf16[304,768]{1,0:T(8,128)(2,1)S(1)} %hop.4), channel_id=1, source_target_pairs={{0,2},{1,3},{6,4},{7,5},{8,10},{9,11},{14,12},{15,13},{16,18},{17,... | collective-permute-start | bytes 1400840 | tf_op jit(solution)/shard_map/ppermute | solution.py:585
  145.4 21.6 %collective-permute-start.29 = (bf16[4,64,384]{2,1,0:T(8,128)(2,1)}, bf16[4,64,384]{2,1,0:T(8,128)(2,1)S(1)}, u32[]{:S(2)}, u32[]{:S(2)}) collective-permute-start(bf16[4,64,384]{2,1,0:T(8,128)(2,1)} %get-tuple-element.137), channel_id=1, source_target_pairs={{0,8},{8,0},{16,24},{24,16},{1,9},{9,1},{17,25},{25,17},{2,10},{10... | collective-permute-start | bytes 589832 | tf_op jit(solution)/shard_map/ppermute | solution.py:844
  159.2 8.2 %collective-permute-start.30 = (bf16[4,64,384]{2,1,0:T(8,128)(2,1)}, bf16[4,64,384]{2,1,0:T(8,128)(2,1)S(1)}, u32[]{:S(2)}, u32[]{:S(2)}) collective-permute-start(bf16[4,64,384]{2,1,0:T(8,128)(2,1)} %get-tuple-element.138), channel_id=1, source_target_pairs={{0,16},{8,24},{16,0},{24,8},{1,17},{9,25},{17,1},{25,9},{2,18},{10... | collective-permute-start | bytes 589832 | tf_op jit(solution)/shard_map/ppermute | solution.py:844
  160.1 8.0 %copy-start.51 = (bf16[4,64,384]{2,1,0:T(8,128)(2,1)S(1)}, bf16[4,64,384]{2,1,0:T(8,128)(2,1)}, u32[]{:S(2)}) copy-start(bf16[4,64,384]{2,1,0:T(8,128)(2,1)} %copy-done.50) | copy-start | bytes 589828
  162.2 16.5 %collective-permute-start.26 = (bf16[304,768]{1,0:T(8,128)(2,1)S(1)}, bf16[304,768]{1,0:T(8,128)(2,1)S(1)}, u32[]{:S(2)}, u32[]{:S(2)}) collective-permute-start(bf16[304,768]{1,0:T(8,128)(2,1)S(1)} %get-tuple-element.130), channel_id=1, source_target_pairs={{0,2},{1,3},{2,4},{3,5},{8,10},{9,11},{10,12},{11,13},{16,18},{17,... | collective-permute-start | bytes 1400840 | tf_op jit(solution)/shard_map/ppermute | solution.py:585
  165.3 13.4 %collective-permute-start.27 = (bf16[304,768]{1,0:T(8,128)(2,1)S(1)}, bf16[304,768]{1,0:T(8,128)(2,1)S(1)}, u32[]{:S(2)}, u32[]{:S(2)}) collective-permute-start(bf16[304,768]{1,0:T(8,128)(2,1)S(1)} %get-tuple-element.131), channel_id=1, source_target_pairs={{6,4},{7,5},{4,2},{5,3},{14,12},{15,13},{12,10},{13,11},{22,20},{2... | collective-permute-start | bytes 1400840 | tf_op jit(solution)/shard_map/ppermute | solution.py:585
  166.8 16.9 %copy-start.16 = (bf16[256,1536]{1,0:T(8,128)(2,1)}, bf16[256,1536]{1,0:T(8,128)(2,1)S(1)}, u32[]{:S(2)}) copy-start(bf16[256,1536]{1,0:T(8,128)(2,1)S(1)} %collective-permute-done.28.refs_2_) | copy-start | bytes 2359300
  166.8 16.9 %collective-permute-start.35 = (bf16[192,1536]{1,0:T(8,128)(2,1)}, bf16[192,1536]{1,0:T(8,128)(2,1)}, u32[]{:S(2)}, u32[]{:S(2)}) collective-permute-start(bf16[192,1536]{1,0:T(8,128)(2,1)} %collective-permute-done.20.refs_11_), channel_id=1, source_target_pairs={{0,1},{1,0},{2,3},{3,2},{4,5},{5,4},{6,7},{7,6},{8,9},{9,8},{10,11... | collective-permute-start | bytes 1769480 | tf_op jit(solution)/shard_map/ppermute | solution.py:844
  166.9 21.4 %collective-permute-start.36 = (bf16[192,1536]{1,0:T(8,128)(2,1)}, bf16[192,1536]{1,0:T(8,128)(2,1)}, u32[]{:S(2)}, u32[]{:S(2)}) collective-permute-start(bf16[192,1536]{1,0:T(8,128)(2,1)} %collective-permute-done.21.refs_12_), channel_id=1, source_target_pairs={{0,1},{1,0},{2,3},{3,2},{4,5},{5,4},{6,7},{7,6},{8,9},{9,8},{10,11... | collective-permute-start | bytes 1769480 | tf_op jit(solution)/shard_map/ppermute | solution.py:844
  168.1 7.8 %collective-permute-start.31 = (bf16[4,64,384]{2,1,0:T(8,128)(2,1)S(1)}, bf16[4,64,384]{2,1,0:T(8,128)(2,1)S(1)}, u32[]{:S(2)}, u32[]{:S(2)}) collective-permute-start(bf16[4,64,384]{2,1,0:T(8,128)(2,1)S(1)} %copy-done.51), channel_id=1, source_target_pairs={{0,24},{8,16},{16,8},{24,0},{1,25},{9,17},{17,9},{25,1},{2,26},{10... | collective-permute-start | bytes 589832 | tf_op jit(solution)/shard_map/ppermute | solution.py:844
  176.6 25.4 %collective-permute-start.41 = (bf16[256,1536]{1,0:T(8,128)(2,1)}, bf16[256,1536]{1,0:T(8,128)(2,1)}, u32[]{:S(2)}, u32[]{:S(2)}) collective-permute-start(bf16[256,1536]{1,0:T(8,128)(2,1)} %get-tuple-element.145), channel_id=1, source_target_pairs={{0,24},{8,16},{16,8},{24,0},{1,25},{9,17},{17,9},{25,1},{2,26},{10... | collective-permute-start | bytes 2359304 | tf_op jit(solution)/shard_map/ppermute | solution.py:844
  178.6 11.9 %collective-permute-start.37 = (bf16[192,1536]{1,0:T(8,128)(2,1)}, bf16[192,1536]{1,0:T(8,128)(2,1)}, u32[]{:S(2)}, u32[]{:S(2)}) collective-permute-start(bf16[192,1536]{1,0:T(8,128)(2,1)} %collective-permute-done.22.refs_13_), channel_id=1, source_target_pairs={{0,1},{1,0},{2,3},{3,2},{4,5},{5,4},{6,7},{7,6},{8,9},{9,8},{10,11... | collective-permute-start | bytes 1769480 | tf_op jit(solution)/shard_map/ppermute | solution.py:844
  179.4 11.1 %collective-permute-start.38 = (bf16[192,1536]{1,0:T(8,128)(2,1)}, bf16[192,1536]{1,0:T(8,128)(2,1)}, u32[]{:S(2)}, u32[]{:S(2)}) collective-permute-start(bf16[192,1536]{1,0:T(8,128)(2,1)} %collective-permute-done.23.refs_14_), channel_id=1, source_target_pairs={{0,1},{1,0},{2,3},{3,2},{4,5},{5,4},{6,7},{7,6},{8,9},{9,8},{10,11... | collective-permute-start | bytes 1769480 | tf_op jit(solution)/shard_map/ppermute | solution.py:844
  181.0 9.5 %copy-start.45 = (bf16[4,64,384]{2,1,0:T(8,128)(2,1)S(1)}, bf16[4,64,384]{2,1,0:T(8,128)(2,1)}, u32[]{:S(2)}) copy-start(bf16[4,64,384]{2,1,0:T(8,128)(2,1)} %copy-done.44) | copy-start | bytes 589828
  183.7 18.2 %collective-permute-start.39 = (bf16[304,768]{1,0:T(8,128)(2,1)}, bf16[304,768]{1,0:T(8,128)(2,1)S(1)}, u32[]{:S(2)}, u32[]{:S(2)}) collective-permute-start(bf16[304,768]{1,0:T(8,128)(2,1)} %get-tuple-element.142), channel_id=1, source_target_pairs={{0,2},{1,3},{2,4},{3,5},{4,6},{5,7},{8,10},{9,11},{10,12},{11,13},... | collective-permute-start | bytes 1400840 | tf_op jit(solution)/shard_map/ppermute | solution.py:585
  188.3 14.4 %collective-permute-start.40 = (bf16[304,768]{1,0:T(8,128)(2,1)}, bf16[304,768]{1,0:T(8,128)(2,1)S(1)}, u32[]{:S(2)}, u32[]{:S(2)}) collective-permute-start(bf16[304,768]{1,0:T(8,128)(2,1)} %get-tuple-element.144), channel_id=1, source_target_pairs={{6,4},{7,5},{4,2},{5,3},{2,0},{3,1},{14,12},{15,13},{12,10},{13,11... | collective-permute-start | bytes 1400840 | tf_op jit(solution)/shard_map/ppermute | solution.py:585
  205.6 5.7 %copy-start.8 = (bf16[4,64,1536]{2,1,0:T(8,128)(2,1)S(1)}, bf16[4,64,1536]{2,1,0:T(8,128)(2,1)}, u32[]{:S(2)}) copy-start(bf16[4,64,1536]{2,1,0:T(8,128)(2,1)} %param.10) | copy-start | bytes 2359300
  206.8 4.4 %copy-start.5 = (bf16[4,64,1536]{2,1,0:T(8,128)(2,1)S(1)}, bf16[4,64,1536]{2,1,0:T(8,128)(2,1)}, u32[]{:S(2)}) copy-start(bf16[4,64,1536]{2,1,0:T(8,128)(2,1)} %param.9) | copy-start | bytes 2359300
  206.9 14.3 %collective-permute-start.42 = (bf16[160,768]{1,0:T(8,128)(2,1)S(1)}, bf16[160,768]{1,0:T(8,128)(2,1)}, u32[]{:S(2)}, u32[]{:S(2)}) collective-permute-start(bf16[160,768]{1,0:T(8,128)(2,1)S(1)} %slice.75.refs_0_), channel_id=1, source_target_pairs={{0,8},{8,0},{16,24},{24,16},{1,9},{9,1},{17,25},{25,17},{2,10},{10... | collective-permute-start | bytes 737288 | tf_op jit(solution)/shard_map/ppermute | solution.py:844
  207.6 21.4 %collective-permute-start.43 = (bf16[160,768]{1,0:T(8,128)(2,1)S(1)}, bf16[160,768]{1,0:T(8,128)(2,1)}, u32[]{:S(2)}, u32[]{:S(2)}) collective-permute-start(bf16[160,768]{1,0:T(8,128)(2,1)S(1)} %slice.75.refs_0_), channel_id=1, source_target_pairs={{0,16},{8,24},{16,0},{24,8},{1,17},{9,25},{17,1},{25,9},{2,18},{10... | collective-permute-start | bytes 737288 | tf_op jit(solution)/shard_map/ppermute | solution.py:844
  208.6 11.2 %collective-permute-start.45 = (bf16[144,768]{1,0:T(8,128)(2,1)S(1)}, bf16[144,768]{1,0:T(8,128)(2,1)S(1)}, u32[]{:S(2)}, u32[]{:S(2)}) collective-permute-start(bf16[144,768]{1,0:T(8,128)(2,1)S(1)} %slice.76.refs_4_), channel_id=1, source_target_pairs={{0,16},{8,24},{16,0},{24,8},{1,17},{9,25},{17,1},{25,9},{2,18},{10... | collective-permute-start | bytes 663560 | tf_op jit(solution)/shard_map/ppermute | solution.py:844
  209.8 12.0 %collective-permute-start.47 = (bf16[144,768]{1,0:T(8,128)(2,1)S(1)}, bf16[144,768]{1,0:T(8,128)(2,1)S(1)}, u32[]{:S(2)}, u32[]{:S(2)}) collective-permute-start(bf16[144,768]{1,0:T(8,128)(2,1)S(1)} %slice.76.refs_4_), channel_id=1, source_target_pairs={{0,8},{8,0},{16,24},{24,16},{1,9},{9,1},{17,25},{25,17},{2,10},{10... | collective-permute-start | bytes 663560 | tf_op jit(solution)/shard_map/ppermute | solution.py:844
  218.8 10.3 %copy-start.10 = (bf16[192,3072]{1,0:T(8,128)(2,1)S(1)}, bf16[192,3072]{1,0:T(8,128)(2,1)}, u32[]{:S(2)}) copy-start(bf16[192,3072]{1,0:T(8,128)(2,1)} %refs_8_.2) | copy-start | bytes 3538948
  219.8 5.9 %collective-permute-start.46 = (bf16[144,768]{1,0:T(8,128)(2,1)S(1)}, bf16[144,768]{1,0:T(8,128)(2,1)S(1)}, u32[]{:S(2)}, u32[]{:S(2)}) collective-permute-start(bf16[144,768]{1,0:T(8,128)(2,1)S(1)} %collective-permute-done.45.refs_6_), channel_id=1, source_target_pairs={{0,8},{8,0},{16,24},{24,16},{1,9},{9,1},{17,25},{25,17},{2,10},{10... | collective-permute-start | bytes 663560 | tf_op jit(solution)/shard_map/ppermute | solution.py:844
  221.2 6.4 %collective-permute-start.44 = (bf16[160,768]{1,0:T(8,128)(2,1)}, bf16[160,768]{1,0:T(8,128)(2,1)S(1)}, u32[]{:S(2)}, u32[]{:S(2)}) collective-permute-start(bf16[160,768]{1,0:T(8,128)(2,1)} %collective-permute-done.42.refs_1_), channel_id=1, source_target_pairs={{0,16},{8,24},{16,0},{24,8},{1,17},{9,25},{17,1},{25,9},{2,18},{10... | collective-permute-start | bytes 737288 | tf_op jit(solution)/shard_map/ppermute | solution.py:844
  228.5 7.1 %copy-start.52 = (f32[192,32]{0,1:T(8,128)}, f32[192,32]{0,1:T(8,128)S(1)}, u32[]{:S(2)}) copy-start(f32[192,32]{0,1:T(8,128)S(1)} %reshape.81) | copy-start | bytes 73732
  (39 other events, 45.8 us)

commit v4 on v1

--- a/solution.py
+++ b/solution.py
@@ -1,11 +1,879 @@
+import functools
+
 import jax
 import jax.numpy as jnp
 from jax import lax
+from jax.experimental import pallas as pl
+from jax.experimental.pallas import tpu as pltpu
 from jax.sharding import PartitionSpec as P
 
 EPS = 1e-05
 F32 = jnp.float32
 BF16 = jnp.bfloat16
+LANES = 128
+MARGIN = 16
+NT = (((1,), (1,)), ((), ()))
+TN = (((0,), (0,)), ((), ()))
+VMEM_PACK = 60
+VMEM_CHUNK = 60
+VMEM_ENCODE = 60
+VMEM_FRAME = 60
+VMEM_HOP = 60
+VMEM_UNPACK = 28
+LIGHT = pl.CostEstimate(flops=1, bytes_accessed=1, transcendentals=0)
+
+
+def route(dims, refs, meta, s, base):
+    count, length, taps = dims
+    source = lax.axis_index("dp") ^ s
+    copies = []
+    for q in range(count):
+        chosen = base + length * meta[source, count + (lax.axis_index("dp") ^ q)]
+        copies.append(
+            pltpu.make_async_copy(
+                refs["sw"].at[pl.ds(pl.multiple_of(chosen, length), length)],
+                refs["pieces"][q].at[pl.ds(pl.multiple_of(s * length, length), length)],
+                refs["route_sems"].at[s, q],
+            )
+        )
+    return copies
+
+
+def one_source(dims, refs, meta, s, base, ready):
+    count, length, taps = dims
+    rows = count * length
+    we, ab, pad, gpad, slope = (refs[n] for n in ("we", "ab", "pad", "gpad", "slope"))
+    normed, sw, ge, taps_ref, small = (refs[n] for n in ("normed", "sw", "ge", "taps", "small"))
+    width, wide = we.shape
+    channels = wide // 2
+    tiles = channels // LANES
+    own = pl.ds(base, rows)
+    step = 64
+    ready("we")
+    gain = refs["gain"][...]
+    ready("x")
+
+    @pl.loop(0, rows // step)
+    def _(index):
+        at = pl.ds(pl.multiple_of(base + index * step, step), step)
+        x = refs["x"][at, :].astype(F32)
+        centred = x - jnp.mean(x, axis=1, keepdims=True)
+        variance = jnp.mean(centred * centred, axis=1, keepdims=True)
+        normed[at, :] = (centred * lax.rsqrt(variance + EPS) * gain).astype(BF16)
+
+    expanded = jnp.dot(normed[own, :], we[...], preferred_element_type=F32)
+    for tile in range(2 * tiles):
+        ab[tile] = expanded[:, tile * LANES : (tile + 1) * LANES]
+
+    first = (taps - 1) // 2
+    positions = lax.broadcasted_iota(jnp.int32, (length, LANES), 0)
+    source = lax.axis_index("dp") ^ s
+
+    @pl.loop(0, count)
+    def _(u):
+        at = pl.ds(pl.multiple_of(u * length, length), length)
+        out = pl.ds(pl.multiple_of(base + u * length, length), length)
+        live = positions < meta[source, u]
+        for tile in range(tiles):
+            lanes = pl.ds(tile * LANES, LANES)
+            gate = jax.nn.sigmoid(ab[tiles + tile, at, :])
+            glu = jnp.where(live, ab[tile, at, :] * gate, 0.0).astype(BF16).astype(F32)
+            pad[u, tile, MARGIN : MARGIN + length, :] = glu
+            ab[tiles + tile, at, :] = gate
+            conv = jnp.broadcast_to(taps_ref[taps : taps + 1, lanes], (length, LANES))
+            for t in range(taps):
+                conv += taps_ref[t : t + 1, lanes] * pad[u, tile, pl.ds(MARGIN - first + t, length), :]
+            sig = jax.nn.sigmoid(conv)
+            sw[out, lanes] = jnp.where(live, conv * sig, 0.0).astype(BF16)
+            slope[u, tile] = jnp.where(live, sig * (1.0 + conv * (1.0 - sig)), 0.0)
+
+    for copy in route(dims, refs, meta, s, base):
+        copy.start()
+
+    ready("g")
+    ready("wp")
+    grad_swish = lax.dot_general(
+        refs["g"][own, :], refs["wp"][...], NT, preferred_element_type=F32
+    )
+    for u in range(count):
+        for tile in range(tiles):
+            gpad[u, tile, MARGIN : MARGIN + length, :] = (
+                grad_swish[u * length : (u + 1) * length, tile * LANES : (tile + 1) * LANES]
+                * slope[u, tile]
+            )
+
+    def fold(value):
+        return jnp.sum(value.reshape(length // 8, 8, LANES), axis=0)
+
+    @pl.loop(0, count)
+    def _(u):
+        at = pl.ds(pl.multiple_of(u * length, length), length)
+        out = pl.ds(pl.multiple_of(base + u * length, length), length)
+        live = positions < meta[source, u]
+        for tile in range(tiles):
+            lanes = pl.ds(tile * LANES, LANES)
+            grad_conv = gpad[u, tile, MARGIN : MARGIN + length, :]
+            grad_glu = jnp.zeros((length, LANES), F32)
+            for t in range(taps):
+                small[tile, t] += fold(
+                    pad[u, tile, pl.ds(MARGIN - first + t, length), :] * grad_conv
+                )
+                grad_glu += (
+                    taps_ref[t : t + 1, lanes] * gpad[u, tile, pl.ds(MARGIN + first - t, length), :]
+                )
+            small[tile, taps] += fold(grad_conv)
+            grad_glu = jnp.where(live, grad_glu, 0.0)
+            gate = ab[tiles + tile, at, :]
+            through = grad_glu * gate
+            ge[out, lanes] = through.astype(BF16)
+            ge[out, pl.ds(channels + tile * LANES, LANES)] = (
+                through * ab[tile, at, :] * (1.0 - gate)
+            ).astype(BF16)
+
+    span = 512
+    for start in range(0, width, span):
+        cols = pl.ds(start, span)
+        refs["gn"][own, cols] = lax.dot_general(
+            ge[own, :], we[cols, :], NT, preferred_element_type=F32
+        ).astype(BF16)
+
+
+def clear_margins(*padded):
+    for ref in padded:
+        count, tiles, height, lanes = ref.shape
+        zeros = jnp.zeros((MARGIN, lanes), F32)
+        for u in range(count):
+            for tile in range(tiles):
+                ref[u, tile, :MARGIN, :] = zeros
+                ref[u, tile, height - MARGIN :, :] = zeros
+
+
+def source_scratch(count, length, channels):
+    tiles = channels // LANES
+    padded = pltpu.VMEM((count, tiles, length + 2 * MARGIN, LANES), F32)
+    return [
+        pltpu.VMEM((2 * tiles, count * length, LANES), F32),
+        padded,
+        padded,
+        pltpu.VMEM((count, tiles, length, LANES), F32),
+    ]
+
+
+def weight_copies(blocks, owned, part, we, wp, small, sems):
+    me = lax.axis_index("shard")
+    width, wide = we.shape
+    halves = width // wide
+    move = pltpu.make_async_copy
+    first, second = [], []
+    for b, block in enumerate(blocks):
+        offset = 2 * (b % (len(blocks) // 2)) + b // (len(blocks) // 2)
+        owner = me ^ offset
+        first.append(
+            move(block.at[pl.ds(owned + halves * part, 16)], small.at[owner], sems.at[b, 0])
+        )
+        rows = pl.ds(pl.multiple_of(owner * owned, owned), owned)
+        first.append(move(block.at[pl.ds(0, owned)], we.at[rows], sems.at[b, 1]))
+        rows = pl.ds(pl.multiple_of(owner * part, part), part)
+        for h in range(halves):
+            second.append(
+                move(
+                    block.at[pl.ds(owned + h * part, part)],
+                    wp.at[rows, pl.ds(h * wide, wide)],
+                    sems.at[b, 2 + h],
+                )
+            )
+    return first, second
+
+
+def fill_tables(small, owned, part, taps_ref, gain_ref):
+    rows = [small[j].astype(F32) for j in range(small.shape[0])]
+    taps_ref[:16] = jnp.concatenate([r[:, :part] for r in rows], axis=1)
+    taps_ref[16:] = jnp.concatenate([r[:, LANES : LANES + part] for r in rows], axis=1)
+    gain_ref[...] = jnp.concatenate([r[:1, 2 * LANES : 2 * LANES + owned] for r in rows], axis=1)
+
+
+def weight_scratch(owners, owned, width, wide, taps):
+    return [
+        pltpu.VMEM((width, wide), BF16),
+        pltpu.VMEM((wide // 2, width), BF16),
+        pltpu.VMEM((owners, 16, wide), BF16),
+        pltpu.VMEM((taps + 1, wide // 2), F32),
+        pltpu.SemaphoreType.DMA((owners, 2 + width // wide)),
+    ]
+
+
+def near_kernel(dims, n, owned, meta, *refs):
+    count, length, taps = dims
+    rows = count * length
+    x_hbm, g_hbm, refs = refs[:n], refs[n : 2 * n], refs[2 * n :]
+    outs = refs[-24 - n - count : -19]
+    blocks = refs[: -24 - n - count]
+    normed_hbm, sw_hbm, ge_hbm = outs[:3]
+    gn_hbm, small, gain_ref, pieces = outs[3 : 3 + n], outs[3 + n], outs[4 + n], outs[5 + n :]
+    x, normed, g, sw, ge, gn, ab, pad, gpad, slope = refs[-19:-9]
+    we, wp, shares, taps_ref, weight_sems = refs[-9:-4]
+    in_sems, out_sems, route_sems, _ = refs[-4:]
+    part = owned * (we.shape[1] // 2) // we.shape[0]
+    move = pltpu.make_async_copy
+
+    def place(s):
+        return pl.ds(s * rows, rows)
+
+    incoming = {}
+    for s in range(n):
+        incoming["x", s] = move(x_hbm[s].at[pl.ds(0, rows)], x.at[place(s)], in_sems.at[s, 0])
+        incoming["g", s] = move(
+            g_hbm[s].at[pl.ds(g_hbm[s].shape[0] - rows, rows)], g.at[place(s)], in_sems.at[s, 1]
+        )
+    weights = weight_copies(blocks, owned, part, we, wp, shares, weight_sems)
+    incoming["x", 0].start()
+    for copy in weights[0]:
+        copy.start()
+    incoming["g", 0].start()
+    for copy in weights[1]:
+        copy.start()
+    for s in range(1, n):
+        incoming["x", s].start()
+        incoming["g", s].start()
+    clear_margins(pad, gpad)
+    small[...] = jnp.zeros_like(small)
+    views = dict(
+        x=x, normed=normed, g=g, we=we, wp=wp, sw=sw, ge=ge, gn=gn, ab=ab, pad=pad, gpad=gpad,
+        slope=slope, taps=taps_ref, gain=gain_ref, small=small, pieces=pieces, route_sems=route_sems,
+    )
+
+    @pl.loop(0, n)
+    def _(s):
+        def ready(what):
+            if what in ("we", "wp"):
+                @pl.when(s == 0)
+                def _():
+                    for copy in weights[what == "wp"]:
+                        copy.wait()
+                    if what == "we":
+                        fill_tables(shares, owned, part, taps_ref, gain_ref)
+            else:
+                for at in range(n):
+                    @pl.when(s == at)
+                    def _():
+                        incoming[what, at].wait()
+
+        base = pl.multiple_of(s * rows, rows)
+        one_source(dims, views, meta, s, base, ready)
+        own = pl.ds(base, rows)
+        for i, (source, target) in enumerate(((normed, normed_hbm), (sw, sw_hbm), (ge, ge_hbm))):
+            move(source.at[own], target.at[own], out_sems.at[s, i]).start()
+        for at in range(n):
+            @pl.when(s == at)
+            def _():
+                move(gn.at[place(at)], gn_hbm[at], out_sems.at[at, 3]).start()
+
+    for s in range(n):
+        for i, (source, target) in enumerate(((normed, normed_hbm), (sw, sw_hbm), (ge, ge_hbm))):
+            move(source.at[place(s)], target.at[place(s)], out_sems.at[s, i]).wait()
+        move(gn.at[place(s)], gn_hbm[s], out_sems.at[s, 3]).wait()
+        for copy in route(dims, views, meta, s, s * rows):
+            copy.wait()
+
+
+def near_call(ints, xs, gs, blocks, owned, dims):
+    count, length, taps = dims
+    n = len(xs)
+    rows, width = count * length, xs[0].shape[1]
+    wide = blocks[0].shape[1]
+    channels = wide // 2
+    owners = len(blocks)
+    anywhere = pl.BlockSpec(memory_space=pl.ANY)
+    return pl.pallas_call(
+        functools.partial(near_kernel, dims, n, owned),
+        out_shape=(
+            jax.ShapeDtypeStruct((n * rows, width), BF16),
+            jax.ShapeDtypeStruct((n * rows, channels), BF16),
+            jax.ShapeDtypeStruct((n * rows, wide), BF16),
+        )
+        + (jax.ShapeDtypeStruct((rows, width), BF16),) * n
+        + (
+            jax.ShapeDtypeStruct((channels // LANES, taps + 1, 8, LANES), F32),
+            jax.ShapeDtypeStruct((1, width), F32),
+        )
+        + (jax.ShapeDtypeStruct((rows, channels), BF16),) * count,
+        in_specs=[in_smem()] + [anywhere] * (2 * n + owners),
+        out_specs=(anywhere,) * (3 + n) + (in_vmem(), in_vmem()) + (anywhere,) * count,
+        scratch_shapes=[
+            pltpu.VMEM((n * rows, width), BF16),
+            pltpu.VMEM((n * rows, width), BF16),
+            pltpu.VMEM((n * rows, width), BF16),
+            pltpu.VMEM((n * rows, channels), BF16),
+            pltpu.VMEM((n * rows, wide), BF16),
+            pltpu.VMEM((n * rows, width), BF16),
+        ]
+        + source_scratch(count, length, channels)
+        + weight_scratch(owners, owned, width, wide, taps)
+        + [
+            pltpu.SemaphoreType.DMA((n, 2)),
+            pltpu.SemaphoreType.DMA((n, 4)),
+            pltpu.SemaphoreType.DMA((n, count)),
+            pltpu.SemaphoreType.DMA,
+        ],
+        compiler_params=vmem_params(VMEM_CHUNK),
+        cost_estimate=LIGHT,
+        name="near_sources",
+    )(ints, *xs, *gs, *blocks)
+
+
+def far_kernel(dims, n, owned, meta, *refs):
+    count, length, taps = dims
+    rows = count * length
+    core = lax.axis_index("shard") % 2
+    x_hbm, normed_hbm, sw_hbm, ge_hbm = refs[:4]
+    g_hbm, near_small = refs[4 : 5 + n], refs[5 + n]
+    blocks, outs, refs = refs[6 + n : -25 - 2 * count], refs[-25 - count : -22], refs[-22:]
+    gn_hbm, keep_hbm, give_hbm, pieces = outs[0], outs[1], outs[2], outs[3:]
+    x, normed, g, sw, ge, gn, ab, pad, gpad, slope = refs[:10]
+    we, wp, shares, taps_ref, weight_sems = refs[10:15]
+    gain_ref, small, block, in_sems, out_sems, route_sems, _ = refs[15:]
+    width, wide = we.shape
+    channels = wide // 2
+    tiles = channels // LANES
+    chips = width // owned // 2
+    halves = width // wide
+    part = channels // (2 * chips)
+    move = pltpu.make_async_copy
+    base = n * rows
+    near, last = pl.ds(0, base), pl.ds(base, rows)
+    tail = [pl.ds(ref.shape[0] - rows, rows) for ref in g_hbm]
+    incoming = dict(
+        x=[move(x_hbm.at[pl.ds(0, rows)], x.at[last], in_sems.at[0])],
+        g=[move(g_hbm[n].at[tail[n]], g.at[last], in_sems.at[2])],
+    )
+    incoming["we"], incoming["wp"] = weight_copies(
+        blocks, owned, part, we, wp, shares, weight_sems
+    )
+    later = [
+        move(normed_hbm, normed.at[near], in_sems.at[4]),
+        move(sw_hbm, sw.at[near], in_sems.at[5]),
+        move(ge_hbm, ge.at[near], in_sems.at[6]),
+    ]
+    later += [
+        move(g_hbm[s].at[tail[s]], g.at[pl.ds(s * rows, rows)], in_sems.at[7 + s])
+        for s in range(n)
+    ]
+    for copy in incoming["x"] + incoming["we"] + incoming["g"] + incoming["wp"] + later:
+        copy.start()
+
+    def ready(what):
+        for copy in incoming[what]:
+            copy.wait()
+        if what == "we":
+            fill_tables(shares, owned, part, taps_ref, gain_ref)
+
+    clear_margins(pad, gpad)
+    small[...] = near_small[...]
+    views = dict(
+        x=x, normed=normed, g=g, we=we, wp=wp, sw=sw, ge=ge, gn=gn, ab=ab, pad=pad, gpad=gpad,
+        slope=slope, taps=taps_ref, gain=gain_ref, small=small, pieces=pieces, route_sems=route_sems,
+    )
+    one_source(dims, views, meta, n, base, ready)
+    gn_out = move(gn.at[last], gn_hbm, out_sems.at[2])
+    gn_out.start()
+    routed = route(dims, views, meta, n, base)
+    for copy in later:
+        copy.wait()
+
+    sums = jnp.sum(small[...], axis=2)
+    sums = jnp.concatenate([sums[tile] for tile in range(tiles)], axis=1)
+    span = 2 * owned
+    bottom = owned + halves * part
+    for chip in range(chips):
+        total = lax.dot_general(
+            normed[:, chip * span : (chip + 1) * span], ge[...], TN, preferred_element_type=F32
+        ).astype(BF16)
+        for which in range(2):
+            block[which, chip, :owned] = total[which * owned : (which + 1) * owned]
+    for h in range(halves):
+        total = lax.dot_general(
+            sw[...], g[:, h * wide : (h + 1) * wide], TN, preferred_element_type=F32
+        ).astype(BF16)
+        for owner in range(2 * chips):
+            block[owner % 2, owner // 2, owned + h * part : owned + (h + 1) * part] = total[
+                owner * part : (owner + 1) * part
+            ]
+    fill = jnp.zeros((16, LANES - part), F32)
+    blank = jnp.zeros((16, wide - 2 * LANES), F32)
+    for owner in range(2 * chips):
+        table = sums[:, owner * part : (owner + 1) * part]
+        line = jnp.concatenate([table[:16], fill, table[16:], fill, blank], axis=1)
+        block[owner % 2, owner // 2, bottom:] = line.astype(BF16)
+    outward = [
+        move(block.at[1 - core], give_hbm, out_sems.at[0]),
+        move(block.at[core], keep_hbm, out_sems.at[1]),
+    ]
+    for copy in outward:
+        copy.start()
+    for copy in outward + routed + [gn_out]:
+        copy.wait()
+
+
+def far_call(ints, x, near, gs, blocks, before, owned, dims):
+    count, length, taps = dims
+    n = len(gs) - 1
+    rows = count * length
+    width, wide = x.shape[1], blocks[0].shape[1]
+    channels = wide // 2
+    tiles = channels // LANES
+    owners = len(blocks)
+    chips = owners // 2
+    halves = width // wide
+    height = owned + halves * (channels // owners) + 16
+    anywhere = pl.BlockSpec(memory_space=pl.ANY)
+    normed, sw, ge, small = near
+    every = (n + 1) * rows
+    return pl.pallas_call(
+        functools.partial(far_kernel, dims, n, owned),
+        out_shape=(jax.ShapeDtypeStruct((rows, width), BF16),)
+        + (jax.ShapeDtypeStruct((chips, height, wide), BF16),) * 2
+        + (jax.ShapeDtypeStruct(before[0].shape, BF16),) * count,
+        in_specs=[in_smem()] + [anywhere] * (5 + n) + [in_vmem()] + [anywhere] * (owners + count),
+        out_specs=(anywhere,) * (3 + count),
+        input_output_aliases={7 + n + owners + m: 3 + m for m in range(count)},
+        scratch_shapes=[
+            pltpu.VMEM((every, width), BF16),
+            pltpu.VMEM((every, width), BF16),
+            pltpu.VMEM((every, width), BF16),
+            pltpu.VMEM((every, channels), BF16),
+            pltpu.VMEM((every, wide), BF16),
+            pltpu.VMEM((every, width), BF16),
+        ]
+        + source_scratch(count, length, channels)
+        + weight_scratch(owners, owned, width, wide, taps)
+        + [
+            pltpu.VMEM((1, width), F32),
+            pltpu.VMEM((tiles, taps + 1, 8, LANES), F32),
+            pltpu.VMEM((2, chips, height, wide), BF16),
+            pltpu.SemaphoreType.DMA((7 + n,)),
+            pltpu.SemaphoreType.DMA((3,)),
+            pltpu.SemaphoreType.DMA((n + 1, count)),
+            pltpu.SemaphoreType.DMA,
+        ],
+        compiler_params=vmem_params(VMEM_CHUNK),
+        cost_estimate=LIGHT,
+        name="far_source",
+    )(ints, x, normed, sw, ge, *gs, small, *blocks, *before)
+
+
+def vmem_params(mib):
+    return pltpu.CompilerParams(vmem_limit_bytes=mib * 1024 * 1024)
+
+
+def in_vmem():
+    return pl.BlockSpec(memory_space=pltpu.VMEM)
+
+
+def in_smem():
+    return pl.BlockSpec(memory_space=pltpu.SMEM)
+
+
+def owned_column(channel, index, owned, part):
+    return (channel // part) * owned + index * part + channel % part
+
+
+def pack_kernel(expand_hbm, project_hbm, kernel_ref, bias_ref, gain_ref, x_hbm, g_hbm, *refs):
+    pack_ref, both_hbm, copies_hbm, both, expand_ref, whole, sems = refs
+    rows_in = x_hbm.shape[0]
+    inward = [
+        pltpu.make_async_copy(x_hbm, both.at[pl.ds(0, rows_in)], sems.at[2]),
+        pltpu.make_async_copy(g_hbm, both.at[pl.ds(rows_in, rows_in)], sems.at[3]),
+    ]
+    owned, width = project_hbm.shape
+    wide = pack_ref.shape[1]
+    channels = wide // 2
+    part = owned * channels // width
+    index = lax.axis_index("dp")
+    rows = pl.ds(pl.multiple_of(index * part, part), part)
+    chips = copies_hbm.shape[0]
+    copies = [
+        pltpu.make_async_copy(expand_hbm, expand_ref, sems.at[0]),
+        pltpu.make_async_copy(project_hbm, whole, sems.at[1]),
+    ]
+    for copy in inward + copies:
+        copy.start()
+    row = lax.broadcasted_iota(jnp.int32, (width, channels), 0)
+    col = lax.broadcasted_iota(jnp.int32, (1, channels), 1)
+    pick = jnp.where(row == owned_column(col, index, owned, part), 1.0, 0.0).astype(BF16)
+    mine = lax.broadcasted_iota(jnp.int32, (owned, LANES), 1) + index * part
+    mine = jnp.where(lax.broadcasted_iota(jnp.int32, (owned, LANES), 0) == mine, 1.0, 0.0)
+    mine = mine.astype(BF16)
+    table = jnp.concatenate(
+        [
+            jnp.dot(kernel_ref[...], mine, preferred_element_type=F32),
+            jnp.dot(bias_ref[...].reshape(1, owned), mine, preferred_element_type=F32),
+        ],
+        axis=0,
+    )
+    base = owned + width // wide * part
+    gain = jnp.broadcast_to(gain_ref[...].reshape(1, owned).astype(F32), (16, owned))
+    blank = jnp.zeros((16, wide - 2 * LANES - owned), F32)
+    pack_ref[base:, :] = jnp.concatenate(
+        [table[:16], table[16:], gain, blank], axis=1
+    ).astype(BF16)
+    for copy in inward:
+        copy.wait()
+    outward = [pltpu.make_async_copy(both, both_hbm, sems.at[4])]
+    outward[0].start()
+    for copy in copies:
+        copy.wait()
+    for i in range(chips):
+        outward.append(pltpu.make_async_copy(whole, copies_hbm.at[i], sems.at[5 + i]))
+        outward[-1].start()
+    block = whole[rows, :]
+    for h in range(2):
+        pack_ref[:owned, h * channels : (h + 1) * channels] = jnp.dot(
+            expand_ref[:, h * width : (h + 1) * width], pick, preferred_element_type=F32
+        ).astype(BF16)
+    for h in range(width // wide):
+        pack_ref[owned + h * part : owned + (h + 1) * part, :] = block[:, h * wide : (h + 1) * wide]
+    for copy in outward:
+        copy.wait()
+
+
+def pack_call(expand_weight, project_weight, kernel, bias, gain, x, g, part, wide):
+    owned, width = project_weight.shape
+    height = owned + width // wide * part + 16
+    chips = width // owned // 2
+    rows = x.shape[0]
+    anywhere = pl.BlockSpec(memory_space=pl.ANY)
+    return pl.pallas_call(
+        pack_kernel,
+        out_shape=(
+            jax.ShapeDtypeStruct((height, wide), BF16),
+            jax.ShapeDtypeStruct((2 * rows, width), BF16),
+            jax.ShapeDtypeStruct((chips, owned, width), BF16),
+        ),
+        in_specs=[anywhere] * 2 + [in_vmem()] * 3 + [anywhere] * 2,
+        out_specs=(in_vmem(), anywhere, anywhere),
+        scratch_shapes=[
+            pltpu.VMEM((2 * rows, width), BF16),
+            pltpu.VMEM(expand_weight.shape, BF16),
+            pltpu.VMEM((owned, width), BF16),
+            pltpu.SemaphoreType.DMA((5 + chips,)),
+        ],
+        compiler_params=vmem_params(VMEM_PACK),
+        cost_estimate=LIGHT,
+        name="pack",
+    )(expand_weight, project_weight, kernel.T, bias, gain, x, g)
+
+
+def encode_kernel(dims, meta, *refs):
+    n, length, owned = dims
+    frames = refs[:n]
+    pieces, blocks, refs = refs[n : 2 * n], refs[2 * n : 2 * n + 2], refs[2 * n + 2 :]
+    out_ref, cat, weight, residual, sems = refs
+    shard = lax.axis_index("shard")
+    channels = pieces[0].shape[1]
+    part = owned // n
+    me = lax.axis_index("dp")
+
+    def rows(at, size):
+        return pl.ds(pl.multiple_of(at * size, size), size)
+
+    moves = []
+    for which, block in enumerate(blocks):
+        for chip in range(block.shape[0]):
+            owner = 2 * chip + ((shard % 2) ^ which)
+            for i in range(n):
+                start = pl.multiple_of(i * channels + owner * part, part)
+                moves.append((block.at[chip, pl.ds(i * part, part)], weight.at[pl.ds(start, part)]))
+    for k in range(n):
+        moves.append(
+            (
+                frames[k].at[rows(meta[me ^ k, n + me], length)],
+                residual.at[rows(me ^ k, length)],
+            )
+        )
+    for m in range(n):
+        lanes = pl.ds(pl.multiple_of((me ^ m) * channels, channels), channels)
+        for k in range(n):
+            source = pieces[m].at[pl.ds(k * length, length)]
+            moves.append((source, cat.at[rows(me ^ m ^ k, length), lanes]))
+    copies = [
+        pltpu.make_async_copy(source, target, sems.at[i])
+        for i, (source, target) in enumerate(moves)
+    ]
+    for copy in copies:
+        copy.start()
+    for copy in copies:
+        copy.wait()
+    span = 512
+    for start in range(0, cat.shape[1], span):
+        cols = slice(start, start + span)
+        term = jnp.dot(cat[...], weight[:, cols], preferred_element_type=F32)
+        out_ref[:, cols] = (residual[:, cols].astype(F32) + term).astype(BF16)
+
+
+def encode_call(ints, pieces, frames, blocks, length):
+    n = len(frames)
+    owned, width = blocks[0].shape[1:]
+    anywhere = pl.BlockSpec(memory_space=pl.ANY)
+    return pl.pallas_call(
+        functools.partial(encode_kernel, (n, length, owned)),
+        out_shape=jax.ShapeDtypeStruct((n * length, width), BF16),
+        in_specs=[in_smem()] + [anywhere] * (2 * n + len(blocks)),
+        out_specs=in_vmem(),
+        scratch_shapes=[
+            pltpu.VMEM((n * length, width), BF16),
+            pltpu.VMEM((width, width), BF16),
+            pltpu.VMEM((n * length, width), BF16),
+            pltpu.SemaphoreType.DMA((width // owned * n + n + n * n,)),
+        ],
+        compiler_params=vmem_params(VMEM_ENCODE),
+        cost_estimate=LIGHT,
+        name="encode",
+    )(ints, *frames, *pieces, *blocks)
+
+
+def frame_grad_kernel(n, x_ref, g_ref, gain_ref, *refs):
+    out_ref = refs[n]
+    x = x_ref[...].astype(F32)
+    centred = x - jnp.mean(x, axis=1, keepdims=True)
+    inverse = lax.rsqrt(jnp.mean(centred * centred, axis=1, keepdims=True) + EPS)
+    standard = centred * inverse
+    grad = sum(ref[...].astype(F32) for ref in refs[:n]) * gain_ref[...]
+    grad_in = inverse * (
+        grad
+        - jnp.mean(grad, axis=1, keepdims=True)
+        - standard * jnp.mean(grad * standard, axis=1, keepdims=True)
+    )
+    out_ref[...] = (g_ref[...].astype(F32) + grad_in).astype(BF16)
+
+
+def frame_grad_call(x, g, gain, returned):
+    count, length, width = x.shape
+    rows = count * length
+    step = 64
+    block = pl.BlockSpec((step, width), lambda s: (s, 0))
+    out = pl.pallas_call(
+        functools.partial(frame_grad_kernel, len(returned)),
+        out_shape=jax.ShapeDtypeStruct((rows, width), BF16),
+        grid=(rows // step,),
+        in_specs=[block, block, pl.BlockSpec((1, width), lambda s: (0, 0))]
+        + [block] * len(returned),
+        out_specs=block,
+        compiler_params=vmem_params(VMEM_FRAME),
+        cost_estimate=LIGHT,
+        name="frame_grad",
+    )(x.reshape(rows, width), g.reshape(rows, width), gain, *returned)
+    return out.reshape(count, length, width)
+
+
+def unpack_kernel(dims, *refs):
+    n, owned, part = dims
+    blocks, refs = (refs[:n], refs[n : 2 * n]), refs[2 * n :]
+    weight_ref, gain_ref, expand_ref, project_ref, gain_out, cat, grads, project, sems = refs
+    channels = blocks[0][0].shape[1]
+    wide = 2 * channels
+    width = cat.shape[2]
+    halves = width // wide
+    me = lax.axis_index("dp")
+    for k in range(n):
+        lanes = pl.ds(pl.multiple_of((me ^ k) * channels, channels), channels)
+        rows = pl.ds(pl.multiple_of((me ^ k) * part, part), part)
+        for half in range(2):
+            block = blocks[half][k]
+            cat[half, :, lanes] = block[:owned]
+            for h in range(halves):
+                start = h * wide + half * channels
+                project[rows, start : start + channels] = block[
+                    owned + h * part : owned + (h + 1) * part
+                ].astype(F32)
+    copies = [pltpu.make_async_copy(project, project_ref, sems.at[2, 0])]
+    copies[0].start()
+    along = jnp.zeros((owned, 1), F32)
+    span = 512
+    for start in range(0, width, span):
+        row = lax.broadcasted_iota(jnp.int32, (width, span), 0)
+        col = lax.broadcasted_iota(jnp.int32, (1, span), 1) + start
+        place = col % owned // part * channels + col // owned * part + col % part
+        spread = jnp.where(row == place, 1.0, 0.0).astype(BF16)
+        for half in range(2):
+            cols = pl.ds(half * width + start, span)
+            grad = jnp.dot(cat[half], spread, preferred_element_type=F32)
+            grads[:, cols] = grad
+            copy = pltpu.make_async_copy(
+                grads.at[:, cols], expand_ref.at[:, cols], sems.at[half, start // span]
+            )
+            copy.start()
+            copies.append(copy)
+            along += jnp.sum(grad * weight_ref[:, cols].astype(F32), axis=1, keepdims=True)
+    row = jnp.transpose(jnp.broadcast_to(along, (owned, LANES)))[:1]
+    gain_out[...] = row / gain_ref[...].astype(F32)
+    for copy in copies:
+        copy.wait()
+
+
+def unpack_call(low, high, weight, gain, owned, part, width):
+    anywhere = pl.BlockSpec(memory_space=pl.ANY)
+    return pl.pallas_call(
+        functools.partial(unpack_kernel, (len(low), owned, part)),
+        out_shape=(
+            jax.ShapeDtypeStruct((owned, 2 * width), F32),
+            jax.ShapeDtypeStruct((owned, width), F32),
+            jax.ShapeDtypeStruct((1, owned), F32),
+        ),
+        in_specs=[in_vmem()] * (2 * len(low) + 2),
+        out_specs=(anywhere, anywhere, in_vmem()),
+        scratch_shapes=[
+            pltpu.VMEM((2, owned, width), BF16),
+            pltpu.VMEM((owned, 2 * width), F32),
+            pltpu.VMEM((owned, width), F32),
+            pltpu.SemaphoreType.DMA((3, width // 512)),
+        ],
+        compiler_params=vmem_params(VMEM_UNPACK),
+        cost_estimate=LIGHT,
+        name="unpack",
+    )(*low, *high, weight, gain)
+
+
+def tie(value, *after):
+    return lax.optimization_barrier((value,) + after)[0]
+
+
+def gather_owners(x):
+    blocks = [x] + [swap(x, "shard", 8, 2 * m) for m in (1, 2, 3)]
+    return blocks + [swap(block, "shard", 8, 1) for block in blocks]
+
+
+def add_cores_kernel(keep_hbm, got_hbm, out_hbm, keep, got, sems):
+    n = keep.shape[0]
+    move = pltpu.make_async_copy
+    inward = [
+        (move(keep_hbm.at[i], keep.at[i], sems.at[i, 0]), move(got_hbm.at[i], got.at[i], sems.at[i, 1]))
+        for i in range(n)
+    ]
+    outward = [move(keep.at[i], out_hbm.at[i], sems.at[i, 2]) for i in range(n)]
+    for i in range(n):
+        for copy in inward[i]:
+            copy.start()
+    for i in range(n):
+        for copy in inward[i]:
+            copy.wait()
+        keep[i] = (keep[i].astype(F32) + got[i].astype(F32)).astype(BF16)
+        outward[i].start()
+    for copy in outward:
+        copy.wait()
+
+
+def add_cores(keep, got):
+    anywhere = pl.BlockSpec(memory_space=pl.ANY)
+    return pl.pallas_call(
+        add_cores_kernel,
+        out_shape=jax.ShapeDtypeStruct(keep.shape, BF16),
+        in_specs=[anywhere] * 2,
+        out_specs=anywhere,
+        scratch_shapes=[
+            pltpu.VMEM(keep.shape, BF16),
+            pltpu.VMEM(keep.shape, BF16),
+            pltpu.SemaphoreType.DMA((keep.shape[0], 3)),
+        ],
+        compiler_params=vmem_params(VMEM_HOP),
+        cost_estimate=LIGHT,
+        name="add_cores",
+    )(keep, got)
+
+
+def add_chips_kernel(come_ref, *refs):
+    total = jnp.sum(come_ref[...].astype(F32), axis=0).astype(BF16)
+    channels = refs[0].shape[1]
+    for half, ref in enumerate(refs):
+        ref[...] = total[:, half * channels : (half + 1) * channels]
+
+
+def add_chips(come):
+    rows, wide = come.shape[1:]
+    return pl.pallas_call(
+        add_chips_kernel,
+        out_shape=(jax.ShapeDtypeStruct((rows, wide // 2), BF16),) * 2,
+        in_specs=[in_vmem()],
+        out_specs=(in_vmem(),) * 2,
+        compiler_params=vmem_params(VMEM_HOP),
+        cost_estimate=LIGHT,
+        name="add_chips",
+    )(come)
+
+
+def fast_body(
+    frames,
+    cotangent,
+    lengths,
+    send_order,
+    norm_gain,
+    conv_bias,
+    kernel,
+    expand_weight,
+    project_weight,
+):
+    n_dp, n_shard = lax.axis_size("dp"), lax.axis_size("shard")
+    count, length, width = frames.shape
+    owned, taps = kernel.shape
+    part = owned // n_dp
+    wide = 2 * n_shard * part
+    rows = count * length
+    dims = (count, length, taps)
+    ints = jnp.concatenate([lengths, send_order])
+    ints = lax.all_to_all(jnp.broadcast_to(ints, (n_dp, 2 * count)), "dp", 0, 0, tiled=True)
+    x_own = frames.reshape(rows, width)
+    g_own = cotangent.reshape(rows, width)
+    pack, both, project = pack_call(
+        expand_weight, project_weight, kernel, conv_bias, norm_gain, x_own, g_own, part, wide
+    )
+    pack, both, ints = lax.optimization_barrier((pack, both, ints))
+    both_x = swap(both, "dp", 4, 1)
+    both_y = swap(both, "dp", 4, 2)
+    packs = [pack] + [swap(pack, "shard", 8, 2 * m) for m in (1, 2, 3)]
+    *packs, both_x, both_y = lax.optimization_barrier((*packs, both_x, both_y))
+    packs += [swap(block, "shard", 8, 1) for block in packs]
+    x_all = [x_own, both_x, both_y, swap(both_x[:rows], "dp", 4, 2)]
+    g_all = [g_own, both_x, both_y, swap(both_y[rows:], "dp", 4, 1)]
+    line = [[2 * c + i for c in range(n_shard // 2)] for i in range(2)]
+    project = tie(project, *packs[1:4])
+    project = lax.all_to_all(project, "shard", 0, 0, axis_index_groups=line, tiled=True)
+
+    near = near_call(ints, x_all[:3], g_all[:3], packs, owned, dims)
+    returned = [near[3]] + [swap(near[3 + k], "dp", n_dp, k) for k in (1, 2)]
+    gain = near[7]
+    far = far_call(ints, x_all[3], near[:3] + near[6:7], g_all, packs, near[8:], owned, dims)
+
+    keep, give = far[1:3]
+    give, keep = lax.optimization_barrier((give, keep, project, *returned[1:3]))[:2]
+    sums = add_cores(keep, swap(give, "shard", 8, 1))
+    come = lax.all_to_all(sums, "shard", 0, 0, axis_index_groups=line, tiled=True)
+    last, *pieces = lax.optimization_barrier((far[0], *far[3:], sums))[:-1]
+    returned.append(swap(last, "dp", n_dp, 3))
+    pieces = [pieces[0]] + [swap(pieces[m], "dp", n_dp, m) for m in (1, 2, 3)]
+    project = [project, swap(project, "shard", 8, 1)]
+    encoded = encode_call(ints, pieces, x_all, project, length)
+    frame_grad = frame_grad_call(frames, tie(cotangent, sums), gain, returned)
+
+    gathered = [
+        [half] + [swap(half, "dp", 4, k) for k in (1, 2, 3)]
+        for half in add_chips(tie(come, encoded, frame_grad))
+    ]
+    base = owned + width // wide * part
+    table = jnp.stack([a[base:] for a in gathered[0]])
+    table = jnp.take(table, lax.axis_index("dp") ^ jnp.arange(n_dp), axis=0).astype(F32)
+    table = jnp.concatenate([table[:, :, :part], table[:, :, LANES : LANES + part]], axis=1)
+    table = table.transpose(0, 2, 1).reshape(owned, taps + 1)
+    expand_grad, project_grad, along = unpack_call(
+        *gathered, expand_weight, norm_gain[None], owned, part, width
+    )
+    return (
+        encoded.reshape(frames.shape),
+        frame_grad,
+        along.reshape(owned),
+        table[:, taps],
+        table[:, :taps],
+        expand_grad,
+        project_grad,
+    )
 
 
 def depthwise(signal, taps_table):
@@ -119,7 +987,7 @@
     return lax.psum_scatter(x, "shard", scatter_dimension=0, tiled=False).astype(F32)
 
 
-def body(
+def generic_body(
     frames,
     cotangent,
     lengths,
@@ -295,6 +1163,11 @@
     bias_grad = small_grad[:, part * taps : part * (taps + 1)].reshape(owned)
     gain_grad = jnp.sum(small_grad[:, part * (taps + 1) : part * (taps + 1) + owned], axis=0)
     return encoded, frame_grad, gain_grad, bias_grad, kernel_grad, expand_grad, project_grad
+
+
+def body(*arrays):
+    fast = lax.axis_size("dp") == 4 and lax.axis_size("shard") == 8
+    return (fast_body if fast else generic_body)(*arrays)
 
 
 def solution(mesh):

time: 479 us -> 205 us (0.43); the launches traced: 471 us -> 202 us
  local copies, waits for them, and re-layouts: 195 us -> 12.3 us
  other arithmetic: 96.2 us -> 0.87 us
  Pallas kernels: 0 us -> 66.6 us
  matrix products: 38.2 us -> 0 us
  waiting for transfers between devices: 99.7 us -> 86.6 us
  starting transfers between devices: 39.8 us -> 34.8 us
    another operation x132 -> x4, local copies, waits for them, and re-layouts: 97.3 us -> 0.75 us  [fast_body(): table = jnp.stack([a[base:] for a in gathered[0]])]
    pallas_call x0 -> x8, Pallas kernels: none -> 66.6 us  [the longest x1 24.9 us: near_call(): pl.pallas_call(functools.partial(near_kernel, dims, n, owned), out_shape=...]
    ppermute x9 -> x0, waiting for transfers between devices: 64.7 us -> none  [the longest x3 35.7 us: reduce_shard(): lax.ppermute(piece, 'shard', [(p, (p + 2 * k) % 8) for p in range(8)])]
    ppermute x24 -> x25, waiting for transfers between devices: 35 us -> 86.6 us  [swap(): return lax.ppermute(x, axis, [(p, p ^ k) for p in range(size)])]
    dot_general x24 -> x0, matrix products: 38.2 us -> none  [the longest x4 11.7 us: body(): lax.dot_general(a, b, (((0,), (0,)), ((), ())), preferred_element_type=F32)]
    convert_element_type x24 -> x1, other arithmetic: 25.2 us -> 0.08 us  [fast_body(): jnp.take(table, lax.axis_index('dp') ^ jnp.arange(n_dp), axis=0).astype(F32)]
    slice x25 -> x4, local copies, waits for them, and re-layouts: 25.1 us -> 1.56 us  [the longest x1 0.93 us: fast_body(): x_all = [x_own, both_x, both_y, swap(both_x[:rows], 'dp', 4, 2)]]
    select_n x15 -> x1, other arithmetic: 21.9 us -> 0.01 us  [fast_body(): jnp.take(table, lax.axis_index('dp') ^ jnp.arange(n_dp), axis=0).astype(F32)]
  transfers between devices with their start and end apart: 33 -> 28, of which waited for: 14 -> 16; matrix products, arithmetic and copies ran while one was open for 59% -> 2% of each run, Pallas kernels for 0% -> 28%
where the time goes in v4:
time: 205 us; the launch traced here: 202 us
  waiting for transfers between devices  86.6 us (42%)
  Pallas kernels  66.6 us (32%)
  starting transfers between devices  34.8 us (17%)
  local copies, waits for them, and re-layouts  12.3 us (6%)
    ppermute x25, waiting for transfers between devices, swap(): return lax.ppermute(x, axis, [(p, p ^ k) for p in range(size)])  86.6 us
    pallas_call x1, Pallas kernels, near_call(): pl.pallas_call(functools.partial(near_kernel, dims, n, owned), out_shape=...  24.9 us
    ppermute x25, starting transfers between devices, swap(): return lax.ppermute(x, axis, [(p, p ^ k) for p in range(size)])  20.7 us
    pallas_call x1, Pallas kernels, far_call(): pl.pallas_call(functools.partial(far_kernel, dims, n, owned), out_shape=(...  16 us
    unnamed x48, local copies, waits for them, and re-layouts  8.73 us
    pallas_call x1, Pallas kernels, encode_call(): pl.pallas_call(functools.partial(encode_kernel, (n, length, owned)), out_...  6.21 us
    all_to_all x1, starting transfers between devices, fast_body(): lax.all_to_all(sums, 'shard', 0, 0, axis_index_groups=line, tiled=True)  5.86 us
    pallas_call x1, Pallas kernels, pack_call(): pl.pallas_call(pack_kernel, out_shape=(jax.ShapeDtypeStruct((height, wide...  4.88 us
  transfers between devices with their start and end apart: 28, of which 16 were waited for; matrix products, arithmetic and copies ran while one was open for 2% of the time, Pallas kernels for 28%

profile of v4, /device:TPU:8, one launch (start us, length us, event | category | flops | bytes accessed | tf_op | source)
XLA Modules:
  0.0 202.2 jit_solution(16696005700121443877)
XLA Ops:
  0.6 0.7 pad_add_fusion
  1.4 0.6 broadcast_in_dim.16
  2.0 3.7 %all-to-all-start = ((s32[4,1,8]{2,1,0:T(1,128)}), s32[4,1,8]{2,1,0:T(1,128)S(1)}, u32[]{:S(2)}, u32[]{:S(2)}) async-start(s32[4,1,8]{2,1,0:T(1,128)} %broadcast_in_dim.16), calls=%async_computation | async-start | bytes 4096 | tf_op jit(solution)/shard_map/all_to_all | solution.py:822
  5.7 4.9 %pack.1 = (bf16[304,768]{1,0:T(8,128)(2,1)}, bf16[512,1536]{1,0:T(8,128)(2,1)}, bf16[4,192,1536]{2,1,0:T(8,128)(2,1)}) custom-call(bf16[192,3072]{1,0:T(8,128)(2,1)} %refs_8_.1, bf16[192,1536]{1,0:T(8,128)(2,1)} %project_hbm.1, bf16[31,192]{1,0:T(8,128)(2,1)} %bitcast.38, bf16[192]{0:T(256)(128)(2,1)} %bias_ref.1, bf16[192]{0:T(256)(128)(2,1)} %gain_ref.1, ...), custom_call_target="tpu_custom_call" | custom-call | flops 1 | bytes 1 | tf_op jit(solution)/shard_map/pack/pallas_call | solution.py:545
  10.6 2.1 %collective-permute-start.3 = (bf16[512,1536]{1,0:T(8,128)(2,1)}, bf16[512,1536]{1,0:T(8,128)(2,1)S(1)}, u32[]{:S(2)}, u32[]{:S(2)}) collective-permute-start(bf16[512,1536]{1,0:T(8,128)(2,1)} %get-tuple-element.57), channel_id=1, source_target_pairs={{0,8},{8,0},{16,24},{24,16},{1,9},{9,1},{17,25},{25,17},{2,10},{10... | collective-permute-start | bytes 4718600 | tf_op jit(solution)/shard_map/ppermute | solution.py:941
  12.7 1.5 collective-permute-start.4
  14.1 0.4 collective-permute-start
  14.6 2.6 %collective-permute-start.1 = (bf16[304,768]{1,0:T(8,128)(2,1)}, bf16[304,768]{1,0:T(8,128)(2,1)S(1)}, u32[]{:S(2)}, u32[]{:S(2)}) collective-permute-start(bf16[304,768]{1,0:T(8,128)(2,1)} %get-tuple-element.60.refs_6_.refs_9_), channel_id=1, source_target_pairs={{0,4},{1,5},{2,6},{3,7},{4,0},{5,1},{6,2},{7,3},{8,12},{9,13},{10,... | collective-permute-start | bytes 1400840 | tf_op jit(solution)/shard_map/ppermute | solution.py:941
  17.2 0.5 collective-permute-start.2
  17.6 14.8 %collective-permute-done.refs_7_.refs_10_ = bf16[304,768]{1,0:T(8,128)(2,1)S(1)} collective-permute-done((bf16[304,768]{1,0:T(8,128)(2,1)}, bf16[304,768]{1,0:T(8,128)(2,1)S(1)}, u32[]{:S(2)}, u32[]{:S(2)}) %collective-permute-start) | collective-permute-done | bytes 466976 | tf_op jit(solution)/shard_map/ppermute | solution.py:941
  32.4 16.2 %collective-permute-done.1.refs_8_.refs_11_ = bf16[304,768]{1,0:T(8,128)(2,1)S(1)} collective-permute-done((bf16[304,768]{1,0:T(8,128)(2,1)}, bf16[304,768]{1,0:T(8,128)(2,1)S(1)}, u32[]{:S(2)}, u32[]{:S(2)}) %collective-permute-start.1) | collective-permute-done | bytes 466976 | tf_op jit(solution)/shard_map/ppermute | solution.py:941
  48.7 8.3 %collective-permute-done.2.refs_9_.refs_12_ = bf16[304,768]{1,0:T(8,128)(2,1)S(1)} collective-permute-done((bf16[304,768]{1,0:T(8,128)(2,1)}, bf16[304,768]{1,0:T(8,128)(2,1)S(1)}, u32[]{:S(2)}, u32[]{:S(2)}) %collective-permute-start.2) | collective-permute-done | bytes 466976 | tf_op jit(solution)/shard_map/ppermute | solution.py:941
  57.0 0.8 copy-done.9
  57.7 4.5 %all-to-all-start.1 = ((bf16[4,192,1536]{2,1,0:T(8,128)(2,1)}), bf16[4,192,1536]{2,1,0:T(8,128)(2,1)}, u32[]{:S(2)}, u32[]{:S(2)}) async-start(bf16[4,192,1536]{2,1,0:T(8,128)(2,1)} %get-tuple-element.80), calls=%async_computation.1 | async-start | bytes 4718592 | tf_op jit(solution)/shard_map/all_to_all | solution.py:838
  62.3 0.5 collective-permute-start.8
  62.9 0.4 collective-permute-start.6
  63.3 0.9 slice.30
  64.2 0.6 collective-permute-start.5
  64.9 0.4 collective-permute-start.10
  65.3 0.5 collective-permute-done.9.refs_13_.refs_16_
  65.8 0.7 collective-permute-done.6.refs_10_.refs_13_
  66.5 24.9 %near_sources.1 = (bf16[768,1536]{1,0:T(8,128)(2,1)}, bf16[768,384]{1,0:T(8,128)(2,1)}, bf16[768,768]{1,0:T(8,128)(2,1)}, bf16[256,1536]{1,0:T(8,128)(2,1)}, bf1...) custom-call(s32[4,8]{1,0:T(4,128)} %bitcast.35, ...), custom_call_target="tpu_custom_call" | custom-call | flops 1 | bytes 1 | tf_op jit(solution)/shard_map/near_sources/pallas_call | solution.py:287
  91.3 0.6 collective-permute-start.11
  92.0 1.4 collective-permute-start.12
  93.4 0.9 copy-done.6
  94.3 0.3 copy-done.14
  94.6 16.0 %far_source.1 = (bf16[256,1536]{1,0:T(8,128)(2,1)}, bf16[4,304,768]{2,1,0:T(8,128)(2,1)}, bf16[4,304,768]{2,1,0:T(8,128)(2,1)}, bf16[256,384]{1,0:T(8,128)(2,1)}...) custom-call(s32[4,8]{1,0:T(4,128)} %bitcast.36, ...), custom_call_target="tpu_custom_call", output_to_operand_aliasing={{3}: (18, {}), {4}: (19, {}), {5}: (20, {}), {6}: (21, {})} | custom-call | flops 1 | bytes 1 | tf_op jit(solution)/shard_map/far_source/pallas_call | solution.py:431
  110.6 0.6 collective-permute-done.11.refs_1_
  111.2 0.3 collective-permute-done.12.refs_2_
  111.5 0.6 copy-done.11
  112.1 0.3 copy-done.12
  112.4 4.0 %collective-permute-done.13.got_hbm = bf16[4,304,768]{2,1,0:T(8,128)(2,1)S(1)} collective-permute-done((bf16[4,304,768]{2,1,0:T(8,128)(2,1)}, bf16[4,304,768]{2,1,0:T(8,128)(2,1)S(1)}, u32[]{:S(2)}, u32[]{:S(2)}) %collective-permute-start.13) | collective-permute-done | bytes 1867808 | tf_op jit(solution)/shard_map/ppermute | solution.py:941
  116.4 1.2 copy-done.10
  117.6 3.0 %add_cores.1 = bf16[4,304,768]{2,1,0:T(8,128)(2,1)} custom-call(bf16[4,304,768]{2,1,0:T(8,128)(2,1)} %get-tuple-element.83.keep_hbm, bf16[4,304,768]{2,1,0:T(8,128)(2,1)} %copy-done.10), custom_call_target="tpu_custom_call" | custom-call | flops 1 | bytes 1 | tf_op jit(solution)/shard_map/add_cores/pallas_call | solution.py:767
  120.7 5.9 %all-to-all-start.2 = ((bf16[4,304,768]{2,1,0:T(8,128)(2,1)}), bf16[4,304,768]{2,1,0:T(8,128)(2,1)S(1)}, u32[]{:S(2)}, u32[]{:S(2)}) async-start(bf16[4,304,768]{2,1,0:T(8,128)(2,1)} %add_cores.1), calls=%async_computation.2 | async-start | bytes 3735552 | tf_op jit(solution)/shard_map/all_to_all | solution.py:848
  126.6 0.6 collective-permute-start.18
  127.2 1.4 collective-permute-start.14
  128.6 1.5 collective-permute-start.15
  130.1 0.6 collective-permute-start.16
  130.7 20.7 %collective-permute-done.14.refs_5_ = bf16[256,384]{1,0:T(8,128)(2,1)S(1)} collective-permute-done((bf16[256,384]{1,0:T(8,128)(2,1)S(1)}, bf16[256,384]{1,0:T(8,128)(2,1)S(1)}, u32[]{:S(2)}, u32[]{:S(2)}) %collective-permute-start.14) | collective-permute-done | bytes 196640 | tf_op jit(solution)/shard_map/ppermute | solution.py:941
  151.4 0.8 collective-permute-done.15.refs_6_
  152.2 3.9 %collective-permute-done.16.refs_7_ = bf16[256,384]{1,0:T(8,128)(2,1)S(1)} collective-permute-done((bf16[256,384]{1,0:T(8,128)(2,1)S(1)}, bf16[256,384]{1,0:T(8,128)(2,1)S(1)}, u32[]{:S(2)}, u32[]{:S(2)}) %collective-permute-start.16) | collective-permute-done | bytes 196640 | tf_op jit(solution)/shard_map/ppermute | solution.py:941
  156.1 0.7 copy-done.20
  156.8 6.2 %encode.1 = bf16[256,1536]{1,0:T(8,128)(2,1)} custom-call(s32[4,8]{1,0:T(4,128)} %bitcast.37, bf16[256,1536]{1,0:T(8,128)(2,1)} %bitcast.26, bf16[512,1536]{1,0:T(8,128)(2,1)} %copy-done.3, bf16[512,1536]{1,0:T(8,128)(2,1)} %copy-done.4, bf16[256,1536]{1,0:T(8,128)(2,1)} %copy-done.6, bf16[256,384]{1,0:T(8,128)(2,1)} %get-tuple-element.85.refs_4_, ...), custom_call_target="tpu_custom_call" | custom-call | flops 1 | bytes 1 | tf_op jit(solution)/shard_map/encode/pallas_call | solution.py:617
  163.0 0.9 copy-done.13
  163.9 4.9 %frame_grad.1 = bf16[256,1536]{1,0:T(8,128)(2,1)} custom-call(bf16[256,1536]{1,0:T(8,128)(2,1)} %bitcast.27, bf16[256,1536]{1,0:T(8,128)(2,1)} %bitcast.31, f32[1,1536]{1,0:T(1,128)} %get-tuple-element.90.gain_ref, bf16[256,1536]{1,0:T(8,128)(2,1)} %get-tuple-element.91.refs_0_, bf16[256,1536]{1,0:T(8,128)(2,1)} %copy-done.11, bf16[256,1536]{1,0:T(8,128)(2,1)} %copy-done.12, ...), custom_call_target="tpu_custom_call" | custom-call | flops 1 | bytes 1 | tf_op jit(solution)/shard_map/frame_grad/pallas_call | solution.py:654
  168.8 1.2 copy-done.5
  170.1 2.4 %add_chips.1 = (bf16[304,384]{1,0:T(8,128)(2,1)}, bf16[304,384]{1,0:T(8,128)(2,1)}) custom-call(bf16[4,304,768]{2,1,0:T(8,128)(2,1)} %copy-done.5), custom_call_target="tpu_custom_call" | custom-call | flops 1 | bytes 1 | tf_op jit(solution)/shard_map/add_chips/pallas_call | solution.py:792
  172.5 0.6 collective-permute-start.21
  173.1 1.5 collective-permute-start.20
  174.6 1.5 collective-permute-start.19
  176.1 0.7 slice_bitcast_fusion.3
  176.8 0.6 collective-permute-start.22
  177.4 0.6 collective-permute-start.23
  178.0 4.2 %collective-permute-done.21.refs_3_ = bf16[304,384]{1,0:T(8,128)(2,1)S(1)} collective-permute-done((bf16[304,384]{1,0:T(8,128)(2,1)}, bf16[304,384]{1,0:T(8,128)(2,1)S(1)}, u32[]{:S(2)}, u32[]{:S(2)}) %collective-permute-start.21) | collective-permute-done | bytes 233504 | tf_op jit(solution)/shard_map/ppermute | solution.py:941
  182.2 0.7 collective-permute-start.24
  182.9 3.2 %collective-permute-done.20.refs_2_ = bf16[304,384]{1,0:T(8,128)(2,1)S(1)} collective-permute-done((bf16[304,384]{1,0:T(8,128)(2,1)}, bf16[304,384]{1,0:T(8,128)(2,1)S(1)}, u32[]{:S(2)}, u32[]{:S(2)}) %collective-permute-start.20) | collective-permute-done | bytes 233504 | tf_op jit(solution)/shard_map/ppermute | solution.py:941
  186.3 0.6 gather_fusion
  187.2 0.6 slice.47
  187.8 3.6 %collective-permute-done.22.refs_5_ = bf16[304,384]{1,0:T(8,128)(2,1)S(1)} collective-permute-done((bf16[304,384]{1,0:T(8,128)(2,1)}, bf16[304,384]{1,0:T(8,128)(2,1)S(1)}, u32[]{:S(2)}, u32[]{:S(2)}) %collective-permute-start.22) | collective-permute-done | bytes 233504 | tf_op jit(solution)/shard_map/ppermute | solution.py:941
  191.3 4.6 %collective-permute-done.24.refs_7_ = bf16[304,384]{1,0:T(8,128)(2,1)S(1)} collective-permute-done((bf16[304,384]{1,0:T(8,128)(2,1)}, bf16[304,384]{1,0:T(8,128)(2,1)S(1)}, u32[]{:S(2)}, u32[]{:S(2)}) %collective-permute-start.24) | collective-permute-done | bytes 233504 | tf_op jit(solution)/shard_map/ppermute | solution.py:941
  196.0 0.9 copy-done.1
  196.9 0.9 copy-done.2
  197.9 4.2 %unpack.1 = (f32[192,3072]{1,0:T(8,128)}, f32[192,1536]{1,0:T(8,128)}, f32[1,192]{1,0:T(1,128)}) custom-call(bf16[304,384]{1,0:T(8,128)(2,1)S(1)} %copy-done.1, bf16[304,384]{1,0:T(8,128)(2,1)S(1)} %collective-permute-done.19.refs_1_, bf16[304,384]{1,0:T(8,128)(2,1)S(1)} %collective-permute-done.20.refs_2_, ...), custom_call_target="tpu_custom_call" | custom-call | flops 1 | bytes 1 | tf_op jit(solution)/shard_map/unpack/pallas_call | solution.py:715
  (68 shorter events, 0.8 us)
Async XLA Ops:
  2.0 8.6 %all-to-all-start = ((s32[4,1,8]{2,1,0:T(1,128)}), s32[4,1,8]{2,1,0:T(1,128)S(1)}, u32[]{:S(2)}, u32[]{:S(2)}) async-start(s32[4,1,8]{2,1,0:T(1,128)} %broadcast_in_dim.16), calls=%async_computation | async-start | bytes 4096 | tf_op jit(solution)/shard_map/all_to_all | solution.py:822
  10.6 47.1 %copy-start.22 = (s32[4,1,8]{2,1,0:T(1,128)}, s32[4,1,8]{2,1,0:T(1,128)S(1)}, u32[]{:S(2)}) copy-start(s32[4,1,8]{2,1,0:T(1,128)S(1)} %all-to-all-done) | copy-start | bytes 388
  10.6 46.4 %collective-permute-start.3 = (bf16[512,1536]{1,0:T(8,128)(2,1)}, bf16[512,1536]{1,0:T(8,128)(2,1)S(1)}, u32[]{:S(2)}, u32[]{:S(2)}) collective-permute-start(bf16[512,1536]{1,0:T(8,128)(2,1)} %get-tuple-element.57), channel_id=1, source_target_pairs={{0,8},{8,0},{16,24},{24,16},{1,9},{9,1},{17,25},{25,17},{2,10},{10... | collective-permute-start | bytes 4718600 | tf_op jit(solution)/shard_map/ppermute | solution.py:941
  12.7 44.3 %collective-permute-start.4 = (bf16[512,1536]{1,0:T(8,128)(2,1)}, bf16[512,1536]{1,0:T(8,128)(2,1)S(1)}, u32[]{:S(2)}, u32[]{:S(2)}) collective-permute-start(bf16[512,1536]{1,0:T(8,128)(2,1)} %get-tuple-element.57), channel_id=1, source_target_pairs={{0,16},{8,24},{16,0},{24,8},{1,17},{9,25},{17,1},{25,9},{2,18},{10... | collective-permute-start | bytes 4718600 | tf_op jit(solution)/shard_map/ppermute | solution.py:941
  14.1 18.3 %collective-permute-start = (bf16[304,768]{1,0:T(8,128)(2,1)}, bf16[304,768]{1,0:T(8,128)(2,1)S(1)}, u32[]{:S(2)}, u32[]{:S(2)}) collective-permute-start(bf16[304,768]{1,0:T(8,128)(2,1)} %get-tuple-element.60.refs_6_.refs_9_), channel_id=1, source_target_pairs={{0,2},{1,3},{2,0},{3,1},{4,6},{5,7},{6,4},{7,5},{8,10},{9,11},{10,... | collective-permute-start | bytes 1400840 | tf_op jit(solution)/shard_map/ppermute | solution.py:941
  14.6 34.1 %collective-permute-start.1 = (bf16[304,768]{1,0:T(8,128)(2,1)}, bf16[304,768]{1,0:T(8,128)(2,1)S(1)}, u32[]{:S(2)}, u32[]{:S(2)}) collective-permute-start(bf16[304,768]{1,0:T(8,128)(2,1)} %get-tuple-element.60.refs_6_.refs_9_), channel_id=1, source_target_pairs={{0,4},{1,5},{2,6},{3,7},{4,0},{5,1},{6,2},{7,3},{8,12},{9,13},{10,... | collective-permute-start | bytes 1400840 | tf_op jit(solution)/shard_map/ppermute | solution.py:941
  17.2 39.8 %collective-permute-start.2 = (bf16[304,768]{1,0:T(8,128)(2,1)}, bf16[304,768]{1,0:T(8,128)(2,1)S(1)}, u32[]{:S(2)}, u32[]{:S(2)}) collective-permute-start(bf16[304,768]{1,0:T(8,128)(2,1)} %get-tuple-element.60.refs_6_.refs_9_), channel_id=1, source_target_pairs={{0,6},{1,7},{2,4},{3,5},{4,2},{5,3},{6,0},{7,1},{8,14},{9,15},{10,... | collective-permute-start | bytes 1400840 | tf_op jit(solution)/shard_map/ppermute | solution.py:941
  32.4 24.5 %copy-start.7 = (bf16[304,768]{1,0:T(8,128)(2,1)}, bf16[304,768]{1,0:T(8,128)(2,1)S(1)}, u32[]{:S(2)}) copy-start(bf16[304,768]{1,0:T(8,128)(2,1)S(1)} %collective-permute-done.refs_7_.refs_10_) | copy-start | bytes 1400836
  48.7 8.3 %copy-start.8 = (bf16[304,768]{1,0:T(8,128)(2,1)}, bf16[304,768]{1,0:T(8,128)(2,1)S(1)}, u32[]{:S(2)}) copy-start(bf16[304,768]{1,0:T(8,128)(2,1)S(1)} %collective-permute-done.1.refs_8_.refs_11_) | copy-start | bytes 1400836
  56.9 0.8 copy-start.9
  56.9 6.4 %copy-start.3 = (bf16[512,1536]{1,0:T(8,128)(2,1)}, bf16[512,1536]{1,0:T(8,128)(2,1)S(1)}, u32[]{:S(2)}) copy-start(bf16[512,1536]{1,0:T(8,128)(2,1)S(1)} %collective-permute-done.3.refs_1_.refs_4_.refs_5_) | copy-start | bytes 4718596
  57.7 7.1 %copy-start.4 = (bf16[512,1536]{1,0:T(8,128)(2,1)}, bf16[512,1536]{1,0:T(8,128)(2,1)S(1)}, u32[]{:S(2)}) copy-start(bf16[512,1536]{1,0:T(8,128)(2,1)S(1)} %collective-permute-done.4.refs_2_.refs_5_.refs_6_) | copy-start | bytes 4718596
  57.7 53.8 %all-to-all-start.1 = ((bf16[4,192,1536]{2,1,0:T(8,128)(2,1)}), bf16[4,192,1536]{2,1,0:T(8,128)(2,1)}, u32[]{:S(2)}, u32[]{:S(2)}) async-start(bf16[4,192,1536]{2,1,0:T(8,128)(2,1)} %get-tuple-element.80), calls=%async_computation.1 | async-start | bytes 4718592 | tf_op jit(solution)/shard_map/all_to_all | solution.py:838
  62.2 2.6 %collective-permute-start.7 = (bf16[304,768]{1,0:T(8,128)(2,1)}, bf16[304,768]{1,0:T(8,128)(2,1)}, u32[]{:S(2)}, u32[]{:S(2)}) collective-permute-start(bf16[304,768]{1,0:T(8,128)(2,1)} %copy-done.7), channel_id=1, source_target_pairs={{0,1},{1,0},{2,3},{3,2},{4,5},{5,4},{6,7},{7,6},{8,9},{9,8},{10,11... | collective-permute-start | bytes 1400840 | tf_op jit(solution)/shard_map/ppermute | solution.py:941
  62.3 3.0 %collective-permute-start.8 = (bf16[304,768]{1,0:T(8,128)(2,1)}, bf16[304,768]{1,0:T(8,128)(2,1)}, u32[]{:S(2)}, u32[]{:S(2)}) collective-permute-start(bf16[304,768]{1,0:T(8,128)(2,1)} %copy-done.8), channel_id=1, source_target_pairs={{0,1},{1,0},{2,3},{3,2},{4,5},{5,4},{6,7},{7,6},{8,9},{9,8},{10,11... | collective-permute-start | bytes 1400840 | tf_op jit(solution)/shard_map/ppermute | solution.py:941
  62.8 3.0 %collective-permute-start.9 = (bf16[304,768]{1,0:T(8,128)(2,1)}, bf16[304,768]{1,0:T(8,128)(2,1)}, u32[]{:S(2)}, u32[]{:S(2)}) collective-permute-start(bf16[304,768]{1,0:T(8,128)(2,1)} %copy-done.9), channel_id=1, source_target_pairs={{0,1},{1,0},{2,3},{3,2},{4,5},{5,4},{6,7},{7,6},{8,9},{9,8},{10,11... | collective-permute-start | bytes 1400840 | tf_op jit(solution)/shard_map/ppermute | solution.py:941
  62.9 3.6 %collective-permute-start.6 = (bf16[304,768]{1,0:T(8,128)(2,1)}, bf16[304,768]{1,0:T(8,128)(2,1)}, u32[]{:S(2)}, u32[]{:S(2)}) collective-permute-start(bf16[304,768]{1,0:T(8,128)(2,1)} %get-tuple-element.60.refs_6_.refs_9_), channel_id=1, source_target_pairs={{0,1},{1,0},{2,3},{3,2},{4,5},{5,4},{6,7},{7,6},{8,9},{9,8},{10,11... | collective-permute-start | bytes 1400840 | tf_op jit(solution)/shard_map/ppermute | solution.py:941
  64.2 29.2 %collective-permute-start.5 = (bf16[256,1536]{1,0:T(8,128)(2,1)}, bf16[256,1536]{1,0:T(8,128)(2,1)S(1)}, u32[]{:S(2)}, u32[]{:S(2)}) collective-permute-start(bf16[256,1536]{1,0:T(8,128)(2,1)} %slice.30), channel_id=1, source_target_pairs={{0,16},{8,24},{16,0},{24,8},{1,17},{9,25},{17,1},{25,9},{2,18},{10... | collective-permute-start | bytes 2359304 | tf_op jit(solution)/shard_map/ppermute | solution.py:941
  64.9 28.5 %collective-permute-start.10 = (bf16[256,1536]{1,0:T(8,128)(2,1)S(1)}, bf16[256,1536]{1,0:T(8,128)(2,1)S(1)}, u32[]{:S(2)}, u32[]{:S(2)}) collective-permute-start(bf16[256,1536]{1,0:T(8,128)(2,1)S(1)} %slice.31), channel_id=1, source_target_pairs={{0,8},{8,0},{16,24},{24,16},{1,9},{9,1},{17,25},{25,17},{2,10},{10... | collective-permute-start | bytes 2359304 | tf_op jit(solution)/shard_map/ppermute | solution.py:941
  91.3 19.9 %collective-permute-start.11 = (bf16[256,1536]{1,0:T(8,128)(2,1)}, bf16[256,1536]{1,0:T(8,128)(2,1)S(1)}, u32[]{:S(2)}, u32[]{:S(2)}) collective-permute-start(bf16[256,1536]{1,0:T(8,128)(2,1)} %get-tuple-element.81), channel_id=1, source_target_pairs={{0,8},{8,0},{16,24},{24,16},{1,9},{9,1},{17,25},{25,17},{2,10},{10... | collective-permute-start | bytes 2359304 | tf_op jit(solution)/shard_map/ppermute | solution.py:941
  92.0 19.5 %collective-permute-start.12 = (bf16[256,1536]{1,0:T(8,128)(2,1)}, bf16[256,1536]{1,0:T(8,128)(2,1)S(1)}, u32[]{:S(2)}, u32[]{:S(2)}) collective-permute-start(bf16[256,1536]{1,0:T(8,128)(2,1)} %get-tuple-element.82), channel_id=1, source_target_pairs={{0,16},{8,24},{16,0},{24,8},{1,17},{9,25},{17,1},{25,9},{2,18},{10... | collective-permute-start | bytes 2359304 | tf_op jit(solution)/shard_map/ppermute | solution.py:941
  93.4 0.9 copy-start.6
  93.4 1.2 copy-start.14
  111.2 0.9 copy-start.11
  111.5 0.9 copy-start.12
  112.4 4.0 %collective-permute-start.13 = (bf16[4,304,768]{2,1,0:T(8,128)(2,1)}, bf16[4,304,768]{2,1,0:T(8,128)(2,1)S(1)}, u32[]{:S(2)}, u32[]{:S(2)}) collective-permute-start(bf16[4,304,768]{2,1,0:T(8,128)(2,1)} %get-tuple-element.84), channel_id=1, source_target_pairs={{0,1},{1,0},{2,3},{3,2},{4,5},{5,4},{6,7},{7,6},{8,9},{9,8},{10,11... | collective-permute-start | bytes 5603336 | tf_op jit(solution)/shard_map/ppermute | solution.py:941
  116.4 1.2 copy-start.10
  120.7 6.5 %copy-start.15 = (bf16[256,384]{1,0:T(8,128)(2,1)S(1)}, bf16[256,384]{1,0:T(8,128)(2,1)}, u32[]{:S(2)}) copy-start(bf16[256,384]{1,0:T(8,128)(2,1)} %get-tuple-element.86) | copy-start | bytes 589828
  120.7 7.9 %copy-start.16 = (bf16[256,384]{1,0:T(8,128)(2,1)S(1)}, bf16[256,384]{1,0:T(8,128)(2,1)}, u32[]{:S(2)}) copy-start(bf16[256,384]{1,0:T(8,128)(2,1)} %get-tuple-element.87) | copy-start | bytes 589828
  120.7 9.4 %copy-start.17 = (bf16[256,384]{1,0:T(8,128)(2,1)S(1)}, bf16[256,384]{1,0:T(8,128)(2,1)}, u32[]{:S(2)}) copy-start(bf16[256,384]{1,0:T(8,128)(2,1)} %get-tuple-element.88) | copy-start | bytes 589828
  120.7 48.1 %all-to-all-start.2 = ((bf16[4,304,768]{2,1,0:T(8,128)(2,1)}), bf16[4,304,768]{2,1,0:T(8,128)(2,1)S(1)}, u32[]{:S(2)}, u32[]{:S(2)}) async-start(bf16[4,304,768]{2,1,0:T(8,128)(2,1)} %add_cores.1), calls=%async_computation.2 | async-start | bytes 3735552 | tf_op jit(solution)/shard_map/all_to_all | solution.py:848
  126.6 29.5 %collective-permute-start.17 = (bf16[4,192,1536]{2,1,0:T(8,128)(2,1)}, bf16[4,192,1536]{2,1,0:T(8,128)(2,1)}, u32[]{:S(2)}, u32[]{:S(2)}) collective-permute-start(bf16[4,192,1536]{2,1,0:T(8,128)(2,1)} %all-to-all-done.1.refs_8_), channel_id=1, source_target_pairs={{0,1},{1,0},{2,3},{3,2},{4,5},{5,4},{6,7},{7,6},{8,9},{9,8},{10,11... | collective-permute-start | bytes 7077896 | tf_op jit(solution)/shard_map/ppermute | solution.py:941
  126.6 36.4 %collective-permute-start.18 = (bf16[256,1536]{1,0:T(8,128)(2,1)}, bf16[256,1536]{1,0:T(8,128)(2,1)S(1)}, u32[]{:S(2)}, u32[]{:S(2)}) collective-permute-start(bf16[256,1536]{1,0:T(8,128)(2,1)} %get-tuple-element.92), channel_id=1, source_target_pairs={{0,24},{8,16},{16,8},{24,0},{1,25},{9,17},{17,9},{25,1},{2,26},{10... | collective-permute-start | bytes 2359304 | tf_op jit(solution)/shard_map/ppermute | solution.py:941
  127.2 24.2 %collective-permute-start.14 = (bf16[256,384]{1,0:T(8,128)(2,1)S(1)}, bf16[256,384]{1,0:T(8,128)(2,1)S(1)}, u32[]{:S(2)}, u32[]{:S(2)}) collective-permute-start(bf16[256,384]{1,0:T(8,128)(2,1)S(1)} %copy-done.15), channel_id=1, source_target_pairs={{0,8},{8,0},{16,24},{24,16},{1,9},{9,1},{17,25},{25,17},{2,10},{10... | collective-permute-start | bytes 589832 | tf_op jit(solution)/shard_map/ppermute | solution.py:941
  128.6 23.6 %collective-permute-start.15 = (bf16[256,384]{1,0:T(8,128)(2,1)S(1)}, bf16[256,384]{1,0:T(8,128)(2,1)S(1)}, u32[]{:S(2)}, u32[]{:S(2)}) collective-permute-start(bf16[256,384]{1,0:T(8,128)(2,1)S(1)} %copy-done.16), channel_id=1, source_target_pairs={{0,16},{8,24},{16,0},{24,8},{1,17},{9,25},{17,1},{25,9},{2,18},{10... | collective-permute-start | bytes 589832 | tf_op jit(solution)/shard_map/ppermute | solution.py:941
  130.1 26.0 %collective-permute-start.16 = (bf16[256,384]{1,0:T(8,128)(2,1)S(1)}, bf16[256,384]{1,0:T(8,128)(2,1)S(1)}, u32[]{:S(2)}, u32[]{:S(2)}) collective-permute-start(bf16[256,384]{1,0:T(8,128)(2,1)S(1)} %copy-done.17), channel_id=1, source_target_pairs={{0,24},{8,16},{16,8},{24,0},{1,25},{9,17},{17,9},{25,1},{2,26},{10... | collective-permute-start | bytes 589832 | tf_op jit(solution)/shard_map/ppermute | solution.py:941
  151.4 4.7 %copy-start.18 = (bf16[256,384]{1,0:T(8,128)(2,1)}, bf16[256,384]{1,0:T(8,128)(2,1)S(1)}, u32[]{:S(2)}) copy-start(bf16[256,384]{1,0:T(8,128)(2,1)S(1)} %collective-permute-done.14.refs_5_) | copy-start | bytes 589828
  152.2 3.9 %copy-start.19 = (bf16[256,384]{1,0:T(8,128)(2,1)}, bf16[256,384]{1,0:T(8,128)(2,1)S(1)}, u32[]{:S(2)}) copy-start(bf16[256,384]{1,0:T(8,128)(2,1)S(1)} %collective-permute-done.15.refs_6_) | copy-start | bytes 589828
  156.1 0.7 copy-start.20
  163.0 0.9 copy-start.13
  168.8 4.3 %copy-start.23 = (bf16[192]{0:T(256)(128)(2,1)S(1)}, bf16[192]{0:T(256)(128)(2,1)}, u32[]{:S(2)}) copy-start(bf16[192]{0:T(256)(128)(2,1)} %gain_ref.1) | copy-start | bytes 1156
  168.8 27.2 %copy-start = (bf16[192,3072]{1,0:T(8,128)(2,1)S(1)}, bf16[192,3072]{1,0:T(8,128)(2,1)}, u32[]{:S(2)}) copy-start(bf16[192,3072]{1,0:T(8,128)(2,1)} %refs_8_.1) | copy-start | bytes 3538948
  168.8 1.2 copy-start.5
  172.5 9.7 %collective-permute-start.21 = (bf16[304,384]{1,0:T(8,128)(2,1)}, bf16[304,384]{1,0:T(8,128)(2,1)S(1)}, u32[]{:S(2)}, u32[]{:S(2)}) collective-permute-start(bf16[304,384]{1,0:T(8,128)(2,1)} %get-tuple-element.94.refs_0_), channel_id=1, source_target_pairs={{0,24},{8,16},{16,8},{24,0},{1,25},{9,17},{17,9},{25,1},{2,26},{10... | collective-permute-start | bytes 700424 | tf_op jit(solution)/shard_map/ppermute | solution.py:941
  173.1 12.9 %collective-permute-start.20 = (bf16[304,384]{1,0:T(8,128)(2,1)}, bf16[304,384]{1,0:T(8,128)(2,1)S(1)}, u32[]{:S(2)}, u32[]{:S(2)}) collective-permute-start(bf16[304,384]{1,0:T(8,128)(2,1)} %get-tuple-element.94.refs_0_), channel_id=1, source_target_pairs={{0,16},{8,24},{16,0},{24,8},{1,17},{9,25},{17,1},{25,9},{2,18},{10... | collective-permute-start | bytes 700424 | tf_op jit(solution)/shard_map/ppermute | solution.py:941
  174.6 11.7 %collective-permute-start.19 = (bf16[304,384]{1,0:T(8,128)(2,1)}, bf16[304,384]{1,0:T(8,128)(2,1)S(1)}, u32[]{:S(2)}, u32[]{:S(2)}) collective-permute-start(bf16[304,384]{1,0:T(8,128)(2,1)} %get-tuple-element.94.refs_0_), channel_id=1, source_target_pairs={{0,8},{8,0},{16,24},{24,16},{1,9},{9,1},{17,25},{25,17},{2,10},{10... | collective-permute-start | bytes 700424 | tf_op jit(solution)/shard_map/ppermute | solution.py:941
  176.8 14.5 %collective-permute-start.22 = (bf16[304,384]{1,0:T(8,128)(2,1)}, bf16[304,384]{1,0:T(8,128)(2,1)S(1)}, u32[]{:S(2)}, u32[]{:S(2)}) collective-permute-start(bf16[304,384]{1,0:T(8,128)(2,1)} %get-tuple-element.95.refs_4_), channel_id=1, source_target_pairs={{0,8},{8,0},{16,24},{24,16},{1,9},{9,1},{17,25},{25,17},{2,10},{10... | collective-permute-start | bytes 700424 | tf_op jit(solution)/shard_map/ppermute | solution.py:941
  177.4 14.0 %collective-permute-start.23 = (bf16[304,384]{1,0:T(8,128)(2,1)}, bf16[304,384]{1,0:T(8,128)(2,1)S(1)}, u32[]{:S(2)}, u32[]{:S(2)}) collective-permute-start(bf16[304,384]{1,0:T(8,128)(2,1)} %get-tuple-element.95.refs_4_), channel_id=1, source_target_pairs={{0,16},{8,24},{16,0},{24,8},{1,17},{9,25},{17,1},{25,9},{2,18},{10... | collective-permute-start | bytes 700424 | tf_op jit(solution)/shard_map/ppermute | solution.py:941
  182.2 13.8 %collective-permute-start.24 = (bf16[304,384]{1,0:T(8,128)(2,1)}, bf16[304,384]{1,0:T(8,128)(2,1)S(1)}, u32[]{:S(2)}, u32[]{:S(2)}) collective-permute-start(bf16[304,384]{1,0:T(8,128)(2,1)} %get-tuple-element.95.refs_4_), channel_id=1, source_target_pairs={{0,24},{8,16},{16,8},{24,0},{1,25},{9,17},{17,9},{25,1},{2,26},{10... | collective-permute-start | bytes 700424 | tf_op jit(solution)/shard_map/ppermute | solution.py:941
  187.2 14.9 %copy-start.21 = (f32[192,32]{0,1:T(8,128)}, f32[192,32]{0,1:T(8,128)S(1)}, u32[]{:S(2)}) copy-start(f32[192,32]{0,1:T(8,128)S(1)} %reshape.67) | copy-start | bytes 73732
  196.0 0.9 copy-start.1
  196.9 0.9 copy-start.2

commit v5 on v4

--- a/solution.py
+++ b/solution.py
@@ -14,11 +14,11 @@
 MARGIN = 16
 NT = (((1,), (1,)), ((), ()))
 TN = (((0,), (0,)), ((), ()))
-VMEM_PACK = 60
-VMEM_CHUNK = 60
-VMEM_ENCODE = 60
-VMEM_FRAME = 60
-VMEM_HOP = 60
+VMEM_PACK = 63
+VMEM_CHUNK = 63
+VMEM_ENCODE = 63
+VMEM_FRAME = 63
+VMEM_HOP = 63
 VMEM_UNPACK = 28
 LIGHT = pl.CostEstimate(flops=1, bytes_accessed=1, transcendentals=0)
 
@@ -666,71 +666,85 @@
 
 
 def unpack_kernel(dims, *refs):
-    n, owned, part = dims
-    blocks, refs = (refs[:n], refs[n : 2 * n]), refs[2 * n :]
-    weight_ref, gain_ref, expand_ref, project_ref, gain_out, cat, grads, project, sems = refs
-    channels = blocks[0][0].shape[1]
+    n, owned, part, half = dims
+    blocks, (weight_ref, before, gain_ref) = refs[:n], refs[n : n + 3]
+    expand_ref, project_ref, gain_out, cat, grads, project, sems = refs[-7:]
+    channels = blocks[0].shape[1]
+    width = cat.shape[1]
     wide = 2 * channels
-    width = cat.shape[2]
     halves = width // wide
     me = lax.axis_index("dp")
     for k in range(n):
-        lanes = pl.ds(pl.multiple_of((me ^ k) * channels, channels), channels)
+        cat[:, pl.ds(pl.multiple_of((me ^ k) * channels, channels), channels)] = blocks[k][:owned]
         rows = pl.ds(pl.multiple_of((me ^ k) * part, part), part)
-        for half in range(2):
-            block = blocks[half][k]
-            cat[half, :, lanes] = block[:owned]
-            for h in range(halves):
-                start = h * wide + half * channels
-                project[rows, start : start + channels] = block[
-                    owned + h * part : owned + (h + 1) * part
-                ].astype(F32)
-    copies = [pltpu.make_async_copy(project, project_ref, sems.at[2, 0])]
-    copies[0].start()
-    along = jnp.zeros((owned, 1), F32)
+        for h in range(halves):
+            project[h, rows, :] = blocks[k][owned + h * part : owned + (h + 1) * part].astype(F32)
+    copies = [
+        pltpu.make_async_copy(
+            project.at[h],
+            project_ref.at[:, pl.ds(h * wide + half * channels, channels)],
+            sems.at[0, h],
+        )
+        for h in range(halves)
+    ]
+    for copy in copies:
+        copy.start()
+    along = before[...]
     span = 512
-    for start in range(0, width, span):
+    for i, start in enumerate(range(0, width, span)):
         row = lax.broadcasted_iota(jnp.int32, (width, span), 0)
         col = lax.broadcasted_iota(jnp.int32, (1, span), 1) + start
         place = col % owned // part * channels + col // owned * part + col % part
         spread = jnp.where(row == place, 1.0, 0.0).astype(BF16)
-        for half in range(2):
-            cols = pl.ds(half * width + start, span)
-            grad = jnp.dot(cat[half], spread, preferred_element_type=F32)
-            grads[:, cols] = grad
-            copy = pltpu.make_async_copy(
-                grads.at[:, cols], expand_ref.at[:, cols], sems.at[half, start // span]
-            )
-            copy.start()
-            copies.append(copy)
-            along += jnp.sum(grad * weight_ref[:, cols].astype(F32), axis=1, keepdims=True)
-    row = jnp.transpose(jnp.broadcast_to(along, (owned, LANES)))[:1]
-    gain_out[...] = row / gain_ref[...].astype(F32)
+        grad = jnp.dot(cat[...], spread, preferred_element_type=F32)
+        grads[i] = grad
+        copy = pltpu.make_async_copy(
+            grads.at[i],
+            expand_ref.at[:, pl.ds(half * width + start, span)],
+            sems.at[1, i],
+        )
+        copy.start()
+        copies.append(copy)
+        along += jnp.sum(
+            grad * weight_ref[:, start : start + span].astype(F32), axis=1, keepdims=True
+        )
+    if half == 0:
+        gain_out[...] = along
+    else:
+        row = jnp.transpose(jnp.broadcast_to(along, (owned, LANES)))[:1]
+        gain_out[...] = row / gain_ref[...].astype(F32)
     for copy in copies:
         copy.wait()
 
 
-def unpack_call(low, high, weight, gain, owned, part, width):
+def unpack_call(half, blocks, weight, before, gain, outputs, owned, part, width):
+    n = len(blocks)
+    channels = blocks[0].shape[1]
+    halves = width // (2 * channels)
     anywhere = pl.BlockSpec(memory_space=pl.ANY)
     return pl.pallas_call(
-        functools.partial(unpack_kernel, (len(low), owned, part)),
+        functools.partial(unpack_kernel, (n, owned, part, half)),
         out_shape=(
             jax.ShapeDtypeStruct((owned, 2 * width), F32),
             jax.ShapeDtypeStruct((owned, width), F32),
-            jax.ShapeDtypeStruct((1, owned), F32),
+            jax.ShapeDtypeStruct((1, owned) if half else (owned, 1), F32),
         ),
-        in_specs=[in_vmem()] * (2 * len(low) + 2),
+        grid=(1,),
+        in_specs=[in_vmem()] * n
+        + [pl.BlockSpec((owned, width), lambda s: (0, half)), in_vmem(), in_vmem()]
+        + [anywhere] * len(outputs),
         out_specs=(anywhere, anywhere, in_vmem()),
         scratch_shapes=[
-            pltpu.VMEM((2, owned, width), BF16),
-            pltpu.VMEM((owned, 2 * width), F32),
-            pltpu.VMEM((owned, width), F32),
-            pltpu.SemaphoreType.DMA((3, width // 512)),
+            pltpu.VMEM((owned, width), BF16),
+            pltpu.VMEM((width // 512, owned, 512), F32),
+            pltpu.VMEM((halves, owned, channels), F32),
+            pltpu.SemaphoreType.DMA((2, max(halves, width // 512))),
         ],
+        input_output_aliases={n + 3 + i: i for i in range(len(outputs))},
         compiler_params=vmem_params(VMEM_UNPACK),
         cost_estimate=LIGHT,
         name="unpack",
-    )(*low, *high, weight, gain)
+    )(*blocks, weight, before, gain, *outputs)
 
 
 def tie(value, *after):
@@ -742,37 +756,39 @@
     return blocks + [swap(block, "shard", 8, 1) for block in blocks]
 
 
-def add_cores_kernel(keep_hbm, got_hbm, out_hbm, keep, got, sems):
+def add_cores_kernel(keep_hbm, got_hbm, *refs):
+    n = len(refs) - 3
+    outs, (keep, got, sems) = refs[:n], refs[n:]
+    chip = lax.axis_index("shard") // 2
+    copies = [
+        (
+            pltpu.make_async_copy(keep_hbm.at[chip ^ m], keep.at[m], sems.at[m, 0]),
+            pltpu.make_async_copy(got_hbm.at[chip ^ m], got.at[m], sems.at[m, 1]),
+        )
+        for m in range(n)
+    ]
+    order = list(range(1, n)) + [0]
+    for m in order:
+        for copy in copies[m]:
+            copy.start()
+    for m in order:
+        for copy in copies[m]:
+            copy.wait()
+        outs[m][...] = (keep[m].astype(F32) + got[m].astype(F32)).astype(BF16)
+
+
+def add_cores(keep, got):
     n = keep.shape[0]
-    move = pltpu.make_async_copy
-    inward = [
-        (move(keep_hbm.at[i], keep.at[i], sems.at[i, 0]), move(got_hbm.at[i], got.at[i], sems.at[i, 1]))
-        for i in range(n)
-    ]
-    outward = [move(keep.at[i], out_hbm.at[i], sems.at[i, 2]) for i in range(n)]
-    for i in range(n):
-        for copy in inward[i]:
-            copy.start()
-    for i in range(n):
-        for copy in inward[i]:
-            copy.wait()
-        keep[i] = (keep[i].astype(F32) + got[i].astype(F32)).astype(BF16)
-        outward[i].start()
-    for copy in outward:
-        copy.wait()
-
-
-def add_cores(keep, got):
     anywhere = pl.BlockSpec(memory_space=pl.ANY)
     return pl.pallas_call(
         add_cores_kernel,
-        out_shape=jax.ShapeDtypeStruct(keep.shape, BF16),
+        out_shape=(jax.ShapeDtypeStruct(keep.shape[1:], BF16),) * n,
         in_specs=[anywhere] * 2,
-        out_specs=anywhere,
+        out_specs=(in_vmem(),) * n,
         scratch_shapes=[
             pltpu.VMEM(keep.shape, BF16),
             pltpu.VMEM(keep.shape, BF16),
-            pltpu.SemaphoreType.DMA((keep.shape[0], 3)),
+            pltpu.SemaphoreType.DMA((n, 2)),
         ],
         compiler_params=vmem_params(VMEM_HOP),
         cost_estimate=LIGHT,
@@ -780,24 +796,24 @@
     )(keep, got)
 
 
-def add_chips_kernel(come_ref, *refs):
-    total = jnp.sum(come_ref[...].astype(F32), axis=0).astype(BF16)
-    channels = refs[0].shape[1]
-    for half, ref in enumerate(refs):
+def add_chips_kernel(n, *refs):
+    total = sum(ref[...].astype(F32) for ref in refs[:n]).astype(BF16)
+    channels = refs[n].shape[1]
+    for half, ref in enumerate(refs[n:]):
         ref[...] = total[:, half * channels : (half + 1) * channels]
 
 
 def add_chips(come):
-    rows, wide = come.shape[1:]
+    rows, wide = come[0].shape
     return pl.pallas_call(
-        add_chips_kernel,
+        functools.partial(add_chips_kernel, len(come)),
         out_shape=(jax.ShapeDtypeStruct((rows, wide // 2), BF16),) * 2,
-        in_specs=[in_vmem()],
+        in_specs=[in_vmem()] * len(come),
         out_specs=(in_vmem(),) * 2,
         compiler_params=vmem_params(VMEM_HOP),
         cost_estimate=LIGHT,
         name="add_chips",
-    )(come)
+    )(*come)
 
 
 def fast_body(
@@ -818,13 +834,13 @@
     wide = 2 * n_shard * part
     rows = count * length
     dims = (count, length, taps)
-    ints = jnp.concatenate([lengths, send_order])
-    ints = lax.all_to_all(jnp.broadcast_to(ints, (n_dp, 2 * count)), "dp", 0, 0, tiled=True)
     x_own = frames.reshape(rows, width)
     g_own = cotangent.reshape(rows, width)
     pack, both, project = pack_call(
         expand_weight, project_weight, kernel, conv_bias, norm_gain, x_own, g_own, part, wide
     )
+    ints = jnp.concatenate([lengths, send_order])
+    ints = lax.all_to_all(jnp.broadcast_to(ints, (n_dp, 2 * count)), "dp", 0, 0, tiled=True)
     pack, both, ints = lax.optimization_barrier((pack, both, ints))
     both_x = swap(both, "dp", 4, 1)
     both_y = swap(both, "dp", 4, 2)
@@ -845,26 +861,29 @@
     keep, give = far[1:3]
     give, keep = lax.optimization_barrier((give, keep, project, *returned[1:3]))[:2]
     sums = add_cores(keep, swap(give, "shard", 8, 1))
-    come = lax.all_to_all(sums, "shard", 0, 0, axis_index_groups=line, tiled=True)
-    last, *pieces = lax.optimization_barrier((far[0], *far[3:], sums))[:-1]
+    come = [sums[0]] + [swap(sums[m], "shard", 8, 2 * m) for m in (1, 2, 3)]
+    last, *pieces = lax.optimization_barrier((far[0], *far[3:], sums[1]))[:-1]
     returned.append(swap(last, "dp", n_dp, 3))
     pieces = [pieces[0]] + [swap(pieces[m], "dp", n_dp, m) for m in (1, 2, 3)]
-    project = [project, swap(project, "shard", 8, 1)]
+    project = [project, swap(tie(project, sums[1]), "shard", 8, 1)]
+
+    pieces[0] = tie(pieces[0], come[1])
     encoded = encode_call(ints, pieces, x_all, project, length)
-    frame_grad = frame_grad_call(frames, tie(cotangent, sums), gain, returned)
-
-    gathered = [
-        [half] + [swap(half, "dp", 4, k) for k in (1, 2, 3)]
-        for half in add_chips(tie(come, encoded, frame_grad))
-    ]
+    frame_grad = frame_grad_call(frames, tie(cotangent, come[1]), gain, returned)
+
+    come[0] = tie(come[0], encoded, frame_grad)
+    gathered = [[half] + [swap(half, "dp", 4, k) for k in (1, 2, 3)] for half in add_chips(come)]
     base = owned + width // wide * part
     table = jnp.stack([a[base:] for a in gathered[0]])
     table = jnp.take(table, lax.axis_index("dp") ^ jnp.arange(n_dp), axis=0).astype(F32)
     table = jnp.concatenate([table[:, :, :part], table[:, :, LANES : LANES + part]], axis=1)
     table = table.transpose(0, 2, 1).reshape(owned, taps + 1)
-    expand_grad, project_grad, along = unpack_call(
-        *gathered, expand_weight, norm_gain[None], owned, part, width
-    )
+    outputs, along = (), jnp.zeros((owned, 1), F32)
+    for half in range(2):
+        *outputs, along = unpack_call(
+            half, gathered[half], expand_weight, along, norm_gain[None], outputs, owned, part, width
+        )
+    expand_grad, project_grad = outputs
     return (
         encoded.reshape(frames.shape),
         frame_grad,

time: 205 us -> 195 us (0.951)
  waiting for transfers between devices: 86.6 us -> 79.3 us
  local copies, waits for them, and re-layouts: 12.3 us -> 7.39 us
  starting transfers between devices: 34.8 us -> 37.6 us
    ppermute x25 -> x28, starting transfers between devices: 20.7 us -> 29.4 us  [swap(): return lax.ppermute(x, axis, [(p, p ^ k) for p in range(size)])]
    ppermute x25 -> x28, waiting for transfers between devices: 86.6 us -> 79.3 us  [swap(): return lax.ppermute(x, axis, [(p, p ^ k) for p in range(size)])]
    all_to_all x1 -> x0, starting transfers between devices: 5.86 us -> none  [fast_body(): lax.all_to_all(sums, 'shard', 0, 0, axis_index_groups=line, tiled=True)]
    unnamed x48 -> x34, local copies, waits for them, and re-layouts: 8.73 us -> 3.67 us
    pallas_call x3 -> x4, Pallas kernels: 9.68 us -> 10.4 us  [the longest x2 4.75 us: unpack_call(): pl.pallas_call(functools.partial(unpack_kernel, (n, owned, part, half)),...]
  transfers between devices with their start and end apart: 28 -> 30, of which waited for: 16 -> 15; matrix products, arithmetic and copies ran while one was open for 2% -> 2% of each run, Pallas kernels for 28% -> 30%
where the time goes in v5:
time: 195 us; the launch traced here: 194 us
  waiting for transfers between devices  79.3 us (41%)
  Pallas kernels  67.4 us (35%)
  starting transfers between devices  37.6 us (19%)
  local copies, waits for them, and re-layouts  7.39 us (4%)
    ppermute x28, waiting for transfers between devices, swap(): return lax.ppermute(x, axis, [(p, p ^ k) for p in range(size)])  79.3 us
    ppermute x28, starting transfers between devices, swap(): return lax.ppermute(x, axis, [(p, p ^ k) for p in range(size)])  29.4 us
    pallas_call x1, Pallas kernels, near_call(): pl.pallas_call(functools.partial(near_kernel, dims, n, owned), out_shape=...  25 us
    pallas_call x1, Pallas kernels, far_call(): pl.pallas_call(functools.partial(far_kernel, dims, n, owned), out_shape=(...  16 us
    pallas_call x1, Pallas kernels, encode_call(): pl.pallas_call(functools.partial(encode_kernel, (n, length, owned)), out_...  6.21 us
    pallas_call x1, Pallas kernels, pack_call(): pl.pallas_call(pack_kernel, out_shape=(jax.ShapeDtypeStruct((height, wide...  4.9 us
    pallas_call x1, Pallas kernels, frame_grad_call(): pl.pallas_call(functools.partial(frame_grad_kernel, len(returned)), out_s...  4.89 us
    pallas_call x2, Pallas kernels, unpack_call(): pl.pallas_call(functools.partial(unpack_kernel, (n, owned, part, half)),...  4.75 us
  transfers between devices with their start and end apart: 30, of which 15 were waited for; matrix products, arithmetic and copies ran while one was open for 2% of the time, Pallas kernels for 30%

profile of v5, /device:TPU:8, one launch (start us, length us, event | category | flops | bytes accessed | tf_op | source)
XLA Modules:
  0.0 194.2 jit_solution(8576457196742286789)
XLA Ops:
  0.6 0.7 pad_add_fusion
  1.4 0.6 broadcast_in_dim.20
  2.0 3.7 %all-to-all-start = ((s32[4,1,8]{2,1,0:T(1,128)}), s32[4,1,8]{2,1,0:T(1,128)S(1)}, u32[]{:S(2)}, u32[]{:S(2)}) async-start(s32[4,1,8]{2,1,0:T(1,128)} %broadcast_in_dim.20), calls=%async_computation | async-start | bytes 4096 | tf_op jit(solution)/shard_map/all_to_all | solution.py:843
  5.7 4.9 %pack.1 = (bf16[304,768]{1,0:T(8,128)(2,1)}, bf16[512,1536]{1,0:T(8,128)(2,1)}, bf16[4,192,1536]{2,1,0:T(8,128)(2,1)}) custom-call(bf16[192,3072]{1,0:T(8,128)(2,1)} %refs_4_.3, bf16[192,1536]{1,0:T(8,128)(2,1)} %project_hbm.1, bf16[31,192]{1,0:T(8,128)(2,1)} %bitcast.38, bf16[192]{0:T(256)(128)(2,1)} %bias_ref.1, bf16[192]{0:T(256)(128)(2,1)} %gain_ref.1, ...), custom_call_target="tpu_custom_call" | custom-call | flops 1 | bytes 1 | tf_op jit(solution)/shard_map/pack/pallas_call | solution.py:545
  10.6 2.1 %collective-permute-start.3 = (bf16[512,1536]{1,0:T(8,128)(2,1)}, bf16[512,1536]{1,0:T(8,128)(2,1)S(1)}, u32[]{:S(2)}, u32[]{:S(2)}) collective-permute-start(bf16[512,1536]{1,0:T(8,128)(2,1)} %get-tuple-element.66), channel_id=1, source_target_pairs={{0,8},{8,0},{16,24},{24,16},{1,9},{9,1},{17,25},{25,17},{2,10},{10... | collective-permute-start | bytes 4718600 | tf_op jit(solution)/shard_map/ppermute | solution.py:960
  12.7 1.5 collective-permute-start.4
  14.2 0.4 collective-permute-start
  14.6 2.6 %collective-permute-start.1 = (bf16[304,768]{1,0:T(8,128)(2,1)}, bf16[304,768]{1,0:T(8,128)(2,1)S(1)}, u32[]{:S(2)}, u32[]{:S(2)}) collective-permute-start(bf16[304,768]{1,0:T(8,128)(2,1)} %get-tuple-element.69.refs_6_.refs_9_), channel_id=1, source_target_pairs={{0,4},{1,5},{2,6},{3,7},{4,0},{5,1},{6,2},{7,3},{8,12},{9,13},{10,... | collective-permute-start | bytes 1400840 | tf_op jit(solution)/shard_map/ppermute | solution.py:960
  17.2 0.5 collective-permute-start.2
  17.6 14.8 %collective-permute-done.refs_7_.refs_10_ = bf16[304,768]{1,0:T(8,128)(2,1)S(1)} collective-permute-done((bf16[304,768]{1,0:T(8,128)(2,1)}, bf16[304,768]{1,0:T(8,128)(2,1)S(1)}, u32[]{:S(2)}, u32[]{:S(2)}) %collective-permute-start) | collective-permute-done | bytes 466976 | tf_op jit(solution)/shard_map/ppermute | solution.py:960
  32.4 16.2 %collective-permute-done.1.refs_8_.refs_11_ = bf16[304,768]{1,0:T(8,128)(2,1)S(1)} collective-permute-done((bf16[304,768]{1,0:T(8,128)(2,1)}, bf16[304,768]{1,0:T(8,128)(2,1)S(1)}, u32[]{:S(2)}, u32[]{:S(2)}) %collective-permute-start.1) | collective-permute-done | bytes 466976 | tf_op jit(solution)/shard_map/ppermute | solution.py:960
  48.7 8.3 %collective-permute-done.2.refs_9_.refs_12_ = bf16[304,768]{1,0:T(8,128)(2,1)S(1)} collective-permute-done((bf16[304,768]{1,0:T(8,128)(2,1)}, bf16[304,768]{1,0:T(8,128)(2,1)S(1)}, u32[]{:S(2)}, u32[]{:S(2)}) %collective-permute-start.2) | collective-permute-done | bytes 466976 | tf_op jit(solution)/shard_map/ppermute | solution.py:960
  57.0 0.7 copy-done.8
  57.7 4.5 %all-to-all-start.1 = ((bf16[4,192,1536]{2,1,0:T(8,128)(2,1)}), bf16[4,192,1536]{2,1,0:T(8,128)(2,1)}, u32[]{:S(2)}, u32[]{:S(2)}) async-start(bf16[4,192,1536]{2,1,0:T(8,128)(2,1)} %get-tuple-element.89), calls=%async_computation.1 | async-start | bytes 4718592 | tf_op jit(solution)/shard_map/all_to_all | solution.py:854
  62.3 0.5 collective-permute-start.8
  62.9 0.4 collective-permute-start.6
  63.3 0.9 slice.30
  64.3 0.6 collective-permute-start.5
  64.9 0.4 collective-permute-start.10
  65.3 0.5 collective-permute-done.9.refs_13_.refs_16_
  65.8 0.7 collective-permute-done.6.refs_10_.refs_13_
  66.5 25.0 %near_sources.1 = (bf16[768,1536]{1,0:T(8,128)(2,1)}, bf16[768,384]{1,0:T(8,128)(2,1)}, bf16[768,768]{1,0:T(8,128)(2,1)}, bf16[256,1536]{1,0:T(8,128)(2,1)}, bf1...) custom-call(s32[4,8]{1,0:T(4,128)} %bitcast.35, ...), custom_call_target="tpu_custom_call" | custom-call | flops 1 | bytes 1 | tf_op jit(solution)/shard_map/near_sources/pallas_call | solution.py:287
  91.4 0.6 collective-permute-start.11
  92.1 1.4 collective-permute-start.12
  93.5 16.0 %far_source.1 = (bf16[256,1536]{1,0:T(8,128)(2,1)}, bf16[4,304,768]{2,1,0:T(8,128)(2,1)}, bf16[4,304,768]{2,1,0:T(8,128)(2,1)}, bf16[256,384]{1,0:T(8,128)(2,1)}...) custom-call(s32[4,8]{1,0:T(4,128)} %bitcast.36, ...), custom_call_target="tpu_custom_call", output_to_operand_aliasing={{3}: (18, {}), {4}: (19, {}), {5}: (20, {}), {6}: (21, {})} | custom-call | flops 1 | bytes 1 | tf_op jit(solution)/shard_map/far_source/pallas_call | solution.py:431
  109.5 1.9 collective-permute-done.11.refs_1_
  111.4 0.3 collective-permute-done.12.refs_2_
  111.7 4.2 %collective-permute-done.13.got_hbm = bf16[4,304,768]{2,1,0:T(8,128)(2,1)} collective-permute-done((bf16[4,304,768]{2,1,0:T(8,128)(2,1)}, bf16[4,304,768]{2,1,0:T(8,128)(2,1)}, u32[]{:S(2)}, u32[]{:S(2)}) %collective-permute-start.13) | collective-permute-done | bytes 1867808 | tf_op jit(solution)/shard_map/ppermute | solution.py:960
  115.9 3.3 %add_cores.1 = (bf16[304,768]{1,0:T(8,128)(2,1)}, bf16[304,768]{1,0:T(8,128)(2,1)}, bf16[304,768]{1,0:T(8,128)(2,1)}, bf16[304,768]{1,0:T(8,128)(2,1)}) custom-call(bf16[4,304,768]{2,1,0:T(8,128)(2,1)} %get-tuple-element.92.keep_hbm, bf16[4,304,768]{2,1,0:T(8,128)(2,1)} %collective-permute-done.13.got_hbm), custom_call_target="tpu_custom_call" | custom-call | flops 1 | bytes 1 | tf_op jit(solution)/shard_map/add_cores/pallas_call | solution.py:783
  119.2 0.2 collective-permute-start.18
  119.4 1.5 collective-permute-start.19
  120.9 2.0 %collective-permute-start.14 = (bf16[304,768]{1,0:T(8,128)(2,1)}, bf16[304,768]{1,0:T(8,128)(2,1)S(1)}, u32[]{:S(2)}, u32[]{:S(2)}) collective-permute-start(bf16[304,768]{1,0:T(8,128)(2,1)} %get-tuple-element.94), channel_id=1, source_target_pairs={{0,2},{1,3},{2,0},{3,1},{4,6},{5,7},{6,4},{7,5},{8,10},{9,11},{10,... | collective-permute-start | bytes 1400840 | tf_op jit(solution)/shard_map/ppermute | solution.py:960
  122.8 1.4 collective-permute-start.15
  124.2 0.5 collective-permute-start.20
  124.7 19.2 %collective-permute-done.15.refs_5_ = bf16[256,384]{1,0:T(8,128)(2,1)S(1)} collective-permute-done((bf16[256,384]{1,0:T(8,128)(2,1)S(1)}, bf16[256,384]{1,0:T(8,128)(2,1)S(1)}, u32[]{:S(2)}, u32[]{:S(2)}) %collective-permute-start.15) | collective-permute-done | bytes 196640 | tf_op jit(solution)/shard_map/ppermute | solution.py:960
  143.9 1.5 collective-permute-start.21
  145.4 1.2 collective-permute-start.16
  146.6 1.7 collective-permute-start.17
  148.3 0.6 pad_clamp_fusion
  148.9 4.9 %frame_grad.1 = bf16[256,1536]{1,0:T(8,128)(2,1)} custom-call(bf16[256,1536]{1,0:T(8,128)(2,1)} %bitcast.26, bf16[256,1536]{1,0:T(8,128)(2,1)} %bitcast.31, f32[1,1536]{1,0:T(1,128)} %get-tuple-element.102.gain_ref, bf16[256,1536]{1,0:T(8,128)(2,1)} %get-tuple-element.103.refs_0_, bf16[256,1536]{1,0:T(8,128)(2,1)} %collective-permute-done.11.refs_1_, ...), custom_call_target="tpu_custom_call" | custom-call | flops 1 | bytes 1 | tf_op jit(solution)/shard_map/frame_grad/pallas_call | solution.py:654
  153.8 2.2 %collective-permute-done.16.refs_6_ = bf16[256,384]{1,0:T(8,128)(2,1)S(1)} collective-permute-done((bf16[256,384]{1,0:T(8,128)(2,1)}, bf16[256,384]{1,0:T(8,128)(2,1)S(1)}, u32[]{:S(2)}, u32[]{:S(2)}) %collective-permute-start.16) | collective-permute-done | bytes 196640 | tf_op jit(solution)/shard_map/ppermute | solution.py:960
  156.1 0.7 copy-done.13
  156.7 6.2 %encode.1 = bf16[256,1536]{1,0:T(8,128)(2,1)} custom-call(s32[4,8]{1,0:T(4,128)} %bitcast.37, bf16[256,1536]{1,0:T(8,128)(2,1)} %bitcast.27, bf16[512,1536]{1,0:T(8,128)(2,1)} %copy-done.4, bf16[512,1536]{1,0:T(8,128)(2,1)} %copy-done.5, bf16[256,1536]{1,0:T(8,128)(2,1)} %collective-permute-done.5.refs_0_.refs_3_, ...), custom_call_target="tpu_custom_call" | custom-call | flops 1 | bytes 1 | tf_op jit(solution)/shard_map/encode/pallas_call | solution.py:617
  163.0 3.5 %collective-permute-done.21.refs_3_ = bf16[304,768]{1,0:T(8,128)(2,1)} collective-permute-done((bf16[304,768]{1,0:T(8,128)(2,1)}, bf16[304,768]{1,0:T(8,128)(2,1)}, u32[]{:S(2)}, u32[]{:S(2)}) %collective-permute-start.21) | collective-permute-done | bytes 466976 | tf_op jit(solution)/shard_map/ppermute | solution.py:960
  166.5 2.4 %add_chips.1 = (bf16[304,384]{1,0:T(8,128)(2,1)}, bf16[304,384]{1,0:T(8,128)(2,1)}) custom-call(bf16[304,768]{1,0:T(8,128)(2,1)} %get-tuple-element.106.refs_0_, bf16[304,768]{1,0:T(8,128)(2,1)} %copy-done.10, bf16[304,768]{1,0:T(8,128)(2,1)} %collective-permute-done.20.refs_2_, bf16[304,768]{1,0:T(8,128)(2,1)} %collective-permute-done.21.refs_3_), custom_call_target="tpu_custom_call" | custom-call | flops 1 | bytes 1 | tf_op jit(solution)/shard_map/add_chips/pallas_call | solution.py:808
  168.8 2.1 %collective-permute-start.27 = (bf16[304,384]{1,0:T(8,128)(2,1)}, bf16[304,384]{1,0:T(8,128)(2,1)S(1)}, u32[]{:S(2)}, u32[]{:S(2)}) collective-permute-start(bf16[304,384]{1,0:T(8,128)(2,1)} %get-tuple-element.110.refs_0_), channel_id=1, source_target_pairs={{0,24},{8,16},{16,8},{24,0},{1,25},{9,17},{17,9},{25,1},{2,26},{10... | collective-permute-start | bytes 700424 | tf_op jit(solution)/shard_map/ppermute | solution.py:960
  171.0 0.6 collective-permute-start.26
  171.6 0.8 collective-permute-start.25
  172.4 0.7 slice_bitcast_fusion.3
  173.2 1.2 collective-permute-start.22
  174.4 1.5 collective-permute-start.23
  175.8 2.8 %collective-permute-done.27.refs_3_ = bf16[304,384]{1,0:T(8,128)(2,1)S(1)} collective-permute-done((bf16[304,384]{1,0:T(8,128)(2,1)}, bf16[304,384]{1,0:T(8,128)(2,1)S(1)}, u32[]{:S(2)}, u32[]{:S(2)}) %collective-permute-start.27) | collective-permute-done | bytes 233504 | tf_op jit(solution)/shard_map/ppermute | solution.py:960
  178.6 2.1 %collective-permute-start.24 = (bf16[304,384]{1,0:T(8,128)(2,1)}, bf16[304,384]{1,0:T(8,128)(2,1)S(1)}, u32[]{:S(2)}, u32[]{:S(2)}) collective-permute-start(bf16[304,384]{1,0:T(8,128)(2,1)} %get-tuple-element.109.refs_0_), channel_id=1, source_target_pairs={{0,24},{8,16},{16,8},{24,0},{1,25},{9,17},{17,9},{25,1},{2,26},{10... | collective-permute-start | bytes 700424 | tf_op jit(solution)/shard_map/ppermute | solution.py:960
  180.7 1.1 collective-permute-done.26.refs_2_
  181.8 1.8 collective-permute-done.25.refs_1_
  183.6 0.7 gather_fusion
  184.3 0.1 select_convert_fusion
  184.4 1.3 copy-done
  185.6 0.9 copy-done.2
  186.6 2.1 %unpack.2 = (f32[192,3072]{1,0:T(8,128)}, f32[192,1536]{1,0:T(8,128)}, f32[192,1]{1,0:T(8,128)S(1)}) custom-call(bf16[304,384]{1,0:T(8,128)(2,1)S(1)} %copy-done.2, bf16[304,384]{1,0:T(8,128)(2,1)S(1)} %collective-permute-done.25.refs_1_, bf16[304,384]{1,0:T(8,128)(2,1)S(1)} %collective-permute-done.26.refs_2_, ...), custom_call_target="tpu_custom_call" | custom-call | flops 1 | bytes 1 | tf_op jit(solution)/shard_map/unpack/pallas_call | solution.py:725
  188.8 0.1 reshape.67
  188.9 0.6 slice.47
  189.5 1.9 collective-permute-done.24.refs_3_
  191.4 2.7 %unpack.3 = (f32[192,3072]{1,0:T(8,128)}, f32[192,1536]{1,0:T(8,128)}, f32[1,192]{1,0:T(1,128)}) custom-call(bf16[304,384]{1,0:T(8,128)(2,1)S(1)} %copy-done.3, bf16[304,384]{1,0:T(8,128)(2,1)S(1)} %collective-permute-done.22.refs_1_, bf16[304,384]{1,0:T(8,128)(2,1)S(1)} %collective-permute-done.23.refs_2_, ...), custom_call_target="tpu_custom_call", output_to_operand_aliasing={{0}: (7, {}), {1}: (8, {})} | custom-call | flops 1 | bytes 1 | tf_op jit(solution)/shard_map/unpack/pallas_call | solution.py:725
  (60 shorter events, 0.4 us)
Async XLA Ops:
  2.0 8.6 %all-to-all-start = ((s32[4,1,8]{2,1,0:T(1,128)}), s32[4,1,8]{2,1,0:T(1,128)S(1)}, u32[]{:S(2)}, u32[]{:S(2)}) async-start(s32[4,1,8]{2,1,0:T(1,128)} %broadcast_in_dim.20), calls=%async_computation | async-start | bytes 4096 | tf_op jit(solution)/shard_map/all_to_all | solution.py:843
  10.6 47.1 %copy-start.15 = (s32[4,1,8]{2,1,0:T(1,128)}, s32[4,1,8]{2,1,0:T(1,128)S(1)}, u32[]{:S(2)}) copy-start(s32[4,1,8]{2,1,0:T(1,128)S(1)} %all-to-all-done) | copy-start | bytes 388
  10.6 46.4 %collective-permute-start.3 = (bf16[512,1536]{1,0:T(8,128)(2,1)}, bf16[512,1536]{1,0:T(8,128)(2,1)S(1)}, u32[]{:S(2)}, u32[]{:S(2)}) collective-permute-start(bf16[512,1536]{1,0:T(8,128)(2,1)} %get-tuple-element.66), channel_id=1, source_target_pairs={{0,8},{8,0},{16,24},{24,16},{1,9},{9,1},{17,25},{25,17},{2,10},{10... | collective-permute-start | bytes 4718600 | tf_op jit(solution)/shard_map/ppermute | solution.py:960
  12.7 44.3 %collective-permute-start.4 = (bf16[512,1536]{1,0:T(8,128)(2,1)}, bf16[512,1536]{1,0:T(8,128)(2,1)S(1)}, u32[]{:S(2)}, u32[]{:S(2)}) collective-permute-start(bf16[512,1536]{1,0:T(8,128)(2,1)} %get-tuple-element.66), channel_id=1, source_target_pairs={{0,16},{8,24},{16,0},{24,8},{1,17},{9,25},{17,1},{25,9},{2,18},{10... | collective-permute-start | bytes 4718600 | tf_op jit(solution)/shard_map/ppermute | solution.py:960
  14.2 18.3 %collective-permute-start = (bf16[304,768]{1,0:T(8,128)(2,1)}, bf16[304,768]{1,0:T(8,128)(2,1)S(1)}, u32[]{:S(2)}, u32[]{:S(2)}) collective-permute-start(bf16[304,768]{1,0:T(8,128)(2,1)} %get-tuple-element.69.refs_6_.refs_9_), channel_id=1, source_target_pairs={{0,2},{1,3},{2,0},{3,1},{4,6},{5,7},{6,4},{7,5},{8,10},{9,11},{10,... | collective-permute-start | bytes 1400840 | tf_op jit(solution)/shard_map/ppermute | solution.py:960
  14.6 34.1 %collective-permute-start.1 = (bf16[304,768]{1,0:T(8,128)(2,1)}, bf16[304,768]{1,0:T(8,128)(2,1)S(1)}, u32[]{:S(2)}, u32[]{:S(2)}) collective-permute-start(bf16[304,768]{1,0:T(8,128)(2,1)} %get-tuple-element.69.refs_6_.refs_9_), channel_id=1, source_target_pairs={{0,4},{1,5},{2,6},{3,7},{4,0},{5,1},{6,2},{7,3},{8,12},{9,13},{10,... | collective-permute-start | bytes 1400840 | tf_op jit(solution)/shard_map/ppermute | solution.py:960
  17.2 39.8 %collective-permute-start.2 = (bf16[304,768]{1,0:T(8,128)(2,1)}, bf16[304,768]{1,0:T(8,128)(2,1)S(1)}, u32[]{:S(2)}, u32[]{:S(2)}) collective-permute-start(bf16[304,768]{1,0:T(8,128)(2,1)} %get-tuple-element.69.refs_6_.refs_9_), channel_id=1, source_target_pairs={{0,6},{1,7},{2,4},{3,5},{4,2},{5,3},{6,0},{7,1},{8,14},{9,15},{10,... | collective-permute-start | bytes 1400840 | tf_op jit(solution)/shard_map/ppermute | solution.py:960
  32.4 24.5 %copy-start.6 = (bf16[304,768]{1,0:T(8,128)(2,1)}, bf16[304,768]{1,0:T(8,128)(2,1)S(1)}, u32[]{:S(2)}) copy-start(bf16[304,768]{1,0:T(8,128)(2,1)S(1)} %collective-permute-done.refs_7_.refs_10_) | copy-start | bytes 1400836
  48.7 8.3 %copy-start.7 = (bf16[304,768]{1,0:T(8,128)(2,1)}, bf16[304,768]{1,0:T(8,128)(2,1)S(1)}, u32[]{:S(2)}) copy-start(bf16[304,768]{1,0:T(8,128)(2,1)S(1)} %collective-permute-done.1.refs_8_.refs_11_) | copy-start | bytes 1400836
  57.0 0.8 copy-start.8
  57.0 6.4 %copy-start.4 = (bf16[512,1536]{1,0:T(8,128)(2,1)}, bf16[512,1536]{1,0:T(8,128)(2,1)S(1)}, u32[]{:S(2)}) copy-start(bf16[512,1536]{1,0:T(8,128)(2,1)S(1)} %collective-permute-done.3.refs_1_.refs_4_.refs_5_) | copy-start | bytes 4718596
  57.7 7.1 %copy-start.5 = (bf16[512,1536]{1,0:T(8,128)(2,1)}, bf16[512,1536]{1,0:T(8,128)(2,1)S(1)}, u32[]{:S(2)}) copy-start(bf16[512,1536]{1,0:T(8,128)(2,1)S(1)} %collective-permute-done.4.refs_2_.refs_5_.refs_6_) | copy-start | bytes 4718596
  57.7 54.0 %all-to-all-start.1 = ((bf16[4,192,1536]{2,1,0:T(8,128)(2,1)}), bf16[4,192,1536]{2,1,0:T(8,128)(2,1)}, u32[]{:S(2)}, u32[]{:S(2)}) async-start(bf16[4,192,1536]{2,1,0:T(8,128)(2,1)} %get-tuple-element.89), calls=%async_computation.1 | async-start | bytes 4718592 | tf_op jit(solution)/shard_map/all_to_all | solution.py:854
  62.2 2.6 %collective-permute-start.7 = (bf16[304,768]{1,0:T(8,128)(2,1)}, bf16[304,768]{1,0:T(8,128)(2,1)}, u32[]{:S(2)}, u32[]{:S(2)}) collective-permute-start(bf16[304,768]{1,0:T(8,128)(2,1)} %copy-done.6), channel_id=1, source_target_pairs={{0,1},{1,0},{2,3},{3,2},{4,5},{5,4},{6,7},{7,6},{8,9},{9,8},{10,11... | collective-permute-start | bytes 1400840 | tf_op jit(solution)/shard_map/ppermute | solution.py:960
  62.3 3.0 %collective-permute-start.8 = (bf16[304,768]{1,0:T(8,128)(2,1)}, bf16[304,768]{1,0:T(8,128)(2,1)}, u32[]{:S(2)}, u32[]{:S(2)}) collective-permute-start(bf16[304,768]{1,0:T(8,128)(2,1)} %copy-done.7), channel_id=1, source_target_pairs={{0,1},{1,0},{2,3},{3,2},{4,5},{5,4},{6,7},{7,6},{8,9},{9,8},{10,11... | collective-permute-start | bytes 1400840 | tf_op jit(solution)/shard_map/ppermute | solution.py:960
  62.8 3.0 %collective-permute-start.9 = (bf16[304,768]{1,0:T(8,128)(2,1)}, bf16[304,768]{1,0:T(8,128)(2,1)}, u32[]{:S(2)}, u32[]{:S(2)}) collective-permute-start(bf16[304,768]{1,0:T(8,128)(2,1)} %copy-done.8), channel_id=1, source_target_pairs={{0,1},{1,0},{2,3},{3,2},{4,5},{5,4},{6,7},{7,6},{8,9},{9,8},{10,11... | collective-permute-start | bytes 1400840 | tf_op jit(solution)/shard_map/ppermute | solution.py:960
  62.9 3.6 %collective-permute-start.6 = (bf16[304,768]{1,0:T(8,128)(2,1)}, bf16[304,768]{1,0:T(8,128)(2,1)}, u32[]{:S(2)}, u32[]{:S(2)}) collective-permute-start(bf16[304,768]{1,0:T(8,128)(2,1)} %get-tuple-element.69.refs_6_.refs_9_), channel_id=1, source_target_pairs={{0,1},{1,0},{2,3},{3,2},{4,5},{5,4},{6,7},{7,6},{8,9},{9,8},{10,11... | collective-permute-start | bytes 1400840 | tf_op jit(solution)/shard_map/ppermute | solution.py:960
  64.3 29.3 %collective-permute-start.5 = (bf16[256,1536]{1,0:T(8,128)(2,1)}, bf16[256,1536]{1,0:T(8,128)(2,1)}, u32[]{:S(2)}, u32[]{:S(2)}) collective-permute-start(bf16[256,1536]{1,0:T(8,128)(2,1)} %slice.30), channel_id=1, source_target_pairs={{0,16},{8,24},{16,0},{24,8},{1,17},{9,25},{17,1},{25,9},{2,18},{10... | collective-permute-start | bytes 2359304 | tf_op jit(solution)/shard_map/ppermute | solution.py:960
  64.9 28.6 %collective-permute-start.10 = (bf16[256,1536]{1,0:T(8,128)(2,1)S(1)}, bf16[256,1536]{1,0:T(8,128)(2,1)}, u32[]{:S(2)}, u32[]{:S(2)}) collective-permute-start(bf16[256,1536]{1,0:T(8,128)(2,1)S(1)} %slice.31), channel_id=1, source_target_pairs={{0,8},{8,0},{16,24},{24,16},{1,9},{9,1},{17,25},{25,17},{2,10},{10... | collective-permute-start | bytes 2359304 | tf_op jit(solution)/shard_map/ppermute | solution.py:960
  91.4 20.0 %collective-permute-start.11 = (bf16[256,1536]{1,0:T(8,128)(2,1)}, bf16[256,1536]{1,0:T(8,128)(2,1)}, u32[]{:S(2)}, u32[]{:S(2)}) collective-permute-start(bf16[256,1536]{1,0:T(8,128)(2,1)} %get-tuple-element.90), channel_id=1, source_target_pairs={{0,8},{8,0},{16,24},{24,16},{1,9},{9,1},{17,25},{25,17},{2,10},{10... | collective-permute-start | bytes 2359304 | tf_op jit(solution)/shard_map/ppermute | solution.py:960
  92.1 19.6 %collective-permute-start.12 = (bf16[256,1536]{1,0:T(8,128)(2,1)}, bf16[256,1536]{1,0:T(8,128)(2,1)}, u32[]{:S(2)}, u32[]{:S(2)}) collective-permute-start(bf16[256,1536]{1,0:T(8,128)(2,1)} %get-tuple-element.91), channel_id=1, source_target_pairs={{0,16},{8,24},{16,0},{24,8},{1,17},{9,25},{17,1},{25,9},{2,18},{10... | collective-permute-start | bytes 2359304 | tf_op jit(solution)/shard_map/ppermute | solution.py:960
  111.7 11.2 %copy-start.11 = (bf16[256,384]{1,0:T(8,128)(2,1)S(1)}, bf16[256,384]{1,0:T(8,128)(2,1)}, u32[]{:S(2)}) copy-start(bf16[256,384]{1,0:T(8,128)(2,1)} %get-tuple-element.97) | copy-start | bytes 589828
  111.7 4.2 %collective-permute-start.13 = (bf16[4,304,768]{2,1,0:T(8,128)(2,1)}, bf16[4,304,768]{2,1,0:T(8,128)(2,1)}, u32[]{:S(2)}, u32[]{:S(2)}) collective-permute-start(bf16[4,304,768]{2,1,0:T(8,128)(2,1)} %get-tuple-element.93), channel_id=1, source_target_pairs={{0,1},{1,0},{2,3},{3,2},{4,5},{5,4},{6,7},{7,6},{8,9},{9,8},{10,11... | collective-permute-start | bytes 5603336 | tf_op jit(solution)/shard_map/ppermute | solution.py:960
  119.2 36.9 %collective-permute-start.18 = (bf16[4,192,1536]{2,1,0:T(8,128)(2,1)}, bf16[4,192,1536]{2,1,0:T(8,128)(2,1)}, u32[]{:S(2)}, u32[]{:S(2)}) collective-permute-start(bf16[4,192,1536]{2,1,0:T(8,128)(2,1)} %all-to-all-done.1.refs_8_), channel_id=1, source_target_pairs={{0,1},{1,0},{2,3},{3,2},{4,5},{5,4},{6,7},{7,6},{8,9},{9,8},{10,11... | collective-permute-start | bytes 7077896 | tf_op jit(solution)/shard_map/ppermute | solution.py:960
  119.4 27.3 %collective-permute-start.19 = (bf16[256,1536]{1,0:T(8,128)(2,1)}, bf16[256,1536]{1,0:T(8,128)(2,1)S(1)}, u32[]{:S(2)}, u32[]{:S(2)}) collective-permute-start(bf16[256,1536]{1,0:T(8,128)(2,1)} %get-tuple-element.104), channel_id=1, source_target_pairs={{0,24},{8,16},{16,8},{24,0},{1,25},{9,17},{17,9},{25,1},{2,26},{10... | collective-permute-start | bytes 2359304 | tf_op jit(solution)/shard_map/ppermute | solution.py:960
  120.9 24.6 %collective-permute-start.14 = (bf16[304,768]{1,0:T(8,128)(2,1)}, bf16[304,768]{1,0:T(8,128)(2,1)S(1)}, u32[]{:S(2)}, u32[]{:S(2)}) collective-permute-start(bf16[304,768]{1,0:T(8,128)(2,1)} %get-tuple-element.94), channel_id=1, source_target_pairs={{0,2},{1,3},{2,0},{3,1},{4,6},{5,7},{6,4},{7,5},{8,10},{9,11},{10,... | collective-permute-start | bytes 1400840 | tf_op jit(solution)/shard_map/ppermute | solution.py:960
  122.8 21.1 %collective-permute-start.15 = (bf16[256,384]{1,0:T(8,128)(2,1)S(1)}, bf16[256,384]{1,0:T(8,128)(2,1)S(1)}, u32[]{:S(2)}, u32[]{:S(2)}) collective-permute-start(bf16[256,384]{1,0:T(8,128)(2,1)S(1)} %copy-done.11), channel_id=1, source_target_pairs={{0,8},{8,0},{16,24},{24,16},{1,9},{9,1},{17,25},{25,17},{2,10},{10... | collective-permute-start | bytes 589832 | tf_op jit(solution)/shard_map/ppermute | solution.py:960
  124.2 38.7 %collective-permute-start.20 = (bf16[304,768]{1,0:T(8,128)(2,1)}, bf16[304,768]{1,0:T(8,128)(2,1)}, u32[]{:S(2)}, u32[]{:S(2)}) collective-permute-start(bf16[304,768]{1,0:T(8,128)(2,1)} %get-tuple-element.107), channel_id=1, source_target_pairs={{0,4},{1,5},{2,6},{3,7},{4,0},{5,1},{6,2},{7,3},{8,12},{9,13},{10,... | collective-permute-start | bytes 1400840 | tf_op jit(solution)/shard_map/ppermute | solution.py:960
  143.9 4.4 %copy-start.12 = (bf16[256,384]{1,0:T(8,128)(2,1)}, bf16[256,384]{1,0:T(8,128)(2,1)S(1)}, u32[]{:S(2)}) copy-start(bf16[256,384]{1,0:T(8,128)(2,1)S(1)} %collective-permute-done.15.refs_5_) | copy-start | bytes 589828
  143.9 22.6 %collective-permute-start.21 = (bf16[304,768]{1,0:T(8,128)(2,1)}, bf16[304,768]{1,0:T(8,128)(2,1)}, u32[]{:S(2)}, u32[]{:S(2)}) collective-permute-start(bf16[304,768]{1,0:T(8,128)(2,1)} %get-tuple-element.108), channel_id=1, source_target_pairs={{0,6},{1,7},{2,4},{3,5},{4,2},{5,3},{6,0},{7,1},{8,14},{9,15},{10,... | collective-permute-start | bytes 1400840 | tf_op jit(solution)/shard_map/ppermute | solution.py:960
  145.4 1.2 copy-start.10
  145.4 10.6 %collective-permute-start.16 = (bf16[256,384]{1,0:T(8,128)(2,1)}, bf16[256,384]{1,0:T(8,128)(2,1)S(1)}, u32[]{:S(2)}, u32[]{:S(2)}) collective-permute-start(bf16[256,384]{1,0:T(8,128)(2,1)} %get-tuple-element.98), channel_id=1, source_target_pairs={{0,16},{8,24},{16,0},{24,8},{1,17},{9,25},{17,1},{25,9},{2,18},{10... | collective-permute-start | bytes 589832 | tf_op jit(solution)/shard_map/ppermute | solution.py:960
  146.6 2.3 %copy-start.9 = (bf16[256,1536]{1,0:T(8,128)(2,1)}, bf16[256,1536]{1,0:T(8,128)(2,1)S(1)}, u32[]{:S(2)}) copy-start(bf16[256,1536]{1,0:T(8,128)(2,1)S(1)} %collective-permute-done.19.refs_3_) | copy-start | bytes 2359300
  146.6 9.4 %collective-permute-start.17 = (bf16[256,384]{1,0:T(8,128)(2,1)}, bf16[256,384]{1,0:T(8,128)(2,1)}, u32[]{:S(2)}, u32[]{:S(2)}) collective-permute-start(bf16[256,384]{1,0:T(8,128)(2,1)} %get-tuple-element.99), channel_id=1, source_target_pairs={{0,24},{8,16},{16,8},{24,0},{1,25},{9,17},{17,9},{25,1},{2,26},{10... | collective-permute-start | bytes 589832 | tf_op jit(solution)/shard_map/ppermute | solution.py:960
  156.1 0.7 copy-start.13
  162.9 8.0 %copy-start.16 = (bf16[192]{0:T(256)(128)(2,1)S(1)}, bf16[192]{0:T(256)(128)(2,1)}, u32[]{:S(2)}) copy-start(bf16[192]{0:T(256)(128)(2,1)} %gain_ref.1) | copy-start | bytes 1156
  168.8 22.5 %copy-start.3 = (bf16[304,384]{1,0:T(8,128)(2,1)S(1)}, bf16[304,384]{1,0:T(8,128)(2,1)}, u32[]{:S(2)}) copy-start(bf16[304,384]{1,0:T(8,128)(2,1)} %get-tuple-element.109.refs_0_) | copy-start | bytes 700420
  168.8 9.8 %collective-permute-start.27 = (bf16[304,384]{1,0:T(8,128)(2,1)}, bf16[304,384]{1,0:T(8,128)(2,1)S(1)}, u32[]{:S(2)}, u32[]{:S(2)}) collective-permute-start(bf16[304,384]{1,0:T(8,128)(2,1)} %get-tuple-element.110.refs_0_), channel_id=1, source_target_pairs={{0,24},{8,16},{16,8},{24,0},{1,25},{9,17},{17,9},{25,1},{2,26},{10... | collective-permute-start | bytes 700424 | tf_op jit(solution)/shard_map/ppermute | solution.py:960
  171.0 10.8 %collective-permute-start.26 = (bf16[304,384]{1,0:T(8,128)(2,1)}, bf16[304,384]{1,0:T(8,128)(2,1)S(1)}, u32[]{:S(2)}, u32[]{:S(2)}) collective-permute-start(bf16[304,384]{1,0:T(8,128)(2,1)} %get-tuple-element.110.refs_0_), channel_id=1, source_target_pairs={{0,16},{8,24},{16,0},{24,8},{1,17},{9,25},{17,1},{25,9},{2,18},{10... | collective-permute-start | bytes 700424 | tf_op jit(solution)/shard_map/ppermute | solution.py:960
  171.6 12.0 %collective-permute-start.25 = (bf16[304,384]{1,0:T(8,128)(2,1)}, bf16[304,384]{1,0:T(8,128)(2,1)S(1)}, u32[]{:S(2)}, u32[]{:S(2)}) collective-permute-start(bf16[304,384]{1,0:T(8,128)(2,1)} %get-tuple-element.110.refs_0_), channel_id=1, source_target_pairs={{0,8},{8,0},{16,24},{24,16},{1,9},{9,1},{17,25},{25,17},{2,10},{10... | collective-permute-start | bytes 700424 | tf_op jit(solution)/shard_map/ppermute | solution.py:960
  173.2 16.3 %collective-permute-start.22 = (bf16[304,384]{1,0:T(8,128)(2,1)}, bf16[304,384]{1,0:T(8,128)(2,1)S(1)}, u32[]{:S(2)}, u32[]{:S(2)}) collective-permute-start(bf16[304,384]{1,0:T(8,128)(2,1)} %get-tuple-element.109.refs_0_), channel_id=1, source_target_pairs={{0,8},{8,0},{16,24},{24,16},{1,9},{9,1},{17,25},{25,17},{2,10},{10... | collective-permute-start | bytes 700424 | tf_op jit(solution)/shard_map/ppermute | solution.py:960
  174.4 15.1 %collective-permute-start.23 = (bf16[304,384]{1,0:T(8,128)(2,1)}, bf16[304,384]{1,0:T(8,128)(2,1)S(1)}, u32[]{:S(2)}, u32[]{:S(2)}) collective-permute-start(bf16[304,384]{1,0:T(8,128)(2,1)} %get-tuple-element.109.refs_0_), channel_id=1, source_target_pairs={{0,16},{8,24},{16,0},{24,8},{1,17},{9,25},{17,1},{25,9},{2,18},{10... | collective-permute-start | bytes 700424 | tf_op jit(solution)/shard_map/ppermute | solution.py:960
  178.6 12.7 %collective-permute-start.24 = (bf16[304,384]{1,0:T(8,128)(2,1)}, bf16[304,384]{1,0:T(8,128)(2,1)S(1)}, u32[]{:S(2)}, u32[]{:S(2)}) collective-permute-start(bf16[304,384]{1,0:T(8,128)(2,1)} %get-tuple-element.109.refs_0_), channel_id=1, source_target_pairs={{0,24},{8,16},{16,8},{24,0},{1,25},{9,17},{17,9},{25,1},{2,26},{10... | collective-permute-start | bytes 700424 | tf_op jit(solution)/shard_map/ppermute | solution.py:960
  184.4 1.3 copy-start
  185.6 0.9 copy-start.2
  186.6 4.8 %copy-start.1 = (bf16[192,3072]{1,0:T(8,128)(2,1)S(1)}, bf16[192,3072]{1,0:T(8,128)(2,1)}, u32[]{:S(2)}) copy-start(bf16[192,3072]{1,0:T(8,128)(2,1)} %refs_4_.3) | copy-start | bytes 3538948
  188.9 5.2 %copy-start.14 = (f32[192,32]{0,1:T(8,128)}, f32[192,32]{0,1:T(8,128)S(1)}, u32[]{:S(2)}) copy-start(f32[192,32]{0,1:T(8,128)S(1)} %reshape.67) | copy-start | bytes 73732

commit v6 on v5

--- a/solution.py
+++ b/solution.py
@@ -23,19 +23,14 @@
 LIGHT = pl.CostEstimate(flops=1, bytes_accessed=1, transcendentals=0)
 
 
-def route(dims, refs, meta, s, base):
+def route(dims, sw, meta, s, base, targets, sems):
     count, length, taps = dims
-    source = lax.axis_index("dp") ^ s
+    me = lax.axis_index("dp")
     copies = []
-    for q in range(count):
-        chosen = base + length * meta[source, count + (lax.axis_index("dp") ^ q)]
-        copies.append(
-            pltpu.make_async_copy(
-                refs["sw"].at[pl.ds(pl.multiple_of(chosen, length), length)],
-                refs["pieces"][q].at[pl.ds(pl.multiple_of(s * length, length), length)],
-                refs["route_sems"].at[s, q],
-            )
-        )
+    for i, (q, target) in enumerate(targets):
+        chosen = base + length * meta[me ^ s, count + (me ^ q)]
+        source = sw.at[pl.ds(pl.multiple_of(chosen, length), length)]
+        copies.append(pltpu.make_async_copy(source, target, sems.at[i]))
     return copies
 
 
@@ -48,7 +43,7 @@
     channels = wide // 2
     tiles = channels // LANES
     own = pl.ds(base, rows)
-    step = 64
+    step = 256
     ready("we")
     gain = refs["gain"][...]
     ready("x")
@@ -87,7 +82,7 @@
             sw[out, lanes] = jnp.where(live, conv * sig, 0.0).astype(BF16)
             slope[u, tile] = jnp.where(live, sig * (1.0 + conv * (1.0 - sig)), 0.0)
 
-    for copy in route(dims, refs, meta, s, base):
+    for copy in refs["route"](s, base):
         copy.start()
 
     ready("g")
@@ -206,10 +201,10 @@
     count, length, taps = dims
     rows = count * length
     x_hbm, g_hbm, refs = refs[:n], refs[n : 2 * n], refs[2 * n :]
-    outs = refs[-24 - n - count : -19]
-    blocks = refs[: -24 - n - count]
+    outs = refs[-24 - n : -19]
+    blocks = refs[: -24 - n]
     normed_hbm, sw_hbm, ge_hbm = outs[:3]
-    gn_hbm, small, gain_ref, pieces = outs[3 : 3 + n], outs[3 + n], outs[4 + n], outs[5 + n :]
+    gn_hbm, small, gain_ref = outs[3 : 3 + n], outs[3 + n], outs[4 + n]
     x, normed, g, sw, ge, gn, ab, pad, gpad, slope = refs[-19:-9]
     we, wp, shares, taps_ref, weight_sems = refs[-9:-4]
     in_sems, out_sems, route_sems, _ = refs[-4:]
@@ -239,7 +234,7 @@
     small[...] = jnp.zeros_like(small)
     views = dict(
         x=x, normed=normed, g=g, we=we, wp=wp, sw=sw, ge=ge, gn=gn, ab=ab, pad=pad, gpad=gpad,
-        slope=slope, taps=taps_ref, gain=gain_ref, small=small, pieces=pieces, route_sems=route_sems,
+        slope=slope, taps=taps_ref, gain=gain_ref, small=small, route=lambda s, base: [],
     )
 
     @pl.loop(0, n)
@@ -271,9 +266,7 @@
     for s in range(n):
         for i, (source, target) in enumerate(((normed, normed_hbm), (sw, sw_hbm), (ge, ge_hbm))):
             move(source.at[place(s)], target.at[place(s)], out_sems.at[s, i]).wait()
-        move(gn.at[place(s)], gn_hbm[s], out_sems.at[s, 3]).wait()
-        for copy in route(dims, views, meta, s, s * rows):
-            copy.wait()
+        move(gn.at[place(s)], gn_hbm[s].at[pl.ds(0, rows)], out_sems.at[s, 3]).wait()
 
 
 def near_call(ints, xs, gs, blocks, owned, dims):
@@ -295,10 +288,9 @@
         + (
             jax.ShapeDtypeStruct((channels // LANES, taps + 1, 8, LANES), F32),
             jax.ShapeDtypeStruct((1, width), F32),
-        )
-        + (jax.ShapeDtypeStruct((rows, channels), BF16),) * count,
+        ),
         in_specs=[in_smem()] + [anywhere] * (2 * n + owners),
-        out_specs=(anywhere,) * (3 + n) + (in_vmem(), in_vmem()) + (anywhere,) * count,
+        out_specs=(anywhere,) * (3 + n) + (in_vmem(), in_vmem()),
         scratch_shapes=[
             pltpu.VMEM((n * rows, width), BF16),
             pltpu.VMEM((n * rows, width), BF16),
@@ -327,8 +319,8 @@
     core = lax.axis_index("shard") % 2
     x_hbm, normed_hbm, sw_hbm, ge_hbm = refs[:4]
     g_hbm, near_small = refs[4 : 5 + n], refs[5 + n]
-    blocks, outs, refs = refs[6 + n : -25 - 2 * count], refs[-25 - count : -22], refs[-22:]
-    gn_hbm, keep_hbm, give_hbm, pieces = outs[0], outs[1], outs[2], outs[3:]
+    blocks, outs, refs = refs[6 + n : -25 - n], refs[-25 - n : -22], refs[-22:]
+    gn_hbm, keep_hbm, give_hbm, own_hbm, single_hbm = *outs[:4], outs[4:]
     x, normed, g, sw, ge, gn, ab, pad, gpad, slope = refs[:10]
     we, wp, shares, taps_ref, weight_sems = refs[10:15]
     gain_ref, small, block, in_sems, out_sems, route_sems, _ = refs[15:]
@@ -369,27 +361,32 @@
 
     clear_margins(pad, gpad)
     small[...] = near_small[...]
+
+    def pieces(s, base):
+        cols = pl.ds(s * channels, channels)
+        targets = [(0, own_hbm.at[:, cols]), (n, gn_hbm.at[pl.ds(rows, length), cols])]
+        targets += [(1 + i, ref.at[:, cols]) for i, ref in enumerate(single_hbm)]
+        return route(dims, sw, meta, s, base, targets, route_sems.at[s])
+
     views = dict(
         x=x, normed=normed, g=g, we=we, wp=wp, sw=sw, ge=ge, gn=gn, ab=ab, pad=pad, gpad=gpad,
-        slope=slope, taps=taps_ref, gain=gain_ref, small=small, pieces=pieces, route_sems=route_sems,
+        slope=slope, taps=taps_ref, gain=gain_ref, small=small, route=pieces,
     )
     one_source(dims, views, meta, n, base, ready)
-    gn_out = move(gn.at[last], gn_hbm, out_sems.at[2])
+    gn_out = move(gn.at[last], gn_hbm.at[pl.ds(0, rows)], out_sems.at[0])
     gn_out.start()
-    routed = route(dims, views, meta, n, base)
+    routed = pieces(n, base)
     for copy in later:
         copy.wait()
+    for s in range(n):
+        for copy in pieces(s, s * rows):
+            copy.start()
+            routed.append(copy)
 
     sums = jnp.sum(small[...], axis=2)
     sums = jnp.concatenate([sums[tile] for tile in range(tiles)], axis=1)
     span = 2 * owned
     bottom = owned + halves * part
-    for chip in range(chips):
-        total = lax.dot_general(
-            normed[:, chip * span : (chip + 1) * span], ge[...], TN, preferred_element_type=F32
-        ).astype(BF16)
-        for which in range(2):
-            block[which, chip, :owned] = total[which * owned : (which + 1) * owned]
     for h in range(halves):
         total = lax.dot_general(
             sw[...], g[:, h * wide : (h + 1) * wide], TN, preferred_element_type=F32
@@ -404,17 +401,23 @@
         table = sums[:, owner * part : (owner + 1) * part]
         line = jnp.concatenate([table[:16], fill, table[16:], fill, blank], axis=1)
         block[owner % 2, owner // 2, bottom:] = line.astype(BF16)
-    outward = [
-        move(block.at[1 - core], give_hbm, out_sems.at[0]),
-        move(block.at[core], keep_hbm, out_sems.at[1]),
-    ]
-    for copy in outward:
-        copy.start()
+    outward = []
+    for chip in range(chips):
+        total = lax.dot_general(
+            normed[:, chip * span : (chip + 1) * span], ge[...], TN, preferred_element_type=F32
+        ).astype(BF16)
+        for which in range(2):
+            block[which, chip, :owned] = total[which * owned : (which + 1) * owned]
+        for i, (which, target) in enumerate(((1 - core, give_hbm), (core, keep_hbm))):
+            outward.append(
+                move(block.at[which, chip], target.at[chip], out_sems.at[1 + 2 * chip + i])
+            )
+            outward[-1].start()
     for copy in outward + routed + [gn_out]:
         copy.wait()
 
 
-def far_call(ints, x, near, gs, blocks, before, owned, dims):
+def far_call(ints, x, near, gs, blocks, owned, dims):
     count, length, taps = dims
     n = len(gs) - 1
     rows = count * length
@@ -430,12 +433,12 @@
     every = (n + 1) * rows
     return pl.pallas_call(
         functools.partial(far_kernel, dims, n, owned),
-        out_shape=(jax.ShapeDtypeStruct((rows, width), BF16),)
+        out_shape=(jax.ShapeDtypeStruct((rows + length, width), BF16),)
         + (jax.ShapeDtypeStruct((chips, height, wide), BF16),) * 2
-        + (jax.ShapeDtypeStruct(before[0].shape, BF16),) * count,
-        in_specs=[in_smem()] + [anywhere] * (5 + n) + [in_vmem()] + [anywhere] * (owners + count),
-        out_specs=(anywhere,) * (3 + count),
-        input_output_aliases={7 + n + owners + m: 3 + m for m in range(count)},
+        + (jax.ShapeDtypeStruct((length, width), BF16),)
+        + (jax.ShapeDtypeStruct((length, width), BF16),) * (n - 1),
+        in_specs=[in_smem()] + [anywhere] * (5 + n) + [in_vmem()] + [anywhere] * owners,
+        out_specs=(anywhere,) * (3 + n),
         scratch_shapes=[
             pltpu.VMEM((every, width), BF16),
             pltpu.VMEM((every, width), BF16),
@@ -451,14 +454,14 @@
             pltpu.VMEM((tiles, taps + 1, 8, LANES), F32),
             pltpu.VMEM((2, chips, height, wide), BF16),
             pltpu.SemaphoreType.DMA((7 + n,)),
-            pltpu.SemaphoreType.DMA((3,)),
+            pltpu.SemaphoreType.DMA((1 + 2 * chips,)),
             pltpu.SemaphoreType.DMA((n + 1, count)),
             pltpu.SemaphoreType.DMA,
         ],
         compiler_params=vmem_params(VMEM_CHUNK),
         cost_estimate=LIGHT,
         name="far_source",
-    )(ints, x, normed, sw, ge, *gs, small, *blocks, *before)
+    )(ints, x, normed, sw, ge, *gs, small, *blocks)
 
 
 def vmem_params(mib):
@@ -481,8 +484,8 @@
     pack_ref, both_hbm, copies_hbm, both, expand_ref, whole, sems = refs
     rows_in = x_hbm.shape[0]
     inward = [
-        pltpu.make_async_copy(x_hbm, both.at[pl.ds(0, rows_in)], sems.at[2]),
-        pltpu.make_async_copy(g_hbm, both.at[pl.ds(rows_in, rows_in)], sems.at[3]),
+        pltpu.make_async_copy(x_hbm, both.at[pl.ds(0, rows_in)], sems.at[2, 0]),
+        pltpu.make_async_copy(g_hbm, both.at[pl.ds(rows_in, rows_in)], sems.at[3, 0]),
     ]
     owned, width = project_hbm.shape
     wide = pack_ref.shape[1]
@@ -492,8 +495,8 @@
     rows = pl.ds(pl.multiple_of(index * part, part), part)
     chips = copies_hbm.shape[0]
     copies = [
-        pltpu.make_async_copy(expand_hbm, expand_ref, sems.at[0]),
-        pltpu.make_async_copy(project_hbm, whole, sems.at[1]),
+        pltpu.make_async_copy(expand_hbm, expand_ref, sems.at[0, 0]),
+        pltpu.make_async_copy(project_hbm, whole, sems.at[1, 0]),
     ]
     for copy in inward + copies:
         copy.start()
@@ -518,13 +521,20 @@
     ).astype(BF16)
     for copy in inward:
         copy.wait()
-    outward = [pltpu.make_async_copy(both, both_hbm, sems.at[4])]
+    outward = [pltpu.make_async_copy(both, both_hbm, sems.at[4, 0])]
     outward[0].start()
     for copy in copies:
         copy.wait()
     for i in range(chips):
-        outward.append(pltpu.make_async_copy(whole, copies_hbm.at[i], sems.at[5 + i]))
-        outward[-1].start()
+        for k in range(1, owned // part):
+            outward.append(
+                pltpu.make_async_copy(
+                    whole.at[pl.ds(pl.multiple_of((index ^ k) * part, part), part)],
+                    copies_hbm.at[i, pl.ds((k - 1) * part, part)],
+                    sems.at[5 + i, k],
+                )
+            )
+            outward[-1].start()
     block = whole[rows, :]
     for h in range(2):
         pack_ref[:owned, h * channels : (h + 1) * channels] = jnp.dot(
@@ -547,7 +557,7 @@
         out_shape=(
             jax.ShapeDtypeStruct((height, wide), BF16),
             jax.ShapeDtypeStruct((2 * rows, width), BF16),
-            jax.ShapeDtypeStruct((chips, owned, width), BF16),
+            jax.ShapeDtypeStruct((chips, owned - part, width), BF16),
         ),
         in_specs=[anywhere] * 2 + [in_vmem()] * 3 + [anywhere] * 2,
         out_specs=(in_vmem(), anywhere, anywhere),
@@ -555,7 +565,7 @@
             pltpu.VMEM((2 * rows, width), BF16),
             pltpu.VMEM(expand_weight.shape, BF16),
             pltpu.VMEM((owned, width), BF16),
-            pltpu.SemaphoreType.DMA((5 + chips,)),
+            pltpu.SemaphoreType.DMA((5 + chips, owned // part)),
         ],
         compiler_params=vmem_params(VMEM_PACK),
         cost_estimate=LIGHT,
@@ -566,10 +576,10 @@
 def encode_kernel(dims, meta, *refs):
     n, length, owned = dims
     frames = refs[:n]
-    pieces, blocks, refs = refs[n : 2 * n], refs[2 * n : 2 * n + 2], refs[2 * n + 2 :]
-    out_ref, cat, weight, residual, sems = refs
+    pieces, below, blocks = refs[n : 2 * n - 1], refs[2 * n - 1], refs[2 * n : 2 * n + 2]
+    packs, (out_ref, cat, weight, residual, sems) = refs[2 * n + 2 : -5], refs[-5:]
     shard = lax.axis_index("shard")
-    channels = pieces[0].shape[1]
+    channels = cat.shape[1] // n
     part = owned // n
     me = lax.axis_index("dp")
 
@@ -580,9 +590,17 @@
     for which, block in enumerate(blocks):
         for chip in range(block.shape[0]):
             owner = 2 * chip + ((shard % 2) ^ which)
-            for i in range(n):
-                start = pl.multiple_of(i * channels + owner * part, part)
-                moves.append((block.at[chip, pl.ds(i * part, part)], weight.at[pl.ds(start, part)]))
+            for k in range(1, n):
+                start = pl.multiple_of((me ^ k) * channels + owner * part, part)
+                source = block.at[chip, pl.ds((k - 1) * part, part)]
+                moves.append((source, weight.at[pl.ds(start, part)]))
+    wide = packs[0].shape[1]
+    for b, block in enumerate(packs):
+        owner = shard ^ (2 * (b % (len(packs) // 2)) + b // (len(packs) // 2))
+        start = pl.multiple_of(me * channels + owner * part, part)
+        for h in range(weight.shape[1] // wide):
+            source = block.at[pl.ds(owned + h * part, part)]
+            moves.append((source, weight.at[pl.ds(start, part), pl.ds(h * wide, wide)]))
     for k in range(n):
         moves.append(
             (
@@ -593,7 +611,11 @@
     for m in range(n):
         lanes = pl.ds(pl.multiple_of((me ^ m) * channels, channels), channels)
         for k in range(n):
-            source = pieces[m].at[pl.ds(k * length, length)]
+            cols = pl.ds(k * channels, channels)
+            if m < n - 1:
+                source = pieces[m].at[:, cols]
+            else:
+                source = below.at[pl.ds(n * length, length), cols]
             moves.append((source, cat.at[rows(me ^ m ^ k, length), lanes]))
     copies = [
         pltpu.make_async_copy(source, target, sems.at[i])
@@ -610,25 +632,27 @@
         out_ref[:, cols] = (residual[:, cols].astype(F32) + term).astype(BF16)
 
 
-def encode_call(ints, pieces, frames, blocks, length):
+def encode_call(ints, pieces, below, frames, blocks, packs, length):
     n = len(frames)
-    owned, width = blocks[0].shape[1:]
+    width = blocks[0].shape[2]
+    owned = width // len(packs)
+    halves = width // packs[0].shape[1]
     anywhere = pl.BlockSpec(memory_space=pl.ANY)
     return pl.pallas_call(
         functools.partial(encode_kernel, (n, length, owned)),
         out_shape=jax.ShapeDtypeStruct((n * length, width), BF16),
-        in_specs=[in_smem()] + [anywhere] * (2 * n + len(blocks)),
+        in_specs=[in_smem()] + [anywhere] * (2 * n + len(blocks) + len(packs)),
         out_specs=in_vmem(),
         scratch_shapes=[
             pltpu.VMEM((n * length, width), BF16),
             pltpu.VMEM((width, width), BF16),
             pltpu.VMEM((n * length, width), BF16),
-            pltpu.SemaphoreType.DMA((width // owned * n + n + n * n,)),
+            pltpu.SemaphoreType.DMA((len(packs) * (n - 1 + halves) + n + n * n,)),
         ],
         compiler_params=vmem_params(VMEM_ENCODE),
         cost_estimate=LIGHT,
         name="encode",
-    )(ints, *frames, *pieces, *blocks)
+    )(ints, *frames, *pieces, below, *blocks, *packs)
 
 
 def frame_grad_kernel(n, x_ref, g_ref, gain_ref, *refs):
@@ -760,21 +784,26 @@
     n = len(refs) - 3
     outs, (keep, got, sems) = refs[:n], refs[n:]
     chip = lax.axis_index("shard") // 2
-    copies = [
+    move = pltpu.make_async_copy
+    order = list(range(1, n)) + [0]
+    inward = [
         (
-            pltpu.make_async_copy(keep_hbm.at[chip ^ m], keep.at[m], sems.at[m, 0]),
-            pltpu.make_async_copy(got_hbm.at[chip ^ m], got.at[m], sems.at[m, 1]),
+            move(keep_hbm.at[chip ^ m], keep.at[m], sems.at[m, 0]),
+            move(got_hbm.at[chip ^ m], got.at[m], sems.at[m, 1]),
         )
         for m in range(n)
     ]
-    order = list(range(1, n)) + [0]
+    outward = [move(keep.at[m], outs[m], sems.at[m, 2]) for m in range(n)]
     for m in order:
-        for copy in copies[m]:
+        for copy in inward[m]:
             copy.start()
     for m in order:
-        for copy in copies[m]:
+        for copy in inward[m]:
             copy.wait()
-        outs[m][...] = (keep[m].astype(F32) + got[m].astype(F32)).astype(BF16)
+        keep[m] = (keep[m].astype(F32) + got[m].astype(F32)).astype(BF16)
+        outward[m].start()
+    for copy in outward:
+        copy.wait()
 
 
 def add_cores(keep, got):
@@ -784,11 +813,11 @@
         add_cores_kernel,
         out_shape=(jax.ShapeDtypeStruct(keep.shape[1:], BF16),) * n,
         in_specs=[anywhere] * 2,
-        out_specs=(in_vmem(),) * n,
+        out_specs=(anywhere,) * n,
         scratch_shapes=[
             pltpu.VMEM(keep.shape, BF16),
             pltpu.VMEM(keep.shape, BF16),
-            pltpu.SemaphoreType.DMA((n, 2)),
+            pltpu.SemaphoreType.DMA((n, 3)),
         ],
         compiler_params=vmem_params(VMEM_HOP),
         cost_estimate=LIGHT,
@@ -856,20 +885,19 @@
     near = near_call(ints, x_all[:3], g_all[:3], packs, owned, dims)
     returned = [near[3]] + [swap(near[3 + k], "dp", n_dp, k) for k in (1, 2)]
     gain = near[7]
-    far = far_call(ints, x_all[3], near[:3] + near[6:7], g_all, packs, near[8:], owned, dims)
-
-    keep, give = far[1:3]
-    give, keep = lax.optimization_barrier((give, keep, project, *returned[1:3]))[:2]
+    far = far_call(ints, x_all[3], near[:3] + near[6:7], g_all, packs, owned, dims)
+
+    keep, give = lax.optimization_barrier((*far[1:3], project, *returned[1:3]))[:2]
     sums = add_cores(keep, swap(give, "shard", 8, 1))
     come = [sums[0]] + [swap(sums[m], "shard", 8, 2 * m) for m in (1, 2, 3)]
-    last, *pieces = lax.optimization_barrier((far[0], *far[3:], sums[1]))[:-1]
-    returned.append(swap(last, "dp", n_dp, 3))
-    pieces = [pieces[0]] + [swap(pieces[m], "dp", n_dp, m) for m in (1, 2, 3)]
+    below, *single = lax.optimization_barrier((far[0], *far[4:], sums[1]))[:-1]
+    single = [swap(piece, "dp", n_dp, 1 + i) for i, piece in enumerate(single)]
+    returned.append(swap(below, "dp", n_dp, 3))
     project = [project, swap(tie(project, sums[1]), "shard", 8, 1)]
-
-    pieces[0] = tie(pieces[0], come[1])
-    encoded = encode_call(ints, pieces, x_all, project, length)
+    pieces = [tie(far[3], come[1])] + single
+    encoded = encode_call(ints, pieces, returned[3], x_all, project, packs, length)
     frame_grad = frame_grad_call(frames, tie(cotangent, come[1]), gain, returned)
+    come[0] = tie(come[0], encoded, frame_grad)
 
     come[0] = tie(come[0], encoded, frame_grad)
     gathered = [[half] + [swap(half, "dp", 4, k) for k in (1, 2, 3)] for half in add_chips(come)]

time: 195 us -> 192 us (0.985)
  Pallas kernels: 67.4 us -> 64.1 us
  starting transfers between devices: 37.6 us -> 35.3 us
    ppermute x28 -> x27, starting transfers between devices: 29.4 us -> 27.2 us  [swap(): return lax.ppermute(x, axis, [(p, p ^ k) for p in range(size)])]
    ppermute x28 -> x27, waiting for transfers between devices: 79.3 us -> 80.5 us  [swap(): return lax.ppermute(x, axis, [(p, p ^ k) for p in range(size)])]
  transfers between devices with their start and end apart: 30 -> 29, of which waited for: 15 -> 14; matrix products, arithmetic and copies ran while one was open for 2% -> 2% of each run, Pallas kernels for 30% -> 29%
where the time goes in v6:
time: 192 us; the launch traced here: 191 us
  waiting for transfers between devices  80.5 us (42%)
  Pallas kernels  64.1 us (33%)
  starting transfers between devices  35.3 us (18%)
  local copies, waits for them, and re-layouts  8.49 us (4%)
    ppermute x27, waiting for transfers between devices, swap(): return lax.ppermute(x, axis, [(p, p ^ k) for p in range(size)])  80.5 us
    ppermute x27, starting transfers between devices, swap(): return lax.ppermute(x, axis, [(p, p ^ k) for p in range(size)])  27.2 us
    pallas_call x1, Pallas kernels, near_call(): pl.pallas_call(functools.partial(near_kernel, dims, n, owned), out_shape=...  23.2 us
    pallas_call x1, Pallas kernels, far_call(): pl.pallas_call(functools.partial(far_kernel, dims, n, owned), out_shape=(...  14.7 us
    pallas_call x1, Pallas kernels, encode_call(): pl.pallas_call(functools.partial(encode_kernel, (n, length, owned)), out_...  6.31 us
    pallas_call x1, Pallas kernels, pack_call(): pl.pallas_call(pack_kernel, out_shape=(jax.ShapeDtypeStruct((height, wide...  4.92 us
    pallas_call x1, Pallas kernels, frame_grad_call(): pl.pallas_call(functools.partial(frame_grad_kernel, len(returned)), out_s...  4.89 us
    pallas_call x2, Pallas kernels, unpack_call(): pl.pallas_call(functools.partial(unpack_kernel, (n, owned, part, half)),...  4.76 us
  transfers between devices with their start and end apart: 29, of which 14 were waited for; matrix products, arithmetic and copies ran while one was open for 2% of the time, Pallas kernels for 29%

profile of v6, /device:TPU:8, one launch (start us, length us, event | category | flops | bytes accessed | tf_op | source)
XLA Modules:
  0.0 191.0 jit_solution(5547921703100363231)
XLA Ops:
  0.6 0.7 pad_add_fusion
  1.4 0.6 broadcast_in_dim.20
  2.0 3.7 %all-to-all-start = ((s32[4,1,8]{2,1,0:T(1,128)}), s32[4,1,8]{2,1,0:T(1,128)S(1)}, u32[]{:S(2)}, u32[]{:S(2)}) async-start(s32[4,1,8]{2,1,0:T(1,128)} %broadcast_in_dim.20), calls=%async_computation | async-start | bytes 4096 | tf_op jit(solution)/shard_map/all_to_all | solution.py:872
  5.7 4.9 %pack.1 = (bf16[304,768]{1,0:T(8,128)(2,1)}, bf16[512,1536]{1,0:T(8,128)(2,1)}, bf16[4,144,1536]{2,1,0:T(8,128)(2,1)}) custom-call(bf16[192,3072]{1,0:T(8,128)(2,1)} %refs_4_.3, bf16[192,1536]{1,0:T(8,128)(2,1)} %project_hbm.1, bf16[31,192]{1,0:T(8,128)(2,1)} %bitcast.38, bf16[192]{0:T(256)(128)(2,1)} %bias_ref.1, bf16[192]{0:T(256)(128)(2,1)} %gain_ref.1, ...), custom_call_target="tpu_custom_call" | custom-call | flops 1 | bytes 1 | tf_op jit(solution)/shard_map/pack/pallas_call | solution.py:555
  10.6 2.1 %collective-permute-start.3 = (bf16[512,1536]{1,0:T(8,128)(2,1)}, bf16[512,1536]{1,0:T(8,128)(2,1)S(1)}, u32[]{:S(2)}, u32[]{:S(2)}) collective-permute-start(bf16[512,1536]{1,0:T(8,128)(2,1)} %get-tuple-element.60), channel_id=1, source_target_pairs={{0,8},{8,0},{16,24},{24,16},{1,9},{9,1},{17,25},{25,17},{2,10},{10... | collective-permute-start | bytes 4718600 | tf_op jit(solution)/shard_map/ppermute | solution.py:988
  12.7 1.5 collective-permute-start.4
  14.2 0.4 collective-permute-start
  14.6 2.6 %collective-permute-start.1 = (bf16[304,768]{1,0:T(8,128)(2,1)}, bf16[304,768]{1,0:T(8,128)(2,1)S(1)}, u32[]{:S(2)}, u32[]{:S(2)}) collective-permute-start(bf16[304,768]{1,0:T(8,128)(2,1)} %get-tuple-element.63.refs_6_.refs_9_.refs_10_), channel_id=1, source_target_pairs={{0,4},{1,5},{2,6},{3,7},{4,0},{5,1},{6,2},{7,3},{8,12},{9,13},{10,... | collective-permute-start | bytes 1400840 | tf_op jit(solution)/shard_map/ppermute | solution.py:988
  17.2 0.5 collective-permute-start.2
  17.7 14.8 %collective-permute-done.refs_7_.refs_10_.refs_11_ = bf16[304,768]{1,0:T(8,128)(2,1)S(1)} collective-permute-done((bf16[304,768]{1,0:T(8,128)(2,1)}, bf16[304,768]{1,0:T(8,128)(2,1)S(1)}, u32[]{:S(2)}, u32[]{:S(2)}) %collective-permute-start) | collective-permute-done | bytes 466976 | tf_op jit(solution)/shard_map/ppermute | solution.py:988
  32.5 16.2 %collective-permute-done.1.refs_8_.refs_11_.refs_12_ = bf16[304,768]{1,0:T(8,128)(2,1)S(1)} collective-permute-done((bf16[304,768]{1,0:T(8,128)(2,1)}, bf16[304,768]{1,0:T(8,128)(2,1)S(1)}, u32[]{:S(2)}, u32[]{:S(2)}) %collective-permute-start.1) | collective-permute-done | bytes 466976 | tf_op jit(solution)/shard_map/ppermute | solution.py:988
  48.7 8.3 %collective-permute-done.2.refs_9_.refs_12_.refs_13_ = bf16[304,768]{1,0:T(8,128)(2,1)S(1)} collective-permute-done((bf16[304,768]{1,0:T(8,128)(2,1)}, bf16[304,768]{1,0:T(8,128)(2,1)S(1)}, u32[]{:S(2)}, u32[]{:S(2)}) %collective-permute-start.2) | collective-permute-done | bytes 466976 | tf_op jit(solution)/shard_map/ppermute | solution.py:988
  57.0 0.7 copy-done.8
  57.7 4.4 %all-to-all-start.1 = ((bf16[4,144,1536]{2,1,0:T(8,128)(2,1)}), bf16[4,144,1536]{2,1,0:T(8,128)(2,1)}, u32[]{:S(2)}, u32[]{:S(2)}) async-start(bf16[4,144,1536]{2,1,0:T(8,128)(2,1)} %get-tuple-element.75), calls=%async_computation.1 | async-start | bytes 3538944 | tf_op jit(solution)/shard_map/all_to_all | solution.py:883
  62.1 0.1 collective-permute-start.7
  62.2 0.5 collective-permute-start.8
  62.7 0.1 collective-permute-start.9
  62.8 0.4 collective-permute-start.6
  63.2 0.9 slice.30
  64.2 0.6 collective-permute-start.5
  64.7 0.9 slice.31
  65.6 0.4 collective-permute-start.10
  66.0 0.4 collective-permute-done.6.refs_10_.refs_13_.refs_14_
  66.4 23.2 %near_sources.1 = (bf16[768,1536]{1,0:T(8,128)(2,1)}, bf16[768,384]{1,0:T(8,128)(2,1)}, bf16[768,768]{1,0:T(8,128)(2,1)}, bf16[256,1536]{1,0:T(8,128)(2,1)}, bf1...) custom-call(s32[4,8]{1,0:T(4,128)} %bitcast.35, ...), custom_call_target="tpu_custom_call" | custom-call | flops 1 | bytes 1 | tf_op jit(solution)/shard_map/near_sources/pallas_call | solution.py:280
  89.5 1.4 collective-permute-start.11
  90.9 1.5 collective-permute-start.12
  92.4 0.9 copy-done.10
  93.3 14.7 %far_source.1 = (bf16[320,1536]{1,0:T(8,128)(2,1)}, bf16[4,304,768]{2,1,0:T(8,128)(2,1)}, bf16[4,304,768]{2,1,0:T(8,128)(2,1)}, bf16[64,1536]{1,0:T(8,128)(2,1)}...) custom-call(s32[4,8]{1,0:T(4,128)} %bitcast.36, bf16[256,1536]{1,0:T(8,128)(2,1)} %copy-done.10, ...), custom_call_target="tpu_custom_call" | custom-call | flops 1 | bytes 1 | tf_op jit(solution)/shard_map/far_source/pallas_call | solution.py:434
  108.1 1.5 collective-permute-done.11.refs_1_
  109.5 0.4 collective-permute-done.12.refs_2_
  109.9 4.2 %collective-permute-done.13.got_hbm = bf16[4,304,768]{2,1,0:T(8,128)(2,1)} collective-permute-done((bf16[4,304,768]{2,1,0:T(8,128)(2,1)}, bf16[4,304,768]{2,1,0:T(8,128)(2,1)}, u32[]{:S(2)}, u32[]{:S(2)}) %collective-permute-start.13) | collective-permute-done | bytes 1867808 | tf_op jit(solution)/shard_map/ppermute | solution.py:988
  114.1 3.0 %add_cores.1 = (bf16[304,768]{1,0:T(8,128)(2,1)}, bf16[304,768]{1,0:T(8,128)(2,1)}, bf16[304,768]{1,0:T(8,128)(2,1)}, bf16[304,768]{1,0:T(8,128)(2,1)}) custom-call(bf16[4,304,768]{2,1,0:T(8,128)(2,1)} %get-tuple-element.78.keep_hbm, bf16[4,304,768]{2,1,0:T(8,128)(2,1)} %collective-permute-done.13.got_hbm), custom_call_target="tpu_custom_call" | custom-call | flops 1 | bytes 1 | tf_op jit(solution)/shard_map/add_cores/pallas_call | solution.py:812
  117.1 0.2 collective-permute-start.18
  117.3 1.5 collective-permute-start.17
  118.8 3.0 %collective-permute-start.19 = (bf16[304,768]{1,0:T(8,128)(2,1)}, bf16[304,768]{1,0:T(8,128)(2,1)}, u32[]{:S(2)}, u32[]{:S(2)}) collective-permute-start(bf16[304,768]{1,0:T(8,128)(2,1)} %get-tuple-element.95), channel_id=1, source_target_pairs={{0,4},{1,5},{2,6},{3,7},{4,0},{5,1},{6,2},{7,3},{8,12},{9,13},{10,... | collective-permute-start | bytes 1400840 | tf_op jit(solution)/shard_map/ppermute | solution.py:988
  121.8 0.5 collective-permute-start.20
  122.3 16.7 %collective-permute-done.14.refs_1_ = bf16[304,768]{1,0:T(8,128)(2,1)S(1)} collective-permute-done((bf16[304,768]{1,0:T(8,128)(2,1)}, bf16[304,768]{1,0:T(8,128)(2,1)S(1)}, u32[]{:S(2)}, u32[]{:S(2)}) %collective-permute-start.14) | collective-permute-done | bytes 466976 | tf_op jit(solution)/shard_map/ppermute | solution.py:988
  138.9 1.5 collective-permute-start.15
  140.4 2.4 %collective-permute-done.17.refs_7_.refs_3_ = bf16[320,1536]{1,0:T(8,128)(2,1)S(1)} collective-permute-done((bf16[320,1536]{1,0:T(8,128)(2,1)}, bf16[320,1536]{1,0:T(8,128)(2,1)S(1)}, u32[]{:S(2)}, u32[]{:S(2)}) %collective-permute-start.17) | collective-permute-done | bytes 983072 | tf_op jit(solution)/shard_map/ppermute | solution.py:988
  142.8 1.7 collective-permute-start.16
  144.5 0.6 pad_clamp_fusion
  145.1 4.9 %frame_grad.1 = bf16[256,1536]{1,0:T(8,128)(2,1)} custom-call(bf16[256,1536]{1,0:T(8,128)(2,1)} %bitcast.30, bf16[256,1536]{1,0:T(8,128)(2,1)} %bitcast.27, f32[1,1536]{1,0:T(1,128)} %get-tuple-element.90.gain_ref, bf16[256,1536]{1,0:T(8,128)(2,1)} %get-tuple-element.91.refs_0_, bf16[256,1536]{1,0:T(8,128)(2,1)} %collective-permute-done.11.refs_1_, ...), custom_call_target="tpu_custom_call" | custom-call | flops 1 | bytes 1 | tf_op jit(solution)/shard_map/frame_grad/pallas_call | solution.py:678
  150.0 6.3 %encode.1 = bf16[256,1536]{1,0:T(8,128)(2,1)} custom-call(s32[4,8]{1,0:T(4,128)} %bitcast.37, bf16[256,1536]{1,0:T(8,128)(2,1)} %bitcast.31, bf16[512,1536]{1,0:T(8,128)(2,1)} %copy-done.4, bf16[512,1536]{1,0:T(8,128)(2,1)} %copy-done.5, bf16[256,1536]{1,0:T(8,128)(2,1)} %copy-done.10, bf16[64,1536]{1,0:T(8,128)(2,1)} %get-tuple-element.81.refs_4_, ...), custom_call_target="tpu_custom_call" | custom-call | flops 1 | bytes 1 | tf_op jit(solution)/shard_map/encode/pallas_call | solution.py:641
  156.3 6.7 %collective-permute-done.20.refs_3_ = bf16[304,768]{1,0:T(8,128)(2,1)} collective-permute-done((bf16[304,768]{1,0:T(8,128)(2,1)}, bf16[304,768]{1,0:T(8,128)(2,1)}, u32[]{:S(2)}, u32[]{:S(2)}) %collective-permute-start.20) | collective-permute-done | bytes 466976 | tf_op jit(solution)/shard_map/ppermute | solution.py:988
  163.0 2.4 %add_chips.1 = (bf16[304,384]{1,0:T(8,128)(2,1)}, bf16[304,384]{1,0:T(8,128)(2,1)}) custom-call(bf16[304,768]{1,0:T(8,128)(2,1)} %get-tuple-element.94.refs_0_, bf16[304,768]{1,0:T(8,128)(2,1)} %copy-done.11, bf16[304,768]{1,0:T(8,128)(2,1)} %collective-permute-done.19.refs_2_, bf16[304,768]{1,0:T(8,128)(2,1)} %collective-permute-done.20.refs_3_), custom_call_target="tpu_custom_call" | custom-call | flops 1 | bytes 1 | tf_op jit(solution)/shard_map/add_chips/pallas_call | solution.py:837
  165.4 1.5 collective-permute-start.26
  166.9 1.5 collective-permute-start.25
  168.4 0.6 collective-permute-start.24
  169.0 0.7 slice_bitcast_fusion.3
  169.7 1.5 collective-permute-start.21
  171.2 0.6 collective-permute-start.22
  171.8 3.4 %collective-permute-done.26.refs_3_ = bf16[304,384]{1,0:T(8,128)(2,1)S(1)} collective-permute-done((bf16[304,384]{1,0:T(8,128)(2,1)}, bf16[304,384]{1,0:T(8,128)(2,1)S(1)}, u32[]{:S(2)}, u32[]{:S(2)}) %collective-permute-start.26) | collective-permute-done | bytes 233504 | tf_op jit(solution)/shard_map/ppermute | solution.py:988
  175.2 1.5 collective-permute-start.23
  176.6 1.5 collective-permute-done.25.refs_2_
  178.2 1.9 collective-permute-done.24.refs_1_
  180.1 0.7 gather_fusion
  180.7 0.1 select_convert_fusion
  180.9 1.3 copy-done
  182.1 0.9 copy-done.2
  183.1 2.1 %unpack.2 = (f32[192,3072]{1,0:T(8,128)}, f32[192,1536]{1,0:T(8,128)}, f32[192,1]{1,0:T(8,128)S(1)}) custom-call(bf16[304,384]{1,0:T(8,128)(2,1)S(1)} %copy-done.2, bf16[304,384]{1,0:T(8,128)(2,1)S(1)} %collective-permute-done.24.refs_1_, bf16[304,384]{1,0:T(8,128)(2,1)S(1)} %collective-permute-done.25.refs_2_, ...), custom_call_target="tpu_custom_call" | custom-call | flops 1 | bytes 1 | tf_op jit(solution)/shard_map/unpack/pallas_call | solution.py:749
  185.3 0.1 reshape.67
  185.4 0.6 slice.47
  185.9 2.2 %collective-permute-done.23.refs_3_ = bf16[304,384]{1,0:T(8,128)(2,1)S(1)} collective-permute-done((bf16[304,384]{1,0:T(8,128)(2,1)}, bf16[304,384]{1,0:T(8,128)(2,1)S(1)}, u32[]{:S(2)}, u32[]{:S(2)}) %collective-permute-start.23) | collective-permute-done | bytes 233504 | tf_op jit(solution)/shard_map/ppermute | solution.py:988
  188.1 2.7 %unpack.3 = (f32[192,3072]{1,0:T(8,128)}, f32[192,1536]{1,0:T(8,128)}, f32[1,192]{1,0:T(1,128)}) custom-call(bf16[304,384]{1,0:T(8,128)(2,1)S(1)} %copy-done.3, bf16[304,384]{1,0:T(8,128)(2,1)S(1)} %collective-permute-done.21.refs_1_, bf16[304,384]{1,0:T(8,128)(2,1)S(1)} %collective-permute-done.22.refs_2_, ...), custom_call_target="tpu_custom_call", output_to_operand_aliasing={{0}: (7, {}), {1}: (8, {})} | custom-call | flops 1 | bytes 1 | tf_op jit(solution)/shard_map/unpack/pallas_call | solution.py:749
  (54 shorter events, 0.2 us)
Async XLA Ops:
  2.0 8.6 %all-to-all-start = ((s32[4,1,8]{2,1,0:T(1,128)}), s32[4,1,8]{2,1,0:T(1,128)S(1)}, u32[]{:S(2)}, u32[]{:S(2)}) async-start(s32[4,1,8]{2,1,0:T(1,128)} %broadcast_in_dim.20), calls=%async_computation | async-start | bytes 4096 | tf_op jit(solution)/shard_map/all_to_all | solution.py:872
  10.6 47.1 %copy-start.13 = (s32[4,1,8]{2,1,0:T(1,128)}, s32[4,1,8]{2,1,0:T(1,128)S(1)}, u32[]{:S(2)}) copy-start(s32[4,1,8]{2,1,0:T(1,128)S(1)} %all-to-all-done) | copy-start | bytes 388
  10.6 46.4 %collective-permute-start.3 = (bf16[512,1536]{1,0:T(8,128)(2,1)}, bf16[512,1536]{1,0:T(8,128)(2,1)S(1)}, u32[]{:S(2)}, u32[]{:S(2)}) collective-permute-start(bf16[512,1536]{1,0:T(8,128)(2,1)} %get-tuple-element.60), channel_id=1, source_target_pairs={{0,8},{8,0},{16,24},{24,16},{1,9},{9,1},{17,25},{25,17},{2,10},{10... | collective-permute-start | bytes 4718600 | tf_op jit(solution)/shard_map/ppermute | solution.py:988
  12.7 44.3 %collective-permute-start.4 = (bf16[512,1536]{1,0:T(8,128)(2,1)}, bf16[512,1536]{1,0:T(8,128)(2,1)S(1)}, u32[]{:S(2)}, u32[]{:S(2)}) collective-permute-start(bf16[512,1536]{1,0:T(8,128)(2,1)} %get-tuple-element.60), channel_id=1, source_target_pairs={{0,16},{8,24},{16,0},{24,8},{1,17},{9,25},{17,1},{25,9},{2,18},{10... | collective-permute-start | bytes 4718600 | tf_op jit(solution)/shard_map/ppermute | solution.py:988
  14.2 18.3 %collective-permute-start = (bf16[304,768]{1,0:T(8,128)(2,1)}, bf16[304,768]{1,0:T(8,128)(2,1)S(1)}, u32[]{:S(2)}, u32[]{:S(2)}) collective-permute-start(bf16[304,768]{1,0:T(8,128)(2,1)} %get-tuple-element.63.refs_6_.refs_9_.refs_10_), channel_id=1, source_target_pairs={{0,2},{1,3},{2,0},{3,1},{4,6},{5,7},{6,4},{7,5},{8,10},{9,11},{10,... | collective-permute-start | bytes 1400840 | tf_op jit(solution)/shard_map/ppermute | solution.py:988
  14.6 34.1 %collective-permute-start.1 = (bf16[304,768]{1,0:T(8,128)(2,1)}, bf16[304,768]{1,0:T(8,128)(2,1)S(1)}, u32[]{:S(2)}, u32[]{:S(2)}) collective-permute-start(bf16[304,768]{1,0:T(8,128)(2,1)} %get-tuple-element.63.refs_6_.refs_9_.refs_10_), channel_id=1, source_target_pairs={{0,4},{1,5},{2,6},{3,7},{4,0},{5,1},{6,2},{7,3},{8,12},{9,13},{10,... | collective-permute-start | bytes 1400840 | tf_op jit(solution)/shard_map/ppermute | solution.py:988
  17.2 39.8 %collective-permute-start.2 = (bf16[304,768]{1,0:T(8,128)(2,1)}, bf16[304,768]{1,0:T(8,128)(2,1)S(1)}, u32[]{:S(2)}, u32[]{:S(2)}) collective-permute-start(bf16[304,768]{1,0:T(8,128)(2,1)} %get-tuple-element.63.refs_6_.refs_9_.refs_10_), channel_id=1, source_target_pairs={{0,6},{1,7},{2,4},{3,5},{4,2},{5,3},{6,0},{7,1},{8,14},{9,15},{10,... | collective-permute-start | bytes 1400840 | tf_op jit(solution)/shard_map/ppermute | solution.py:988
  32.4 24.5 %copy-start.6 = (bf16[304,768]{1,0:T(8,128)(2,1)}, bf16[304,768]{1,0:T(8,128)(2,1)S(1)}, u32[]{:S(2)}) copy-start(bf16[304,768]{1,0:T(8,128)(2,1)S(1)} %collective-permute-done.refs_7_.refs_10_.refs_11_) | copy-start | bytes 1400836
  48.7 8.3 %copy-start.7 = (bf16[304,768]{1,0:T(8,128)(2,1)}, bf16[304,768]{1,0:T(8,128)(2,1)S(1)}, u32[]{:S(2)}) copy-start(bf16[304,768]{1,0:T(8,128)(2,1)S(1)} %collective-permute-done.1.refs_8_.refs_11_.refs_12_) | copy-start | bytes 1400836
  57.0 0.8 copy-start.8
  57.0 6.3 %copy-start.4 = (bf16[512,1536]{1,0:T(8,128)(2,1)}, bf16[512,1536]{1,0:T(8,128)(2,1)S(1)}, u32[]{:S(2)}) copy-start(bf16[512,1536]{1,0:T(8,128)(2,1)S(1)} %collective-permute-done.3.refs_1_.refs_4_.refs_5_) | copy-start | bytes 4718596
  57.7 7.0 %copy-start.5 = (bf16[512,1536]{1,0:T(8,128)(2,1)}, bf16[512,1536]{1,0:T(8,128)(2,1)S(1)}, u32[]{:S(2)}) copy-start(bf16[512,1536]{1,0:T(8,128)(2,1)S(1)} %collective-permute-done.4.refs_2_.refs_5_.refs_6_) | copy-start | bytes 4718596
  57.7 52.2 %all-to-all-start.1 = ((bf16[4,144,1536]{2,1,0:T(8,128)(2,1)}), bf16[4,144,1536]{2,1,0:T(8,128)(2,1)}, u32[]{:S(2)}, u32[]{:S(2)}) async-start(bf16[4,144,1536]{2,1,0:T(8,128)(2,1)} %get-tuple-element.75), calls=%async_computation.1 | async-start | bytes 3538944 | tf_op jit(solution)/shard_map/all_to_all | solution.py:883
  62.1 3.5 %collective-permute-start.7 = (bf16[304,768]{1,0:T(8,128)(2,1)}, bf16[304,768]{1,0:T(8,128)(2,1)}, u32[]{:S(2)}, u32[]{:S(2)}) collective-permute-start(bf16[304,768]{1,0:T(8,128)(2,1)} %copy-done.6), channel_id=1, source_target_pairs={{0,1},{1,0},{2,3},{3,2},{4,5},{5,4},{6,7},{7,6},{8,9},{9,8},{10,11... | collective-permute-start | bytes 1400840 | tf_op jit(solution)/shard_map/ppermute | solution.py:988
  62.2 3.8 %collective-permute-start.8 = (bf16[304,768]{1,0:T(8,128)(2,1)}, bf16[304,768]{1,0:T(8,128)(2,1)}, u32[]{:S(2)}, u32[]{:S(2)}) collective-permute-start(bf16[304,768]{1,0:T(8,128)(2,1)} %copy-done.7), channel_id=1, source_target_pairs={{0,1},{1,0},{2,3},{3,2},{4,5},{5,4},{6,7},{7,6},{8,9},{9,8},{10,11... | collective-permute-start | bytes 1400840 | tf_op jit(solution)/shard_map/ppermute | solution.py:988
  62.7 3.3 %collective-permute-start.9 = (bf16[304,768]{1,0:T(8,128)(2,1)}, bf16[304,768]{1,0:T(8,128)(2,1)}, u32[]{:S(2)}, u32[]{:S(2)}) collective-permute-start(bf16[304,768]{1,0:T(8,128)(2,1)} %copy-done.8), channel_id=1, source_target_pairs={{0,1},{1,0},{2,3},{3,2},{4,5},{5,4},{6,7},{7,6},{8,9},{9,8},{10,11... | collective-permute-start | bytes 1400840 | tf_op jit(solution)/shard_map/ppermute | solution.py:988
  62.8 3.6 %collective-permute-start.6 = (bf16[304,768]{1,0:T(8,128)(2,1)}, bf16[304,768]{1,0:T(8,128)(2,1)}, u32[]{:S(2)}, u32[]{:S(2)}) collective-permute-start(bf16[304,768]{1,0:T(8,128)(2,1)} %get-tuple-element.63.refs_6_.refs_9_.refs_10_), channel_id=1, source_target_pairs={{0,1},{1,0},{2,3},{3,2},{4,5},{5,4},{6,7},{7,6},{8,9},{9,8},{10,11... | collective-permute-start | bytes 1400840 | tf_op jit(solution)/shard_map/ppermute | solution.py:988
  64.2 28.2 %collective-permute-start.5 = (bf16[256,1536]{1,0:T(8,128)(2,1)}, bf16[256,1536]{1,0:T(8,128)(2,1)S(1)}, u32[]{:S(2)}, u32[]{:S(2)}) collective-permute-start(bf16[256,1536]{1,0:T(8,128)(2,1)} %slice.30), channel_id=1, source_target_pairs={{0,16},{8,24},{16,0},{24,8},{1,17},{9,25},{17,1},{25,9},{2,18},{10... | collective-permute-start | bytes 2359304 | tf_op jit(solution)/shard_map/ppermute | solution.py:988
  65.6 26.8 %collective-permute-start.10 = (bf16[256,1536]{1,0:T(8,128)(2,1)}, bf16[256,1536]{1,0:T(8,128)(2,1)}, u32[]{:S(2)}, u32[]{:S(2)}) collective-permute-start(bf16[256,1536]{1,0:T(8,128)(2,1)} %slice.31), channel_id=1, source_target_pairs={{0,8},{8,0},{16,24},{24,16},{1,9},{9,1},{17,25},{25,17},{2,10},{10... | collective-permute-start | bytes 2359304 | tf_op jit(solution)/shard_map/ppermute | solution.py:988
  89.5 20.0 %collective-permute-start.11 = (bf16[256,1536]{1,0:T(8,128)(2,1)}, bf16[256,1536]{1,0:T(8,128)(2,1)}, u32[]{:S(2)}, u32[]{:S(2)}) collective-permute-start(bf16[256,1536]{1,0:T(8,128)(2,1)} %get-tuple-element.76), channel_id=1, source_target_pairs={{0,8},{8,0},{16,24},{24,16},{1,9},{9,1},{17,25},{25,17},{2,10},{10... | collective-permute-start | bytes 2359304 | tf_op jit(solution)/shard_map/ppermute | solution.py:988
  90.9 19.0 %collective-permute-start.12 = (bf16[256,1536]{1,0:T(8,128)(2,1)}, bf16[256,1536]{1,0:T(8,128)(2,1)}, u32[]{:S(2)}, u32[]{:S(2)}) collective-permute-start(bf16[256,1536]{1,0:T(8,128)(2,1)} %get-tuple-element.77), channel_id=1, source_target_pairs={{0,16},{8,24},{16,0},{24,8},{1,17},{9,25},{17,1},{25,9},{2,18},{10... | collective-permute-start | bytes 2359304 | tf_op jit(solution)/shard_map/ppermute | solution.py:988
  92.4 0.9 copy-start.10
  109.9 4.2 %collective-permute-start.13 = (bf16[4,304,768]{2,1,0:T(8,128)(2,1)}, bf16[4,304,768]{2,1,0:T(8,128)(2,1)}, u32[]{:S(2)}, u32[]{:S(2)}) collective-permute-start(bf16[4,304,768]{2,1,0:T(8,128)(2,1)} %get-tuple-element.79), channel_id=1, source_target_pairs={{0,1},{1,0},{2,3},{3,2},{4,5},{5,4},{6,7},{7,6},{8,9},{9,8},{10,11... | collective-permute-start | bytes 5603336 | tf_op jit(solution)/shard_map/ppermute | solution.py:988
  117.1 32.9 %collective-permute-start.18 = (bf16[4,144,1536]{2,1,0:T(8,128)(2,1)}, bf16[4,144,1536]{2,1,0:T(8,128)(2,1)}, u32[]{:S(2)}, u32[]{:S(2)}) collective-permute-start(bf16[4,144,1536]{2,1,0:T(8,128)(2,1)} %all-to-all-done.1.refs_8_), channel_id=1, source_target_pairs={{0,1},{1,0},{2,3},{3,2},{4,5},{5,4},{6,7},{7,6},{8,9},{9,8},{10,11... | collective-permute-start | bytes 5308424 | tf_op jit(solution)/shard_map/ppermute | solution.py:988
  117.3 25.5 %collective-permute-start.17 = (bf16[320,1536]{1,0:T(8,128)(2,1)}, bf16[320,1536]{1,0:T(8,128)(2,1)S(1)}, u32[]{:S(2)}, u32[]{:S(2)}) collective-permute-start(bf16[320,1536]{1,0:T(8,128)(2,1)} %get-tuple-element.87), channel_id=1, source_target_pairs={{0,24},{8,16},{16,8},{24,0},{1,25},{9,17},{17,9},{25,1},{2,26},{10... | collective-permute-start | bytes 2949128 | tf_op jit(solution)/shard_map/ppermute | solution.py:988
  118.8 20.2 %collective-permute-start.14 = (bf16[304,768]{1,0:T(8,128)(2,1)}, bf16[304,768]{1,0:T(8,128)(2,1)S(1)}, u32[]{:S(2)}, u32[]{:S(2)}) collective-permute-start(bf16[304,768]{1,0:T(8,128)(2,1)} %get-tuple-element.80), channel_id=1, source_target_pairs={{0,2},{1,3},{2,0},{3,1},{4,6},{5,7},{6,4},{7,5},{8,10},{9,11},{10,... | collective-permute-start | bytes 1400840 | tf_op jit(solution)/shard_map/ppermute | solution.py:988
  118.8 37.5 %collective-permute-start.19 = (bf16[304,768]{1,0:T(8,128)(2,1)}, bf16[304,768]{1,0:T(8,128)(2,1)}, u32[]{:S(2)}, u32[]{:S(2)}) collective-permute-start(bf16[304,768]{1,0:T(8,128)(2,1)} %get-tuple-element.95), channel_id=1, source_target_pairs={{0,4},{1,5},{2,6},{3,7},{4,0},{5,1},{6,2},{7,3},{8,12},{9,13},{10,... | collective-permute-start | bytes 1400840 | tf_op jit(solution)/shard_map/ppermute | solution.py:988
  121.8 41.2 %collective-permute-start.20 = (bf16[304,768]{1,0:T(8,128)(2,1)}, bf16[304,768]{1,0:T(8,128)(2,1)}, u32[]{:S(2)}, u32[]{:S(2)}) collective-permute-start(bf16[304,768]{1,0:T(8,128)(2,1)} %get-tuple-element.96), channel_id=1, source_target_pairs={{0,6},{1,7},{2,4},{3,5},{4,2},{5,3},{6,0},{7,1},{8,14},{9,15},{10,... | collective-permute-start | bytes 1400840 | tf_op jit(solution)/shard_map/ppermute | solution.py:988
  138.9 3.9 %copy-start.11 = (bf16[304,768]{1,0:T(8,128)(2,1)}, bf16[304,768]{1,0:T(8,128)(2,1)S(1)}, u32[]{:S(2)}) copy-start(bf16[304,768]{1,0:T(8,128)(2,1)S(1)} %collective-permute-done.14.refs_1_) | copy-start | bytes 1400836
  138.9 11.0 %collective-permute-start.15 = (bf16[64,1536]{1,0:T(8,128)(2,1)}, bf16[64,1536]{1,0:T(8,128)(2,1)}, u32[]{:S(2)}, u32[]{:S(2)}) collective-permute-start(bf16[64,1536]{1,0:T(8,128)(2,1)} %get-tuple-element.85), channel_id=1, source_target_pairs={{0,8},{8,0},{16,24},{24,16},{1,9},{9,1},{17,25},{25,17},{2,10},{10... | collective-permute-start | bytes 589832 | tf_op jit(solution)/shard_map/ppermute | solution.py:988
  142.8 2.3 %copy-start.9 = (bf16[320,1536]{1,0:T(8,128)(2,1)}, bf16[320,1536]{1,0:T(8,128)(2,1)S(1)}, u32[]{:S(2)}) copy-start(bf16[320,1536]{1,0:T(8,128)(2,1)S(1)} %collective-permute-done.17.refs_7_.refs_3_) | copy-start | bytes 2949124
  142.8 7.2 %collective-permute-start.16 = (bf16[64,1536]{1,0:T(8,128)(2,1)}, bf16[64,1536]{1,0:T(8,128)(2,1)}, u32[]{:S(2)}, u32[]{:S(2)}) collective-permute-start(bf16[64,1536]{1,0:T(8,128)(2,1)} %get-tuple-element.86), channel_id=1, source_target_pairs={{0,16},{8,24},{16,0},{24,8},{1,17},{9,25},{17,1},{25,9},{2,18},{10... | collective-permute-start | bytes 589832 | tf_op jit(solution)/shard_map/ppermute | solution.py:988
  156.3 10.6 %copy-start.14 = (bf16[192]{0:T(256)(128)(2,1)S(1)}, bf16[192]{0:T(256)(128)(2,1)}, u32[]{:S(2)}) copy-start(bf16[192]{0:T(256)(128)(2,1)} %gain_ref.1) | copy-start | bytes 1156
  165.4 22.7 %copy-start.3 = (bf16[304,384]{1,0:T(8,128)(2,1)S(1)}, bf16[304,384]{1,0:T(8,128)(2,1)}, u32[]{:S(2)}) copy-start(bf16[304,384]{1,0:T(8,128)(2,1)} %get-tuple-element.97.refs_0_) | copy-start | bytes 700420
  165.4 9.8 %collective-permute-start.26 = (bf16[304,384]{1,0:T(8,128)(2,1)}, bf16[304,384]{1,0:T(8,128)(2,1)S(1)}, u32[]{:S(2)}, u32[]{:S(2)}) collective-permute-start(bf16[304,384]{1,0:T(8,128)(2,1)} %get-tuple-element.98.refs_0_), channel_id=1, source_target_pairs={{0,24},{8,16},{16,8},{24,0},{1,25},{9,17},{17,9},{25,1},{2,26},{10... | collective-permute-start | bytes 700424 | tf_op jit(solution)/shard_map/ppermute | solution.py:988
  166.9 11.3 %collective-permute-start.25 = (bf16[304,384]{1,0:T(8,128)(2,1)}, bf16[304,384]{1,0:T(8,128)(2,1)S(1)}, u32[]{:S(2)}, u32[]{:S(2)}) collective-permute-start(bf16[304,384]{1,0:T(8,128)(2,1)} %get-tuple-element.98.refs_0_), channel_id=1, source_target_pairs={{0,16},{8,24},{16,0},{24,8},{1,17},{9,25},{17,1},{25,9},{2,18},{10... | collective-permute-start | bytes 700424 | tf_op jit(solution)/shard_map/ppermute | solution.py:988
  168.4 11.6 %collective-permute-start.24 = (bf16[304,384]{1,0:T(8,128)(2,1)}, bf16[304,384]{1,0:T(8,128)(2,1)S(1)}, u32[]{:S(2)}, u32[]{:S(2)}) collective-permute-start(bf16[304,384]{1,0:T(8,128)(2,1)} %get-tuple-element.98.refs_0_), channel_id=1, source_target_pairs={{0,8},{8,0},{16,24},{24,16},{1,9},{9,1},{17,25},{25,17},{2,10},{10... | collective-permute-start | bytes 700424 | tf_op jit(solution)/shard_map/ppermute | solution.py:988
  169.7 16.2 %collective-permute-start.21 = (bf16[304,384]{1,0:T(8,128)(2,1)}, bf16[304,384]{1,0:T(8,128)(2,1)S(1)}, u32[]{:S(2)}, u32[]{:S(2)}) collective-permute-start(bf16[304,384]{1,0:T(8,128)(2,1)} %get-tuple-element.97.refs_0_), channel_id=1, source_target_pairs={{0,8},{8,0},{16,24},{24,16},{1,9},{9,1},{17,25},{25,17},{2,10},{10... | collective-permute-start | bytes 700424 | tf_op jit(solution)/shard_map/ppermute | solution.py:988
  171.2 14.8 %collective-permute-start.22 = (bf16[304,384]{1,0:T(8,128)(2,1)}, bf16[304,384]{1,0:T(8,128)(2,1)S(1)}, u32[]{:S(2)}, u32[]{:S(2)}) collective-permute-start(bf16[304,384]{1,0:T(8,128)(2,1)} %get-tuple-element.97.refs_0_), channel_id=1, source_target_pairs={{0,16},{8,24},{16,0},{24,8},{1,17},{9,25},{17,1},{25,9},{2,18},{10... | collective-permute-start | bytes 700424 | tf_op jit(solution)/shard_map/ppermute | solution.py:988
  175.2 13.0 %collective-permute-start.23 = (bf16[304,384]{1,0:T(8,128)(2,1)}, bf16[304,384]{1,0:T(8,128)(2,1)S(1)}, u32[]{:S(2)}, u32[]{:S(2)}) collective-permute-start(bf16[304,384]{1,0:T(8,128)(2,1)} %get-tuple-element.97.refs_0_), channel_id=1, source_target_pairs={{0,24},{8,16},{16,8},{24,0},{1,25},{9,17},{17,9},{25,1},{2,26},{10... | collective-permute-start | bytes 700424 | tf_op jit(solution)/shard_map/ppermute | solution.py:988
  180.8 1.3 copy-start
  182.1 0.9 copy-start.2
  183.1 5.1 %copy-start.1 = (bf16[192,3072]{1,0:T(8,128)(2,1)S(1)}, bf16[192,3072]{1,0:T(8,128)(2,1)}, u32[]{:S(2)}) copy-start(bf16[192,3072]{1,0:T(8,128)(2,1)} %refs_4_.3) | copy-start | bytes 3538948
  185.3 5.5 %copy-start.12 = (f32[192,32]{0,1:T(8,128)}, f32[192,32]{0,1:T(8,128)S(1)}, u32[]{:S(2)}) copy-start(f32[192,32]{0,1:T(8,128)S(1)} %reshape.67) | copy-start | bytes 73732

commit v7 on v6

--- a/solution.py
+++ b/solution.py
@@ -44,7 +44,7 @@
     tiles = channels // LANES
     own = pl.ds(base, rows)
     step = 256
-    ready("we")
+    ready("tables")
     gain = refs["gain"][...]
     ready("x")
 
@@ -56,6 +56,7 @@
         variance = jnp.mean(centred * centred, axis=1, keepdims=True)
         normed[at, :] = (centred * lax.rsqrt(variance + EPS) * gain).astype(BF16)
 
+    ready("we")
     expanded = jnp.dot(normed[own, :], we[...], preferred_element_type=F32)
     for tile in range(2 * tiles):
         ab[tile] = expanded[:, tile * LANES : (tile + 1) * LANES]
@@ -125,7 +126,7 @@
                 through * ab[tile, at, :] * (1.0 - gate)
             ).astype(BF16)
 
-    span = 512
+    span = 768
     for start in range(0, width, span):
         cols = pl.ds(start, span)
         refs["gn"][own, cols] = lax.dot_general(
@@ -159,11 +160,11 @@
     width, wide = we.shape
     halves = width // wide
     move = pltpu.make_async_copy
-    first, second = [], []
+    tables, first, second = [], [], []
     for b, block in enumerate(blocks):
         offset = 2 * (b % (len(blocks) // 2)) + b // (len(blocks) // 2)
         owner = me ^ offset
-        first.append(
+        tables.append(
             move(block.at[pl.ds(owned + halves * part, 16)], small.at[owner], sems.at[b, 0])
         )
         rows = pl.ds(pl.multiple_of(owner * owned, owned), owned)
@@ -177,7 +178,7 @@
                     sems.at[b, 2 + h],
                 )
             )
-    return first, second
+    return dict(tables=tables, we=first, wp=second)
 
 
 def fill_tables(small, owned, part, taps_ref, gain_ref):
@@ -221,11 +222,13 @@
             g_hbm[s].at[pl.ds(g_hbm[s].shape[0] - rows, rows)], g.at[place(s)], in_sems.at[s, 1]
         )
     weights = weight_copies(blocks, owned, part, we, wp, shares, weight_sems)
+    for copy in weights["tables"]:
+        copy.start()
     incoming["x", 0].start()
-    for copy in weights[0]:
+    for copy in weights["we"]:
         copy.start()
     incoming["g", 0].start()
-    for copy in weights[1]:
+    for copy in weights["wp"]:
         copy.start()
     for s in range(1, n):
         incoming["x", s].start()
@@ -240,12 +243,12 @@
     @pl.loop(0, n)
     def _(s):
         def ready(what):
-            if what in ("we", "wp"):
+            if what in weights:
                 @pl.when(s == 0)
                 def _():
-                    for copy in weights[what == "wp"]:
+                    for copy in weights[what]:
                         copy.wait()
-                    if what == "we":
+                    if what == "tables":
                         fill_tables(shares, owned, part, taps_ref, gain_ref)
             else:
                 for at in range(n):
@@ -338,9 +341,7 @@
         x=[move(x_hbm.at[pl.ds(0, rows)], x.at[last], in_sems.at[0])],
         g=[move(g_hbm[n].at[tail[n]], g.at[last], in_sems.at[2])],
     )
-    incoming["we"], incoming["wp"] = weight_copies(
-        blocks, owned, part, we, wp, shares, weight_sems
-    )
+    incoming.update(weight_copies(blocks, owned, part, we, wp, shares, weight_sems))
     later = [
         move(normed_hbm, normed.at[near], in_sems.at[4]),
         move(sw_hbm, sw.at[near], in_sems.at[5]),
@@ -350,13 +351,16 @@
         move(g_hbm[s].at[tail[s]], g.at[pl.ds(s * rows, rows)], in_sems.at[7 + s])
         for s in range(n)
     ]
-    for copy in incoming["x"] + incoming["we"] + incoming["g"] + incoming["wp"] + later:
+    for what in ("tables", "x", "we", "g", "wp"):
+        for copy in incoming[what]:
+            copy.start()
+    for copy in later:
         copy.start()
 
     def ready(what):
         for copy in incoming[what]:
             copy.wait()
-        if what == "we":
+        if what == "tables":
             fill_tables(shares, owned, part, taps_ref, gain_ref)
 
     clear_margins(pad, gpad)

time: 192 us -> 192 us (level)
  transfers between devices with their start and end apart: 29 -> 29, of which waited for: 14 -> 14; matrix products, arithmetic and copies ran while one was open for 2% -> 2% of each run, Pallas kernels for 29% -> 30%
where the time goes in v7:
time: 192 us; the launch traced here: 191 us
  waiting for transfers between devices  80.3 us (42%)
  Pallas kernels  64.7 us (34%)
  starting transfers between devices  35.4 us (18%)
  local copies, waits for them, and re-layouts  8.49 us (4%)
    ppermute x27, waiting for transfers between devices, swap(): return lax.ppermute(x, axis, [(p, p ^ k) for p in range(size)])  80.3 us
    ppermute x27, starting transfers between devices, swap(): return lax.ppermute(x, axis, [(p, p ^ k) for p in range(size)])  27.3 us
    pallas_call x1, Pallas kernels, near_call(): pl.pallas_call(functools.partial(near_kernel, dims, n, owned), out_shape=...  23.5 us
    pallas_call x1, Pallas kernels, far_call(): pl.pallas_call(functools.partial(far_kernel, dims, n, owned), out_shape=(...  14.9 us
    pallas_call x1, Pallas kernels, encode_call(): pl.pallas_call(functools.partial(encode_kernel, (n, length, owned)), out_...  6.31 us
    pallas_call x1, Pallas kernels, pack_call(): pl.pallas_call(pack_kernel, out_shape=(jax.ShapeDtypeStruct((height, wide...  4.92 us
    pallas_call x1, Pallas kernels, frame_grad_call(): pl.pallas_call(functools.partial(frame_grad_kernel, len(returned)), out_s...  4.89 us
    pallas_call x2, Pallas kernels, unpack_call(): pl.pallas_call(functools.partial(unpack_kernel, (n, owned, part, half)),...  4.75 us
  transfers between devices with their start and end apart: 29, of which 14 were waited for; matrix products, arithmetic and copies ran while one was open for 2% of the time, Pallas kernels for 30%

profile of v7, /device:TPU:8, one launch (start us, length us, event | category | flops | bytes accessed | tf_op | source)
XLA Modules:
  0.0 191.3 jit_solution(2331391488149447680)
XLA Ops:
  0.6 0.7 pad_add_fusion
  1.4 0.6 broadcast_in_dim.20
  2.0 3.7 %all-to-all-start = ((s32[4,1,8]{2,1,0:T(1,128)}), s32[4,1,8]{2,1,0:T(1,128)S(1)}, u32[]{:S(2)}, u32[]{:S(2)}) async-start(s32[4,1,8]{2,1,0:T(1,128)} %broadcast_in_dim.20), calls=%async_computation | async-start | bytes 4096 | tf_op jit(solution)/shard_map/all_to_all | solution.py:876
  5.7 4.9 %pack.1 = (bf16[304,768]{1,0:T(8,128)(2,1)}, bf16[512,1536]{1,0:T(8,128)(2,1)}, bf16[4,144,1536]{2,1,0:T(8,128)(2,1)}) custom-call(bf16[192,3072]{1,0:T(8,128)(2,1)} %refs_4_.3, bf16[192,1536]{1,0:T(8,128)(2,1)} %project_hbm.1, bf16[31,192]{1,0:T(8,128)(2,1)} %bitcast.38, bf16[192]{0:T(256)(128)(2,1)} %bias_ref.1, bf16[192]{0:T(256)(128)(2,1)} %gain_ref.1, ...), custom_call_target="tpu_custom_call" | custom-call | flops 1 | bytes 1 | tf_op jit(solution)/shard_map/pack/pallas_call | solution.py:559
  10.6 2.1 %collective-permute-start.3 = (bf16[512,1536]{1,0:T(8,128)(2,1)}, bf16[512,1536]{1,0:T(8,128)(2,1)S(1)}, u32[]{:S(2)}, u32[]{:S(2)}) collective-permute-start(bf16[512,1536]{1,0:T(8,128)(2,1)} %get-tuple-element.60), channel_id=1, source_target_pairs={{0,8},{8,0},{16,24},{24,16},{1,9},{9,1},{17,25},{25,17},{2,10},{10... | collective-permute-start | bytes 4718600 | tf_op jit(solution)/shard_map/ppermute | solution.py:992
  12.7 1.5 collective-permute-start.4
  14.2 0.4 collective-permute-start
  14.6 2.6 %collective-permute-start.1 = (bf16[304,768]{1,0:T(8,128)(2,1)}, bf16[304,768]{1,0:T(8,128)(2,1)S(1)}, u32[]{:S(2)}, u32[]{:S(2)}) collective-permute-start(bf16[304,768]{1,0:T(8,128)(2,1)} %get-tuple-element.63.refs_6_.refs_9_.refs_10_), channel_id=1, source_target_pairs={{0,4},{1,5},{2,6},{3,7},{4,0},{5,1},{6,2},{7,3},{8,12},{9,13},{10,... | collective-permute-start | bytes 1400840 | tf_op jit(solution)/shard_map/ppermute | solution.py:992
  17.2 0.5 collective-permute-start.2
  17.7 14.8 %collective-permute-done.refs_7_.refs_10_.refs_11_ = bf16[304,768]{1,0:T(8,128)(2,1)S(1)} collective-permute-done((bf16[304,768]{1,0:T(8,128)(2,1)}, bf16[304,768]{1,0:T(8,128)(2,1)S(1)}, u32[]{:S(2)}, u32[]{:S(2)}) %collective-permute-start) | collective-permute-done | bytes 466976 | tf_op jit(solution)/shard_map/ppermute | solution.py:992
  32.5 16.2 %collective-permute-done.1.refs_8_.refs_11_.refs_12_ = bf16[304,768]{1,0:T(8,128)(2,1)S(1)} collective-permute-done((bf16[304,768]{1,0:T(8,128)(2,1)}, bf16[304,768]{1,0:T(8,128)(2,1)S(1)}, u32[]{:S(2)}, u32[]{:S(2)}) %collective-permute-start.1) | collective-permute-done | bytes 466976 | tf_op jit(solution)/shard_map/ppermute | solution.py:992
  48.7 8.3 %collective-permute-done.2.refs_9_.refs_12_.refs_13_ = bf16[304,768]{1,0:T(8,128)(2,1)S(1)} collective-permute-done((bf16[304,768]{1,0:T(8,128)(2,1)}, bf16[304,768]{1,0:T(8,128)(2,1)S(1)}, u32[]{:S(2)}, u32[]{:S(2)}) %collective-permute-start.2) | collective-permute-done | bytes 466976 | tf_op jit(solution)/shard_map/ppermute | solution.py:992
  57.0 0.7 copy-done.8
  57.7 4.4 %all-to-all-start.1 = ((bf16[4,144,1536]{2,1,0:T(8,128)(2,1)}), bf16[4,144,1536]{2,1,0:T(8,128)(2,1)}, u32[]{:S(2)}, u32[]{:S(2)}) async-start(bf16[4,144,1536]{2,1,0:T(8,128)(2,1)} %get-tuple-element.75), calls=%async_computation.1 | async-start | bytes 3538944 | tf_op jit(solution)/shard_map/all_to_all | solution.py:887
  62.1 0.1 collective-permute-start.7
  62.2 0.5 collective-permute-start.8
  62.7 0.1 collective-permute-start.9
  62.8 0.4 collective-permute-start.6
  63.2 0.9 slice.30
  64.2 0.6 collective-permute-start.5
  64.7 0.9 slice.31
  65.6 0.4 collective-permute-start.10
  66.0 0.4 collective-permute-done.6.refs_10_.refs_13_.refs_14_
  66.4 23.5 %near_sources.1 = (bf16[768,1536]{1,0:T(8,128)(2,1)}, bf16[768,384]{1,0:T(8,128)(2,1)}, bf16[768,768]{1,0:T(8,128)(2,1)}, bf16[256,1536]{1,0:T(8,128)(2,1)}, bf1...) custom-call(s32[4,8]{1,0:T(4,128)} %bitcast.35, ...), custom_call_target="tpu_custom_call" | custom-call | flops 1 | bytes 1 | tf_op jit(solution)/shard_map/near_sources/pallas_call | solution.py:283
  89.9 1.4 collective-permute-start.11
  91.3 1.5 collective-permute-start.12
  92.8 0.9 copy-done.10
  93.7 14.9 %far_source.1 = (bf16[320,1536]{1,0:T(8,128)(2,1)}, bf16[4,304,768]{2,1,0:T(8,128)(2,1)}, bf16[4,304,768]{2,1,0:T(8,128)(2,1)}, bf16[64,1536]{1,0:T(8,128)(2,1)}...) custom-call(s32[4,8]{1,0:T(4,128)} %bitcast.36, bf16[256,1536]{1,0:T(8,128)(2,1)} %copy-done.10, ...), custom_call_target="tpu_custom_call" | custom-call | flops 1 | bytes 1 | tf_op jit(solution)/shard_map/far_source/pallas_call | solution.py:438
  108.6 1.3 collective-permute-done.11.refs_1_
  109.9 0.4 collective-permute-done.12.refs_2_
  110.3 4.2 %collective-permute-done.13.got_hbm = bf16[4,304,768]{2,1,0:T(8,128)(2,1)} collective-permute-done((bf16[4,304,768]{2,1,0:T(8,128)(2,1)}, bf16[4,304,768]{2,1,0:T(8,128)(2,1)}, u32[]{:S(2)}, u32[]{:S(2)}) %collective-permute-start.13) | collective-permute-done | bytes 1867808 | tf_op jit(solution)/shard_map/ppermute | solution.py:992
  114.5 3.0 %add_cores.1 = (bf16[304,768]{1,0:T(8,128)(2,1)}, bf16[304,768]{1,0:T(8,128)(2,1)}, bf16[304,768]{1,0:T(8,128)(2,1)}, bf16[304,768]{1,0:T(8,128)(2,1)}) custom-call(bf16[4,304,768]{2,1,0:T(8,128)(2,1)} %get-tuple-element.78.keep_hbm, bf16[4,304,768]{2,1,0:T(8,128)(2,1)} %collective-permute-done.13.got_hbm), custom_call_target="tpu_custom_call" | custom-call | flops 1 | bytes 1 | tf_op jit(solution)/shard_map/add_cores/pallas_call | solution.py:816
  117.5 0.2 collective-permute-start.18
  117.7 1.5 collective-permute-start.17
  119.2 3.0 %collective-permute-start.19 = (bf16[304,768]{1,0:T(8,128)(2,1)}, bf16[304,768]{1,0:T(8,128)(2,1)}, u32[]{:S(2)}, u32[]{:S(2)}) collective-permute-start(bf16[304,768]{1,0:T(8,128)(2,1)} %get-tuple-element.95), channel_id=1, source_target_pairs={{0,4},{1,5},{2,6},{3,7},{4,0},{5,1},{6,2},{7,3},{8,12},{9,13},{10,... | collective-permute-start | bytes 1400840 | tf_op jit(solution)/shard_map/ppermute | solution.py:992
  122.2 0.5 collective-permute-start.20
  122.6 16.7 %collective-permute-done.14.refs_1_ = bf16[304,768]{1,0:T(8,128)(2,1)S(1)} collective-permute-done((bf16[304,768]{1,0:T(8,128)(2,1)}, bf16[304,768]{1,0:T(8,128)(2,1)S(1)}, u32[]{:S(2)}, u32[]{:S(2)}) %collective-permute-start.14) | collective-permute-done | bytes 466976 | tf_op jit(solution)/shard_map/ppermute | solution.py:992
  139.3 1.5 collective-permute-start.15
  140.8 2.4 %collective-permute-done.17.refs_7_.refs_3_ = bf16[320,1536]{1,0:T(8,128)(2,1)S(1)} collective-permute-done((bf16[320,1536]{1,0:T(8,128)(2,1)}, bf16[320,1536]{1,0:T(8,128)(2,1)S(1)}, u32[]{:S(2)}, u32[]{:S(2)}) %collective-permute-start.17) | collective-permute-done | bytes 983072 | tf_op jit(solution)/shard_map/ppermute | solution.py:992
  143.2 1.7 collective-permute-start.16
  144.9 0.6 pad_clamp_fusion
  145.5 4.9 %frame_grad.1 = bf16[256,1536]{1,0:T(8,128)(2,1)} custom-call(bf16[256,1536]{1,0:T(8,128)(2,1)} %bitcast.30, bf16[256,1536]{1,0:T(8,128)(2,1)} %bitcast.27, f32[1,1536]{1,0:T(1,128)} %get-tuple-element.90.gain_ref, bf16[256,1536]{1,0:T(8,128)(2,1)} %get-tuple-element.91.refs_0_, bf16[256,1536]{1,0:T(8,128)(2,1)} %collective-permute-done.11.refs_1_, ...), custom_call_target="tpu_custom_call" | custom-call | flops 1 | bytes 1 | tf_op jit(solution)/shard_map/frame_grad/pallas_call | solution.py:682
  150.4 6.3 %encode.1 = bf16[256,1536]{1,0:T(8,128)(2,1)} custom-call(s32[4,8]{1,0:T(4,128)} %bitcast.37, bf16[256,1536]{1,0:T(8,128)(2,1)} %bitcast.31, bf16[512,1536]{1,0:T(8,128)(2,1)} %copy-done.4, bf16[512,1536]{1,0:T(8,128)(2,1)} %copy-done.5, bf16[256,1536]{1,0:T(8,128)(2,1)} %copy-done.10, bf16[64,1536]{1,0:T(8,128)(2,1)} %get-tuple-element.81.refs_4_, ...), custom_call_target="tpu_custom_call" | custom-call | flops 1 | bytes 1 | tf_op jit(solution)/shard_map/encode/pallas_call | solution.py:645
  156.7 6.7 %collective-permute-done.20.refs_3_ = bf16[304,768]{1,0:T(8,128)(2,1)} collective-permute-done((bf16[304,768]{1,0:T(8,128)(2,1)}, bf16[304,768]{1,0:T(8,128)(2,1)}, u32[]{:S(2)}, u32[]{:S(2)}) %collective-permute-start.20) | collective-permute-done | bytes 466976 | tf_op jit(solution)/shard_map/ppermute | solution.py:992
  163.4 2.4 %add_chips.1 = (bf16[304,384]{1,0:T(8,128)(2,1)}, bf16[304,384]{1,0:T(8,128)(2,1)}) custom-call(bf16[304,768]{1,0:T(8,128)(2,1)} %get-tuple-element.94.refs_0_, bf16[304,768]{1,0:T(8,128)(2,1)} %copy-done.11, bf16[304,768]{1,0:T(8,128)(2,1)} %collective-permute-done.19.refs_2_, bf16[304,768]{1,0:T(8,128)(2,1)} %collective-permute-done.20.refs_3_), custom_call_target="tpu_custom_call" | custom-call | flops 1 | bytes 1 | tf_op jit(solution)/shard_map/add_chips/pallas_call | solution.py:841
  165.8 1.5 collective-permute-start.26
  167.2 1.5 collective-permute-start.25
  168.8 0.6 collective-permute-start.24
  169.3 0.7 slice_bitcast_fusion.3
  170.1 1.5 collective-permute-start.21
  171.6 0.6 collective-permute-start.22
  172.1 3.4 %collective-permute-done.26.refs_3_ = bf16[304,384]{1,0:T(8,128)(2,1)S(1)} collective-permute-done((bf16[304,384]{1,0:T(8,128)(2,1)}, bf16[304,384]{1,0:T(8,128)(2,1)S(1)}, u32[]{:S(2)}, u32[]{:S(2)}) %collective-permute-start.26) | collective-permute-done | bytes 233504 | tf_op jit(solution)/shard_map/ppermute | solution.py:992
  175.5 1.5 collective-permute-start.23
  177.0 1.5 collective-permute-done.25.refs_2_
  178.5 1.9 collective-permute-done.24.refs_1_
  180.4 0.7 gather_fusion
  181.1 0.1 select_convert_fusion
  181.2 1.3 copy-done
  182.5 0.9 copy-done.2
  183.4 2.1 %unpack.2 = (f32[192,3072]{1,0:T(8,128)}, f32[192,1536]{1,0:T(8,128)}, f32[192,1]{1,0:T(8,128)S(1)}) custom-call(bf16[304,384]{1,0:T(8,128)(2,1)S(1)} %copy-done.2, bf16[304,384]{1,0:T(8,128)(2,1)S(1)} %collective-permute-done.24.refs_1_, bf16[304,384]{1,0:T(8,128)(2,1)S(1)} %collective-permute-done.25.refs_2_, ...), custom_call_target="tpu_custom_call" | custom-call | flops 1 | bytes 1 | tf_op jit(solution)/shard_map/unpack/pallas_call | solution.py:753
  185.6 0.1 reshape.67
  185.7 0.6 slice.47
  186.3 2.2 %collective-permute-done.23.refs_3_ = bf16[304,384]{1,0:T(8,128)(2,1)S(1)} collective-permute-done((bf16[304,384]{1,0:T(8,128)(2,1)}, bf16[304,384]{1,0:T(8,128)(2,1)S(1)}, u32[]{:S(2)}, u32[]{:S(2)}) %collective-permute-start.23) | collective-permute-done | bytes 233504 | tf_op jit(solution)/shard_map/ppermute | solution.py:992
  188.5 2.7 %unpack.3 = (f32[192,3072]{1,0:T(8,128)}, f32[192,1536]{1,0:T(8,128)}, f32[1,192]{1,0:T(1,128)}) custom-call(bf16[304,384]{1,0:T(8,128)(2,1)S(1)} %copy-done.3, bf16[304,384]{1,0:T(8,128)(2,1)S(1)} %collective-permute-done.21.refs_1_, bf16[304,384]{1,0:T(8,128)(2,1)S(1)} %collective-permute-done.22.refs_2_, ...), custom_call_target="tpu_custom_call", output_to_operand_aliasing={{0}: (7, {}), {1}: (8, {})} | custom-call | flops 1 | bytes 1 | tf_op jit(solution)/shard_map/unpack/pallas_call | solution.py:753
  (54 shorter events, 0.2 us)
Async XLA Ops:
  2.0 8.6 %all-to-all-start = ((s32[4,1,8]{2,1,0:T(1,128)}), s32[4,1,8]{2,1,0:T(1,128)S(1)}, u32[]{:S(2)}, u32[]{:S(2)}) async-start(s32[4,1,8]{2,1,0:T(1,128)} %broadcast_in_dim.20), calls=%async_computation | async-start | bytes 4096 | tf_op jit(solution)/shard_map/all_to_all | solution.py:876
  10.6 47.1 %copy-start.13 = (s32[4,1,8]{2,1,0:T(1,128)}, s32[4,1,8]{2,1,0:T(1,128)S(1)}, u32[]{:S(2)}) copy-start(s32[4,1,8]{2,1,0:T(1,128)S(1)} %all-to-all-done) | copy-start | bytes 388
  10.6 46.4 %collective-permute-start.3 = (bf16[512,1536]{1,0:T(8,128)(2,1)}, bf16[512,1536]{1,0:T(8,128)(2,1)S(1)}, u32[]{:S(2)}, u32[]{:S(2)}) collective-permute-start(bf16[512,1536]{1,0:T(8,128)(2,1)} %get-tuple-element.60), channel_id=1, source_target_pairs={{0,8},{8,0},{16,24},{24,16},{1,9},{9,1},{17,25},{25,17},{2,10},{10... | collective-permute-start | bytes 4718600 | tf_op jit(solution)/shard_map/ppermute | solution.py:992
  12.7 44.3 %collective-permute-start.4 = (bf16[512,1536]{1,0:T(8,128)(2,1)}, bf16[512,1536]{1,0:T(8,128)(2,1)S(1)}, u32[]{:S(2)}, u32[]{:S(2)}) collective-permute-start(bf16[512,1536]{1,0:T(8,128)(2,1)} %get-tuple-element.60), channel_id=1, source_target_pairs={{0,16},{8,24},{16,0},{24,8},{1,17},{9,25},{17,1},{25,9},{2,18},{10... | collective-permute-start | bytes 4718600 | tf_op jit(solution)/shard_map/ppermute | solution.py:992
  14.2 18.3 %collective-permute-start = (bf16[304,768]{1,0:T(8,128)(2,1)}, bf16[304,768]{1,0:T(8,128)(2,1)S(1)}, u32[]{:S(2)}, u32[]{:S(2)}) collective-permute-start(bf16[304,768]{1,0:T(8,128)(2,1)} %get-tuple-element.63.refs_6_.refs_9_.refs_10_), channel_id=1, source_target_pairs={{0,2},{1,3},{2,0},{3,1},{4,6},{5,7},{6,4},{7,5},{8,10},{9,11},{10,... | collective-permute-start | bytes 1400840 | tf_op jit(solution)/shard_map/ppermute | solution.py:992
  14.6 34.1 %collective-permute-start.1 = (bf16[304,768]{1,0:T(8,128)(2,1)}, bf16[304,768]{1,0:T(8,128)(2,1)S(1)}, u32[]{:S(2)}, u32[]{:S(2)}) collective-permute-start(bf16[304,768]{1,0:T(8,128)(2,1)} %get-tuple-element.63.refs_6_.refs_9_.refs_10_), channel_id=1, source_target_pairs={{0,4},{1,5},{2,6},{3,7},{4,0},{5,1},{6,2},{7,3},{8,12},{9,13},{10,... | collective-permute-start | bytes 1400840 | tf_op jit(solution)/shard_map/ppermute | solution.py:992
  17.2 39.8 %collective-permute-start.2 = (bf16[304,768]{1,0:T(8,128)(2,1)}, bf16[304,768]{1,0:T(8,128)(2,1)S(1)}, u32[]{:S(2)}, u32[]{:S(2)}) collective-permute-start(bf16[304,768]{1,0:T(8,128)(2,1)} %get-tuple-element.63.refs_6_.refs_9_.refs_10_), channel_id=1, source_target_pairs={{0,6},{1,7},{2,4},{3,5},{4,2},{5,3},{6,0},{7,1},{8,14},{9,15},{10,... | collective-permute-start | bytes 1400840 | tf_op jit(solution)/shard_map/ppermute | solution.py:992
  32.4 24.5 %copy-start.6 = (bf16[304,768]{1,0:T(8,128)(2,1)}, bf16[304,768]{1,0:T(8,128)(2,1)S(1)}, u32[]{:S(2)}) copy-start(bf16[304,768]{1,0:T(8,128)(2,1)S(1)} %collective-permute-done.refs_7_.refs_10_.refs_11_) | copy-start | bytes 1400836
  48.7 8.3 %copy-start.7 = (bf16[304,768]{1,0:T(8,128)(2,1)}, bf16[304,768]{1,0:T(8,128)(2,1)S(1)}, u32[]{:S(2)}) copy-start(bf16[304,768]{1,0:T(8,128)(2,1)S(1)} %collective-permute-done.1.refs_8_.refs_11_.refs_12_) | copy-start | bytes 1400836
  57.0 0.8 copy-start.8
  57.0 6.3 %copy-start.4 = (bf16[512,1536]{1,0:T(8,128)(2,1)}, bf16[512,1536]{1,0:T(8,128)(2,1)S(1)}, u32[]{:S(2)}) copy-start(bf16[512,1536]{1,0:T(8,128)(2,1)S(1)} %collective-permute-done.3.refs_1_.refs_4_.refs_5_) | copy-start | bytes 4718596
  57.7 7.0 %copy-start.5 = (bf16[512,1536]{1,0:T(8,128)(2,1)}, bf16[512,1536]{1,0:T(8,128)(2,1)S(1)}, u32[]{:S(2)}) copy-start(bf16[512,1536]{1,0:T(8,128)(2,1)S(1)} %collective-permute-done.4.refs_2_.refs_5_.refs_6_) | copy-start | bytes 4718596
  57.7 52.6 %all-to-all-start.1 = ((bf16[4,144,1536]{2,1,0:T(8,128)(2,1)}), bf16[4,144,1536]{2,1,0:T(8,128)(2,1)}, u32[]{:S(2)}, u32[]{:S(2)}) async-start(bf16[4,144,1536]{2,1,0:T(8,128)(2,1)} %get-tuple-element.75), calls=%async_computation.1 | async-start | bytes 3538944 | tf_op jit(solution)/shard_map/all_to_all | solution.py:887
  62.1 3.5 %collective-permute-start.7 = (bf16[304,768]{1,0:T(8,128)(2,1)}, bf16[304,768]{1,0:T(8,128)(2,1)}, u32[]{:S(2)}, u32[]{:S(2)}) collective-permute-start(bf16[304,768]{1,0:T(8,128)(2,1)} %copy-done.6), channel_id=1, source_target_pairs={{0,1},{1,0},{2,3},{3,2},{4,5},{5,4},{6,7},{7,6},{8,9},{9,8},{10,11... | collective-permute-start | bytes 1400840 | tf_op jit(solution)/shard_map/ppermute | solution.py:992
  62.2 3.8 %collective-permute-start.8 = (bf16[304,768]{1,0:T(8,128)(2,1)}, bf16[304,768]{1,0:T(8,128)(2,1)}, u32[]{:S(2)}, u32[]{:S(2)}) collective-permute-start(bf16[304,768]{1,0:T(8,128)(2,1)} %copy-done.7), channel_id=1, source_target_pairs={{0,1},{1,0},{2,3},{3,2},{4,5},{5,4},{6,7},{7,6},{8,9},{9,8},{10,11... | collective-permute-start | bytes 1400840 | tf_op jit(solution)/shard_map/ppermute | solution.py:992
  62.7 3.3 %collective-permute-start.9 = (bf16[304,768]{1,0:T(8,128)(2,1)}, bf16[304,768]{1,0:T(8,128)(2,1)}, u32[]{:S(2)}, u32[]{:S(2)}) collective-permute-start(bf16[304,768]{1,0:T(8,128)(2,1)} %copy-done.8), channel_id=1, source_target_pairs={{0,1},{1,0},{2,3},{3,2},{4,5},{5,4},{6,7},{7,6},{8,9},{9,8},{10,11... | collective-permute-start | bytes 1400840 | tf_op jit(solution)/shard_map/ppermute | solution.py:992
  62.8 3.6 %collective-permute-start.6 = (bf16[304,768]{1,0:T(8,128)(2,1)}, bf16[304,768]{1,0:T(8,128)(2,1)}, u32[]{:S(2)}, u32[]{:S(2)}) collective-permute-start(bf16[304,768]{1,0:T(8,128)(2,1)} %get-tuple-element.63.refs_6_.refs_9_.refs_10_), channel_id=1, source_target_pairs={{0,1},{1,0},{2,3},{3,2},{4,5},{5,4},{6,7},{7,6},{8,9},{9,8},{10,11... | collective-permute-start | bytes 1400840 | tf_op jit(solution)/shard_map/ppermute | solution.py:992
  64.2 28.6 %collective-permute-start.5 = (bf16[256,1536]{1,0:T(8,128)(2,1)}, bf16[256,1536]{1,0:T(8,128)(2,1)S(1)}, u32[]{:S(2)}, u32[]{:S(2)}) collective-permute-start(bf16[256,1536]{1,0:T(8,128)(2,1)} %slice.30), channel_id=1, source_target_pairs={{0,16},{8,24},{16,0},{24,8},{1,17},{9,25},{17,1},{25,9},{2,18},{10... | collective-permute-start | bytes 2359304 | tf_op jit(solution)/shard_map/ppermute | solution.py:992
  65.6 27.1 %collective-permute-start.10 = (bf16[256,1536]{1,0:T(8,128)(2,1)}, bf16[256,1536]{1,0:T(8,128)(2,1)}, u32[]{:S(2)}, u32[]{:S(2)}) collective-permute-start(bf16[256,1536]{1,0:T(8,128)(2,1)} %slice.31), channel_id=1, source_target_pairs={{0,8},{8,0},{16,24},{24,16},{1,9},{9,1},{17,25},{25,17},{2,10},{10... | collective-permute-start | bytes 2359304 | tf_op jit(solution)/shard_map/ppermute | solution.py:992
  89.9 20.0 %collective-permute-start.11 = (bf16[256,1536]{1,0:T(8,128)(2,1)}, bf16[256,1536]{1,0:T(8,128)(2,1)}, u32[]{:S(2)}, u32[]{:S(2)}) collective-permute-start(bf16[256,1536]{1,0:T(8,128)(2,1)} %get-tuple-element.76), channel_id=1, source_target_pairs={{0,8},{8,0},{16,24},{24,16},{1,9},{9,1},{17,25},{25,17},{2,10},{10... | collective-permute-start | bytes 2359304 | tf_op jit(solution)/shard_map/ppermute | solution.py:992
  91.3 19.0 %collective-permute-start.12 = (bf16[256,1536]{1,0:T(8,128)(2,1)}, bf16[256,1536]{1,0:T(8,128)(2,1)}, u32[]{:S(2)}, u32[]{:S(2)}) collective-permute-start(bf16[256,1536]{1,0:T(8,128)(2,1)} %get-tuple-element.77), channel_id=1, source_target_pairs={{0,16},{8,24},{16,0},{24,8},{1,17},{9,25},{17,1},{25,9},{2,18},{10... | collective-permute-start | bytes 2359304 | tf_op jit(solution)/shard_map/ppermute | solution.py:992
  92.8 0.9 copy-start.10
  110.3 4.2 %collective-permute-start.13 = (bf16[4,304,768]{2,1,0:T(8,128)(2,1)}, bf16[4,304,768]{2,1,0:T(8,128)(2,1)}, u32[]{:S(2)}, u32[]{:S(2)}) collective-permute-start(bf16[4,304,768]{2,1,0:T(8,128)(2,1)} %get-tuple-element.79), channel_id=1, source_target_pairs={{0,1},{1,0},{2,3},{3,2},{4,5},{5,4},{6,7},{7,6},{8,9},{9,8},{10,11... | collective-permute-start | bytes 5603336 | tf_op jit(solution)/shard_map/ppermute | solution.py:992
  117.5 32.9 %collective-permute-start.18 = (bf16[4,144,1536]{2,1,0:T(8,128)(2,1)}, bf16[4,144,1536]{2,1,0:T(8,128)(2,1)}, u32[]{:S(2)}, u32[]{:S(2)}) collective-permute-start(bf16[4,144,1536]{2,1,0:T(8,128)(2,1)} %all-to-all-done.1.refs_8_), channel_id=1, source_target_pairs={{0,1},{1,0},{2,3},{3,2},{4,5},{5,4},{6,7},{7,6},{8,9},{9,8},{10,11... | collective-permute-start | bytes 5308424 | tf_op jit(solution)/shard_map/ppermute | solution.py:992
  117.7 25.5 %collective-permute-start.17 = (bf16[320,1536]{1,0:T(8,128)(2,1)}, bf16[320,1536]{1,0:T(8,128)(2,1)S(1)}, u32[]{:S(2)}, u32[]{:S(2)}) collective-permute-start(bf16[320,1536]{1,0:T(8,128)(2,1)} %get-tuple-element.87), channel_id=1, source_target_pairs={{0,24},{8,16},{16,8},{24,0},{1,25},{9,17},{17,9},{25,1},{2,26},{10... | collective-permute-start | bytes 2949128 | tf_op jit(solution)/shard_map/ppermute | solution.py:992
  119.2 20.2 %collective-permute-start.14 = (bf16[304,768]{1,0:T(8,128)(2,1)}, bf16[304,768]{1,0:T(8,128)(2,1)S(1)}, u32[]{:S(2)}, u32[]{:S(2)}) collective-permute-start(bf16[304,768]{1,0:T(8,128)(2,1)} %get-tuple-element.80), channel_id=1, source_target_pairs={{0,2},{1,3},{2,0},{3,1},{4,6},{5,7},{6,4},{7,5},{8,10},{9,11},{10,... | collective-permute-start | bytes 1400840 | tf_op jit(solution)/shard_map/ppermute | solution.py:992
  119.2 37.6 %collective-permute-start.19 = (bf16[304,768]{1,0:T(8,128)(2,1)}, bf16[304,768]{1,0:T(8,128)(2,1)}, u32[]{:S(2)}, u32[]{:S(2)}) collective-permute-start(bf16[304,768]{1,0:T(8,128)(2,1)} %get-tuple-element.95), channel_id=1, source_target_pairs={{0,4},{1,5},{2,6},{3,7},{4,0},{5,1},{6,2},{7,3},{8,12},{9,13},{10,... | collective-permute-start | bytes 1400840 | tf_op jit(solution)/shard_map/ppermute | solution.py:992
  122.2 41.2 %collective-permute-start.20 = (bf16[304,768]{1,0:T(8,128)(2,1)}, bf16[304,768]{1,0:T(8,128)(2,1)}, u32[]{:S(2)}, u32[]{:S(2)}) collective-permute-start(bf16[304,768]{1,0:T(8,128)(2,1)} %get-tuple-element.96), channel_id=1, source_target_pairs={{0,6},{1,7},{2,4},{3,5},{4,2},{5,3},{6,0},{7,1},{8,14},{9,15},{10,... | collective-permute-start | bytes 1400840 | tf_op jit(solution)/shard_map/ppermute | solution.py:992
  139.3 3.9 %copy-start.11 = (bf16[304,768]{1,0:T(8,128)(2,1)}, bf16[304,768]{1,0:T(8,128)(2,1)S(1)}, u32[]{:S(2)}) copy-start(bf16[304,768]{1,0:T(8,128)(2,1)S(1)} %collective-permute-done.14.refs_1_) | copy-start | bytes 1400836
  139.3 11.0 %collective-permute-start.15 = (bf16[64,1536]{1,0:T(8,128)(2,1)}, bf16[64,1536]{1,0:T(8,128)(2,1)}, u32[]{:S(2)}, u32[]{:S(2)}) collective-permute-start(bf16[64,1536]{1,0:T(8,128)(2,1)} %get-tuple-element.85), channel_id=1, source_target_pairs={{0,8},{8,0},{16,24},{24,16},{1,9},{9,1},{17,25},{25,17},{2,10},{10... | collective-permute-start | bytes 589832 | tf_op jit(solution)/shard_map/ppermute | solution.py:992
  143.2 2.3 %copy-start.9 = (bf16[320,1536]{1,0:T(8,128)(2,1)}, bf16[320,1536]{1,0:T(8,128)(2,1)S(1)}, u32[]{:S(2)}) copy-start(bf16[320,1536]{1,0:T(8,128)(2,1)S(1)} %collective-permute-done.17.refs_7_.refs_3_) | copy-start | bytes 2949124
  143.2 7.2 %collective-permute-start.16 = (bf16[64,1536]{1,0:T(8,128)(2,1)}, bf16[64,1536]{1,0:T(8,128)(2,1)}, u32[]{:S(2)}, u32[]{:S(2)}) collective-permute-start(bf16[64,1536]{1,0:T(8,128)(2,1)} %get-tuple-element.86), channel_id=1, source_target_pairs={{0,16},{8,24},{16,0},{24,8},{1,17},{9,25},{17,1},{25,9},{2,18},{10... | collective-permute-start | bytes 589832 | tf_op jit(solution)/shard_map/ppermute | solution.py:992
  156.7 10.5 %copy-start.14 = (bf16[192]{0:T(256)(128)(2,1)S(1)}, bf16[192]{0:T(256)(128)(2,1)}, u32[]{:S(2)}) copy-start(bf16[192]{0:T(256)(128)(2,1)} %gain_ref.1) | copy-start | bytes 1156
  165.8 22.7 %copy-start.3 = (bf16[304,384]{1,0:T(8,128)(2,1)S(1)}, bf16[304,384]{1,0:T(8,128)(2,1)}, u32[]{:S(2)}) copy-start(bf16[304,384]{1,0:T(8,128)(2,1)} %get-tuple-element.97.refs_0_) | copy-start | bytes 700420
  165.8 9.8 %collective-permute-start.26 = (bf16[304,384]{1,0:T(8,128)(2,1)}, bf16[304,384]{1,0:T(8,128)(2,1)S(1)}, u32[]{:S(2)}, u32[]{:S(2)}) collective-permute-start(bf16[304,384]{1,0:T(8,128)(2,1)} %get-tuple-element.98.refs_0_), channel_id=1, source_target_pairs={{0,24},{8,16},{16,8},{24,0},{1,25},{9,17},{17,9},{25,1},{2,26},{10... | collective-permute-start | bytes 700424 | tf_op jit(solution)/shard_map/ppermute | solution.py:992
  167.2 11.3 %collective-permute-start.25 = (bf16[304,384]{1,0:T(8,128)(2,1)}, bf16[304,384]{1,0:T(8,128)(2,1)S(1)}, u32[]{:S(2)}, u32[]{:S(2)}) collective-permute-start(bf16[304,384]{1,0:T(8,128)(2,1)} %get-tuple-element.98.refs_0_), channel_id=1, source_target_pairs={{0,16},{8,24},{16,0},{24,8},{1,17},{9,25},{17,1},{25,9},{2,18},{10... | collective-permute-start | bytes 700424 | tf_op jit(solution)/shard_map/ppermute | solution.py:992
  168.8 11.6 %collective-permute-start.24 = (bf16[304,384]{1,0:T(8,128)(2,1)}, bf16[304,384]{1,0:T(8,128)(2,1)S(1)}, u32[]{:S(2)}, u32[]{:S(2)}) collective-permute-start(bf16[304,384]{1,0:T(8,128)(2,1)} %get-tuple-element.98.refs_0_), channel_id=1, source_target_pairs={{0,8},{8,0},{16,24},{24,16},{1,9},{9,1},{17,25},{25,17},{2,10},{10... | collective-permute-start | bytes 700424 | tf_op jit(solution)/shard_map/ppermute | solution.py:992
  170.1 16.2 %collective-permute-start.21 = (bf16[304,384]{1,0:T(8,128)(2,1)}, bf16[304,384]{1,0:T(8,128)(2,1)S(1)}, u32[]{:S(2)}, u32[]{:S(2)}) collective-permute-start(bf16[304,384]{1,0:T(8,128)(2,1)} %get-tuple-element.97.refs_0_), channel_id=1, source_target_pairs={{0,8},{8,0},{16,24},{24,16},{1,9},{9,1},{17,25},{25,17},{2,10},{10... | collective-permute-start | bytes 700424 | tf_op jit(solution)/shard_map/ppermute | solution.py:992
  171.6 14.8 %collective-permute-start.22 = (bf16[304,384]{1,0:T(8,128)(2,1)}, bf16[304,384]{1,0:T(8,128)(2,1)S(1)}, u32[]{:S(2)}, u32[]{:S(2)}) collective-permute-start(bf16[304,384]{1,0:T(8,128)(2,1)} %get-tuple-element.97.refs_0_), channel_id=1, source_target_pairs={{0,16},{8,24},{16,0},{24,8},{1,17},{9,25},{17,1},{25,9},{2,18},{10... | collective-permute-start | bytes 700424 | tf_op jit(solution)/shard_map/ppermute | solution.py:992
  175.5 13.0 %collective-permute-start.23 = (bf16[304,384]{1,0:T(8,128)(2,1)}, bf16[304,384]{1,0:T(8,128)(2,1)S(1)}, u32[]{:S(2)}, u32[]{:S(2)}) collective-permute-start(bf16[304,384]{1,0:T(8,128)(2,1)} %get-tuple-element.97.refs_0_), channel_id=1, source_target_pairs={{0,24},{8,16},{16,8},{24,0},{1,25},{9,17},{17,9},{25,1},{2,26},{10... | collective-permute-start | bytes 700424 | tf_op jit(solution)/shard_map/ppermute | solution.py:992
  181.2 1.3 copy-start
  182.5 0.9 copy-start.2
  183.4 5.1 %copy-start.1 = (bf16[192,3072]{1,0:T(8,128)(2,1)S(1)}, bf16[192,3072]{1,0:T(8,128)(2,1)}, u32[]{:S(2)}) copy-start(bf16[192,3072]{1,0:T(8,128)(2,1)} %refs_4_.3) | copy-start | bytes 3538948
  185.7 5.4 %copy-start.12 = (f32[192,32]{0,1:T(8,128)}, f32[192,32]{0,1:T(8,128)S(1)}, u32[]{:S(2)}) copy-start(f32[192,32]{0,1:T(8,128)S(1)} %reshape.67) | copy-start | bytes 73732
